TPU v7x, 512 devices: a whole 4x8x8 slice. The times are simulated.
512 devices in a mesh: ep: 128 (over z, y, core), rep: 4 (over x).
Axes of the slice: x: 4, y: 8, z: 8, core: 2. Of those that a mesh axis runs over, the one named last changes fastest.
Arguments:
- tokens: bfloat16 [16384, 4096], P('ep'), may hold values from -54 to 54
- expert_ids: int32 [16384, 8], P('ep'), may hold values from 0 to 127, all different within a row; in each aligned block of 128 rows (0 to 127, 128 to 255, ...) at most 10 rows name the same one
- hidden_grads: bfloat16 [16384, 8, 768], P('ep', None, 'rep'), may hold values from -6 to 6
- gate_weight: bfloat16 [128, 768, 4096], P('ep', 'rep'), may hold values from -0.09375 to 0.09375
- probes: bfloat16 [128, 4096], replicated, may hold values from -1.5 to 1.5
- grad_probes: bfloat16 [128, 768], replicated, may hold values from -6 to 6
- window_counts: int32 [128], P('ep'), may hold values from 1024 to 4095
Outputs:
- input_sketch: float32 [128, 4096, 128], P('ep', 'rep')
- grad_sketch: float32 [128, 768, 128], P('ep', 'rep')
Inputs may be any that keep to these rules, and one draw needn't show every extreme that they name: `expert_ids`: each row names 8 different experts; among the 128 tokens of one index of ep no expert is named more than 10 times, and 10 is reached.
All inputs are finite; a program needn't handle non-finite values.
Results may differ from a plain program's by a relative error of at most 0.0032.
Values may be sent and summed in bfloat16 or wider, within the bound.
No kernel may reach another device: no remote copies, remote signals or barrier semaphores. Data moves between devices by JAX's collectives and lax.ppermute only.
A program may use at most 128 MiB of HBM per device.

v0:
```python
import jax
import jax.numpy as jnp
from jax import lax
from jax.sharding import PartitionSpec as P


def derivative_silu(values):
    sigmoid = jax.nn.sigmoid(values)
    return sigmoid * (1.0 + values * (1.0 - sigmoid))


def local(tokens, expert_ids, hidden_grads, gate_weight, probes, grad_probes, window_counts):
    owners = lax.axis_size("ep")
    replicas = lax.axis_size("rep")
    position = lax.axis_index("rep")
    local_tokens, features = tokens.shape
    choices_made = expert_ids.shape[1]
    units = hidden_grads.shape[2]
    sketch_width = probes.shape[0]
    capacity = min(
        local_tokens, max(2, (5 * local_tokens * choices_made + 4 * owners - 1) // (4 * owners))
    )
    assigned = local_tokens * choices_made
    flat_ids = expert_ids.reshape(assigned)
    member = (flat_ids[:, None] == jnp.arange(owners, dtype=jnp.int32)[None, :]).astype(jnp.int32)
    ranks = jnp.sum((jnp.cumsum(member, axis=0) - 1) * member, axis=1)
    targets = flat_ids * capacity + ranks
    sources = (
        jnp.full((owners * capacity,), assigned, jnp.int32)
        .at[targets]
        .set(jnp.arange(assigned, dtype=jnp.int32))
    )
    contract_last = (((1,), (1,)), ((), ()))
    contract_first = (((0,), (0,)), ((), ()))
    local_projected = lax.dot_general(
        tokens, probes, contract_last, preferred_element_type=jnp.float32
    ).astype(jnp.bfloat16)
    padded_rows = jnp.concatenate([tokens, jnp.zeros((1, features), tokens.dtype)], 0)
    padded_projected = jnp.concatenate(
        [local_projected, jnp.zeros((1, sketch_width), jnp.bfloat16)], 0
    )
    padded_grads = jnp.concatenate(
        [hidden_grads.reshape(assigned, units), jnp.zeros((1, units), hidden_grads.dtype)], 0
    )
    token_slots = sources // choices_made
    outgoing_rows = padded_rows[token_slots].reshape(owners, capacity, features)
    outgoing_projected = padded_projected[token_slots].reshape(owners, capacity, sketch_width)
    outgoing_grads = padded_grads[sources].reshape(owners, capacity, units)
    arrived_rows, arrived_projected = (
        lax.all_to_all(outgoing_rows, "ep", split_axis=0, concat_axis=0, tiled=True),
        lax.all_to_all(outgoing_projected, "ep", split_axis=0, concat_axis=0, tiled=True),
    )
    arrived_grads = lax.all_to_all(outgoing_grads, "ep", split_axis=0, concat_axis=0, tiled=True)
    received = arrived_rows.reshape(owners * capacity, features)
    projected = arrived_projected.reshape(owners * capacity, sketch_width)
    grads_in = arrived_grads.reshape(owners * capacity, units)
    inverse = 1.0 / window_counts.astype(jnp.float32)[0]
    share = features // replicas
    gate_pre = lax.dot_general(
        received, gate_weight[0], contract_last, preferred_element_type=jnp.float32
    )
    gate_grad = (grads_in.astype(jnp.float32) * derivative_silu(gate_pre)).astype(jnp.bfloat16)
    probe_share = lax.dynamic_slice_in_dim(grad_probes, position * units, units, 1)
    partial_projection = lax.dot_general(
        gate_grad, probe_share, contract_last, preferred_element_type=jnp.float32
    )
    gate_grad, partial_projection = (gate_grad, partial_projection)
    grad_projected = lax.psum(partial_projection, "rep").astype(jnp.bfloat16)
    summed = lax.dot_general(
        gate_grad, grad_projected, contract_first, preferred_element_type=jnp.float32
    )
    grad_sketch = (summed * inverse)[None]
    columns = lax.dynamic_slice_in_dim(received, position * share, share, 1)
    summed = lax.dot_general(columns, projected, contract_first, preferred_element_type=jnp.float32)
    input_sketch = (summed * inverse)[None]
    return (input_sketch, grad_sketch)


def solution(mesh):
    placed = (
        P("ep", None),
        P("ep", None),
        P("ep", None, "rep"),
        P("ep", "rep", None),
        P(),
        P(),
        P("ep"),
    )
    return jax.shard_map(
        local,
        mesh=mesh,
        in_specs=placed,
        out_specs=(P("ep", "rep", None), P("ep", "rep", None)),
        check_vma=False,
    )
```

profile of v0, /device:TPU:32, one launch (start us, length us, event | category | flops | bytes accessed | tf_op | source)
XLA Modules:
  0.0 731.5 jit_solution(9311342539343883993)
XLA Ops:
  0.6 0.0 copy-start
  0.6 0.0 copy-start.1
  0.7 0.9 copy.12
  1.6 0.1 eq.29
  1.7 0.1 eq.25
  1.8 0.7 broadcast_multiply_fusion
  2.5 0.1 copy.14
  2.6 0.2 fusion.14
  2.9 0.1 copy.15
  3.0 0.1 copy.11
  3.1 0.1 mul.48
  3.2 0.4 fusion.13
  3.6 4.3 scatter_custom_fusion
  7.9 2.0 convolution_convert_fusion
  9.9 2.8 gather_fusion.1
  12.7 0.9 reshape.78
  13.6 17.5 %all-to-all-start.1 = ((bf16[128,10,128]{2,1,0:T(8,128)(2,1)}), bf16[128,10,128]{2,1,0:T(8,128)(2,1)}, u32[]{:S(2)}, u32[]{:S(2)}) async-start(bf16[128,10,128]{2,1,0:T(8,128)(2,1)} %reshape.78), calls=%async_computation.1 | async-start | bytes 1048576 | tf_op jit(solution)/shard_map/all_to_all | solution.py:51
  31.1 0.0 copy-done.1
  31.1 0.4 copy.16
  31.5 0.1 concatenate.11
  31.6 4.1 gather_fusion.2
  35.7 0.3 reshape.81
  36.0 1.6 reshape.120
  37.6 10.3 %all-to-all-done.1 = bf16[128,10,128]{2,1,0:T(8,128)(2,1)} async-done(((bf16[128,10,128]{2,1,0:T(8,128)(2,1)}), bf16[128,10,128]{2,1,0:T(8,128)(2,1)}, u32[]{:S(2)}, u32[]{:S(2)}) %all-to-all-start.1) | async-done | bytes 327712 | tf_op jit(solution)/shard_map/all_to_all | solution.py:51
  47.9 8.9 %all-to-all-start.2 = ((bf16[128,2,960]{2,1,0:T(2,128)(2,1)}), bf16[128,2,960]{2,1,0:T(2,128)(2,1)S(1)}, u32[]{:S(2)}, u32[]{:S(2)}) async-start(bf16[128,2,960]{2,1,0:T(2,128)(2,1)} %reshape.120), calls=%async_computation.2 | async-start | bytes 1048576 | tf_op jit(solution)/shard_map/all_to_all | solution.py:53
  56.8 1.3 concatenate.9
  58.1 8.4 %gather_fusion = bf16[1280,4096]{1,0:T(8,128)(2,1)} fusion(bf16[129,4096]{1,0:T(8,128)(2,1)S(1)} %concatenate.9, s32[2048]{0:T(1024)S(1)} %get-tuple-element.5), kind=kCustom, calls=%fused_computation | custom fusion | bytes 20976640 | tf_op jit(solution)/shard_map/gather | solution.py:46
  66.5 15.2 %reshape.76 = bf16[128,10,4096]{2,1,0:T(8,128)(2,1)} reshape(bf16[1280,4096]{1,0:T(8,128)(2,1)} %gather_fusion) | data formatting | bytes 20971520 | tf_op jit(solution)/shard_map/reshape | solution.py:46
  81.7 0.0 all-to-all-done.2
  81.7 14.2 %all-to-all-start = ((bf16[128,10,4096]{2,1,0:T(8,128)(2,1)}), bf16[128,10,4096]{2,1,0:T(8,128)(2,1)}, u32[]{:S(2)}, u32[]{:S(2)}) async-start(bf16[128,10,4096]{2,1,0:T(8,128)(2,1)} %reshape.76), calls=%async_computation | async-start | bytes 33554432 | tf_op jit(solution)/shard_map/all_to_all | solution.py:50
  96.5 1.2 reshape.79
  97.7 1.7 reshape.121
  99.4 1.5 reshape.82
  100.9 1.3 copy.17
  102.3 577.2 %all-to-all-done = bf16[128,10,4096]{2,1,0:T(8,128)(2,1)} async-done(((bf16[128,10,4096]{2,1,0:T(8,128)(2,1)}), bf16[128,10,4096]{2,1,0:T(8,128)(2,1)}, u32[]{:S(2)}, u32[]{:S(2)}) %all-to-all-start) | async-done | bytes 10485792 | tf_op jit(solution)/shard_map/all_to_all | solution.py:50
  679.4 16.5 %reshape.77 = bf16[1280,4096]{1,0:T(8,128)(2,1)} reshape(bf16[128,10,4096]{2,1,0:T(8,128)(2,1)} %all-to-all-done) | data formatting | bytes 20971520 | tf_op jit(solution)/shard_map/reshape | solution.py:54
  696.0 0.0 copy-done
  696.0 7.9 %multiply_convert_fusion = bf16[1280,192]{0,1:T(8,128)(2,1)S(1)} fusion(f32[1280,192]{0,1:T(8,128)} %copy.17, bf16[1280,4096]{1,0:T(8,128)(2,1)} %reshape.77, bf16[1,192,4096]{2,1,0:T(8,128)(2,1)S(1)} %copy-done), kind=kOutput, calls=%fused_computation.13 | convolution fusion | flops 2015477760 | bytes 13533184 | tf_op jit(solution)/shard_map/dot_general | solution.py:59
  703.9 1.3 fusion.18
  705.2 22.0 %all-reduce.4 = bf16[1280,128]{1,0:T(8,128)(2,1)S(1)} all-reduce(f32[1280,128]{1,0:T(8,128)S(1)} %fusion.18), channel_id=1, replica_groups=mesh['ep'=128,'rep'=4] {'rep'}, use_global_device_ids=true, to_apply=%region_4.5 | all-reduce | flops 163840 | bytes 983040 | tf_op jit(solution)/shard_map/psum | solution.py:68
  727.2 0.9 fusion.10
  728.1 3.4 fusion.7
  (9 shorter events, 0.1 us)
Async XLA Ops:
  0.6 695.3 %copy-start = (bf16[1,192,4096]{2,1,0:T(8,128)(2,1)S(1)}, bf16[1,192,4096]{2,1,0:T(8,128)(2,1)}, u32[]{:S(2)}) copy-start(bf16[1,192,4096]{2,1,0:T(8,128)(2,1)} %param.10) | copy-start | bytes 4718596
  0.6 30.5 %copy-start.1 = (bf16[128,8,192]{0,2,1:T(8,128)(2,1)S(1)}, bf16[128,8,192]{0,2,1:T(8,128)(2,1)}, u32[]{:S(2)}) copy-start(bf16[128,8,192]{0,2,1:T(8,128)(2,1)} %param.9) | copy-start | bytes 1179652
  13.6 34.3 %all-to-all-start.1 = ((bf16[128,10,128]{2,1,0:T(8,128)(2,1)}), bf16[128,10,128]{2,1,0:T(8,128)(2,1)}, u32[]{:S(2)}, u32[]{:S(2)}) async-start(bf16[128,10,128]{2,1,0:T(8,128)(2,1)} %reshape.78), calls=%async_computation.1 | async-start | bytes 1048576 | tf_op jit(solution)/shard_map/all_to_all | solution.py:51
  47.9 33.8 %all-to-all-start.2 = ((bf16[128,2,960]{2,1,0:T(2,128)(2,1)}), bf16[128,2,960]{2,1,0:T(2,128)(2,1)S(1)}, u32[]{:S(2)}, u32[]{:S(2)}) async-start(bf16[128,2,960]{2,1,0:T(2,128)(2,1)} %reshape.120), calls=%async_computation.2 | async-start | bytes 1048576 | tf_op jit(solution)/shard_map/all_to_all | solution.py:53
  81.7 597.8 %all-to-all-start = ((bf16[128,10,4096]{2,1,0:T(8,128)(2,1)}), bf16[128,10,4096]{2,1,0:T(8,128)(2,1)}, u32[]{:S(2)}, u32[]{:S(2)}) async-start(bf16[128,10,4096]{2,1,0:T(8,128)(2,1)} %reshape.76), calls=%async_computation | async-start | bytes 33554432 | tf_op jit(solution)/shard_map/all_to_all | solution.py:50
where the time goes:
time: 733 us; the launch traced here: 732 us
  waiting for transfers between devices  587 us (80%)
  local copies, waits for them, and re-layouts  63.1 us (9%)
  starting transfers between devices  40.5 us (6%)
  blocking collectives  22 us (3%)
  matrix products  15.5 us (2%)
    all_to_all x1, waiting for transfers between devices, local(): lax.all_to_all(outgoing_rows, 'ep', split_axis=0, concat_axis=0, tiled=True)  577 us
    psum x1, blocking collectives, local(): grad_projected = lax.psum(partial_projection, 'rep').astype(jnp.bfloat16)  22 us
    all_to_all x1, starting transfers between devices, local(): lax.all_to_all(outgoing_projected, 'ep', split_axis=0, concat_axis=0, til...  17.5 us
    reshape x1, local copies, waits for them, and re-layouts, local(): received = arrived_rows.reshape(owners * capacity, features)  16.5 us
    reshape x1, local copies, waits for them, and re-layouts, local(): outgoing_rows = padded_rows[token_slots].reshape(owners, capacity, features)  15.2 us
  transfers between devices with their start and end apart: 3, of which 2 were waited for; matrix products, arithmetic and copies ran while one was open for 5% of the time, Pallas kernels for 0%

commit v1 on v0

v1 whole, which is shorter than its diff:
```python
import jax
import jax.numpy as jnp
from jax import lax
from jax.experimental import pallas as pl
from jax.experimental.pallas import tpu as pltpu
from jax.sharding import PartitionSpec as P

OWNERS = 128
REPS = 4
TOK = 128
TOP = 8
D = 4096
SHARE = D // REPS
FFW = 768
UNITS = FFW // REPS
R = 128
FIRST = 8
EXTRA = 2
ROWS = OWNERS * FIRST
QUARTER = ROWS // REPS
EXTRA_ROWS = OWNERS * EXTRA
EXTRA_QUARTER = EXTRA_ROWS // REPS
STACK = FFW + R
HALF = STACK // 2

BF = jnp.bfloat16
F32 = jnp.float32
NT = (((1,), (1,)), ((), ()))
NN = (((1,), (0,)), ((), ()))

VM = pl.BlockSpec(memory_space=pltpu.VMEM)
SM = pl.BlockSpec(memory_space=pltpu.SMEM)


def dot(a, b, dims=NN):
    return lax.dot_general(a, b, dims, preferred_element_type=F32)


def iota(shape, axis):
    return lax.broadcasted_iota(jnp.int32, shape, axis)


def ones_where(mask):
    return jnp.where(mask, 1.0, 0.0).astype(BF)


def kernel_call(body, out_shape, in_specs, flops, bytes_accessed, scratch=()):
    return pl.pallas_call(
        body,
        out_shape=out_shape,
        in_specs=in_specs,
        out_specs=jax.tree.map(lambda _: VM, out_shape),
        scratch_shapes=list(scratch),
        compiler_params=pltpu.CompilerParams(vmem_limit_bytes=50 * 1024 * 1024),
        cost_estimate=pl.CostEstimate(
            flops=flops, bytes_accessed=bytes_accessed, transcendentals=0
        ),
    )


def places(ids_t):
    experts = iota((OWNERS, TOK), 0)
    named = jnp.zeros((OWNERS, TOK), F32)
    for k in range(TOP):
        named += jnp.where(ids_t[k : k + 1, :] == experts, 1.0, 0.0)
    before = ones_where(iota((TOK, TOK), 0) < iota((TOK, TOK), 1))
    rank = dot(named.astype(BF), before)
    return jnp.where(named > 0.0, rank, -1.0)


def each_eight(table):
    spread = ones_where(iota((ROWS, OWNERS), 0) // FIRST == iota((ROWS, OWNERS), 1))
    return dot(spread, table.astype(BF))


def send_first(ids_ref, tokens_ref, out_ref):
    spread = each_eight(places(ids_ref[...]))
    place = iota((ROWS, TOK), 0) % FIRST
    chosen = ones_where(spread == place.astype(F32))
    out_ref[...] = dot(chosen, tokens_ref[...]).astype(BF)


def send_second(ids_ref, flat_ref, tokens_ref, grads_ref, out_ref):
    table = places(ids_ref[...])
    width = SHARE // 4
    spread = each_eight(table)
    row = iota((ROWS, TOK), 0)
    wanted = (FIRST + (row % 8) // 4).astype(F32)
    rows = jnp.zeros((ROWS, width), F32)
    for b in range(4):
        chosen = ones_where((spread == wanted) & (row % 4 == b))
        rows += dot(chosen, tokens_ref[:, b * width : (b + 1) * width])
    out_ref[:, :width] = rows.astype(BF)

    pairs = TOK * TOP
    widen = ones_where(iota((TOK, pairs), 1) // TOP == iota((TOK, pairs), 0))
    ranks = dot(table.astype(BF), widen)
    named = flat_ref[...] == iota((OWNERS, pairs), 0)
    pair_table = jnp.where(named, ranks, -1.0).astype(BF)
    source, lane = iota((UNITS, width), 0), iota((UNITS, width), 1)
    grads = grads_ref[...]
    main = dot(grads, ones_where(source == lane)).astype(BF)
    tails = [
        dot(grads, ones_where((source // 64 == b) & (lane == 192 + source % 64))).astype(BF)
        for b in range(3)
    ]
    block = 256
    for start in range(0, ROWS, block):
        spread = dot(
            ones_where(
                (iota((block, OWNERS), 0) + start) // FIRST == iota((block, OWNERS), 1)
            ),
            pair_table,
        )
        row = iota((block, pairs), 0)
        total = dot(ones_where(spread == (row % 8).astype(F32)), main)
        late = spread == (FIRST + (row % 8) // 4).astype(F32)
        for b in range(3):
            total += dot(ones_where(late & (row % 4 == b)), tails[b])
        out_ref[start : start + block, width:] = total.astype(BF)


def stack_weights(pos_ref, probes_ref, w0, w1, w2, w3, out_ref):
    x = pos_ref[0]
    for k, w in enumerate((w0, w1, w2, w3)):
        block = lax.rem(x - k + REPS, REPS)
        out_ref[pl.ds(pl.multiple_of(block * UNITS, UNITS), UNITS), :] = w[...]
    out_ref[FFW:, :] = probes_ref[...]


def first_products(pos_ref, rows_ref, weights_ref, *outs):
    x = pos_ref[0]
    for k, out in enumerate(outs):
        q = lax.rem(x + k, REPS)
        rows = rows_ref[pl.ds(pl.multiple_of(q * QUARTER, QUARTER), QUARTER), :]
        out[...] = dot(weights_ref[...], rows, NT)


def second_products(pos_ref, got_ref, weights_ref, extra_ref, *outs):
    x = pos_ref[0]
    width = SHARE // 4
    target, source = iota((EXTRA_ROWS, ROWS), 0), iota((EXTRA_ROWS, ROWS), 1)
    got = got_ref[:, :width]
    for b in range(4):
        extra_ref[:, b * width : (b + 1) * width] = dot(
            ones_where(source == 4 * target + b), got
        ).astype(BF)
    blank = jnp.zeros((EXTRA_QUARTER, SHARE), BF)
    for k, out in enumerate(outs):
        q = lax.rem(x + k, REPS)
        rows = extra_ref[
            pl.ds(pl.multiple_of(q * EXTRA_QUARTER, EXTRA_QUARTER), EXTRA_QUARTER), :
        ]
        low = dot(weights_ref[:HALF, :], jnp.concatenate([rows, blank], 0), NT)
        high = dot(weights_ref[HALF:, :], jnp.concatenate([blank, rows], 0), NT)
        out[:HALF, :] = (low + high).astype(BF)
        at = pl.ds(pl.multiple_of(q * QUARTER, QUARTER), QUARTER)
        out[HALF : HALF + QUARTER, :] = got_ref[at, width : width + 128]
        out[HALF + QUARTER :, :] = got_ref[at, width + 128 : width + 256]


def gate_part(pos_ref, inverse_ref, grad_probes_ref, *refs):
    firsts, seconds, outs = refs[:4], refs[4:8], refs[8:12]
    grads_ref, sketch_ref = refs[12], refs[13]
    x = pos_ref[0]
    same = ones_where(iota((128, 128), 0) == iota((128, 128), 1))
    picked, lane = iota((QUARTER, 128), 0), iota((QUARTER, 128), 1)
    for k, second in enumerate(seconds):
        base = lax.rem(x - k + REPS, REPS) * UNITS
        low = dot(same, second[HALF : HALF + QUARTER, :], NT)
        high = dot(same, second[HALF + QUARTER :, :], NT)
        grads_ref[pl.ds(pl.multiple_of(base, 64), 128), :QUARTER] = low
        grads_ref[pl.ds(pl.multiple_of(base + 128, 64), 64), :QUARTER] = high[:64]
        tail = high[64:].astype(BF)
        for b in range(3):
            pick = ones_where((picked == 4 * lane + b) & (lane < EXTRA_QUARTER))
            grads_ref[pl.ds(pl.multiple_of(base + 64 * b, 64), 64), QUARTER:] = dot(tail, pick)
    first = firsts[0][...] + firsts[1][...] + firsts[2][...] + firsts[3][...]
    second = (
        seconds[0][:HALF, :].astype(F32)
        + seconds[1][:HALF, :].astype(F32)
        + seconds[2][:HALF, :].astype(F32)
        + seconds[3][:HALF, :].astype(F32)
    )
    turned = pltpu.roll(second, EXTRA_QUARTER, 1)
    late = jnp.concatenate([second, turned[: FFW - HALF]], 0)
    gate = jnp.concatenate([first[:FFW], late], 1)
    s = 1.0 / (1.0 + jnp.exp(-gate))
    gate_grad = (grads_ref[...] * (s * (1.0 + gate * (1.0 - s)))).astype(BF)
    projected = dot(grad_probes_ref[...], gate_grad).astype(BF)
    sketch_ref[...] = dot(gate_grad, projected, NT) * inverse_ref[0]
    rows = first[FFW:].astype(BF).astype(F32)
    rows_late = jnp.where(
        iota((R, 128), 1) < EXTRA_QUARTER, turned[FFW - HALF :], 0.0
    ).astype(BF).astype(F32)
    for k, out in enumerate(outs):
        base = lax.rem(x + k, REPS) * UNITS
        out[:UNITS, :] = sketch_ref[pl.ds(pl.multiple_of(base, UNITS), UNITS), :]
        out[UNITS : UNITS + R, :] = rows[:, :128]
        out[UNITS + R : UNITS + 2 * R, :] = rows[:, 128:]
        out[UNITS + 2 * R :, :] = rows_late


def finish(pos_ref, inverse_ref, rows_ref, extra_ref, q0, q1, q2, q3, input_ref, grad_ref):
    x = pos_ref[0]
    grad_ref[...] = (q0[:UNITS] + q1[:UNITS]) + (q2[:UNITS] + q3[:UNITS])
    total = jnp.zeros((R, SHARE), F32)
    for k, got in enumerate((q0, q1, q2, q3)):
        q = lax.rem(x - k + REPS, REPS)
        start = pl.multiple_of(q * QUARTER, QUARTER)
        rows = rows_ref[pl.ds(start, QUARTER), :]
        low = got[UNITS : UNITS + R, :].astype(BF)
        high = got[UNITS + R : UNITS + 2 * R, :].astype(BF)
        total += dot(jnp.concatenate([low, high], 1), rows)
        late = got[UNITS + 2 * R :, :].astype(BF)[:, :EXTRA_QUARTER]
        start = pl.multiple_of(q * EXTRA_QUARTER, EXTRA_QUARTER)
        total += dot(late, extra_ref[pl.ds(start, EXTRA_QUARTER), :])
    input_ref[...] = (total * inverse_ref[0]).T


def shifted(blocks):
    got = [blocks[0]]
    for k in range(1, REPS):
        got.append(lax.ppermute(blocks[k], "rep", [(i, (i + k) % REPS) for i in range(REPS)]))
    return got


def local(tokens, expert_ids, hidden_grads, gate_weight, probes, grad_probes, window_counts):
    sds = jax.ShapeDtypeStruct
    x = lax.axis_index("rep")
    pos = x.astype(jnp.int32).reshape(1)
    inverse = 1.0 / window_counts.astype(F32)
    ids_t = expert_ids.T
    flat_ids = expert_ids.reshape(1, TOK * TOP)
    columns = lax.dynamic_slice_in_dim(tokens, x * SHARE, SHARE, 1)

    out_first = kernel_call(
        send_first, sds((ROWS, SHARE), BF), [VM] * 2, 2 * ROWS * TOK * SHARE, 3 << 20
    )(ids_t, columns)
    rows = lax.all_to_all(
        out_first.reshape(OWNERS, FIRST, SHARE), "ep", split_axis=0, concat_axis=0, tiled=True
    ).reshape(ROWS, SHARE)

    weights = shifted(
        [
            lax.dynamic_slice_in_dim(gate_weight[0], lax.rem(x + k, REPS) * SHARE, SHARE, 1)
            for k in range(REPS)
        ]
    )
    probe_columns = lax.dynamic_slice_in_dim(probes, x * SHARE, SHARE, 1)
    stacked = kernel_call(
        stack_weights, sds((STACK, SHARE), BF), [SM] + [VM] * 5, 1000, 4 << 20
    )(pos, probe_columns, *weights)

    out_second = kernel_call(
        send_second, sds((ROWS, 512), BF), [VM] * 4, 3 << 30, 4 << 20
    )(ids_t, flat_ids, columns, hidden_grads.reshape(TOK * TOP, UNITS))

    firsts = kernel_call(
        first_products,
        [sds((STACK, QUARTER), F32)] * REPS,
        [SM] + [VM] * 2,
        2 * ROWS * SHARE * STACK,
        8 << 20,
    )(pos, rows, stacked)
    firsts = shifted(firsts)

    got = lax.all_to_all(
        out_second.reshape(OWNERS, FIRST, 512), "ep", split_axis=0, concat_axis=0, tiled=True
    ).reshape(ROWS, 512)
    extra, *seconds = kernel_call(
        second_products,
        [sds((EXTRA_ROWS, SHARE), BF)] + [sds((HALF + 2 * QUARTER, 128), BF)] * REPS,
        [SM] + [VM] * 2,
        2 << 30,
        6 << 20,
    )(pos, got, stacked)
    seconds = shifted(seconds)

    thirds = kernel_call(
        gate_part,
        [sds((UNITS + 3 * R, 128), F32)] * REPS,
        [SM] * 2 + [VM] * 9,
        1 << 30,
        8 << 20,
        [pltpu.VMEM((FFW, QUARTER + 128), F32), pltpu.VMEM((FFW, R), F32)],
    )(pos, inverse, grad_probes, *firsts, *seconds)
    thirds = shifted(thirds)

    input_sketch, grad_sketch = kernel_call(
        finish,
        [sds((SHARE, R), F32), sds((UNITS, R), F32)],
        [SM] * 2 + [VM] * 6,
        1 << 29,
        5 << 20,
    )(pos, inverse, rows, extra, *thirds)
    return input_sketch[None], grad_sketch[None]


def solution(mesh):
    placed = (
        P("ep", None),
        P("ep", None),
        P("ep", None, "rep"),
        P("ep", "rep", None),
        P(),
        P(),
        P("ep"),
    )
    return jax.shard_map(
        local,
        mesh=mesh,
        in_specs=placed,
        out_specs=(P("ep", "rep", None), P("ep", "rep", None)),
        check_vma=False,
    )
```

time: 733 us -> 202 us (0.28)
  the two profiles are of different devices: /device:TPU:32 before, /device:TPU:8 now
where the time goes in v1:
time: 202 us; the launch traced here: 201 us
  waiting for transfers between devices  106 us (52%)
  starting transfers between devices  61.6 us (30%)
  Pallas kernels  20.5 us (10%)
  local copies, waits for them, and re-layouts  11.4 us (6%)
    ppermute x12, waiting for transfers between devices, shifted(): lax.ppermute(blocks[k], 'rep', [(i, (i + k) % REPS) for i in range(REPS)])  61.1 us
    all_to_all x1, waiting for transfers between devices, local(): lax.all_to_all(out_first.reshape(OWNERS, FIRST, SHARE), 'ep', split_axis=...  45.2 us
    ppermute x12, starting transfers between devices, shifted(): lax.ppermute(blocks[k], 'rep', [(i, (i + k) % REPS) for i in range(REPS)])  37.5 us
    all_to_all x1, starting transfers between devices, local(): lax.all_to_all(out_first.reshape(OWNERS, FIRST, SHARE), 'ep', split_axis=...  17.5 us
    unnamed x22, local copies, waits for them, and re-layouts  8.79 us
    all_to_all x1, starting transfers between devices, local(): lax.all_to_all(out_second.reshape(OWNERS, FIRST, 512), 'ep', split_axis=0...  6.52 us
    pallas_call x1, Pallas kernels, local(): kernel_call(first_products, [sds((STACK, QUARTER), F32)] * REPS, [SM] + [...  5.16 us
    pallas_call x1, Pallas kernels, local(): kernel_call(second_products, [sds((EXTRA_ROWS, SHARE), BF)] + [sds((HALF...  4.5 us
  transfers between devices with their start and end apart: 14, of which 7 were waited for; matrix products, arithmetic and copies ran while one was open for 2% of the time, Pallas kernels for 7%

profile of v1, /device:TPU:8, one launch (start us, length us, event | category | flops | bytes accessed | tf_op | source)
XLA Modules:
  0.0 201.3 jit_solution(15613529599542698955)
XLA Ops:
  0.6 0.0 copy-start
  0.6 1.2 copy-done
  1.9 0.0 copy-start.8
  1.9 0.7 copy-done.8
  2.6 1.0 shard_map.86
  3.6 1.3 copy-done.3
  4.9 17.5 %all-to-all-start = ((bf16[128,8,1024]{2,1,0:T(8,128)(2,1)}), bf16[128,8,1024]{2,1,0:T(8,128)(2,1)S(1)}, u32[]{:S(2)}, u32[]{:S(2)}) async-start(bf16[128,8,1024]{2,1,0:T(8,128)(2,1)} %bitcast.19), calls=%async_computation | async-start | bytes 4194304 | tf_op jit(solution)/shard_map/all_to_all | solution.py:240
  22.4 0.1 copy.11
  22.5 0.1 reshape.32.flat_ref
  22.6 2.2 %copy.12 = bf16[128,8,192]{2,1,0:T(8,128)(2,1)} copy(bf16[128,8,192]{0,2,1:T(8,128)(2,1)} %param.9) | data formatting | bytes 786432 | tf_op args[2]
  24.8 1.0 copy-done.6
  25.9 4.4 %shard_map.87 = bf16[1024,512]{1,0:T(8,128)(2,1)S(1)} custom-call(s32[8,128]{1,0:T(8,128)S(1)} %bitcast.23, s32[1,1024]{1,0:T(1,128)S(1)} %reshape.32.flat_ref, bf16[128,1024]{1,0:T(8,128)(2,1)S(1)} %constant_dynamic-slice_fusion.1.tokens_ref, bf16[1024,192]{1,0:T(8,128)(2,1)S(1)} %bitcast.21), custom_call_target="tpu_custom_call" | custom-call | flops 3221225472 | bytes 4194304 | tf_op jit(solution)/shard_map/pallas_call | solution.py:255
  30.3 1.0 copy-done.5
  31.3 45.2 %all-to-all-done = bf16[128,8,1024]{2,1,0:T(8,128)(2,1)S(1)} async-done(((bf16[128,8,1024]{2,1,0:T(8,128)(2,1)}), bf16[128,8,1024]{2,1,0:T(8,128)(2,1)S(1)}, u32[]{:S(2)}, u32[]{:S(2)}) %all-to-all-start) | async-done | bytes 2097184 | tf_op jit(solution)/shard_map/all_to_all | solution.py:240
  76.5 6.5 %all-to-all-start.1 = ((bf16[128,8,512]{2,1,0:T(8,128)(2,1)}), bf16[128,8,512]{2,1,0:T(8,128)(2,1)}, u32[]{:S(2)}, u32[]{:S(2)}) async-start(bf16[128,8,512]{2,1,0:T(8,128)(2,1)} %bitcast.20), calls=%async_computation.1 | async-start | bytes 2097152 | tf_op jit(solution)/shard_map/all_to_all | solution.py:268
  83.0 1.5 dynamic-slice_bitcast_fusion
  84.5 4.7 %collective-permute-start.2 = (bf16[192,1024]{1,0:T(8,128)(2,1)S(1)}, bf16[192,1024]{1,0:T(8,128)(2,1)S(1)}, u32[]{:S(2)}, u32[]{:S(2)}) collective-permute-start(bf16[192,1024]{1,0:T(8,128)(2,1)S(1)} %get-tuple-element.32), channel_id=1, source_target_pairs={{0,3},{1,0},{2,1},{3,2},{4,7},{5,4},{6,5},{7,6},{8,11},{9,8},{10,9... | collective-permute-start | bytes 1179656 | tf_op jit(solution)/shard_map/ppermute | solution.py:224
  89.2 1.9 collective-permute-start
  91.2 4.2 %collective-permute-start.1 = (bf16[192,1024]{1,0:T(8,128)(2,1)S(1)}, bf16[192,1024]{1,0:T(8,128)(2,1)S(1)}, u32[]{:S(2)}, u32[]{:S(2)}) collective-permute-start(bf16[192,1024]{1,0:T(8,128)(2,1)S(1)} %get-tuple-element.35), channel_id=1, source_target_pairs={{0,2},{1,3},{2,0},{3,1},{4,6},{5,7},{6,4},{7,5},{8,10},{9,11},{10,... | collective-permute-start | bytes 1179656 | tf_op jit(solution)/shard_map/ppermute | solution.py:224
  95.3 1.0 constant_dynamic-slice_fusion.probes_ref
  96.3 10.0 %collective-permute-done.2.w3 = bf16[192,1024]{1,0:T(8,128)(2,1)S(1)} collective-permute-done((bf16[192,1024]{1,0:T(8,128)(2,1)S(1)}, bf16[192,1024]{1,0:T(8,128)(2,1)S(1)}, u32[]{:S(2)}, u32[]{:S(2)}) %collective-permute-start.2) | collective-permute-done | bytes 393248 | tf_op jit(solution)/shard_map/ppermute | solution.py:224
  106.3 5.3 %collective-permute-done.w1 = bf16[192,1024]{1,0:T(8,128)(2,1)S(1)} collective-permute-done((bf16[192,1024]{1,0:T(8,128)(2,1)S(1)}, bf16[192,1024]{1,0:T(8,128)(2,1)S(1)}, u32[]{:S(2)}, u32[]{:S(2)}) %collective-permute-start) | collective-permute-done | bytes 393248 | tf_op jit(solution)/shard_map/ppermute | solution.py:224
  111.6 0.0 collective-permute-done.1.w2
  111.6 0.1 shard_map.88.weights_ref
  111.8 1.2 copy-done.4
  113.0 5.2 %shard_map.90 = (f32[896,256]{1,0:T(8,128)S(1)}, f32[896,256]{1,0:T(8,128)}, f32[896,256]{1,0:T(8,128)}, f32[896,256]{1,0:T(8,128)S(1)}) custom-call(s32[1]{0:T(128)} %bitcast.pos_ref, bf16[1024,1024]{1,0:T(8,128)(2,1)} %bitcast.17, bf16[896,1024]{1,0:T(8,128)(2,1)} %copy-done.4), custom_call_target="tpu_custom_call" | custom-call | flops 1879048192 | bytes 8388608 | tf_op jit(solution)/shard_map/pallas_call | solution.py:259
  118.2 1.9 collective-permute-start.3
  120.1 2.9 %collective-permute-start.4 = (f32[896,256]{1,0:T(8,128)}, f32[896,256]{1,0:T(8,128)}, u32[]{:S(2)}, u32[]{:S(2)}) collective-permute-start(f32[896,256]{1,0:T(8,128)} %get-tuple-element.20), channel_id=1, source_target_pairs={{0,2},{1,3},{2,0},{3,1},{4,6},{5,7},{6,4},{7,5},{8,10},{9,11},{10,... | collective-permute-start | bytes 2752520 | tf_op jit(solution)/shard_map/ppermute | solution.py:224
  123.0 4.3 %collective-permute-start.5 = (f32[896,256]{1,0:T(8,128)S(1)}, f32[896,256]{1,0:T(8,128)}, u32[]{:S(2)}, u32[]{:S(2)}) collective-permute-start(f32[896,256]{1,0:T(8,128)S(1)} %get-tuple-element.21), channel_id=1, source_target_pairs={{0,3},{1,0},{2,1},{3,2},{4,7},{5,4},{6,5},{7,6},{8,11},{9,8},{10,9... | collective-permute-start | bytes 2752520 | tf_op jit(solution)/shard_map/ppermute | solution.py:224
  127.3 0.0 all-to-all-done.1
  127.4 0.0 copy-start.7
  127.4 4.5 %shard_map.89 = (bf16[256,1024]{1,0:T(8,128)(2,1)S(1)}, bf16[960,128]{1,0:T(8,128)(2,1)S(1)}, bf16[960,128]{1,0:T(8,128)(2,1)S(1)}, bf16[960,128]{1,0:T(8,128)(2,1)S(1)}, bf16[960,128]{1,0:T(8,128)(2,1)S(1)}) custom-call(s32[1]{0:T(128)} %bitcast.pos_ref, bf16[1024,512]{1,0:T(8,128)(2,1)} %bitcast.6.got_ref, bf16[896,1024]{1,0:T(8,128)(2,1)} %copy-done.4), custom_call_target="tpu_custom_call" | custom-call | flops 2147483648 | bytes 6291456 | tf_op jit(solution)/shard_map/pallas_call | solution.py:271
  131.9 2.8 %collective-permute-start.6 = (bf16[960,128]{1,0:T(8,128)(2,1)S(1)}, bf16[960,128]{1,0:T(8,128)(2,1)S(1)}, u32[]{:S(2)}, u32[]{:S(2)}) collective-permute-start(bf16[960,128]{1,0:T(8,128)(2,1)S(1)} %get-tuple-element.23), channel_id=1, source_target_pairs={{0,1},{1,2},{2,3},{3,0},{4,5},{5,6},{6,7},{7,4},{8,9},{9,10},{10,1... | collective-permute-start | bytes 737288 | tf_op jit(solution)/shard_map/ppermute | solution.py:224
  134.7 4.0 %collective-permute-start.7 = (bf16[960,128]{1,0:T(8,128)(2,1)S(1)}, bf16[960,128]{1,0:T(8,128)(2,1)S(1)}, u32[]{:S(2)}, u32[]{:S(2)}) collective-permute-start(bf16[960,128]{1,0:T(8,128)(2,1)S(1)} %get-tuple-element.24), channel_id=1, source_target_pairs={{0,2},{1,3},{2,0},{3,1},{4,6},{5,7},{6,4},{7,5},{8,10},{9,11},{10,... | collective-permute-start | bytes 737288 | tf_op jit(solution)/shard_map/ppermute | solution.py:224
  138.6 33.5 %collective-permute-done.6.refs_5_ = bf16[960,128]{1,0:T(8,128)(2,1)S(1)} collective-permute-done((bf16[960,128]{1,0:T(8,128)(2,1)S(1)}, bf16[960,128]{1,0:T(8,128)(2,1)S(1)}, u32[]{:S(2)}, u32[]{:S(2)}) %collective-permute-start.6) | collective-permute-done | bytes 245792 | tf_op jit(solution)/shard_map/ppermute | solution.py:224
  172.1 1.9 collective-permute-start.8
  174.7 0.0 collective-permute-done.7.refs_6_
  174.7 5.5 %collective-permute-done.8.refs_7_ = bf16[960,128]{1,0:T(8,128)(2,1)S(1)} collective-permute-done((bf16[960,128]{1,0:T(8,128)(2,1)S(1)}, bf16[960,128]{1,0:T(8,128)(2,1)S(1)}, u32[]{:S(2)}, u32[]{:S(2)}) %collective-permute-start.8) | collective-permute-done | bytes 245792 | tf_op jit(solution)/shard_map/ppermute | solution.py:224
  180.2 0.0 collective-permute-done.3.refs_1_
  180.2 0.0 collective-permute-done.4.refs_2_
  180.2 0.0 collective-permute-done.5.refs_3_
  180.2 3.7 %shard_map.91 = (f32[576,128]{1,0:T(8,128)S(1)}, f32[576,128]{1,0:T(8,128)S(1)}, f32[576,128]{1,0:T(8,128)S(1)}, f32[576,128]{1,0:T(8,128)S(1)}) custom-call(s32[1]{0:T(128)} %bitcast.pos_ref, f32[1]{0:T(128)S(6)} %div.3.inverse_ref, bf16[128,768]{1,0:T(8,128)(2,1)S(1)} %copy-done.7, f32[896,256]{1,0:T(8,128)S(1)} %get-tuple-element.18.refs_0_, ...), custom_call_target="tpu_custom_call" | custom-call | flops 1073741824 | bytes 8388608 | tf_op jit(solution)/shard_map/pallas_call | solution.py:280
  183.9 1.9 collective-permute-start.9
  185.8 4.6 %collective-permute-start.10 = (f32[576,128]{1,0:T(8,128)S(1)}, f32[576,128]{1,0:T(8,128)S(1)}, u32[]{:S(2)}, u32[]{:S(2)}) collective-permute-start(f32[576,128]{1,0:T(8,128)S(1)} %get-tuple-element.28), channel_id=1, source_target_pairs={{0,2},{1,3},{2,0},{3,1},{4,6},{5,7},{6,4},{7,5},{8,10},{9,11},{10,... | collective-permute-start | bytes 884744 | tf_op jit(solution)/shard_map/ppermute | solution.py:224
  190.4 2.5 %collective-permute-start.11 = (f32[576,128]{1,0:T(8,128)S(1)}, f32[576,128]{1,0:T(8,128)S(1)}, u32[]{:S(2)}, u32[]{:S(2)}) collective-permute-start(f32[576,128]{1,0:T(8,128)S(1)} %get-tuple-element.29), channel_id=1, source_target_pairs={{0,3},{1,0},{2,1},{3,2},{4,7},{5,4},{6,5},{7,6},{8,11},{9,8},{10,9... | collective-permute-start | bytes 884744 | tf_op jit(solution)/shard_map/ppermute | solution.py:224
  192.9 4.0 %collective-permute-done.9.q1 = f32[576,128]{1,0:T(8,128)S(1)} collective-permute-done((f32[576,128]{1,0:T(8,128)S(1)}, f32[576,128]{1,0:T(8,128)S(1)}, u32[]{:S(2)}, u32[]{:S(2)}) %collective-permute-start.9) | collective-permute-done | bytes 294944 | tf_op jit(solution)/shard_map/ppermute | solution.py:224
  196.9 2.8 %collective-permute-done.11.q3 = f32[576,128]{1,0:T(8,128)S(1)} collective-permute-done((f32[576,128]{1,0:T(8,128)S(1)}, f32[576,128]{1,0:T(8,128)S(1)}, u32[]{:S(2)}, u32[]{:S(2)}) %collective-permute-start.11) | collective-permute-done | bytes 294944 | tf_op jit(solution)/shard_map/ppermute | solution.py:224
  199.7 1.6 shard_map.92
  (13 shorter events, 0.0 us)
Async XLA Ops:
  0.6 1.2 copy-start
  1.9 0.7 copy-start.8
  3.6 1.4 copy-start.3
  4.9 17.5 %copy-start.9 = (s32[128,8]{0,1:T(8,128)S(1)}, s32[128,8]{0,1:T(8,128)}, u32[]{:S(2)}) copy-start(s32[128,8]{0,1:T(8,128)} %param.8) | copy-start | bytes 12292
  4.9 71.6 %all-to-all-start = ((bf16[128,8,1024]{2,1,0:T(8,128)(2,1)}), bf16[128,8,1024]{2,1,0:T(8,128)(2,1)S(1)}, u32[]{:S(2)}, u32[]{:S(2)}) async-start(bf16[128,8,1024]{2,1,0:T(8,128)(2,1)} %bitcast.19), calls=%async_computation | async-start | bytes 4194304 | tf_op jit(solution)/shard_map/all_to_all | solution.py:240
  24.8 1.0 copy-start.6
  30.3 1.0 copy-start.5
  76.5 8.0 %copy-start.1 = (bf16[128,8,1024]{2,1,0:T(8,128)(2,1)}, bf16[128,8,1024]{2,1,0:T(8,128)(2,1)S(1)}, u32[]{:S(2)}) copy-start(bf16[128,8,1024]{2,1,0:T(8,128)(2,1)S(1)} %all-to-all-done) | copy-start | bytes 6291460
  76.5 50.9 %all-to-all-start.1 = ((bf16[128,8,512]{2,1,0:T(8,128)(2,1)}), bf16[128,8,512]{2,1,0:T(8,128)(2,1)}, u32[]{:S(2)}, u32[]{:S(2)}) async-start(bf16[128,8,512]{2,1,0:T(8,128)(2,1)} %bitcast.20), calls=%async_computation.1 | async-start | bytes 2097152 | tf_op jit(solution)/shard_map/all_to_all | solution.py:268
  84.5 21.8 %collective-permute-start.2 = (bf16[192,1024]{1,0:T(8,128)(2,1)S(1)}, bf16[192,1024]{1,0:T(8,128)(2,1)S(1)}, u32[]{:S(2)}, u32[]{:S(2)}) collective-permute-start(bf16[192,1024]{1,0:T(8,128)(2,1)S(1)} %get-tuple-element.32), channel_id=1, source_target_pairs={{0,3},{1,0},{2,1},{3,2},{4,7},{5,4},{6,5},{7,6},{8,11},{9,8},{10,9... | collective-permute-start | bytes 1179656 | tf_op jit(solution)/shard_map/ppermute | solution.py:224
  89.2 22.4 %collective-permute-start = (bf16[192,1024]{1,0:T(8,128)(2,1)S(1)}, bf16[192,1024]{1,0:T(8,128)(2,1)S(1)}, u32[]{:S(2)}, u32[]{:S(2)}) collective-permute-start(bf16[192,1024]{1,0:T(8,128)(2,1)S(1)} %get-tuple-element.33), channel_id=1, source_target_pairs={{0,1},{1,2},{2,3},{3,0},{4,5},{5,6},{6,7},{7,4},{8,9},{9,10},{10,1... | collective-permute-start | bytes 1179656 | tf_op jit(solution)/shard_map/ppermute | solution.py:224
  91.2 20.5 %collective-permute-start.1 = (bf16[192,1024]{1,0:T(8,128)(2,1)S(1)}, bf16[192,1024]{1,0:T(8,128)(2,1)S(1)}, u32[]{:S(2)}, u32[]{:S(2)}) collective-permute-start(bf16[192,1024]{1,0:T(8,128)(2,1)S(1)} %get-tuple-element.35), channel_id=1, source_target_pairs={{0,2},{1,3},{2,0},{3,1},{4,6},{5,7},{6,4},{7,5},{8,10},{9,11},{10,... | collective-permute-start | bytes 1179656 | tf_op jit(solution)/shard_map/ppermute | solution.py:224
  111.8 1.2 copy-start.4
  118.2 62.0 %collective-permute-start.3 = (f32[896,256]{1,0:T(8,128)}, f32[896,256]{1,0:T(8,128)}, u32[]{:S(2)}, u32[]{:S(2)}) collective-permute-start(f32[896,256]{1,0:T(8,128)} %get-tuple-element.19), channel_id=1, source_target_pairs={{0,1},{1,2},{2,3},{3,0},{4,5},{5,6},{6,7},{7,4},{8,9},{9,10},{10,1... | collective-permute-start | bytes 2752520 | tf_op jit(solution)/shard_map/ppermute | solution.py:224
  120.1 60.1 %collective-permute-start.4 = (f32[896,256]{1,0:T(8,128)}, f32[896,256]{1,0:T(8,128)}, u32[]{:S(2)}, u32[]{:S(2)}) collective-permute-start(f32[896,256]{1,0:T(8,128)} %get-tuple-element.20), channel_id=1, source_target_pairs={{0,2},{1,3},{2,0},{3,1},{4,6},{5,7},{6,4},{7,5},{8,10},{9,11},{10,... | collective-permute-start | bytes 2752520 | tf_op jit(solution)/shard_map/ppermute | solution.py:224
  123.0 57.2 %collective-permute-start.5 = (f32[896,256]{1,0:T(8,128)S(1)}, f32[896,256]{1,0:T(8,128)}, u32[]{:S(2)}, u32[]{:S(2)}) collective-permute-start(f32[896,256]{1,0:T(8,128)S(1)} %get-tuple-element.21), channel_id=1, source_target_pairs={{0,3},{1,0},{2,1},{3,2},{4,7},{5,4},{6,5},{7,6},{8,11},{9,8},{10,9... | collective-permute-start | bytes 2752520 | tf_op jit(solution)/shard_map/ppermute | solution.py:224
  127.4 52.9 %copy-start.7 = (bf16[128,768]{1,0:T(8,128)(2,1)S(1)}, bf16[128,768]{1,0:T(8,128)(2,1)}, u32[]{:S(2)}) copy-start(bf16[128,768]{1,0:T(8,128)(2,1)} %grad_probes_ref.1) | copy-start | bytes 589828
  131.9 40.3 %collective-permute-start.6 = (bf16[960,128]{1,0:T(8,128)(2,1)S(1)}, bf16[960,128]{1,0:T(8,128)(2,1)S(1)}, u32[]{:S(2)}, u32[]{:S(2)}) collective-permute-start(bf16[960,128]{1,0:T(8,128)(2,1)S(1)} %get-tuple-element.23), channel_id=1, source_target_pairs={{0,1},{1,2},{2,3},{3,0},{4,5},{5,6},{6,7},{7,4},{8,9},{9,10},{10,1... | collective-permute-start | bytes 737288 | tf_op jit(solution)/shard_map/ppermute | solution.py:224
  134.7 40.1 %collective-permute-start.7 = (bf16[960,128]{1,0:T(8,128)(2,1)S(1)}, bf16[960,128]{1,0:T(8,128)(2,1)S(1)}, u32[]{:S(2)}, u32[]{:S(2)}) collective-permute-start(bf16[960,128]{1,0:T(8,128)(2,1)S(1)} %get-tuple-element.24), channel_id=1, source_target_pairs={{0,2},{1,3},{2,0},{3,1},{4,6},{5,7},{6,4},{7,5},{8,10},{9,11},{10,... | collective-permute-start | bytes 737288 | tf_op jit(solution)/shard_map/ppermute | solution.py:224
  172.1 8.1 %collective-permute-start.8 = (bf16[960,128]{1,0:T(8,128)(2,1)S(1)}, bf16[960,128]{1,0:T(8,128)(2,1)S(1)}, u32[]{:S(2)}, u32[]{:S(2)}) collective-permute-start(bf16[960,128]{1,0:T(8,128)(2,1)S(1)} %get-tuple-element.25), channel_id=1, source_target_pairs={{0,3},{1,0},{2,1},{3,2},{4,7},{5,4},{6,5},{7,6},{8,11},{9,8},{10,9... | collective-permute-start | bytes 737288 | tf_op jit(solution)/shard_map/ppermute | solution.py:224
  180.2 19.5 %copy-start.2 = (bf16[128,8,1024]{2,1,0:T(8,128)(2,1)S(1)}, bf16[128,8,1024]{2,1,0:T(8,128)(2,1)}, u32[]{:S(2)}) copy-start(bf16[128,8,1024]{2,1,0:T(8,128)(2,1)} %copy-done.1) | copy-start | bytes 6291460
  183.9 13.0 %collective-permute-start.9 = (f32[576,128]{1,0:T(8,128)S(1)}, f32[576,128]{1,0:T(8,128)S(1)}, u32[]{:S(2)}, u32[]{:S(2)}) collective-permute-start(f32[576,128]{1,0:T(8,128)S(1)} %get-tuple-element.27), channel_id=1, source_target_pairs={{0,1},{1,2},{2,3},{3,0},{4,5},{5,6},{6,7},{7,4},{8,9},{9,10},{10,1... | collective-permute-start | bytes 884744 | tf_op jit(solution)/shard_map/ppermute | solution.py:224
  185.8 11.1 %collective-permute-start.10 = (f32[576,128]{1,0:T(8,128)S(1)}, f32[576,128]{1,0:T(8,128)S(1)}, u32[]{:S(2)}, u32[]{:S(2)}) collective-permute-start(f32[576,128]{1,0:T(8,128)S(1)} %get-tuple-element.28), channel_id=1, source_target_pairs={{0,2},{1,3},{2,0},{3,1},{4,6},{5,7},{6,4},{7,5},{8,10},{9,11},{10,... | collective-permute-start | bytes 884744 | tf_op jit(solution)/shard_map/ppermute | solution.py:224
  190.4 9.2 %collective-permute-start.11 = (f32[576,128]{1,0:T(8,128)S(1)}, f32[576,128]{1,0:T(8,128)S(1)}, u32[]{:S(2)}, u32[]{:S(2)}) collective-permute-start(f32[576,128]{1,0:T(8,128)S(1)} %get-tuple-element.29), channel_id=1, source_target_pairs={{0,3},{1,0},{2,1},{3,2},{4,7},{5,4},{6,5},{7,6},{8,11},{9,8},{10,9... | collective-permute-start | bytes 884744 | tf_op jit(solution)/shard_map/ppermute | solution.py:224

commit v2 on v0

v2 whole, which is shorter than its diff:
```python
import jax
import jax.numpy as jnp
from jax import lax
from jax.experimental import pallas as pl
from jax.experimental.pallas import tpu as pltpu
from jax.sharding import PartitionSpec as P

OWNERS = 128
REPS = 4
TOK = 128
TOP = 8
D = 4096
SHARE = D // REPS
FFW = 768
UNITS = FFW // REPS
R = 128
FIRST = 8
FOLD = 8
ROWS = OWNERS * FOLD
SLOTS = OWNERS * 2
STRIP = SHARE // 4

BF = jnp.bfloat16
F32 = jnp.float32
NT = (((1,), (1,)), ((), ()))
NN = (((1,), (0,)), ((), ()))

VM = pl.BlockSpec(memory_space=pltpu.VMEM)
SM = pl.BlockSpec(memory_space=pltpu.SMEM)


def dot(a, b, dims=NN):
    return lax.dot_general(a, b, dims, preferred_element_type=F32)


def iota(shape, axis):
    return lax.broadcasted_iota(jnp.int32, shape, axis)


def ones_where(mask):
    return jnp.where(mask, 1.0, 0.0).astype(BF)


def kernel_call(body, out_shape, in_specs, flops, bytes_accessed, scratch=()):
    return pl.pallas_call(
        body,
        out_shape=out_shape,
        in_specs=in_specs,
        out_specs=jax.tree.map(lambda _: VM, out_shape),
        scratch_shapes=list(scratch),
        compiler_params=pltpu.CompilerParams(vmem_limit_bytes=50 * 1024 * 1024),
        cost_estimate=pl.CostEstimate(
            flops=flops, bytes_accessed=bytes_accessed, transcendentals=0
        ),
    )


def places(ids_t):
    experts = iota((OWNERS, TOK), 0)
    named = jnp.zeros((OWNERS, TOK), F32)
    for k in range(TOP):
        named += jnp.where(ids_t[k : k + 1, :] == experts, 1.0, 0.0)
    before = ones_where(iota((TOK, TOK), 0) < iota((TOK, TOK), 1))
    rank = dot(named.astype(BF), before)
    return jnp.where(named > 0.0, rank, -1.0)


def spread(table, times):
    shape = (OWNERS * times, OWNERS)
    return dot(ones_where(iota(shape, 0) // times == iota(shape, 1)), table.astype(BF))


def send_rows(pos_ref, ids_ref, tokens_ref, out_ref):
    x = pos_ref[0]
    table = spread(places(ids_ref[...]), FOLD)
    row = iota((ROWS, TOK), 0)
    half, quarter = row % 8 // 4, row % 4
    whole = table == (2 * x + half).astype(F32)
    picks = jnp.concatenate([ones_where(whole & (quarter == b)) for b in range(4)], 1)
    parts = jnp.concatenate([tokens_ref[:, b * SHARE : (b + 1) * SHARE] for b in range(4)], 0)
    out_ref[:, :SHARE] = dot(picks, parts).astype(BF)
    cut = table == (FIRST + half).astype(F32)
    picks = jnp.concatenate([ones_where(cut & (quarter == b)) for b in range(4)], 1)
    parts = jnp.concatenate(
        [
            tokens_ref[:, pl.ds(pl.multiple_of(x * SHARE + b * STRIP, STRIP), STRIP)]
            for b in range(4)
        ],
        0,
    )
    out_ref[:, SHARE:] = dot(picks, parts).astype(BF)


def pick_grads(pos_ref, ids_ref, flat_ref, grads_ref, tail_ref, *outs):
    x = pos_ref[0]
    pairs = TOK * TOP
    widen = ones_where(iota((TOK, pairs), 1) // TOP == iota((TOK, pairs), 0))
    ranks = dot(places(ids_ref[...]).astype(BF), widen)
    named = flat_ref[...] == iota((OWNERS, pairs), 0)
    table = jnp.where(named, ranks, -1.0)
    source, lane = iota((UNITS, STRIP), 0), iota((UNITS, STRIP), 1)
    grads = grads_ref[...]
    main = dot(grads, ones_where(source == lane)).astype(BF)
    twice = spread(table, 2)
    second = iota((SLOTS, pairs), 0) % 2
    for k, out in enumerate(outs):
        place = 2 * lax.rem(x + k, REPS) + second
        out[...] = dot(ones_where(twice == place.astype(F32)), main).astype(BF)
    tails = [
        dot(grads, ones_where((source // 64 == b) & (lane == 192 + source % 64))).astype(BF)
        for b in range(3)
    ]
    block = 256
    for start in range(0, ROWS, block):
        shape = (block, OWNERS)
        owner = (iota(shape, 0) + start) // FOLD == iota(shape, 1)
        eight = dot(ones_where(owner), table.astype(BF))
        row = iota((block, pairs), 0)
        late = eight == (FIRST + row % 8 // 4).astype(F32)
        total = jnp.zeros((block, STRIP), F32)
        for b in range(3):
            total += dot(ones_where(late & (row % 4 == b)), tails[b])
        tail_ref[start : start + block, :] = total.astype(BF)


def fold_grads(pos_ref, tail_ref, g0, g1, g2, g3, out_ref):
    x = pos_ref[0]
    row, column = iota((ROWS, SLOTS), 0), iota((ROWS, SLOTS), 1)
    total = tail_ref[...].astype(F32)
    for k, got in enumerate((g0, g1, g2, g3)):
        unit = lax.rem(x - k + REPS, REPS)
        total += dot(ones_where((row // 4 == column) & (row % 4 == unit)), got[...])
    out_ref[...] = total.astype(BF)


def products(
    pos_ref, rows_ref, probes_ref, own_ref, left_ref, right_ref, top_ref, bottom_ref,
    gate_ref, cut_ref, o0, o1, o2, o3, i0, i1, i2, i3, whole_ref, partial_ref,
):
    x = pos_ref[0]
    target, source = iota((SLOTS, ROWS), 0), iota((SLOTS, ROWS), 1)
    for b in range(4):
        got = dot(ones_where(source == 4 * target + b), rows_ref[...]).astype(BF)
        whole_ref[:, b * SHARE : (b + 1) * SHARE] = got[:, :SHARE]
        cut_ref[:, b * STRIP : (b + 1) * STRIP] = got[:, SHARE:]
    whole, cut = whole_ref[...], cut_ref[...]
    share = pl.ds(pl.multiple_of(x * SHARE, SHARE), SHARE)
    half = UNITS // 2
    for w, k, start, size, out in (
        (own_ref, 0, 0, UNITS, o0),
        (right_ref, 1, 0, UNITS, o1),
        (top_ref, 2, 0, half, o2),
        (bottom_ref, 2, half, half, o2),
        (left_ref, 3, 0, UNITS, o3),
    ):
        base = lax.rem(x + k, REPS) * UNITS + start
        gate_ref[pl.ds(pl.multiple_of(base, half), size), :] = dot(w[...], whole, NT)
        out[start : start + size, :] = dot(w[:, share], cut, NT).astype(out.dtype)
    cut_projected = dot(probes_ref[:, share], cut, NT)
    for out in (o0, o1, o2, o3):
        out[UNITS:, :] = cut_projected.astype(out.dtype)
    projected = dot(probes_ref[...], whole, NT).astype(BF)
    partial_ref[...] = dot(projected, whole)
    for k, out in enumerate((i0, i1, i2, i3)):
        base = lax.rem(x + k, REPS) * SHARE
        out[...] = partial_ref[:, pl.ds(pl.multiple_of(base, SHARE), SHARE)].astype(out.dtype)


def finish_input(inverse_ref, cut_ref, s0, s1, s2, s3, i0, i1, i2, i3, out_ref):
    projected = s0[UNITS:, :] + (
        s1[UNITS:, :].astype(F32) + s2[UNITS:, :].astype(F32) + s3[UNITS:, :].astype(F32)
    )
    total = dot(projected.astype(BF), cut_ref[...])
    total += i0[...] + (i1[...].astype(F32) + i2[...].astype(F32) + i3[...].astype(F32))
    out_ref[...] = (total * inverse_ref[0]).T


def gate_gradient(gate, grads):
    s = 1.0 / (1.0 + jnp.exp(-gate))
    return (grads * (s * (1.0 + gate * (1.0 - s)))).astype(BF)


def gate_part(
    pos_ref, grad_probes_ref, probe_share_ref, gate_ref, got_ref, s0, s1, s2, s3,
    cut_grad_ref, t0, t1, t2, t3, grads_ref, sketch_ref,
):
    x = pos_ref[0]
    same = ones_where(iota((STRIP, STRIP), 0) == iota((STRIP, STRIP), 1))
    turned = dot(same, got_ref[...], NT).astype(BF)
    source, target = iota((ROWS, SLOTS), 0), iota((ROWS, SLOTS), 1)
    cut_parts = []
    for b in range(4):
        taken = dot(turned, ones_where(source == 4 * target + b))
        grads_ref[b * UNITS : (b + 1) * UNITS, :] = taken[:UNITS]
        if b < 3:
            cut_parts.append(taken[UNITS:])
    cut_gate = s0[:UNITS, :] + (
        s1[:UNITS, :].astype(F32) + s2[:UNITS, :].astype(F32) + s3[:UNITS, :].astype(F32)
    )
    cut_grad = gate_gradient(cut_gate, jnp.concatenate(cut_parts, 0))
    cut_grad_ref[...] = cut_grad
    cut_projected = dot(probe_share_ref[...], cut_grad)
    gate_grad = gate_gradient(gate_ref[...], grads_ref[...])
    projected = dot(grad_probes_ref[...], gate_grad).astype(BF)
    sketch_ref[...] = dot(gate_grad, projected, NT)
    for k, out in enumerate((t0, t1, t2, t3)):
        base = lax.rem(x + k, REPS) * UNITS
        sketch = sketch_ref[pl.ds(pl.multiple_of(base, UNITS), UNITS), :]
        out[:UNITS, :] = sketch.astype(out.dtype)
        out[UNITS : UNITS + R, :] = cut_projected[:, :128].astype(out.dtype)
        out[UNITS + R :, :] = cut_projected[:, 128:].astype(out.dtype)


def finish_grad(inverse_ref, cut_grad_ref, t0, t1, t2, t3, out_ref):
    total = t0[...] + (t1[...].astype(F32) + t2[...].astype(F32) + t3[...].astype(F32))
    projected = total[UNITS:].astype(BF)
    sketch = total[:UNITS] + dot(cut_grad_ref[:, :128], projected[:R], NT)
    sketch += dot(cut_grad_ref[:, 128:], projected[R:], NT)
    out_ref[...] = sketch * inverse_ref[0]


def shift(block, k):
    return lax.ppermute(block, "rep", [(i, (i + k) % REPS) for i in range(REPS)])


def shifted(blocks):
    return [blocks[0]] + [shift(blocks[k], k) for k in range(1, REPS)]


def to_owners(rows):
    width = rows.shape[1]
    rows = rows.reshape(OWNERS, FOLD, width)
    return lax.all_to_all(rows, "ep", split_axis=0, concat_axis=0, tiled=True).reshape(ROWS, width)


def local(tokens, expert_ids, hidden_grads, gate_weight, probes, grad_probes, window_counts):
    sds = jax.ShapeDtypeStruct
    x = lax.axis_index("rep")
    pos = x.astype(jnp.int32).reshape(1)
    inverse = 1.0 / window_counts.astype(F32)
    ids_t = expert_ids.T
    flat_ids = expert_ids.reshape(1, TOK * TOP)
    probe_share = lax.dynamic_slice_in_dim(grad_probes, x * UNITS, UNITS, 1)

    out_rows = kernel_call(
        send_rows, sds((ROWS, SHARE + STRIP), BF), [SM] + [VM] * 2, 1 << 31, 4 << 20
    )(pos, ids_t, tokens)
    rows = to_owners(out_rows)

    own = gate_weight[0]
    own, _ = lax.optimization_barrier((own, out_rows))
    left, right = shift(own, 1), shift(own, REPS - 1)
    top = shift(left[: UNITS // 2], 1)
    bottom = shift(right[UNITS // 2 :], REPS - 1)

    tail, *picked = kernel_call(
        pick_grads,
        [sds((ROWS, STRIP), BF)] + [sds((SLOTS, STRIP), BF)] * REPS,
        [SM] + [VM] * 3,
        4 << 30,
        3 << 20,
    )(pos, ids_t, flat_ids, hidden_grads.reshape(TOK * TOP, UNITS))
    picked = shifted(picked)
    out_grads = kernel_call(
        fold_grads, sds((ROWS, STRIP), BF), [SM] + [VM] * 5, 1 << 29, 3 << 20
    )(pos, tail, *picked)
    out_grads, left, right, top, bottom = lax.optimization_barrier(
        (out_grads, left, right, top, bottom)
    )
    got = to_owners(out_grads)

    kinds = [F32, BF, BF, BF]
    gate, cut, *sums = kernel_call(
        products,
        [sds((FFW, SLOTS), F32), sds((SLOTS, SHARE), BF)]
        + [sds((UNITS + R, SLOTS), kind) for kind in kinds]
        + [sds((R, SHARE), kind) for kind in kinds],
        [SM] + [VM] * 7,
        6 << 30,
        14 << 20,
        [pltpu.VMEM((SLOTS, D), BF), pltpu.VMEM((R, D), F32)],
    )(pos, rows, probes, own, left, right, top, bottom)
    cut_sums = shifted(sums[:REPS])
    input_sums = shifted(sums[REPS:])

    cut_grad, *sketches = kernel_call(
        gate_part,
        [sds((UNITS, SLOTS), BF)] + [sds((UNITS + 2 * R, 128), kind) for kind in kinds],
        [SM] + [VM] * 8,
        2 << 30,
        4 << 20,
        [pltpu.VMEM((FFW, SLOTS), F32), pltpu.VMEM((FFW, R), F32)],
    )(pos, grad_probes, probe_share, gate, got, *cut_sums)
    sketches = shifted(sketches)

    input_sketch = kernel_call(
        finish_input, sds((SHARE, R), F32), [SM] + [VM] * 9, 1 << 28, 4 << 20
    )(inverse, cut, *cut_sums, *input_sums)
    grad_sketch = kernel_call(
        finish_grad, sds((UNITS, R), F32), [SM] + [VM] * 5, 1 << 24, 1 << 20
    )(inverse, cut_grad, *sketches)
    return input_sketch[None], grad_sketch[None]


def solution(mesh):
    placed = (
        P("ep", None),
        P("ep", None),
        P("ep", None, "rep"),
        P("ep", "rep", None),
        P(),
        P(),
        P("ep"),
    )
    return jax.shard_map(
        local,
        mesh=mesh,
        in_specs=placed,
        out_specs=(P("ep", "rep", None), P("ep", "rep", None)),
        check_vma=False,
    )
```

time: 733 us -> 167 us (0.23)
  the two profiles are of different devices: /device:TPU:32 before, /device:TPU:8 now
where the time goes in v2:
time: 167 us; the launch traced here: 166 us
  starting transfers between devices  85.4 us (51%)
  waiting for transfers between devices  41.2 us (25%)
  Pallas kernels  26 us (16%)
  local copies, waits for them, and re-layouts  11.6 us (7%)
    ppermute x16, starting transfers between devices, shift(): lax.ppermute(block, 'rep', [(i, (i + k) % REPS) for i in range(REPS)])  54.3 us
    ppermute x16, waiting for transfers between devices, shift(): lax.ppermute(block, 'rep', [(i, (i + k) % REPS) for i in range(REPS)])  41.2 us
    all_to_all x2, starting transfers between devices, to_owners(): lax.all_to_all(rows, 'ep', split_axis=0, concat_axis=0, tiled=True)  31.1 us
    pallas_call x1, Pallas kernels, local(): kernel_call(products, [sds((FFW, SLOTS), F32), sds((SLOTS, SHARE), BF)] +...  13.5 us
    unnamed x24, local copies, waits for them, and re-layouts  8.46 us
    pallas_call x1, Pallas kernels, local(): kernel_call(pick_grads, [sds((ROWS, STRIP), BF)] + [sds((SLOTS, STRIP), B...  3.91 us
    pallas_call x1, Pallas kernels, local(): kernel_call(send_rows, sds((ROWS, SHARE + STRIP), BF), [SM] + [VM] * 2, 1...  3.43 us
  transfers between devices with their start and end apart: 18, of which 4 were waited for; matrix products, arithmetic and copies ran while one was open for 3% of the time, Pallas kernels for 13%

profile of v2, /device:TPU:8, one launch (start us, length us, event | category | flops | bytes accessed | tf_op | source)
XLA Modules:
  0.0 165.8 jit_solution(10360293863171016374)
XLA Ops:
  0.6 0.0 copy-start.1
  0.6 0.7 copy-done.1
  1.3 1.2 copy-done.3
  2.5 3.4 %shard_map.86 = bf16[1024,1280]{1,0:T(8,128)(2,1)} custom-call(s32[1]{0:T(128)} %bitcast.pos_ref, s32[8,128]{1,0:T(8,128)S(1)} %bitcast.12, bf16[128,4096]{1,0:T(8,128)(2,1)S(1)} %copy-done.3), custom_call_target="tpu_custom_call" | custom-call | flops 2147483648 | bytes 4194304 | tf_op jit(solution)/shard_map/pallas_call | solution.py:245
  6.0 17.4 %all-to-all-start = ((bf16[128,8,1280]{2,1,0:T(8,128)(2,1)}), bf16[128,8,1280]{2,1,0:T(8,128)(2,1)S(1)}, u32[]{:S(2)}, u32[]{:S(2)}) async-start(bf16[128,8,1280]{2,1,0:T(8,128)(2,1)} %bitcast.2), calls=%async_computation | async-start | bytes 5242880 | tf_op jit(solution)/shard_map/all_to_all | solution.py:233
  23.3 0.0 copy-start.2
  23.4 0.0 copy-start.8
  23.4 3.5 %collective-permute-start.3 = (bf16[192,4096]{1,0:T(8,128)(2,1)}, bf16[192,4096]{1,0:T(8,128)(2,1)S(1)}, u32[]{:S(2)}, u32[]{:S(2)}) collective-permute-start(bf16[192,4096]{1,0:T(8,128)(2,1)} %bitcast.17), channel_id=1, source_target_pairs={{0,1},{1,2},{2,3},{3,0},{4,5},{5,6},{6,7},{7,4},{8,9},{9,10},{10,1... | collective-permute-start | bytes 4718600 | tf_op jit(solution)/shard_map/ppermute | solution.py:223
  26.9 3.7 %collective-permute-start.4 = (bf16[192,4096]{1,0:T(8,128)(2,1)}, bf16[192,4096]{1,0:T(8,128)(2,1)S(1)}, u32[]{:S(2)}, u32[]{:S(2)}) collective-permute-start(bf16[192,4096]{1,0:T(8,128)(2,1)} %bitcast.18), channel_id=1, source_target_pairs={{0,3},{1,0},{2,1},{3,2},{4,7},{5,4},{6,5},{7,6},{8,11},{9,8},{10,9... | collective-permute-start | bytes 4718600 | tf_op jit(solution)/shard_map/ppermute | solution.py:223
  30.6 32.7 %collective-permute-done.3.left_ref = bf16[192,4096]{1,0:T(8,128)(2,1)S(1)} collective-permute-done((bf16[192,4096]{1,0:T(8,128)(2,1)}, bf16[192,4096]{1,0:T(8,128)(2,1)S(1)}, u32[]{:S(2)}, u32[]{:S(2)}) %collective-permute-start.3) | collective-permute-done | bytes 1572896 | tf_op jit(solution)/shard_map/ppermute | solution.py:223
  63.3 1.1 slice.8
  64.4 2.2 %collective-permute-start.5 = (bf16[96,4096]{1,0:T(8,128)(2,1)}, bf16[96,4096]{1,0:T(8,128)(2,1)}, u32[]{:S(2)}, u32[]{:S(2)}) collective-permute-start(bf16[96,4096]{1,0:T(8,128)(2,1)} %slice.8), channel_id=1, source_target_pairs={{0,1},{1,2},{2,3},{3,0},{4,5},{5,6},{6,7},{7,4},{8,9},{9,10},{10,1... | collective-permute-start | bytes 2359304 | tf_op jit(solution)/shard_map/ppermute | solution.py:223
  66.5 0.0 collective-permute-done.4.right_ref
  66.6 1.2 copy-done.10
  67.7 1.0 slice.9
  68.7 4.9 %collective-permute-start.6 = (bf16[96,4096]{1,0:T(8,128)(2,1)}, bf16[96,4096]{1,0:T(8,128)(2,1)}, u32[]{:S(2)}, u32[]{:S(2)}) collective-permute-start(bf16[96,4096]{1,0:T(8,128)(2,1)} %slice.9), channel_id=1, source_target_pairs={{0,3},{1,0},{2,1},{3,2},{4,7},{5,4},{6,5},{7,6},{8,11},{9,8},{10,9... | collective-permute-start | bytes 2359304 | tf_op jit(solution)/shard_map/ppermute | solution.py:223
  73.6 0.7 copy.11
  74.3 0.4 copy.12
  74.7 0.9 reshape.28.flat_ref
  75.7 3.9 %shard_map.87 = (bf16[1024,256]{1,0:T(8,128)(2,1)S(1)}, bf16[256,256]{1,0:T(8,128)(2,1)S(1)}, bf16[256,256]{1,0:T(8,128)(2,1)S(1)}, bf16[256,256]{1,0:T(8,128)(2,1)S(1)}, bf16[256,256]{1,0:T(8,128)(2,1)S(1)}) custom-call(s32[1]{0:T(128)} %bitcast.pos_ref, s32[8,128]{1,0:T(8,128)S(1)} %bitcast.13, s32[1,1024]{1,0:T(1,128)S(1)} %reshape.28.flat_ref, ...), custom_call_target="tpu_custom_call" | custom-call | flops 4294967296 | bytes 3145728 | tf_op jit(solution)/shard_map/pallas_call | solution.py:256
  79.6 1.9 %collective-permute-start = (bf16[256,256]{1,0:T(8,128)(2,1)S(1)}, bf16[256,256]{1,0:T(8,128)(2,1)S(1)}, u32[]{:S(2)}, u32[]{:S(2)}) collective-permute-start(bf16[256,256]{1,0:T(8,128)(2,1)S(1)} %get-tuple-element.31), channel_id=1, source_target_pairs={{0,1},{1,2},{2,3},{3,0},{4,5},{5,6},{6,7},{7,4},{8,9},{9,10},{10,1... | collective-permute-start | bytes 393224 | tf_op jit(solution)/shard_map/ppermute | solution.py:223
  81.5 3.7 %collective-permute-start.1 = (bf16[256,256]{1,0:T(8,128)(2,1)S(1)}, bf16[256,256]{1,0:T(8,128)(2,1)S(1)}, u32[]{:S(2)}, u32[]{:S(2)}) collective-permute-start(bf16[256,256]{1,0:T(8,128)(2,1)S(1)} %get-tuple-element.32), channel_id=1, source_target_pairs={{0,2},{1,3},{2,0},{3,1},{4,6},{5,7},{6,4},{7,5},{8,10},{9,11},{10,... | collective-permute-start | bytes 393224 | tf_op jit(solution)/shard_map/ppermute | solution.py:223
  85.2 3.4 %collective-permute-start.2 = (bf16[256,256]{1,0:T(8,128)(2,1)S(1)}, bf16[256,256]{1,0:T(8,128)(2,1)S(1)}, u32[]{:S(2)}, u32[]{:S(2)}) collective-permute-start(bf16[256,256]{1,0:T(8,128)(2,1)S(1)} %get-tuple-element.33), channel_id=1, source_target_pairs={{0,3},{1,0},{2,1},{3,2},{4,7},{5,4},{6,5},{7,6},{8,11},{9,8},{10,9... | collective-permute-start | bytes 393224 | tf_op jit(solution)/shard_map/ppermute | solution.py:223
  88.6 3.4 %collective-permute-done.g1 = bf16[256,256]{1,0:T(8,128)(2,1)S(1)} collective-permute-done((bf16[256,256]{1,0:T(8,128)(2,1)S(1)}, bf16[256,256]{1,0:T(8,128)(2,1)S(1)}, u32[]{:S(2)}, u32[]{:S(2)}) %collective-permute-start) | collective-permute-done | bytes 131104 | tf_op jit(solution)/shard_map/ppermute | solution.py:223
  92.0 0.0 collective-permute-done.1.g2
  92.0 3.4 %collective-permute-done.2.g3 = bf16[256,256]{1,0:T(8,128)(2,1)S(1)} collective-permute-done((bf16[256,256]{1,0:T(8,128)(2,1)S(1)}, bf16[256,256]{1,0:T(8,128)(2,1)S(1)}, u32[]{:S(2)}, u32[]{:S(2)}) %collective-permute-start.2) | collective-permute-done | bytes 131104 | tf_op jit(solution)/shard_map/ppermute | solution.py:223
  95.4 1.5 shard_map.88
  96.9 1.5 copy-done.7
  98.4 13.7 %all-to-all-start.1 = ((bf16[128,8,256]{2,1,0:T(8,128)(2,1)}), bf16[128,8,256]{2,1,0:T(8,128)(2,1)S(1)}, u32[]{:S(2)}, u32[]{:S(2)}) async-start(bf16[128,8,256]{2,1,0:T(8,128)(2,1)} %bitcast.7), calls=%async_computation.1 | async-start | bytes 1048576 | tf_op jit(solution)/shard_map/all_to_all | solution.py:233
  112.2 0.0 copy-start
  112.2 13.5 %shard_map.89 = (f32[768,256]{1,0:T(8,128)S(1)}, bf16[256,1024]{1,0:T(8,128)(2,1)S(1)}, f32[320,256]{1,0:T(8,128)S(1)}, bf16[320,256]{1,0:T(8,128)(2,1)S(1)}, bf...) custom-call(s32[1]{0:T(128)} %bitcast.pos_ref, ...), custom_call_target="tpu_custom_call" | custom-call | flops 6442450944 | bytes 14680064 | tf_op jit(solution)/shard_map/pallas_call | solution.py:273
  125.7 0.7 copy-done.4
  126.4 0.9 copy-done.5
  127.3 2.9 %collective-permute-start.7 = (bf16[320,256]{1,0:T(8,128)(2,1)S(1)}, bf16[320,256]{1,0:T(8,128)(2,1)S(1)}, u32[]{:S(2)}, u32[]{:S(2)}) collective-permute-start(bf16[320,256]{1,0:T(8,128)(2,1)S(1)} %get-tuple-element.40), channel_id=1, source_target_pairs={{0,1},{1,2},{2,3},{3,0},{4,5},{5,6},{6,7},{7,4},{8,9},{9,10},{10,1... | collective-permute-start | bytes 491528 | tf_op jit(solution)/shard_map/ppermute | solution.py:223
  130.3 6.1 %collective-permute-start.8 = (bf16[320,256]{1,0:T(8,128)(2,1)}, bf16[320,256]{1,0:T(8,128)(2,1)S(1)}, u32[]{:S(2)}, u32[]{:S(2)}) collective-permute-start(bf16[320,256]{1,0:T(8,128)(2,1)} %get-tuple-element.41), channel_id=1, source_target_pairs={{0,2},{1,3},{2,0},{3,1},{4,6},{5,7},{6,4},{7,5},{8,10},{9,11},{10,... | collective-permute-start | bytes 491528 | tf_op jit(solution)/shard_map/ppermute | solution.py:223
  136.3 1.9 %collective-permute-start.9 = (bf16[320,256]{1,0:T(8,128)(2,1)}, bf16[320,256]{1,0:T(8,128)(2,1)S(1)}, u32[]{:S(2)}, u32[]{:S(2)}) collective-permute-start(bf16[320,256]{1,0:T(8,128)(2,1)} %get-tuple-element.42), channel_id=1, source_target_pairs={{0,3},{1,0},{2,1},{3,2},{4,7},{5,4},{6,5},{7,6},{8,11},{9,8},{10,9... | collective-permute-start | bytes 491528 | tf_op jit(solution)/shard_map/ppermute | solution.py:223
  138.3 3.9 %collective-permute-start.10 = (bf16[128,1024]{1,0:T(8,128)(2,1)}, bf16[128,1024]{1,0:T(8,128)(2,1)S(1)}, u32[]{:S(2)}, u32[]{:S(2)}) collective-permute-start(bf16[128,1024]{1,0:T(8,128)(2,1)} %get-tuple-element.44), channel_id=1, source_target_pairs={{0,1},{1,2},{2,3},{3,0},{4,5},{5,6},{6,7},{7,4},{8,9},{9,10},{10,1... | collective-permute-start | bytes 786440 | tf_op jit(solution)/shard_map/ppermute | solution.py:223
  142.2 0.1 constant_dynamic-slice_fusion.probe_share_ref
  142.3 1.9 %collective-permute-start.11 = (bf16[128,1024]{1,0:T(8,128)(2,1)}, bf16[128,1024]{1,0:T(8,128)(2,1)S(1)}, u32[]{:S(2)}, u32[]{:S(2)}) collective-permute-start(bf16[128,1024]{1,0:T(8,128)(2,1)} %get-tuple-element.45), channel_id=1, source_target_pairs={{0,2},{1,3},{2,0},{3,1},{4,6},{5,7},{6,4},{7,5},{8,10},{9,11},{10,... | collective-permute-start | bytes 786440 | tf_op jit(solution)/shard_map/ppermute | solution.py:223
  144.2 4.6 %collective-permute-start.12 = (bf16[128,1024]{1,0:T(8,128)(2,1)}, bf16[128,1024]{1,0:T(8,128)(2,1)S(1)}, u32[]{:S(2)}, u32[]{:S(2)}) collective-permute-start(bf16[128,1024]{1,0:T(8,128)(2,1)} %copy-done.4), channel_id=1, source_target_pairs={{0,3},{1,0},{2,1},{3,2},{4,7},{5,4},{6,5},{7,6},{8,11},{9,8},{10,9... | collective-permute-start | bytes 786440 | tf_op jit(solution)/shard_map/ppermute | solution.py:223
  148.9 1.1 copy-done.6
  150.0 1.6 shard_map.91
  151.6 1.9 %collective-permute-start.13 = (bf16[448,128]{1,0:T(8,128)(2,1)S(1)}, bf16[448,128]{1,0:T(8,128)(2,1)S(1)}, u32[]{:S(2)}, u32[]{:S(2)}) collective-permute-start(bf16[448,128]{1,0:T(8,128)(2,1)S(1)} %get-tuple-element.51), channel_id=1, source_target_pairs={{0,1},{1,2},{2,3},{3,0},{4,5},{5,6},{6,7},{7,4},{8,9},{9,10},{10,1... | collective-permute-start | bytes 344072 | tf_op jit(solution)/shard_map/ppermute | solution.py:223
  153.5 4.8 %collective-permute-start.14 = (bf16[448,128]{1,0:T(8,128)(2,1)S(1)}, bf16[448,128]{1,0:T(8,128)(2,1)S(1)}, u32[]{:S(2)}, u32[]{:S(2)}) collective-permute-start(bf16[448,128]{1,0:T(8,128)(2,1)S(1)} %get-tuple-element.52), channel_id=1, source_target_pairs={{0,2},{1,3},{2,0},{3,1},{4,6},{5,7},{6,4},{7,5},{8,10},{9,11},{10,... | collective-permute-start | bytes 344072 | tf_op jit(solution)/shard_map/ppermute | solution.py:223
  158.3 3.1 %collective-permute-start.15 = (bf16[448,128]{1,0:T(8,128)(2,1)S(1)}, bf16[448,128]{1,0:T(8,128)(2,1)S(1)}, u32[]{:S(2)}, u32[]{:S(2)}) collective-permute-start(bf16[448,128]{1,0:T(8,128)(2,1)S(1)} %get-tuple-element.53), channel_id=1, source_target_pairs={{0,3},{1,0},{2,1},{3,2},{4,7},{5,4},{6,5},{7,6},{8,11},{9,8},{10,9... | collective-permute-start | bytes 344072 | tf_op jit(solution)/shard_map/ppermute | solution.py:223
  162.2 1.2 shard_map.90
  163.3 1.7 %collective-permute-done.15.t3 = bf16[448,128]{1,0:T(8,128)(2,1)S(1)} collective-permute-done((bf16[448,128]{1,0:T(8,128)(2,1)S(1)}, bf16[448,128]{1,0:T(8,128)(2,1)S(1)}, u32[]{:S(2)}, u32[]{:S(2)}) %collective-permute-start.15) | collective-permute-done | bytes 114720 | tf_op jit(solution)/shard_map/ppermute | solution.py:223
  165.0 0.8 shard_map.92
  (23 shorter events, 0.1 us)
Async XLA Ops:
  0.6 0.7 copy-start.1
  1.3 1.2 copy-start.3
  6.0 90.9 %all-to-all-start = ((bf16[128,8,1280]{2,1,0:T(8,128)(2,1)}), bf16[128,8,1280]{2,1,0:T(8,128)(2,1)S(1)}, u32[]{:S(2)}, u32[]{:S(2)}) async-start(bf16[128,8,1280]{2,1,0:T(8,128)(2,1)} %bitcast.2), calls=%async_computation | async-start | bytes 5242880 | tf_op jit(solution)/shard_map/all_to_all | solution.py:233
  23.3 50.2 %copy-start.2 = (s32[128,8]{0,1:T(8,128)S(1)}, s32[128,8]{0,1:T(8,128)}, u32[]{:S(2)}) copy-start(s32[128,8]{0,1:T(8,128)} %param.8) | copy-start | bytes 12292
  23.4 51.0 %copy-start.8 = (bf16[128,8,192]{0,2,1:T(8,128)(2,1)S(1)}, bf16[128,8,192]{0,2,1:T(8,128)(2,1)}, u32[]{:S(2)}) copy-start(bf16[128,8,192]{0,2,1:T(8,128)(2,1)} %param.9) | copy-start | bytes 1179652
  23.4 39.9 %collective-permute-start.3 = (bf16[192,4096]{1,0:T(8,128)(2,1)}, bf16[192,4096]{1,0:T(8,128)(2,1)S(1)}, u32[]{:S(2)}, u32[]{:S(2)}) collective-permute-start(bf16[192,4096]{1,0:T(8,128)(2,1)} %bitcast.17), channel_id=1, source_target_pairs={{0,1},{1,2},{2,3},{3,0},{4,5},{5,6},{6,7},{7,4},{8,9},{9,10},{10,1... | collective-permute-start | bytes 4718600 | tf_op jit(solution)/shard_map/ppermute | solution.py:223
  26.9 39.6 %collective-permute-start.4 = (bf16[192,4096]{1,0:T(8,128)(2,1)}, bf16[192,4096]{1,0:T(8,128)(2,1)S(1)}, u32[]{:S(2)}, u32[]{:S(2)}) collective-permute-start(bf16[192,4096]{1,0:T(8,128)(2,1)} %bitcast.18), channel_id=1, source_target_pairs={{0,3},{1,0},{2,1},{3,2},{4,7},{5,4},{6,5},{7,6},{8,11},{9,8},{10,9... | collective-permute-start | bytes 4718600 | tf_op jit(solution)/shard_map/ppermute | solution.py:223
  63.3 5.5 %copy-start.9 = (bf16[192,4096]{1,0:T(8,128)(2,1)}, bf16[192,4096]{1,0:T(8,128)(2,1)S(1)}, u32[]{:S(2)}) copy-start(bf16[192,4096]{1,0:T(8,128)(2,1)S(1)} %collective-permute-done.3.left_ref) | copy-start | bytes 4718596
  64.4 32.6 %collective-permute-start.5 = (bf16[96,4096]{1,0:T(8,128)(2,1)}, bf16[96,4096]{1,0:T(8,128)(2,1)}, u32[]{:S(2)}, u32[]{:S(2)}) collective-permute-start(bf16[96,4096]{1,0:T(8,128)(2,1)} %slice.8), channel_id=1, source_target_pairs={{0,1},{1,2},{2,3},{3,0},{4,5},{5,6},{6,7},{7,4},{8,9},{9,10},{10,1... | collective-permute-start | bytes 2359304 | tf_op jit(solution)/shard_map/ppermute | solution.py:223
  66.6 1.2 copy-start.10
  68.7 28.2 %collective-permute-start.6 = (bf16[96,4096]{1,0:T(8,128)(2,1)}, bf16[96,4096]{1,0:T(8,128)(2,1)}, u32[]{:S(2)}, u32[]{:S(2)}) collective-permute-start(bf16[96,4096]{1,0:T(8,128)(2,1)} %slice.9), channel_id=1, source_target_pairs={{0,3},{1,0},{2,1},{3,2},{4,7},{5,4},{6,5},{7,6},{8,11},{9,8},{10,9... | collective-permute-start | bytes 2359304 | tf_op jit(solution)/shard_map/ppermute | solution.py:223
  79.6 12.4 %collective-permute-start = (bf16[256,256]{1,0:T(8,128)(2,1)S(1)}, bf16[256,256]{1,0:T(8,128)(2,1)S(1)}, u32[]{:S(2)}, u32[]{:S(2)}) collective-permute-start(bf16[256,256]{1,0:T(8,128)(2,1)S(1)} %get-tuple-element.31), channel_id=1, source_target_pairs={{0,1},{1,2},{2,3},{3,0},{4,5},{5,6},{6,7},{7,4},{8,9},{9,10},{10,1... | collective-permute-start | bytes 393224 | tf_op jit(solution)/shard_map/ppermute | solution.py:223
  81.5 10.5 %collective-permute-start.1 = (bf16[256,256]{1,0:T(8,128)(2,1)S(1)}, bf16[256,256]{1,0:T(8,128)(2,1)S(1)}, u32[]{:S(2)}, u32[]{:S(2)}) collective-permute-start(bf16[256,256]{1,0:T(8,128)(2,1)S(1)} %get-tuple-element.32), channel_id=1, source_target_pairs={{0,2},{1,3},{2,0},{3,1},{4,6},{5,7},{6,4},{7,5},{8,10},{9,11},{10,... | collective-permute-start | bytes 393224 | tf_op jit(solution)/shard_map/ppermute | solution.py:223
  85.2 10.2 %collective-permute-start.2 = (bf16[256,256]{1,0:T(8,128)(2,1)S(1)}, bf16[256,256]{1,0:T(8,128)(2,1)S(1)}, u32[]{:S(2)}, u32[]{:S(2)}) collective-permute-start(bf16[256,256]{1,0:T(8,128)(2,1)S(1)} %get-tuple-element.33), channel_id=1, source_target_pairs={{0,3},{1,0},{2,1},{3,2},{4,7},{5,4},{6,5},{7,6},{8,11},{9,8},{10,9... | collective-permute-start | bytes 393224 | tf_op jit(solution)/shard_map/ppermute | solution.py:223
  96.9 1.5 copy-start.7
  98.4 50.4 %all-to-all-start.1 = ((bf16[128,8,256]{2,1,0:T(8,128)(2,1)}), bf16[128,8,256]{2,1,0:T(8,128)(2,1)S(1)}, u32[]{:S(2)}, u32[]{:S(2)}) async-start(bf16[128,8,256]{2,1,0:T(8,128)(2,1)} %bitcast.7), calls=%async_computation.1 | async-start | bytes 1048576 | tf_op jit(solution)/shard_map/all_to_all | solution.py:233
  112.2 30.0 %copy-start = (bf16[128,768]{1,0:T(8,128)(2,1)S(1)}, bf16[128,768]{1,0:T(8,128)(2,1)}, u32[]{:S(2)}) copy-start(bf16[128,768]{1,0:T(8,128)(2,1)} %grad_probes_ref.1) | copy-start | bytes 589828
  125.7 0.7 copy-start.4
  126.4 0.9 copy-start.5
  127.3 16.9 %collective-permute-start.7 = (bf16[320,256]{1,0:T(8,128)(2,1)S(1)}, bf16[320,256]{1,0:T(8,128)(2,1)S(1)}, u32[]{:S(2)}, u32[]{:S(2)}) collective-permute-start(bf16[320,256]{1,0:T(8,128)(2,1)S(1)} %get-tuple-element.40), channel_id=1, source_target_pairs={{0,1},{1,2},{2,3},{3,0},{4,5},{5,6},{6,7},{7,4},{8,9},{9,10},{10,1... | collective-permute-start | bytes 491528 | tf_op jit(solution)/shard_map/ppermute | solution.py:223
  130.3 18.6 %collective-permute-start.8 = (bf16[320,256]{1,0:T(8,128)(2,1)}, bf16[320,256]{1,0:T(8,128)(2,1)S(1)}, u32[]{:S(2)}, u32[]{:S(2)}) collective-permute-start(bf16[320,256]{1,0:T(8,128)(2,1)} %get-tuple-element.41), channel_id=1, source_target_pairs={{0,2},{1,3},{2,0},{3,1},{4,6},{5,7},{6,4},{7,5},{8,10},{9,11},{10,... | collective-permute-start | bytes 491528 | tf_op jit(solution)/shard_map/ppermute | solution.py:223
  136.3 12.5 %collective-permute-start.9 = (bf16[320,256]{1,0:T(8,128)(2,1)}, bf16[320,256]{1,0:T(8,128)(2,1)S(1)}, u32[]{:S(2)}, u32[]{:S(2)}) collective-permute-start(bf16[320,256]{1,0:T(8,128)(2,1)} %get-tuple-element.42), channel_id=1, source_target_pairs={{0,3},{1,0},{2,1},{3,2},{4,7},{5,4},{6,5},{7,6},{8,11},{9,8},{10,9... | collective-permute-start | bytes 491528 | tf_op jit(solution)/shard_map/ppermute | solution.py:223
  138.3 20.0 %collective-permute-start.10 = (bf16[128,1024]{1,0:T(8,128)(2,1)}, bf16[128,1024]{1,0:T(8,128)(2,1)S(1)}, u32[]{:S(2)}, u32[]{:S(2)}) collective-permute-start(bf16[128,1024]{1,0:T(8,128)(2,1)} %get-tuple-element.44), channel_id=1, source_target_pairs={{0,1},{1,2},{2,3},{3,0},{4,5},{5,6},{6,7},{7,4},{8,9},{9,10},{10,1... | collective-permute-start | bytes 786440 | tf_op jit(solution)/shard_map/ppermute | solution.py:223
  142.3 19.8 %collective-permute-start.11 = (bf16[128,1024]{1,0:T(8,128)(2,1)}, bf16[128,1024]{1,0:T(8,128)(2,1)S(1)}, u32[]{:S(2)}, u32[]{:S(2)}) collective-permute-start(bf16[128,1024]{1,0:T(8,128)(2,1)} %get-tuple-element.45), channel_id=1, source_target_pairs={{0,2},{1,3},{2,0},{3,1},{4,6},{5,7},{6,4},{7,5},{8,10},{9,11},{10,... | collective-permute-start | bytes 786440 | tf_op jit(solution)/shard_map/ppermute | solution.py:223
  144.2 17.9 %collective-permute-start.12 = (bf16[128,1024]{1,0:T(8,128)(2,1)}, bf16[128,1024]{1,0:T(8,128)(2,1)S(1)}, u32[]{:S(2)}, u32[]{:S(2)}) collective-permute-start(bf16[128,1024]{1,0:T(8,128)(2,1)} %copy-done.4), channel_id=1, source_target_pairs={{0,3},{1,0},{2,1},{3,2},{4,7},{5,4},{6,5},{7,6},{8,11},{9,8},{10,9... | collective-permute-start | bytes 786440 | tf_op jit(solution)/shard_map/ppermute | solution.py:223
  148.9 1.1 copy-start.6
  151.6 11.7 %collective-permute-start.13 = (bf16[448,128]{1,0:T(8,128)(2,1)S(1)}, bf16[448,128]{1,0:T(8,128)(2,1)S(1)}, u32[]{:S(2)}, u32[]{:S(2)}) collective-permute-start(bf16[448,128]{1,0:T(8,128)(2,1)S(1)} %get-tuple-element.51), channel_id=1, source_target_pairs={{0,1},{1,2},{2,3},{3,0},{4,5},{5,6},{6,7},{7,4},{8,9},{9,10},{10,1... | collective-permute-start | bytes 344072 | tf_op jit(solution)/shard_map/ppermute | solution.py:223
  153.5 9.8 %collective-permute-start.14 = (bf16[448,128]{1,0:T(8,128)(2,1)S(1)}, bf16[448,128]{1,0:T(8,128)(2,1)S(1)}, u32[]{:S(2)}, u32[]{:S(2)}) collective-permute-start(bf16[448,128]{1,0:T(8,128)(2,1)S(1)} %get-tuple-element.52), channel_id=1, source_target_pairs={{0,2},{1,3},{2,0},{3,1},{4,6},{5,7},{6,4},{7,5},{8,10},{9,11},{10,... | collective-permute-start | bytes 344072 | tf_op jit(solution)/shard_map/ppermute | solution.py:223
  158.3 6.7 %collective-permute-start.15 = (bf16[448,128]{1,0:T(8,128)(2,1)S(1)}, bf16[448,128]{1,0:T(8,128)(2,1)S(1)}, u32[]{:S(2)}, u32[]{:S(2)}) collective-permute-start(bf16[448,128]{1,0:T(8,128)(2,1)S(1)} %get-tuple-element.53), channel_id=1, source_target_pairs={{0,3},{1,0},{2,1},{3,2},{4,7},{5,4},{6,5},{7,6},{8,11},{9,8},{10,9... | collective-permute-start | bytes 344072 | tf_op jit(solution)/shard_map/ppermute | solution.py:223

commit v3 on v2

--- a/solution.py
+++ b/solution.py
@@ -19,6 +19,7 @@
 ROWS = OWNERS * FOLD
 SLOTS = OWNERS * 2
 STRIP = SHARE // 4
+LIMIT = 30 * 1024 * 1024
 
 BF = jnp.bfloat16
 F32 = jnp.float32
@@ -41,14 +42,15 @@
     return jnp.where(mask, 1.0, 0.0).astype(BF)
 
 
-def kernel_call(body, out_shape, in_specs, flops, bytes_accessed, scratch=()):
+def kernel_call(body, out_shape, in_specs, flops, bytes_accessed, scratch=(), grid=()):
     return pl.pallas_call(
         body,
+        grid=grid,
         out_shape=out_shape,
         in_specs=in_specs,
         out_specs=jax.tree.map(lambda _: VM, out_shape),
         scratch_shapes=list(scratch),
-        compiler_params=pltpu.CompilerParams(vmem_limit_bytes=50 * 1024 * 1024),
+        compiler_params=pltpu.CompilerParams(vmem_limit_bytes=LIMIT),
         cost_estimate=pl.CostEstimate(
             flops=flops, bytes_accessed=bytes_accessed, transcendentals=0
         ),
@@ -133,46 +135,59 @@
     out_ref[...] = total.astype(BF)
 
 
-def products(
-    pos_ref, rows_ref, probes_ref, own_ref, left_ref, right_ref, top_ref, bottom_ref,
-    gate_ref, cut_ref, o0, o1, o2, o3, i0, i1, i2, i3, whole_ref, partial_ref,
-):
-    x = pos_ref[0]
-    target, source = iota((SLOTS, ROWS), 0), iota((SLOTS, ROWS), 1)
-    for b in range(4):
-        got = dot(ones_where(source == 4 * target + b), rows_ref[...]).astype(BF)
-        whole_ref[:, b * SHARE : (b + 1) * SHARE] = got[:, :SHARE]
-        cut_ref[:, b * STRIP : (b + 1) * STRIP] = got[:, SHARE:]
-    whole, cut = whole_ref[...], cut_ref[...]
-    share = pl.ds(pl.multiple_of(x * SHARE, SHARE), SHARE)
+def stack_weights(pos_ref, probes_ref, own_ref, right_ref, top_ref, bottom_ref, left_ref, out_ref):
+    x = pos_ref[0]
     half = UNITS // 2
-    for w, k, start, size, out in (
-        (own_ref, 0, 0, UNITS, o0),
-        (right_ref, 1, 0, UNITS, o1),
-        (top_ref, 2, 0, half, o2),
-        (bottom_ref, 2, half, half, o2),
-        (left_ref, 3, 0, UNITS, o3),
+    for w, k, start, size in (
+        (own_ref, 0, 0, UNITS),
+        (right_ref, 1, 0, UNITS),
+        (top_ref, 2, 0, half),
+        (bottom_ref, 2, half, half),
+        (left_ref, 3, 0, UNITS),
     ):
         base = lax.rem(x + k, REPS) * UNITS + start
-        gate_ref[pl.ds(pl.multiple_of(base, half), size), :] = dot(w[...], whole, NT)
-        out[start : start + size, :] = dot(w[:, share], cut, NT).astype(out.dtype)
-    cut_projected = dot(probes_ref[:, share], cut, NT)
-    for out in (o0, o1, o2, o3):
-        out[UNITS:, :] = cut_projected.astype(out.dtype)
-    projected = dot(probes_ref[...], whole, NT).astype(BF)
-    partial_ref[...] = dot(projected, whole)
-    for k, out in enumerate((i0, i1, i2, i3)):
-        base = lax.rem(x + k, REPS) * SHARE
-        out[...] = partial_ref[:, pl.ds(pl.multiple_of(base, SHARE), SHARE)].astype(out.dtype)
-
-
-def finish_input(inverse_ref, cut_ref, s0, s1, s2, s3, i0, i1, i2, i3, out_ref):
-    projected = s0[UNITS:, :] + (
-        s1[UNITS:, :].astype(F32) + s2[UNITS:, :].astype(F32) + s3[UNITS:, :].astype(F32)
-    )
-    total = dot(projected.astype(BF), cut_ref[...])
-    total += i0[...] + (i1[...].astype(F32) + i2[...].astype(F32) + i3[...].astype(F32))
-    out_ref[...] = (total * inverse_ref[0]).T
+        out_ref[pl.ds(pl.multiple_of(base, half), size), :] = w[...]
+    out_ref[FFW:, :] = probes_ref[...]
+
+
+def unfold(source, put):
+    shape = (256, 256)
+    order = ones_where(iota(shape, 1) == 4 * (iota(shape, 0) % 64) + iota(shape, 0) // 64)
+    for g in range(4):
+        got = dot(order, source[g * 256 : (g + 1) * 256, :]).astype(BF)
+        for b in range(4):
+            put(b, slice(g * 64, (g + 1) * 64), got[b * 64 : (b + 1) * 64])
+
+
+def cut_products(pos_ref, rows_ref, weights_ref, cut_ref, o0, o1, o2, o3):
+    x = pos_ref[0]
+
+    def put(b, at, got):
+        cut_ref[at, b * STRIP : (b + 1) * STRIP] = got
+
+    unfold(rows_ref, put)
+    cut = cut_ref[...]
+    projected = dot(weights_ref[FFW:, :], cut, NT)
+    for k, out in enumerate((o0, o1, o2, o3)):
+        base = lax.rem(x + k, REPS) * UNITS
+        weights = weights_ref[pl.ds(pl.multiple_of(base, UNITS), UNITS), :]
+        out[:UNITS, :] = dot(weights, cut, NT).astype(out.dtype)
+        out[UNITS:, :] = projected.astype(out.dtype)
+
+
+def whole_products(pos_ref, rows_ref, weights_ref, gate_ref, partial_ref, own_ref, whole_ref, sum_ref):
+    x = pos_ref[0]
+
+    def put(b, at, got):
+        whole_ref[at, b * SHARE : (b + 1) * SHARE] = got
+
+    unfold(rows_ref, put)
+    whole = whole_ref[...]
+    both = dot(weights_ref[...], whole, NT)
+    gate_ref[...] = both[:FFW]
+    sum_ref[...] = dot(both[FFW:].astype(BF), whole)
+    partial_ref[...] = sum_ref[...].astype(BF)
+    own_ref[...] = sum_ref[:, pl.ds(pl.multiple_of(x * SHARE, SHARE), SHARE)]
 
 
 def gate_gradient(gate, grads):
@@ -181,26 +196,26 @@
 
 
 def gate_part(
-    pos_ref, grad_probes_ref, probe_share_ref, gate_ref, got_ref, s0, s1, s2, s3,
+    pos_ref, grad_probes_ref, probe_share_ref, gate_ref, partial_ref, got_ref, s0, s1, s2, s3,
     cut_grad_ref, t0, t1, t2, t3, grads_ref, sketch_ref,
 ):
     x = pos_ref[0]
+
+    def put(b, at, got):
+        grads_ref[b * SLOTS + at.start : b * SLOTS + at.stop, :] = got
+
+    unfold(got_ref, put)
     same = ones_where(iota((STRIP, STRIP), 0) == iota((STRIP, STRIP), 1))
-    turned = dot(same, got_ref[...], NT).astype(BF)
-    source, target = iota((ROWS, SLOTS), 0), iota((ROWS, SLOTS), 1)
-    cut_parts = []
-    for b in range(4):
-        taken = dot(turned, ones_where(source == 4 * target + b))
-        grads_ref[b * UNITS : (b + 1) * UNITS, :] = taken[:UNITS]
-        if b < 3:
-            cut_parts.append(taken[UNITS:])
+    turned = dot(same, grads_ref[...], NT)
+    parts = [turned[:, b * SLOTS : (b + 1) * SLOTS] for b in range(4)]
     cut_gate = s0[:UNITS, :] + (
         s1[:UNITS, :].astype(F32) + s2[:UNITS, :].astype(F32) + s3[:UNITS, :].astype(F32)
     )
-    cut_grad = gate_gradient(cut_gate, jnp.concatenate(cut_parts, 0))
+    cut_grad = gate_gradient(cut_gate, jnp.concatenate([p[UNITS:] for p in parts[:3]], 0))
     cut_grad_ref[...] = cut_grad
     cut_projected = dot(probe_share_ref[...], cut_grad)
-    gate_grad = gate_gradient(gate_ref[...], grads_ref[...])
+    whole = jnp.concatenate([p[:UNITS] for p in parts], 0)
+    gate_grad = gate_gradient(gate_ref[...], whole)
     projected = dot(grad_probes_ref[...], gate_grad).astype(BF)
     sketch_ref[...] = dot(gate_grad, projected, NT)
     for k, out in enumerate((t0, t1, t2, t3)):
@@ -208,15 +223,40 @@
         sketch = sketch_ref[pl.ds(pl.multiple_of(base, UNITS), UNITS), :]
         out[:UNITS, :] = sketch.astype(out.dtype)
         out[UNITS : UNITS + R, :] = cut_projected[:, :128].astype(out.dtype)
-        out[UNITS + R :, :] = cut_projected[:, 128:].astype(out.dtype)
-
-
-def finish_grad(inverse_ref, cut_grad_ref, t0, t1, t2, t3, out_ref):
-    total = t0[...] + (t1[...].astype(F32) + t2[...].astype(F32) + t3[...].astype(F32))
+        out[UNITS + R : UNITS + 2 * R, :] = cut_projected[:, 128:].astype(out.dtype)
+        if k > 0:
+            base = lax.rem(x + k, REPS) * SHARE
+            for j in range(SHARE // 128):
+                start = UNITS + (2 + j) * R
+                columns = pl.ds(pl.multiple_of(base + j * 128, 128), 128)
+                out[start : start + R, :] = partial_ref[:, columns]
+
+
+def finish(
+    inverse_ref, cut_ref, own_ref, s0, s1, s2, s3, cut_grad_ref, t0, t1, t2, t3,
+    input_ref, grad_ref,
+):
+    inverse = inverse_ref[0]
+    others = (t1, t2, t3)
+    mixed = UNITS + 2 * R
+    total = t0[...] + (
+        t1[:mixed, :].astype(F32) + t2[:mixed, :].astype(F32) + t3[:mixed, :].astype(F32)
+    )
     projected = total[UNITS:].astype(BF)
     sketch = total[:UNITS] + dot(cut_grad_ref[:, :128], projected[:R], NT)
     sketch += dot(cut_grad_ref[:, 128:], projected[R:], NT)
-    out_ref[...] = sketch * inverse_ref[0]
+    grad_ref[...] = sketch * inverse
+
+    projected = s0[UNITS:, :] + (
+        s1[UNITS:, :].astype(F32) + s2[UNITS:, :].astype(F32) + s3[UNITS:, :].astype(F32)
+    )
+    total = own_ref[...] + dot(projected.astype(BF), cut_ref[...])
+    for j in range(SHARE // 128):
+        start = mixed + j * R
+        block = total[:, j * 128 : (j + 1) * 128]
+        for other in others:
+            block += other[start : start + R, :].astype(F32)
+        input_ref[j * 128 : (j + 1) * 128, :] = (block * inverse).T
 
 
 def shift(block, k):
@@ -250,8 +290,6 @@
     own = gate_weight[0]
     own, _ = lax.optimization_barrier((own, out_rows))
     left, right = shift(own, 1), shift(own, REPS - 1)
-    top = shift(left[: UNITS // 2], 1)
-    bottom = shift(right[UNITS // 2 :], REPS - 1)
 
     tail, *picked = kernel_call(
         pick_grads,
@@ -264,41 +302,62 @@
     out_grads = kernel_call(
         fold_grads, sds((ROWS, STRIP), BF), [SM] + [VM] * 5, 1 << 29, 3 << 20
     )(pos, tail, *picked)
-    out_grads, left, right, top, bottom = lax.optimization_barrier(
-        (out_grads, left, right, top, bottom)
-    )
+    out_grads, left, right = lax.optimization_barrier((out_grads, left, right))
+    top = shift(left[: UNITS // 2], 1)
+    bottom = shift(right[UNITS // 2 :], REPS - 1)
+    weights = kernel_call(
+        stack_weights, sds((FFW + R, D), BF), [SM] + [VM] * 6, 1000, 14 << 20
+    )(pos, probes, own, right, top, bottom, left)
     got = to_owners(out_grads)
 
     kinds = [F32, BF, BF, BF]
-    gate, cut, *sums = kernel_call(
-        products,
-        [sds((FFW, SLOTS), F32), sds((SLOTS, SHARE), BF)]
-        + [sds((UNITS + R, SLOTS), kind) for kind in kinds]
-        + [sds((R, SHARE), kind) for kind in kinds],
-        [SM] + [VM] * 7,
-        6 << 30,
+    cut, *cut_sums = pl.pallas_call(
+        cut_products,
+        out_shape=[sds((SLOTS, SHARE), BF)] + [sds((UNITS + R, SLOTS), kind) for kind in kinds],
+        grid_spec=pltpu.PrefetchScalarGridSpec(
+            num_scalar_prefetch=1,
+            grid=(1,),
+            in_specs=[
+                pl.BlockSpec((ROWS, STRIP), lambda i, pos: (0, SHARE // STRIP)),
+                pl.BlockSpec((FFW + R, SHARE), lambda i, pos: (0, pos[0])),
+            ],
+            out_specs=[VM] * 5,
+        ),
+        compiler_params=pltpu.CompilerParams(vmem_limit_bytes=LIMIT),
+        cost_estimate=pl.CostEstimate(
+            flops=1 << 29, bytes_accessed=4 << 20, transcendentals=0
+        ),
+    )(pos, rows, weights)
+    cut_sums = shifted(cut_sums)
+    gate, partial, own_partial = kernel_call(
+        whole_products,
+        [sds((FFW, SLOTS), F32), sds((R, D), BF), sds((R, SHARE), F32)],
+        [SM, pl.BlockSpec((ROWS, SHARE), lambda i: (0, 0)), VM],
+        3 << 30,
         14 << 20,
         [pltpu.VMEM((SLOTS, D), BF), pltpu.VMEM((R, D), F32)],
-    )(pos, rows, probes, own, left, right, top, bottom)
-    cut_sums = shifted(sums[:REPS])
-    input_sums = shifted(sums[REPS:])
-
-    cut_grad, *sketches = kernel_call(
+        (1,),
+    )(pos, rows, weights)
+
+    mixed = UNITS + 2 * R
+    cut_grad, *sums = kernel_call(
         gate_part,
-        [sds((UNITS, SLOTS), BF)] + [sds((UNITS + 2 * R, 128), kind) for kind in kinds],
-        [SM] + [VM] * 8,
+        [sds((UNITS, SLOTS), BF), sds((mixed, 128), F32)]
+        + [sds((mixed + SHARE, 128), BF)] * (REPS - 1),
+        [SM] + [VM] * 9,
         2 << 30,
         4 << 20,
-        [pltpu.VMEM((FFW, SLOTS), F32), pltpu.VMEM((FFW, R), F32)],
-    )(pos, grad_probes, probe_share, gate, got, *cut_sums)
-    sketches = shifted(sketches)
-
-    input_sketch = kernel_call(
-        finish_input, sds((SHARE, R), F32), [SM] + [VM] * 9, 1 << 28, 4 << 20
-    )(inverse, cut, *cut_sums, *input_sums)
-    grad_sketch = kernel_call(
-        finish_grad, sds((UNITS, R), F32), [SM] + [VM] * 5, 1 << 24, 1 << 20
-    )(inverse, cut_grad, *sketches)
+        [pltpu.VMEM((ROWS, STRIP), BF), pltpu.VMEM((FFW, R), F32)],
+    )(pos, grad_probes, probe_share, gate, partial, got, *cut_sums)
+    sums = shifted(sums)
+
+    input_sketch, grad_sketch = kernel_call(
+        finish,
+        [sds((SHARE, R), F32), sds((UNITS, R), F32)],
+        [SM] + [VM] * 11,
+        1 << 28,
+        4 << 20,
+    )(inverse, cut, own_partial, *cut_sums, cut_grad, *sums)
     return input_sketch[None], grad_sketch[None]
 
 

time: 167 us -> 155 us (0.928)
  starting transfers between devices: 85.4 us -> 70.9 us
  local copies, waits for them, and re-layouts: 11.6 us -> 19.4 us
  Pallas kernels: 26 us -> 19.6 us
    ppermute x16 -> x13, starting transfers between devices: 54.3 us -> 44.9 us  [shift(): lax.ppermute(block, 'rep', [(i, (i + k) % REPS) for i in range(REPS)])]
    all_to_all x2, waiting for transfers between devices: 0.01 us -> 5.76 us  [to_owners(): lax.all_to_all(rows, 'ep', split_axis=0, concat_axis=0, tiled=True)]
    all_to_all x2, starting transfers between devices: 31.1 us -> 26 us  [to_owners(): lax.all_to_all(rows, 'ep', split_axis=0, concat_axis=0, tiled=True)]
    unnamed x24 -> x32, local copies, waits for them, and re-layouts: 8.46 us -> 13.1 us
    ppermute x16 -> x13, waiting for transfers between devices: 41.2 us -> 36.8 us  [shift(): lax.ppermute(block, 'rep', [(i, (i + k) % REPS) for i in range(REPS)])]
    pallas_call x4 -> x5, Pallas kernels: 17.1 us -> 13.1 us  [the longest x1 3.6 us: local(): kernel_call(whole_products, [sds((FFW, SLOTS), F32), sds((R, D), BF), sds...]
  transfers between devices with their start and end apart: 18 -> 15, of which waited for: 4 -> 7; matrix products, arithmetic and copies ran while one was open for 3% -> 5% of each run, Pallas kernels for 13% -> 8%
where the time goes in v3:
time: 155 us; the launch traced here: 154 us
  starting transfers between devices  70.9 us (46%)
  waiting for transfers between devices  42.5 us (27%)
  Pallas kernels  19.6 us (13%)
  local copies, waits for them, and re-layouts  19.4 us (13%)
  between operations  1.59 us (1%)
    ppermute x13, starting transfers between devices, shift(): lax.ppermute(block, 'rep', [(i, (i + k) % REPS) for i in range(REPS)])  44.9 us
    ppermute x13, waiting for transfers between devices, shift(): lax.ppermute(block, 'rep', [(i, (i + k) % REPS) for i in range(REPS)])  36.8 us
    all_to_all x2, starting transfers between devices, to_owners(): lax.all_to_all(rows, 'ep', split_axis=0, concat_axis=0, tiled=True)  26 us
    unnamed x32, local copies, waits for them, and re-layouts  13.1 us
    all_to_all x2, waiting for transfers between devices, to_owners(): lax.all_to_all(rows, 'ep', split_axis=0, concat_axis=0, tiled=True)  5.76 us
    pallas_call x1, Pallas kernels, local(): kernel_call(pick_grads, [sds((ROWS, STRIP), BF)] + [sds((SLOTS, STRIP), B...  3.91 us
    pallas_call x1, Pallas kernels, local(): kernel_call(whole_products, [sds((FFW, SLOTS), F32), sds((R, D), BF), sds...  3.6 us
  transfers between devices with their start and end apart: 15, of which 7 were waited for; matrix products, arithmetic and copies ran while one was open for 5% of the time, Pallas kernels for 8%

profile of v3, /device:TPU:8, one launch (start us, length us, event | category | flops | bytes accessed | tf_op | source)
XLA Modules:
  0.0 154.0 jit_solution(16360001085026869641)
XLA Ops:
  0.6 0.7 copy-done.7
  1.3 1.2 copy-done.9
  2.5 1.9 %shard_map.86 = bf16[1024,1280]{1,0:T(8,128)(2,1)S(1)} custom-call(s32[1]{0:T(128)} %bitcast.pos_ref, s32[8,128]{1,0:T(8,128)S(1)} %bitcast.18, bf16[128,4096]{1,0:T(8,128)(2,1)S(1)} %copy-done.9), custom_call_target="tpu_custom_call" | custom-call | flops 2147483648 | bytes 4194304 | tf_op jit(solution)/shard_map/pallas_call | solution.py:285
  4.5 1.5 copy-done
  6.0 17.5 %all-to-all-start = ((bf16[128,8,1280]{2,1,0:T(8,128)(2,1)}), bf16[128,8,1280]{2,1,0:T(8,128)(2,1)S(1)}, u32[]{:S(2)}, u32[]{:S(2)}) async-start(bf16[128,8,1280]{2,1,0:T(8,128)(2,1)} %bitcast.12), calls=%async_computation | async-start | bytes 5242880 | tf_op jit(solution)/shard_map/all_to_all | solution.py:273
  23.5 3.4 %collective-permute-start.3 = (bf16[192,4096]{1,0:T(8,128)(2,1)}, bf16[192,4096]{1,0:T(8,128)(2,1)}, u32[]{:S(2)}, u32[]{:S(2)}) collective-permute-start(bf16[192,4096]{1,0:T(8,128)(2,1)} %bitcast.13), channel_id=1, source_target_pairs={{0,1},{1,2},{2,3},{3,0},{4,5},{5,6},{6,7},{7,4},{8,9},{9,10},{10,1... | collective-permute-start | bytes 4718600 | tf_op jit(solution)/shard_map/ppermute | solution.py:263
  26.9 3.7 %collective-permute-start.4 = (bf16[192,4096]{1,0:T(8,128)(2,1)}, bf16[192,4096]{1,0:T(8,128)(2,1)}, u32[]{:S(2)}, u32[]{:S(2)}) collective-permute-start(bf16[192,4096]{1,0:T(8,128)(2,1)} %bitcast.14), channel_id=1, source_target_pairs={{0,3},{1,0},{2,1},{3,2},{4,7},{5,4},{6,5},{7,6},{8,11},{9,8},{10,9... | collective-permute-start | bytes 4718600 | tf_op jit(solution)/shard_map/ppermute | solution.py:263
  30.6 0.7 copy.11
  31.3 0.4 copy.12
  31.7 0.9 reshape.28.flat_ref
  32.6 3.9 %shard_map.87 = (bf16[1024,256]{1,0:T(8,128)(2,1)S(1)}, bf16[256,256]{1,0:T(8,128)(2,1)S(1)}, bf16[256,256]{1,0:T(8,128)(2,1)S(1)}, bf16[256,256]{1,0:T(8,128)(2,1)S(1)}, bf16[256,256]{1,0:T(8,128)(2,1)S(1)}) custom-call(s32[1]{0:T(128)} %bitcast.pos_ref, s32[8,128]{1,0:T(8,128)S(1)} %bitcast.19, s32[1,1024]{1,0:T(1,128)S(1)} %reshape.28.flat_ref, ...), custom_call_target="tpu_custom_call" | custom-call | flops 4294967296 | bytes 3145728 | tf_op jit(solution)/shard_map/pallas_call | solution.py:294
  36.6 2.2 %collective-permute-start = (bf16[256,256]{1,0:T(8,128)(2,1)S(1)}, bf16[256,256]{1,0:T(8,128)(2,1)S(1)}, u32[]{:S(2)}, u32[]{:S(2)}) collective-permute-start(bf16[256,256]{1,0:T(8,128)(2,1)S(1)} %get-tuple-element.29), channel_id=1, source_target_pairs={{0,1},{1,2},{2,3},{3,0},{4,5},{5,6},{6,7},{7,4},{8,9},{9,10},{10,1... | collective-permute-start | bytes 393224 | tf_op jit(solution)/shard_map/ppermute | solution.py:263
  38.8 4.6 %collective-permute-start.1 = (bf16[256,256]{1,0:T(8,128)(2,1)S(1)}, bf16[256,256]{1,0:T(8,128)(2,1)S(1)}, u32[]{:S(2)}, u32[]{:S(2)}) collective-permute-start(bf16[256,256]{1,0:T(8,128)(2,1)S(1)} %get-tuple-element.30), channel_id=1, source_target_pairs={{0,2},{1,3},{2,0},{3,1},{4,6},{5,7},{6,4},{7,5},{8,10},{9,11},{10,... | collective-permute-start | bytes 393224 | tf_op jit(solution)/shard_map/ppermute | solution.py:263
  43.4 3.3 %collective-permute-start.2 = (bf16[256,256]{1,0:T(8,128)(2,1)S(1)}, bf16[256,256]{1,0:T(8,128)(2,1)S(1)}, u32[]{:S(2)}, u32[]{:S(2)}) collective-permute-start(bf16[256,256]{1,0:T(8,128)(2,1)S(1)} %get-tuple-element.31), channel_id=1, source_target_pairs={{0,3},{1,0},{2,1},{3,2},{4,7},{5,4},{6,5},{7,6},{8,11},{9,8},{10,9... | collective-permute-start | bytes 393224 | tf_op jit(solution)/shard_map/ppermute | solution.py:263
  46.7 19.3 %collective-permute-done.g1 = bf16[256,256]{1,0:T(8,128)(2,1)S(1)} collective-permute-done((bf16[256,256]{1,0:T(8,128)(2,1)S(1)}, bf16[256,256]{1,0:T(8,128)(2,1)S(1)}, u32[]{:S(2)}, u32[]{:S(2)}) %collective-permute-start) | collective-permute-done | bytes 131104 | tf_op jit(solution)/shard_map/ppermute | solution.py:263
  66.0 3.8 %collective-permute-done.1.g2 = bf16[256,256]{1,0:T(8,128)(2,1)S(1)} collective-permute-done((bf16[256,256]{1,0:T(8,128)(2,1)S(1)}, bf16[256,256]{1,0:T(8,128)(2,1)S(1)}, u32[]{:S(2)}, u32[]{:S(2)}) %collective-permute-start.1) | collective-permute-done | bytes 131104 | tf_op jit(solution)/shard_map/ppermute | solution.py:263
  69.8 0.9 collective-permute-done.2.g3
  70.8 0.7 shard_map.88
  71.5 2.2 %slice.6 = bf16[96,4096]{1,0:T(8,128)(2,1)} slice(bf16[192,4096]{1,0:T(8,128)(2,1)} %collective-permute-done.3.left_ref), slice={[0:96], [0:4096]} | slice | bytes 1572864 | tf_op jit(solution)/shard_map/slice | solution.py:306
  73.8 3.4 %collective-permute-start.5 = (bf16[96,4096]{1,0:T(8,128)(2,1)}, bf16[96,4096]{1,0:T(8,128)(2,1)S(1)}, u32[]{:S(2)}, u32[]{:S(2)}) collective-permute-start(bf16[96,4096]{1,0:T(8,128)(2,1)} %slice.6), channel_id=1, source_target_pairs={{0,1},{1,2},{2,3},{3,0},{4,5},{5,6},{6,7},{7,4},{8,9},{9,10},{10,1... | collective-permute-start | bytes 2359304 | tf_op jit(solution)/shard_map/ppermute | solution.py:263
  77.2 2.1 %slice.7 = bf16[96,4096]{1,0:T(8,128)(2,1)} slice(bf16[192,4096]{1,0:T(8,128)(2,1)} %collective-permute-done.4.right_ref), slice={[96:192], [0:4096]} | slice | bytes 1572864 | tf_op jit(solution)/shard_map/slice | solution.py:307
  79.3 3.6 %collective-permute-start.6 = (bf16[96,4096]{1,0:T(8,128)(2,1)}, bf16[96,4096]{1,0:T(8,128)(2,1)}, u32[]{:S(2)}, u32[]{:S(2)}) collective-permute-start(bf16[96,4096]{1,0:T(8,128)(2,1)} %slice.7), channel_id=1, source_target_pairs={{0,3},{1,0},{2,1},{3,2},{4,7},{5,4},{6,5},{7,6},{8,11},{9,8},{10,9... | collective-permute-start | bytes 2359304 | tf_op jit(solution)/shard_map/ppermute | solution.py:263
  83.0 5.8 %all-to-all-done = bf16[128,8,1280]{2,1,0:T(8,128)(2,1)S(1)} async-done(((bf16[128,8,1280]{2,1,0:T(8,128)(2,1)}), bf16[128,8,1280]{2,1,0:T(8,128)(2,1)S(1)}, u32[]{:S(2)}, u32[]{:S(2)}) %all-to-all-start) | async-done | bytes 2621472 | tf_op jit(solution)/shard_map/all_to_all | solution.py:273
  88.7 8.5 %all-to-all-start.1 = ((bf16[128,8,256]{2,1,0:T(8,128)(2,1)}), bf16[128,8,256]{2,1,0:T(8,128)(2,1)}, u32[]{:S(2)}, u32[]{:S(2)}) async-start(bf16[128,8,256]{2,1,0:T(8,128)(2,1)} %bitcast.17), calls=%async_computation.1 | async-start | bytes 1048576 | tf_op jit(solution)/shard_map/all_to_all | solution.py:273
  97.2 1.0 constant_dynamic-slice_fusion.probe_share_ref
  98.2 1.4 collective-permute-done.6.bottom_ref
  99.6 1.4 copy-done.1
  101.0 1.2 copy-done.2
  102.3 2.6 %shard_map.89.weights_ref = bf16[896,4096]{1,0:T(8,128)(2,1)S(1)} custom-call(s32[1]{0:T(128)} %bitcast.pos_ref, bf16[128,4096]{1,0:T(8,128)(2,1)S(1)} %copy-done.2, bf16[192,4096]{1,0:T(8,128)(2,1)S(1)} %bitcast.15, bf16[192,4096]{1,0:T(8,128)(2,1)} %collective-permute-done.4.right_ref, bf16[96,4096]{1,0:T(8,128)(2,1)S(1)} %collective-permute-done.5.top_ref, ...), custom_call_target="tpu_custom_call" | custom-call | flops 1000 | bytes 14680064 | tf_op jit(solution)/shard_map/pallas_call | solution.py:308
  104.9 2.0 %shard_map.90 = (bf16[256,1024]{1,0:T(8,128)(2,1)S(1)}, f32[320,256]{1,0:T(8,128)S(1)}, bf16[320,256]{1,0:T(8,128)(2,1)}, bf16[320,256]{1,0:T(8,128)(2,1)}, bf16[320,256]{1,0:T(8,128)(2,1)}) custom-call(s32[1]{0:T(128)} %bitcast.pos_ref, bf16[1024,1280]{1,0:T(8,128)(2,1)S(1)} %bitcast.10, bf16[896,4096]{1,0:T(8,128)(2,1)S(1)} %shard_map.89.weights_ref), custom_call_target="tpu_custom_call" | custom-call | flops 536870912 | bytes 4194304 | tf_op jit(solution)/shard_map/pallas_call | solution.py:314
  106.9 3.1 %collective-permute-start.7 = (bf16[320,256]{1,0:T(8,128)(2,1)}, bf16[320,256]{1,0:T(8,128)(2,1)}, u32[]{:S(2)}, u32[]{:S(2)}) collective-permute-start(bf16[320,256]{1,0:T(8,128)(2,1)} %get-tuple-element.37), channel_id=1, source_target_pairs={{0,1},{1,2},{2,3},{3,0},{4,5},{5,6},{6,7},{7,4},{8,9},{9,10},{10,1... | collective-permute-start | bytes 491528 | tf_op jit(solution)/shard_map/ppermute | solution.py:263
  110.0 5.1 %collective-permute-start.8 = (bf16[320,256]{1,0:T(8,128)(2,1)}, bf16[320,256]{1,0:T(8,128)(2,1)}, u32[]{:S(2)}, u32[]{:S(2)}) collective-permute-start(bf16[320,256]{1,0:T(8,128)(2,1)} %get-tuple-element.38), channel_id=1, source_target_pairs={{0,2},{1,3},{2,0},{3,1},{4,6},{5,7},{6,4},{7,5},{8,10},{9,11},{10,... | collective-permute-start | bytes 491528 | tf_op jit(solution)/shard_map/ppermute | solution.py:263
  115.2 3.0 %collective-permute-start.9 = (bf16[320,256]{1,0:T(8,128)(2,1)}, bf16[320,256]{1,0:T(8,128)(2,1)}, u32[]{:S(2)}, u32[]{:S(2)}) collective-permute-start(bf16[320,256]{1,0:T(8,128)(2,1)} %get-tuple-element.39), channel_id=1, source_target_pairs={{0,3},{1,0},{2,1},{3,2},{4,7},{5,4},{6,5},{7,6},{8,11},{9,8},{10,9... | collective-permute-start | bytes 491528 | tf_op jit(solution)/shard_map/ppermute | solution.py:263
  118.2 3.6 %shard_map.91 = (f32[768,256]{1,0:T(8,128)S(1)}, bf16[128,4096]{1,0:T(8,128)(2,1)S(1)}, f32[128,1024]{1,0:T(8,128)S(1)}) custom-call(s32[1]{0:T(128)} %bitcast.pos_ref, bf16[1024,1280]{1,0:T(8,128)(2,1)S(1)} %bitcast.11, bf16[896,4096]{1,0:T(8,128)(2,1)S(1)} %shard_map.89.weights_ref), custom_call_target="tpu_custom_call" | custom-call | flops 3221225472 | bytes 14680064 | tf_op jit(solution)/shard_map/pallas_call | solution.py:332
  121.8 0.0 copy-start.4
  121.8 0.8 copy-done.4
  122.6 1.0 copy-done.10
  123.6 0.9 copy-done.12
  124.5 0.9 copy-done.6
  125.4 1.2 copy-done.11
  126.7 1.1 copy-done.13
  127.8 2.6 %shard_map.92 = (bf16[192,256]{1,0:T(8,128)(2,1)S(1)}, f32[448,128]{1,0:T(8,128)S(1)}, bf16[1472,128]{1,0:T(8,128)(2,1)S(1)}, bf16[1472,128]{1,0:T(8,128)(2,1)S(1)}, bf16[1472,128]{1,0:T(8,128)(2,1)S(1)}) custom-call(s32[1]{0:T(128)} %bitcast.pos_ref, bf16[128,768]{1,0:T(8,128)(2,1)S(1)} %copy-done.6, ...), custom_call_target="tpu_custom_call" | custom-call | flops 2147483648 | bytes 4194304 | tf_op jit(solution)/shard_map/pallas_call | solution.py:343
  130.4 2.8 %collective-permute-start.10 = (bf16[1472,128]{1,0:T(8,128)(2,1)S(1)}, bf16[1472,128]{1,0:T(8,128)(2,1)S(1)}, u32[]{:S(2)}, u32[]{:S(2)}) collective-permute-start(bf16[1472,128]{1,0:T(8,128)(2,1)S(1)} %get-tuple-element.45), channel_id=1, source_target_pairs={{0,1},{1,2},{2,3},{3,0},{4,5},{5,6},{6,7},{7,4},{8,9},{9,10},{10,1... | collective-permute-start | bytes 1130504 | tf_op jit(solution)/shard_map/ppermute | solution.py:263
  133.2 3.0 %collective-permute-start.11 = (bf16[1472,128]{1,0:T(8,128)(2,1)S(1)}, bf16[1472,128]{1,0:T(8,128)(2,1)S(1)}, u32[]{:S(2)}, u32[]{:S(2)}) collective-permute-start(bf16[1472,128]{1,0:T(8,128)(2,1)S(1)} %get-tuple-element.46), channel_id=1, source_target_pairs={{0,2},{1,3},{2,0},{3,1},{4,6},{5,7},{6,4},{7,5},{8,10},{9,11},{10,... | collective-permute-start | bytes 1130504 | tf_op jit(solution)/shard_map/ppermute | solution.py:263
  136.2 3.5 %collective-permute-start.12 = (bf16[1472,128]{1,0:T(8,128)(2,1)S(1)}, bf16[1472,128]{1,0:T(8,128)(2,1)S(1)}, u32[]{:S(2)}, u32[]{:S(2)}) collective-permute-start(bf16[1472,128]{1,0:T(8,128)(2,1)S(1)} %get-tuple-element.47), channel_id=1, source_target_pairs={{0,3},{1,0},{2,1},{3,2},{4,7},{5,4},{6,5},{7,6},{8,11},{9,8},{10,9... | collective-permute-start | bytes 1130504 | tf_op jit(solution)/shard_map/ppermute | solution.py:263
  140.4 8.8 %collective-permute-done.10.t1 = bf16[1472,128]{1,0:T(8,128)(2,1)S(1)} collective-permute-done((bf16[1472,128]{1,0:T(8,128)(2,1)S(1)}, bf16[1472,128]{1,0:T(8,128)(2,1)S(1)}, u32[]{:S(2)}, u32[]{:S(2)}) %collective-permute-start.10) | collective-permute-done | bytes 376864 | tf_op jit(solution)/shard_map/ppermute | solution.py:263
  149.2 2.5 %collective-permute-done.12.t3 = bf16[1472,128]{1,0:T(8,128)(2,1)S(1)} collective-permute-done((bf16[1472,128]{1,0:T(8,128)(2,1)S(1)}, bf16[1472,128]{1,0:T(8,128)(2,1)S(1)}, u32[]{:S(2)}, u32[]{:S(2)}) %collective-permute-start.12) | collective-permute-done | bytes 376864 | tf_op jit(solution)/shard_map/ppermute | solution.py:263
  151.7 2.3 %shard_map.93 = (f32[1024,128]{1,0:T(8,128)}, f32[192,128]{1,0:T(8,128)}) custom-call(f32[1]{0:T(128)S(6)} %div.3.inverse_ref, bf16[256,1024]{1,0:T(8,128)(2,1)S(1)} %get-tuple-element.34.cut_ref, f32[128,1024]{1,0:T(8,128)S(1)} %copy-done.5, f32[320,256]{1,0:T(8,128)S(1)} %get-tuple-element.36.s0, bf16[320,256]{1,0:T(8,128)(2,1)} %collective-permute-done.7.s1, ...), custom_call_target="tpu_custom_call" | custom-call | flops 268435456 | bytes 4194304 | tf_op jit(solution)/shard_map/pallas_call | solution.py:354
  (26 shorter events, 0.1 us)
Async XLA Ops:
  0.6 0.7 copy-start.7
  1.3 1.2 copy-start.9
  4.5 1.5 copy-start
  6.0 24.6 %copy-start.8 = (s32[128,8]{0,1:T(8,128)S(1)}, s32[128,8]{0,1:T(8,128)}, u32[]{:S(2)}) copy-start(s32[128,8]{0,1:T(8,128)} %param.8) | copy-start | bytes 12292
  6.0 25.3 %copy-start.14 = (bf16[128,8,192]{0,2,1:T(8,128)(2,1)S(1)}, bf16[128,8,192]{0,2,1:T(8,128)(2,1)}, u32[]{:S(2)}) copy-start(bf16[128,8,192]{0,2,1:T(8,128)(2,1)} %param.9) | copy-start | bytes 1179652
  6.0 82.8 %all-to-all-start = ((bf16[128,8,1280]{2,1,0:T(8,128)(2,1)}), bf16[128,8,1280]{2,1,0:T(8,128)(2,1)S(1)}, u32[]{:S(2)}, u32[]{:S(2)}) async-start(bf16[128,8,1280]{2,1,0:T(8,128)(2,1)} %bitcast.12), calls=%async_computation | async-start | bytes 5242880 | tf_op jit(solution)/shard_map/all_to_all | solution.py:273
  23.5 48.0 %collective-permute-start.3 = (bf16[192,4096]{1,0:T(8,128)(2,1)}, bf16[192,4096]{1,0:T(8,128)(2,1)}, u32[]{:S(2)}, u32[]{:S(2)}) collective-permute-start(bf16[192,4096]{1,0:T(8,128)(2,1)} %bitcast.13), channel_id=1, source_target_pairs={{0,1},{1,2},{2,3},{3,0},{4,5},{5,6},{6,7},{7,4},{8,9},{9,10},{10,1... | collective-permute-start | bytes 4718600 | tf_op jit(solution)/shard_map/ppermute | solution.py:263
  26.9 44.6 %collective-permute-start.4 = (bf16[192,4096]{1,0:T(8,128)(2,1)}, bf16[192,4096]{1,0:T(8,128)(2,1)}, u32[]{:S(2)}, u32[]{:S(2)}) collective-permute-start(bf16[192,4096]{1,0:T(8,128)(2,1)} %bitcast.14), channel_id=1, source_target_pairs={{0,3},{1,0},{2,1},{3,2},{4,7},{5,4},{6,5},{7,6},{8,11},{9,8},{10,9... | collective-permute-start | bytes 4718600 | tf_op jit(solution)/shard_map/ppermute | solution.py:263
  36.6 29.5 %collective-permute-start = (bf16[256,256]{1,0:T(8,128)(2,1)S(1)}, bf16[256,256]{1,0:T(8,128)(2,1)S(1)}, u32[]{:S(2)}, u32[]{:S(2)}) collective-permute-start(bf16[256,256]{1,0:T(8,128)(2,1)S(1)} %get-tuple-element.29), channel_id=1, source_target_pairs={{0,1},{1,2},{2,3},{3,0},{4,5},{5,6},{6,7},{7,4},{8,9},{9,10},{10,1... | collective-permute-start | bytes 393224 | tf_op jit(solution)/shard_map/ppermute | solution.py:263
  38.8 31.1 %collective-permute-start.1 = (bf16[256,256]{1,0:T(8,128)(2,1)S(1)}, bf16[256,256]{1,0:T(8,128)(2,1)S(1)}, u32[]{:S(2)}, u32[]{:S(2)}) collective-permute-start(bf16[256,256]{1,0:T(8,128)(2,1)S(1)} %get-tuple-element.30), channel_id=1, source_target_pairs={{0,2},{1,3},{2,0},{3,1},{4,6},{5,7},{6,4},{7,5},{8,10},{9,11},{10,... | collective-permute-start | bytes 393224 | tf_op jit(solution)/shard_map/ppermute | solution.py:263
  43.4 27.4 %collective-permute-start.2 = (bf16[256,256]{1,0:T(8,128)(2,1)S(1)}, bf16[256,256]{1,0:T(8,128)(2,1)S(1)}, u32[]{:S(2)}, u32[]{:S(2)}) collective-permute-start(bf16[256,256]{1,0:T(8,128)(2,1)S(1)} %get-tuple-element.31), channel_id=1, source_target_pairs={{0,3},{1,0},{2,1},{3,2},{4,7},{5,4},{6,5},{7,6},{8,11},{9,8},{10,9... | collective-permute-start | bytes 393224 | tf_op jit(solution)/shard_map/ppermute | solution.py:263
  71.5 7.8 %copy-start.3 = (bf16[1024,256]{1,0:T(8,128)(2,1)}, bf16[1024,256]{1,0:T(8,128)(2,1)S(1)}, u32[]{:S(2)}) copy-start(bf16[1024,256]{1,0:T(8,128)(2,1)S(1)} %shard_map.88) | copy-start | bytes 1572868
  73.8 24.4 %collective-permute-start.5 = (bf16[96,4096]{1,0:T(8,128)(2,1)}, bf16[96,4096]{1,0:T(8,128)(2,1)S(1)}, u32[]{:S(2)}, u32[]{:S(2)}) collective-permute-start(bf16[96,4096]{1,0:T(8,128)(2,1)} %slice.6), channel_id=1, source_target_pairs={{0,1},{1,2},{2,3},{3,0},{4,5},{5,6},{6,7},{7,4},{8,9},{9,10},{10,1... | collective-permute-start | bytes 2359304 | tf_op jit(solution)/shard_map/ppermute | solution.py:263
  79.3 20.3 %collective-permute-start.6 = (bf16[96,4096]{1,0:T(8,128)(2,1)}, bf16[96,4096]{1,0:T(8,128)(2,1)}, u32[]{:S(2)}, u32[]{:S(2)}) collective-permute-start(bf16[96,4096]{1,0:T(8,128)(2,1)} %slice.7), channel_id=1, source_target_pairs={{0,3},{1,0},{2,1},{3,2},{4,7},{5,4},{6,5},{7,6},{8,11},{9,8},{10,9... | collective-permute-start | bytes 2359304 | tf_op jit(solution)/shard_map/ppermute | solution.py:263
  88.7 35.8 %all-to-all-start.1 = ((bf16[128,8,256]{2,1,0:T(8,128)(2,1)}), bf16[128,8,256]{2,1,0:T(8,128)(2,1)}, u32[]{:S(2)}, u32[]{:S(2)}) async-start(bf16[128,8,256]{2,1,0:T(8,128)(2,1)} %bitcast.17), calls=%async_computation.1 | async-start | bytes 1048576 | tf_op jit(solution)/shard_map/all_to_all | solution.py:273
  99.6 1.4 copy-start.1
  101.0 1.2 copy-start.2
  106.9 17.6 %collective-permute-start.7 = (bf16[320,256]{1,0:T(8,128)(2,1)}, bf16[320,256]{1,0:T(8,128)(2,1)}, u32[]{:S(2)}, u32[]{:S(2)}) collective-permute-start(bf16[320,256]{1,0:T(8,128)(2,1)} %get-tuple-element.37), channel_id=1, source_target_pairs={{0,1},{1,2},{2,3},{3,0},{4,5},{5,6},{6,7},{7,4},{8,9},{9,10},{10,1... | collective-permute-start | bytes 491528 | tf_op jit(solution)/shard_map/ppermute | solution.py:263
  110.0 14.5 %collective-permute-start.8 = (bf16[320,256]{1,0:T(8,128)(2,1)}, bf16[320,256]{1,0:T(8,128)(2,1)}, u32[]{:S(2)}, u32[]{:S(2)}) collective-permute-start(bf16[320,256]{1,0:T(8,128)(2,1)} %get-tuple-element.38), channel_id=1, source_target_pairs={{0,2},{1,3},{2,0},{3,1},{4,6},{5,7},{6,4},{7,5},{8,10},{9,11},{10,... | collective-permute-start | bytes 491528 | tf_op jit(solution)/shard_map/ppermute | solution.py:263
  115.2 9.3 %collective-permute-start.9 = (bf16[320,256]{1,0:T(8,128)(2,1)}, bf16[320,256]{1,0:T(8,128)(2,1)}, u32[]{:S(2)}, u32[]{:S(2)}) collective-permute-start(bf16[320,256]{1,0:T(8,128)(2,1)} %get-tuple-element.39), channel_id=1, source_target_pairs={{0,3},{1,0},{2,1},{3,2},{4,7},{5,4},{6,5},{7,6},{8,11},{9,8},{10,9... | collective-permute-start | bytes 491528 | tf_op jit(solution)/shard_map/ppermute | solution.py:263
  121.8 0.8 copy-start.4
  122.6 1.0 copy-start.10
  123.6 0.9 copy-start.12
  124.5 0.9 copy-start.6
  125.4 1.2 copy-start.11
  126.7 1.1 copy-start.13
  127.8 23.9 %copy-start.5 = (f32[128,1024]{1,0:T(8,128)S(1)}, f32[128,1024]{1,0:T(8,128)}, u32[]{:S(2)}) copy-start(f32[128,1024]{1,0:T(8,128)} %copy-done.4) | copy-start | bytes 1572868
  130.4 18.8 %collective-permute-start.10 = (bf16[1472,128]{1,0:T(8,128)(2,1)S(1)}, bf16[1472,128]{1,0:T(8,128)(2,1)S(1)}, u32[]{:S(2)}, u32[]{:S(2)}) collective-permute-start(bf16[1472,128]{1,0:T(8,128)(2,1)S(1)} %get-tuple-element.45), channel_id=1, source_target_pairs={{0,1},{1,2},{2,3},{3,0},{4,5},{5,6},{6,7},{7,4},{8,9},{9,10},{10,1... | collective-permute-start | bytes 1130504 | tf_op jit(solution)/shard_map/ppermute | solution.py:263
  133.2 16.0 %collective-permute-start.11 = (bf16[1472,128]{1,0:T(8,128)(2,1)S(1)}, bf16[1472,128]{1,0:T(8,128)(2,1)S(1)}, u32[]{:S(2)}, u32[]{:S(2)}) collective-permute-start(bf16[1472,128]{1,0:T(8,128)(2,1)S(1)} %get-tuple-element.46), channel_id=1, source_target_pairs={{0,2},{1,3},{2,0},{3,1},{4,6},{5,7},{6,4},{7,5},{8,10},{9,11},{10,... | collective-permute-start | bytes 1130504 | tf_op jit(solution)/shard_map/ppermute | solution.py:263
  136.2 15.5 %collective-permute-start.12 = (bf16[1472,128]{1,0:T(8,128)(2,1)S(1)}, bf16[1472,128]{1,0:T(8,128)(2,1)S(1)}, u32[]{:S(2)}, u32[]{:S(2)}) collective-permute-start(bf16[1472,128]{1,0:T(8,128)(2,1)S(1)} %get-tuple-element.47), channel_id=1, source_target_pairs={{0,3},{1,0},{2,1},{3,2},{4,7},{5,4},{6,5},{7,6},{8,11},{9,8},{10,9... | collective-permute-start | bytes 1130504 | tf_op jit(solution)/shard_map/ppermute | solution.py:263

commit v4 on v2

v4 whole, which is shorter than its diff:
```python
import jax
import jax.numpy as jnp
from jax import lax
from jax.experimental import pallas as pl
from jax.experimental.pallas import tpu as pltpu
from jax.sharding import PartitionSpec as P

OWNERS = 128
PAIRS = OWNERS // 2
REPS = 4
TOK = 128
TOP = 8
D = 4096
HALF = D // 2
SHARE = D // REPS
FFW = 768
UNITS = FFW // REPS
R = 128
FIRST = 8
FOLD = 8
ROWS = OWNERS * FOLD
SLOTS = OWNERS * 2
ALL = SLOTS + 128
STRIP = HALF // FOLD
MIB = 1 << 20

BF = jnp.bfloat16
F32 = jnp.float32
NT = (((1,), (1,)), ((), ()))
NN = (((1,), (0,)), ((), ()))

VM = pl.BlockSpec(memory_space=pltpu.VMEM)
SM = pl.BlockSpec(memory_space=pltpu.SMEM)


def dot(a, b, dims=NN):
    return lax.dot_general(a, b, dims, preferred_element_type=F32)


def iota(shape, axis):
    return lax.broadcasted_iota(jnp.int32, shape, axis)


def ones_where(mask):
    return jnp.where(mask, 1.0, 0.0).astype(BF)


def kernel_call(body, out_shape, in_specs, flops, bytes_accessed, limit, scratch=()):
    return pl.pallas_call(
        body,
        out_shape=out_shape,
        in_specs=in_specs,
        out_specs=jax.tree.map(lambda _: VM, out_shape),
        scratch_shapes=list(scratch),
        compiler_params=pltpu.CompilerParams(vmem_limit_bytes=limit * MIB),
        cost_estimate=pl.CostEstimate(
            flops=flops, bytes_accessed=bytes_accessed, transcendentals=0
        ),
    )


def places(ids_t):
    experts = iota((OWNERS, TOK), 0)
    named = jnp.zeros((OWNERS, TOK), F32)
    for k in range(TOP):
        named += jnp.where(ids_t[k : k + 1, :] == experts, 1.0, 0.0)
    before = ones_where(iota((TOK, TOK), 0) < iota((TOK, TOK), 1))
    rank = dot(named.astype(BF), before)
    return jnp.where(named > 0.0, rank, -1.0)


def pair_places(ids_t):
    pairs = TOK * TOP
    widen = ones_where(iota((TOK, pairs), 1) // TOP == iota((TOK, pairs), 0))
    ranks = dot(places(ids_t).astype(BF), widen)
    ids = dot(ids_t.astype(F32).astype(BF), widen)
    mine = iota((TOP, pairs), 1) % TOP == iota((TOP, pairs), 0)
    flat = jnp.sum(jnp.where(mine, ids, 0.0), axis=0, keepdims=True)
    return jnp.where(flat == iota((OWNERS, pairs), 0).astype(F32), ranks, -1.0)


def spread(table, times):
    shape = (OWNERS * times, OWNERS)
    return dot(ones_where(iota(shape, 0) // times == iota(shape, 1)), table.astype(BF))


def pack_half(pos_ref, ids_ref, tokens_ref, out_ref):
    out_ref[:TOK, :] = tokens_ref[...]
    out_ref[TOK:, :] = jnp.zeros((16, HALF), BF)
    ids = jnp.concatenate([ids_ref[...].astype(F32), jnp.zeros((8, TOK), F32)], 0)
    out_ref[TOK:, :TOK] = ids.astype(BF)


def other_ids(other_ref):
    return other_ref[TOK:, :TOK].astype(F32)[:TOP].astype(jnp.int32)


def send_rows(pos_ref, ids_ref, tokens_ref, other_ref, out_ref, half_ref, half_ids_ref):
    x, c = pos_ref[0], pos_ref[1]
    mine = x // 2 == c
    table = spread(places(ids_ref[...]), FOLD)
    row = iota((ROWS, TOK), 0)
    whole = table == (2 * x + row % 8 // 4).astype(F32)
    picks = jnp.concatenate([ones_where(whole & (row % 4 == b)) for b in range(4)], 1)
    parts = jnp.concatenate([tokens_ref[:, b * SHARE : (b + 1) * SHARE] for b in range(4)], 0)
    out_ref[:, :SHARE] = dot(picks, parts).astype(BF)

    @pl.when(mine)
    def _():
        half_ref[...] = tokens_ref[:, pl.ds(pl.multiple_of(c * HALF, HALF), HALF)]
        half_ids_ref[...] = ids_ref[...]

    @pl.when(jnp.logical_not(mine))
    def _():
        half_ref[...] = other_ref[:TOK, :]
        half_ids_ref[...] = other_ids(other_ref)

    table = spread(places(half_ids_ref[...]), FOLD)
    shared = table == (FIRST + x % 2).astype(F32)
    picks = jnp.concatenate([ones_where(shared & (row % 8 == b)) for b in range(8)], 1)
    parts = jnp.concatenate([half_ref[:, b * STRIP : (b + 1) * STRIP] for b in range(8)], 0)
    out_ref[:, SHARE:] = dot(picks, parts).astype(BF)


def pick_grads(pos_ref, ids_ref, other_ref, grads_ref, other_grads_ref, *outs):
    x, c = pos_ref[0], pos_ref[1]
    pairs = TOK * TOP
    table, other_table = pair_places(ids_ref[...]), pair_places(other_ids(other_ref))
    embed = ones_where(iota((UNITS, 256), 0) == iota((UNITS, 256), 1))
    grads = dot(grads_ref[...], embed).astype(BF)
    other_grads = dot(other_grads_ref[...], embed).astype(BF)
    twice = spread(table, 2)
    second = iota((SLOTS, pairs), 0) % 2
    for k, out in enumerate(outs):
        to = lax.rem(x + k, REPS)
        out[:SLOTS, :] = dot(ones_where(twice == (2 * to + second).astype(F32)), grads).astype(BF)
        shared = FIRST + to % 2
        place = jnp.where(to // 2 == c, shared, -2).astype(F32)
        other_place = jnp.where(to // 2 == c, -2, shared).astype(F32)
        out[SLOTS:, :] = (
            dot(ones_where(table == place), grads)
            + dot(ones_where(other_table == other_place), other_grads)
        ).astype(BF)


def fold_grads(pos_ref, g0, g1, g2, g3, out_ref):
    x, c = pos_ref[0], pos_ref[1]
    row, column = iota((ROWS, SLOTS), 0), iota((ROWS, SLOTS), 1)
    total = jnp.zeros((ROWS, 256), F32)
    for k, got in enumerate((g0, g1, g2, g3)):
        unit = lax.rem(x - k + REPS, REPS)
        total += dot(ones_where((row // 4 == column) & (row % 4 == unit)), got[:SLOTS, :])
        for u in range(3):
            at = jnp.where(unit // 2 == c, unit % 2 * 3 + u, -1)
            source, lane = iota((256, 256), 0), iota((256, 256), 1)
            move = ones_where((source // 64 == u) & (lane == UNITS + source % 64))
            moved = dot(got[SLOTS:, :], move).astype(BF)
            row5, column5 = iota((ROWS, OWNERS), 0), iota((ROWS, OWNERS), 1)
            total += dot(ones_where((row5 // 8 == column5) & (row5 % 8 == at)), moved)
    out_ref[...] = total.astype(BF)


def regroup(source, many, put):
    size = 256 // many
    shape = (256, 256)
    to = iota(shape, 0)
    order = ones_where(iota(shape, 1) == many * (to % size) + to // size)
    for g in range(ROWS // 256):
        got = dot(order, source(slice(g * 256, (g + 1) * 256))).astype(BF)
        for p in range(many):
            put(p, slice(g * size, (g + 1) * size), got[p * size : (p + 1) * size])


def products(
    pos_ref, rows_ref, probes_ref, own_ref, right_ref, top_ref, bottom_ref, left_ref,
    gate_ref, i0, i1, i2, i3, rows_all_ref, sum_ref,
):
    x = pos_ref[0]

    def put_whole(p, at, got):
        rows_all_ref[at, p * SHARE : (p + 1) * SHARE] = got

    def put_shared(p, at, got):
        rows_all_ref[SLOTS + at.start : SLOTS + at.stop, p * STRIP : (p + 1) * STRIP] = got

    regroup(lambda at: rows_ref[at, :SHARE], 4, put_whole)
    regroup(lambda at: rows_ref[at, SHARE:], 16, put_shared)
    rows_all_ref[SLOTS + PAIRS :, :] = jnp.zeros((ALL - SLOTS - PAIRS, D), BF)
    rows = rows_all_ref[...]
    projected = dot(probes_ref[...], rows, NT).astype(BF)
    sum_ref[...] = dot(projected, rows)
    for k, out in enumerate((i0, i1, i2, i3)):
        base = lax.rem(x + k, REPS) * SHARE
        out[...] = sum_ref[:, pl.ds(pl.multiple_of(base, SHARE), SHARE)].astype(out.dtype)
    half = UNITS // 2
    for w, k, start, size in (
        (own_ref, 0, 0, UNITS),
        (right_ref, 1, 0, UNITS),
        (top_ref, 2, 0, half),
        (bottom_ref, 2, half, half),
        (left_ref, 3, 0, UNITS),
    ):
        base = lax.rem(x + k, REPS) * UNITS + start
        gate_ref[pl.ds(pl.multiple_of(base, half), size), :] = dot(w[...], rows, NT)


def gate_part(
    pos_ref, grad_probes_ref, gate_ref, got_ref, t0, t1, t2, t3,
    whole_ref, shared_ref, sketch_ref,
):
    x = pos_ref[0]

    def put_whole(p, at, got):
        whole_ref[p * SLOTS + at.start : p * SLOTS + at.stop, :] = got

    def put_shared(p, at, got):
        shared_ref[p * PAIRS + at.start : p * PAIRS + at.stop, :] = got

    regroup(lambda at: got_ref[at, :], 4, put_whole)
    regroup(lambda at: got_ref[at, :], 16, put_shared)
    same = ones_where(iota((UNITS, 256), 0) == iota((UNITS, 256), 1))
    whole = dot(same, whole_ref[...], NT)
    last = ones_where(iota((64, 256), 0) + UNITS == iota((64, 256), 1))
    shared = dot(last, shared_ref[...], NT)
    turned = pltpu.roll(shared, ROWS - PAIRS, 1)
    parts = []
    for p in (0, 1, 2, 3, 4, 5, 8, 9, 10, 11, 12, 13):
        at = p // 2 * 128
        parts.append((turned if p % 2 else shared)[:, at : at + 128])
    late = jnp.concatenate(parts, 0)
    late = jnp.where(iota((FFW, 128), 1) < PAIRS, late, 0.0)
    early = jnp.concatenate([whole[:, b * SLOTS : (b + 1) * SLOTS] for b in range(4)], 0)
    grads = jnp.concatenate([early, late], 1)
    gate = gate_ref[...]
    s = 1.0 / (1.0 + jnp.exp(-gate))
    gate_grad = (grads * (s * (1.0 + gate * (1.0 - s)))).astype(BF)
    projected = dot(grad_probes_ref[...], gate_grad).astype(BF)
    sketch_ref[...] = dot(gate_grad, projected, NT)
    for k, out in enumerate((t0, t1, t2, t3)):
        base = lax.rem(x + k, REPS) * UNITS
        out[...] = sketch_ref[pl.ds(pl.multiple_of(base, UNITS), UNITS), :].astype(out.dtype)


def finish_input(inverse_ref, i0, i1, i2, i3, out_ref):
    total = i0[...] + (i1[...].astype(F32) + i2[...].astype(F32) + i3[...].astype(F32))
    out_ref[...] = (total * inverse_ref[0]).T


def finish_grad(inverse_ref, t0, t1, t2, t3, out_ref):
    total = t0[...] + (t1[...].astype(F32) + t2[...].astype(F32) + t3[...].astype(F32))
    out_ref[...] = total * inverse_ref[0]


def shift(block, k):
    return lax.ppermute(block, "rep", [(i, (i + k) % REPS) for i in range(REPS)])


def shifted(blocks):
    return [blocks[0]] + [shift(blocks[k], k) for k in range(1, REPS)]


def swap(block):
    return lax.ppermute(block, "ep", [(i, i ^ 1) for i in range(OWNERS)])


def to_owners(rows):
    width = rows.shape[1]
    rows = rows.reshape(OWNERS, FOLD, width)
    return lax.all_to_all(rows, "ep", split_axis=0, concat_axis=0, tiled=True).reshape(ROWS, width)


def local(tokens, expert_ids, hidden_grads, gate_weight, probes, grad_probes, window_counts):
    sds = jax.ShapeDtypeStruct
    pos = jnp.stack([lax.axis_index("rep"), lax.axis_index("ep") % 2]).astype(jnp.int32)
    inverse = 1.0 / window_counts.astype(F32)
    ids_t = expert_ids.T

    packed = pl.pallas_call(
        pack_half,
        out_shape=sds((TOK + 16, HALF), BF),
        grid_spec=pltpu.PrefetchScalarGridSpec(
            num_scalar_prefetch=1,
            grid=(1,),
            in_specs=[VM, pl.BlockSpec((TOK, HALF), lambda i, pos: (0, 1 - pos[1]))],
            out_specs=VM,
        ),
        compiler_params=pltpu.CompilerParams(vmem_limit_bytes=6 * MIB),
        cost_estimate=pl.CostEstimate(flops=1000, bytes_accessed=MIB, transcendentals=0),
    )(pos, ids_t, tokens)
    other = swap(packed)
    out_rows = kernel_call(
        send_rows,
        sds((ROWS, SHARE + STRIP), BF),
        [SM] + [VM] * 3,
        1 << 31,
        5 * MIB,
        20,
        [pltpu.VMEM((TOK, HALF), BF), pltpu.VMEM((TOP, TOK), jnp.int32)],
    )(pos, ids_t, tokens, other)
    rows = to_owners(out_rows)

    own, grads = gate_weight[0], hidden_grads.reshape(TOK * TOP, UNITS)
    own, grads, _ = lax.optimization_barrier((own, grads, out_rows))
    left, right = shift(own, 1), shift(own, REPS - 1)
    other_grads = swap(grads)
    picked = kernel_call(
        pick_grads, [sds((SLOTS + OWNERS, 256), BF)] * REPS, [SM] + [VM] * 4, 5 << 30, 3 * MIB, 20
    )(pos, ids_t, other, grads, other_grads)
    out_grads = kernel_call(
        fold_grads, sds((ROWS, 256), BF), [SM] + [VM] * 4, 1 << 31, 3 * MIB, 12
    )(pos, *shifted(picked))
    out_grads, left, right = lax.optimization_barrier((out_grads, left, right))
    top = shift(left[: UNITS // 2], 1)
    bottom = shift(right[UNITS // 2 :], REPS - 1)
    got = to_owners(out_grads)

    kinds = [F32, BF, BF, BF]
    gate, *inputs = kernel_call(
        products,
        [sds((FFW, ALL), F32)] + [sds((R, SHARE), kind) for kind in kinds],
        [SM] + [VM] * 7,
        4 << 30,
        12 * MIB,
        16,
        [pltpu.VMEM((ALL, D), BF), pltpu.VMEM((R, D), F32)],
    )(pos, rows, probes, own, right, top, bottom, left)
    inputs = shifted(inputs)

    sketches = kernel_call(
        gate_part,
        [sds((UNITS, R), kind) for kind in kinds],
        [SM] + [VM] * 3,
        1 << 30,
        3 * MIB,
        14,
        [pltpu.VMEM((ROWS, 256), BF), pltpu.VMEM((ROWS, 256), BF), pltpu.VMEM((FFW, R), F32)],
    )(pos, grad_probes, gate, got)
    sketches = shifted(sketches)

    input_sketch = kernel_call(
        finish_input, sds((SHARE, R), F32), [SM] + [VM] * 4, 1 << 20, 2 * MIB, 6
    )(inverse, *inputs)
    grad_sketch = kernel_call(
        finish_grad, sds((UNITS, R), F32), [SM] + [VM] * 4, 1 << 18, MIB // 4, 4
    )(inverse, *sketches)
    return input_sketch[None], grad_sketch[None]


def solution(mesh):
    placed = (
        P("ep", None),
        P("ep", None),
        P("ep", None, "rep"),
        P("ep", "rep", None),
        P(),
        P(),
        P("ep"),
    )
    return jax.shard_map(
        local,
        mesh=mesh,
        in_specs=placed,
        out_specs=(P("ep", "rep", None), P("ep", "rep", None)),
        check_vma=False,
    )
```

time: 167 us -> 162 us (0.970)
  starting transfers between devices: 85.4 us -> 79.5 us
  waiting for transfers between devices: 41.2 us -> 35.9 us
  local copies, waits for them, and re-layouts: 11.6 us -> 16.6 us
    ppermute x16 -> x13, starting transfers between devices: 54.3 us -> 44.3 us  [shift(): lax.ppermute(block, 'rep', [(i, (i + k) % REPS) for i in range(REPS)])]
    ppermute x16 -> x13, waiting for transfers between devices: 41.2 us -> 32.1 us  [shift(): lax.ppermute(block, 'rep', [(i, (i + k) % REPS) for i in range(REPS)])]
    unnamed x24 -> x39, local copies, waits for them, and re-layouts: 8.46 us -> 14.4 us
    ppermute x0 -> x2, waiting for transfers between devices: none -> 3.85 us  [swap(): return lax.ppermute(block, 'ep', [(i, i ^ 1) for i in range(OWNERS)])]
    ppermute x0 -> x2, starting transfers between devices: none -> 3.84 us  [swap(): return lax.ppermute(block, 'ep', [(i, i ^ 1) for i in range(OWNERS)])]
    pallas_call x7 -> x8, Pallas kernels: 26 us -> 26.9 us  [the longest x1 9.48 us: local(): kernel_call(products, [sds((FFW, ALL), F32)] + [sds((R, SHARE), kind) for...]
  transfers between devices with their start and end apart: 18 -> 17, of which waited for: 4 -> 7; matrix products, arithmetic and copies ran while one was open for 3% -> 2% of each run, Pallas kernels for 13% -> 13%
where the time goes in v4:
time: 162 us; the launch traced here: 161 us
  starting transfers between devices  79.5 us (49%)
  waiting for transfers between devices  35.9 us (22%)
  Pallas kernels  26.9 us (17%)
  local copies, waits for them, and re-layouts  16.6 us (10%)
    ppermute x13, starting transfers between devices, shift(): lax.ppermute(block, 'rep', [(i, (i + k) % REPS) for i in range(REPS)])  44.3 us
    ppermute x13, waiting for transfers between devices, shift(): lax.ppermute(block, 'rep', [(i, (i + k) % REPS) for i in range(REPS)])  32.1 us
    all_to_all x2, starting transfers between devices, to_owners(): lax.all_to_all(rows, 'ep', split_axis=0, concat_axis=0, tiled=True)  31.4 us
    unnamed x39, local copies, waits for them, and re-layouts  14.4 us
    pallas_call x1, Pallas kernels, local(): kernel_call(products, [sds((FFW, ALL), F32)] + [sds((R, SHARE), kind) for...  9.48 us
    pallas_call x1, Pallas kernels, local(): kernel_call(fold_grads, sds((ROWS, 256), BF), [SM] + [VM] * 4, 1 << 31, 3...  6.65 us
    ppermute x2, waiting for transfers between devices, swap(): return lax.ppermute(block, 'ep', [(i, i ^ 1) for i in range(OWNERS)])  3.85 us
    ppermute x2, starting transfers between devices, swap(): return lax.ppermute(block, 'ep', [(i, i ^ 1) for i in range(OWNERS)])  3.84 us
  transfers between devices with their start and end apart: 17, of which 7 were waited for; matrix products, arithmetic and copies ran while one was open for 2% of the time, Pallas kernels for 13%

profile of v4, /device:TPU:8, one launch (start us, length us, event | category | flops | bytes accessed | tf_op | source)
XLA Modules:
  0.0 160.7 jit_solution(18426236907128902089)
XLA Ops:
  0.7 0.1 pad_add_fusion.pos_ref
  0.7 1.2 copy-done.1
  2.0 0.7 copy-done.9
  2.6 0.6 shard_map.86
  3.2 1.9 %collective-permute-start = (bf16[144,2048]{1,0:T(8,128)(2,1)S(1)}, bf16[144,2048]{1,0:T(8,128)(2,1)S(1)}, u32[]{:S(2)}, u32[]{:S(2)}) collective-permute-start(bf16[144,2048]{1,0:T(8,128)(2,1)S(1)} %shard_map.86), channel_id=1, source_target_pairs={{0,4},{4,0},{8,12},{12,8},{16,20},{20,16},{24,28},{28,24},{32,36},... | collective-permute-start | bytes 1769480 | tf_op jit(solution)/shard_map/ppermute | solution.py:263
  5.2 2.0 %collective-permute-done.other_ref = bf16[144,2048]{1,0:T(8,128)(2,1)S(1)} collective-permute-done((bf16[144,2048]{1,0:T(8,128)(2,1)S(1)}, bf16[144,2048]{1,0:T(8,128)(2,1)S(1)}, u32[]{:S(2)}, u32[]{:S(2)}) %collective-permute-start) | collective-permute-done | bytes 589856 | tf_op jit(solution)/shard_map/ppermute | solution.py:263
  7.1 3.8 %shard_map.87 = bf16[1024,1280]{1,0:T(8,128)(2,1)S(1)} custom-call(s32[2]{0:T(128)S(1)} %pad_add_fusion.pos_ref, s32[8,128]{1,0:T(8,128)S(1)} %bitcast.17, bf16[128,4096]{1,0:T(8,128)(2,1)S(1)} %copy-done.2, bf16[144,2048]{1,0:T(8,128)(2,1)S(1)} %collective-permute-done.other_ref), custom_call_target="tpu_custom_call" | custom-call | flops 2147483648 | bytes 5242880 | tf_op jit(solution)/shard_map/pallas_call | solution.py:291
  10.9 1.5 copy-done
  12.4 17.5 %all-to-all-start = ((bf16[128,8,1280]{2,1,0:T(8,128)(2,1)}), bf16[128,8,1280]{2,1,0:T(8,128)(2,1)S(1)}, u32[]{:S(2)}, u32[]{:S(2)}) async-start(bf16[128,8,1280]{2,1,0:T(8,128)(2,1)} %bitcast.12), calls=%async_computation | async-start | bytes 5242880 | tf_op jit(solution)/shard_map/all_to_all | solution.py:269
  29.9 0.4 copy.9
  30.3 4.7 %collective-permute-start.6 = (bf16[192,4096]{1,0:T(8,128)(2,1)}, bf16[192,4096]{1,0:T(8,128)(2,1)S(1)}, u32[]{:S(2)}, u32[]{:S(2)}) collective-permute-start(bf16[192,4096]{1,0:T(8,128)(2,1)} %bitcast.19), channel_id=1, source_target_pairs={{0,3},{1,0},{2,1},{3,2},{4,7},{5,4},{6,5},{7,6},{8,11},{9,8},{10,9... | collective-permute-start | bytes 4718600 | tf_op jit(solution)/shard_map/ppermute | solution.py:255
  35.0 1.9 %collective-permute-start.5 = (bf16[192,4096]{1,0:T(8,128)(2,1)}, bf16[192,4096]{1,0:T(8,128)(2,1)S(1)}, u32[]{:S(2)}, u32[]{:S(2)}) collective-permute-start(bf16[192,4096]{1,0:T(8,128)(2,1)} %bitcast.20), channel_id=1, source_target_pairs={{0,1},{1,2},{2,3},{3,0},{4,5},{5,6},{6,7},{7,4},{8,9},{9,10},{10,1... | collective-permute-start | bytes 4718600 | tf_op jit(solution)/shard_map/ppermute | solution.py:255
  37.0 1.9 %collective-permute-start.1 = (bf16[1024,192]{1,0:T(8,128)(2,1)S(1)}, bf16[1024,192]{1,0:T(8,128)(2,1)S(1)}, u32[]{:S(2)}, u32[]{:S(2)}) collective-permute-start(bf16[1024,192]{1,0:T(8,128)(2,1)S(1)} %bitcast.13), channel_id=1, source_target_pairs={{0,4},{4,0},{8,12},{12,8},{16,20},{20,16},{24,28},{28,24},{32,36},... | collective-permute-start | bytes 1179656 | tf_op jit(solution)/shard_map/ppermute | solution.py:263
  38.9 1.9 %collective-permute-done.1.other_grads_ref = bf16[1024,192]{1,0:T(8,128)(2,1)S(1)} collective-permute-done((bf16[1024,192]{1,0:T(8,128)(2,1)S(1)}, bf16[1024,192]{1,0:T(8,128)(2,1)S(1)}, u32[]{:S(2)}, u32[]{:S(2)}) %collective-permute-start.1) | collective-permute-done | bytes 393248 | tf_op jit(solution)/shard_map/ppermute | solution.py:263
  40.8 1.1 copy-done.14
  41.8 2.9 %shard_map.88 = (bf16[384,256]{1,0:T(8,128)(2,1)S(1)}, bf16[384,256]{1,0:T(8,128)(2,1)S(1)}, bf16[384,256]{1,0:T(8,128)(2,1)S(1)}, bf16[384,256]{1,0:T(8,128)(2,1)S(1)}) custom-call(s32[2]{0:T(128)S(1)} %pad_add_fusion.pos_ref, s32[8,128]{1,0:T(8,128)S(1)} %bitcast.18, bf16[144,2048]{1,0:T(8,128)(2,1)S(1)} %copy-done.14, bf16[1024,192]{1,0:T(8,128)(2,1)S(1)} %bitcast.14, ...), custom_call_target="tpu_custom_call" | custom-call | flops 5368709120 | bytes 3145728 | tf_op jit(solution)/shard_map/pallas_call | solution.py:306
  44.7 2.6 %collective-permute-start.2 = (bf16[384,256]{1,0:T(8,128)(2,1)S(1)}, bf16[384,256]{1,0:T(8,128)(2,1)S(1)}, u32[]{:S(2)}, u32[]{:S(2)}) collective-permute-start(bf16[384,256]{1,0:T(8,128)(2,1)S(1)} %get-tuple-element.23), channel_id=1, source_target_pairs={{0,1},{1,2},{2,3},{3,0},{4,5},{5,6},{6,7},{7,4},{8,9},{9,10},{10,1... | collective-permute-start | bytes 589832 | tf_op jit(solution)/shard_map/ppermute | solution.py:255
  47.3 5.9 %collective-permute-start.3 = (bf16[384,256]{1,0:T(8,128)(2,1)S(1)}, bf16[384,256]{1,0:T(8,128)(2,1)S(1)}, u32[]{:S(2)}, u32[]{:S(2)}) collective-permute-start(bf16[384,256]{1,0:T(8,128)(2,1)S(1)} %get-tuple-element.24), channel_id=1, source_target_pairs={{0,2},{1,3},{2,0},{3,1},{4,6},{5,7},{6,4},{7,5},{8,10},{9,11},{10,... | collective-permute-start | bytes 589832 | tf_op jit(solution)/shard_map/ppermute | solution.py:255
  53.2 2.1 %collective-permute-start.4 = (bf16[384,256]{1,0:T(8,128)(2,1)S(1)}, bf16[384,256]{1,0:T(8,128)(2,1)S(1)}, u32[]{:S(2)}, u32[]{:S(2)}) collective-permute-start(bf16[384,256]{1,0:T(8,128)(2,1)S(1)} %get-tuple-element.25), channel_id=1, source_target_pairs={{0,3},{1,0},{2,1},{3,2},{4,7},{5,4},{6,5},{7,6},{8,11},{9,8},{10,9... | collective-permute-start | bytes 589832 | tf_op jit(solution)/shard_map/ppermute | solution.py:255
  55.4 27.6 %collective-permute-done.2.g1 = bf16[384,256]{1,0:T(8,128)(2,1)S(1)} collective-permute-done((bf16[384,256]{1,0:T(8,128)(2,1)S(1)}, bf16[384,256]{1,0:T(8,128)(2,1)S(1)}, u32[]{:S(2)}, u32[]{:S(2)}) %collective-permute-start.2) | collective-permute-done | bytes 196640 | tf_op jit(solution)/shard_map/ppermute | solution.py:255
  82.9 6.6 %shard_map.89 = bf16[1024,256]{1,0:T(8,128)(2,1)} custom-call(s32[2]{0:T(128)S(1)} %pad_add_fusion.pos_ref, bf16[384,256]{1,0:T(8,128)(2,1)S(1)} %get-tuple-element.22.g0, bf16[384,256]{1,0:T(8,128)(2,1)S(1)} %collective-permute-done.2.g1, bf16[384,256]{1,0:T(8,128)(2,1)S(1)} %collective-permute-done.3.g2, bf16[384,256]{1,0:T(8,128)(2,1)S(1)} %collective-permute-done.4.g3), custom_call_target="tpu_custom_call" | custom-call | flops 2147483648 | bytes 3145728 | tf_op jit(solution)/shard_map/pallas_call | solution.py:309
  89.6 1.1 slice.7
  90.7 1.2 slice.6
  91.9 1.9 %collective-permute-start.7 = (bf16[96,4096]{1,0:T(8,128)(2,1)}, bf16[96,4096]{1,0:T(8,128)(2,1)}, u32[]{:S(2)}, u32[]{:S(2)}) collective-permute-start(bf16[96,4096]{1,0:T(8,128)(2,1)} %slice.6), channel_id=1, source_target_pairs={{0,1},{1,2},{2,3},{3,0},{4,5},{5,6},{6,7},{7,4},{8,9},{9,10},{10,1... | collective-permute-start | bytes 2359304 | tf_op jit(solution)/shard_map/ppermute | solution.py:255
  93.8 5.1 %collective-permute-start.8 = (bf16[96,4096]{1,0:T(8,128)(2,1)}, bf16[96,4096]{1,0:T(8,128)(2,1)}, u32[]{:S(2)}, u32[]{:S(2)}) collective-permute-start(bf16[96,4096]{1,0:T(8,128)(2,1)} %slice.7), channel_id=1, source_target_pairs={{0,3},{1,0},{2,1},{3,2},{4,7},{5,4},{6,5},{7,6},{8,11},{9,8},{10,9... | collective-permute-start | bytes 2359304 | tf_op jit(solution)/shard_map/ppermute | solution.py:255
  99.0 13.9 %all-to-all-start.1 = ((bf16[128,8,256]{2,1,0:T(8,128)(2,1)}), bf16[128,8,256]{2,1,0:T(8,128)(2,1)S(1)}, u32[]{:S(2)}, u32[]{:S(2)}) async-start(bf16[128,8,256]{2,1,0:T(8,128)(2,1)} %bitcast.8), calls=%async_computation.1 | async-start | bytes 1048576 | tf_op jit(solution)/shard_map/all_to_all | solution.py:269
  112.9 1.1 collective-permute-done.8.bottom_ref
  114.0 1.4 copy-done.6
  115.4 1.4 copy-done.8
  116.9 1.4 copy-done.11
  118.3 1.2 copy-done.12
  119.5 9.5 %shard_map.90 = (f32[768,384]{1,0:T(8,128)S(1)}, f32[128,1024]{1,0:T(8,128)S(1)}, bf16[128,1024]{1,0:T(8,128)(2,1)}, bf16[128,1024]{1,0:T(8,128)(2,1)}, bf16[128,1024]{1,0:T(8,128)(2,1)S(1)}) custom-call(s32[2]{0:T(128)S(1)} %pad_add_fusion.pos_ref, bf16[1024,1280]{1,0:T(8,128)(2,1)S(1)} %bitcast.11, bf16[128,4096]{1,0:T(8,128)(2,1)S(1)} %copy-done.12, ...), custom_call_target="tpu_custom_call" | custom-call | flops 4294967296 | bytes 12582912 | tf_op jit(solution)/shard_map/pallas_call | solution.py:318
  129.0 0.8 copy-done.3
  129.8 1.0 copy-done.16
  130.8 2.9 %collective-permute-start.9 = (bf16[128,1024]{1,0:T(8,128)(2,1)}, bf16[128,1024]{1,0:T(8,128)(2,1)S(1)}, u32[]{:S(2)}, u32[]{:S(2)}) collective-permute-start(bf16[128,1024]{1,0:T(8,128)(2,1)} %get-tuple-element.29), channel_id=1, source_target_pairs={{0,1},{1,2},{2,3},{3,0},{4,5},{5,6},{6,7},{7,4},{8,9},{9,10},{10,1... | collective-permute-start | bytes 786440 | tf_op jit(solution)/shard_map/ppermute | solution.py:255
  133.7 6.1 %collective-permute-start.10 = (bf16[128,1024]{1,0:T(8,128)(2,1)}, bf16[128,1024]{1,0:T(8,128)(2,1)S(1)}, u32[]{:S(2)}, u32[]{:S(2)}) collective-permute-start(bf16[128,1024]{1,0:T(8,128)(2,1)} %get-tuple-element.30), channel_id=1, source_target_pairs={{0,2},{1,3},{2,0},{3,1},{4,6},{5,7},{6,4},{7,5},{8,10},{9,11},{10,... | collective-permute-start | bytes 786440 | tf_op jit(solution)/shard_map/ppermute | solution.py:255
  139.8 1.9 %collective-permute-start.11 = (bf16[128,1024]{1,0:T(8,128)(2,1)S(1)}, bf16[128,1024]{1,0:T(8,128)(2,1)S(1)}, u32[]{:S(2)}, u32[]{:S(2)}) collective-permute-start(bf16[128,1024]{1,0:T(8,128)(2,1)S(1)} %get-tuple-element.31), channel_id=1, source_target_pairs={{0,3},{1,0},{2,1},{3,2},{4,7},{5,4},{6,5},{7,6},{8,11},{9,8},{10,9... | collective-permute-start | bytes 786440 | tf_op jit(solution)/shard_map/ppermute | solution.py:255
  141.7 0.9 copy-done.15
  142.6 1.3 copy-done.17
  143.9 1.9 %shard_map.92 = (f32[192,128]{1,0:T(8,128)S(1)}, bf16[192,128]{1,0:T(8,128)(2,1)S(1)}, bf16[192,128]{1,0:T(8,128)(2,1)S(1)}, bf16[192,128]{1,0:T(8,128)(2,1)S(1)}) custom-call(s32[2]{0:T(128)S(1)} %pad_add_fusion.pos_ref, bf16[128,768]{1,0:T(8,128)(2,1)S(1)} %copy-done.15, f32[768,384]{1,0:T(8,128)S(1)} %copy-done.17, bf16[1024,256]{1,0:T(8,128)(2,1)S(1)} %bitcast.15), custom_call_target="tpu_custom_call" | custom-call | flops 1073741824 | bytes 3145728 | tf_op jit(solution)/shard_map/pallas_call | solution.py:329
  145.8 3.9 %collective-permute-start.12 = (bf16[192,128]{1,0:T(8,128)(2,1)S(1)}, bf16[192,128]{1,0:T(8,128)(2,1)S(1)}, u32[]{:S(2)}, u32[]{:S(2)}) collective-permute-start(bf16[192,128]{1,0:T(8,128)(2,1)S(1)} %get-tuple-element.35), channel_id=1, source_target_pairs={{0,1},{1,2},{2,3},{3,0},{4,5},{5,6},{6,7},{7,4},{8,9},{9,10},{10,1... | collective-permute-start | bytes 147464 | tf_op jit(solution)/shard_map/ppermute | solution.py:255
  149.7 1.9 %collective-permute-start.13 = (bf16[192,128]{1,0:T(8,128)(2,1)S(1)}, bf16[192,128]{1,0:T(8,128)(2,1)S(1)}, u32[]{:S(2)}, u32[]{:S(2)}) collective-permute-start(bf16[192,128]{1,0:T(8,128)(2,1)S(1)} %get-tuple-element.36), channel_id=1, source_target_pairs={{0,2},{1,3},{2,0},{3,1},{4,6},{5,7},{6,4},{7,5},{8,10},{9,11},{10,... | collective-permute-start | bytes 147464 | tf_op jit(solution)/shard_map/ppermute | solution.py:255
  151.7 1.3 collective-permute-done.12.t1
  153.0 3.3 %collective-permute-start.14 = (bf16[192,128]{1,0:T(8,128)(2,1)S(1)}, bf16[192,128]{1,0:T(8,128)(2,1)S(1)}, u32[]{:S(2)}, u32[]{:S(2)}) collective-permute-start(bf16[192,128]{1,0:T(8,128)(2,1)S(1)} %get-tuple-element.37), channel_id=1, source_target_pairs={{0,3},{1,0},{2,1},{3,2},{4,7},{5,4},{6,5},{7,6},{8,11},{9,8},{10,9... | collective-permute-start | bytes 147464 | tf_op jit(solution)/shard_map/ppermute | solution.py:255
  156.9 0.3 collective-permute-done.13.t2
  157.2 1.7 %collective-permute-done.14.t3 = bf16[192,128]{1,0:T(8,128)(2,1)S(1)} collective-permute-done((bf16[192,128]{1,0:T(8,128)(2,1)S(1)}, bf16[192,128]{1,0:T(8,128)(2,1)S(1)}, u32[]{:S(2)}, u32[]{:S(2)}) %collective-permute-start.14) | collective-permute-done | bytes 49184 | tf_op jit(solution)/shard_map/ppermute | solution.py:255
  159.0 0.7 shard_map.93
  159.7 1.0 shard_map.91
  (36 shorter events, 0.1 us)
Async XLA Ops:
  0.6 6.5 %copy-start.10 = (s32[128,8]{0,1:T(8,128)S(1)}, s32[128,8]{0,1:T(8,128)}, u32[]{:S(2)}) copy-start(s32[128,8]{0,1:T(8,128)} %param.8) | copy-start | bytes 12292
  0.7 1.2 copy-start.1
  2.0 0.7 copy-start.9
  2.6 4.5 %copy-start.2 = (bf16[128,4096]{1,0:T(8,128)(2,1)S(1)}, bf16[128,4096]{1,0:T(8,128)(2,1)}, u32[]{:S(2)}) copy-start(bf16[128,4096]{1,0:T(8,128)(2,1)} %tokens_ref.3) | copy-start | bytes 3145732
  3.2 3.9 %collective-permute-start = (bf16[144,2048]{1,0:T(8,128)(2,1)S(1)}, bf16[144,2048]{1,0:T(8,128)(2,1)S(1)}, u32[]{:S(2)}, u32[]{:S(2)}) collective-permute-start(bf16[144,2048]{1,0:T(8,128)(2,1)S(1)} %shard_map.86), channel_id=1, source_target_pairs={{0,4},{4,0},{8,12},{12,8},{16,20},{20,16},{24,28},{28,24},{32,36},... | collective-permute-start | bytes 1769480 | tf_op jit(solution)/shard_map/ppermute | solution.py:263
  7.1 3.8 %copy-start.13 = (bf16[144,2048]{1,0:T(8,128)(2,1)}, bf16[144,2048]{1,0:T(8,128)(2,1)S(1)}, u32[]{:S(2)}) copy-start(bf16[144,2048]{1,0:T(8,128)(2,1)S(1)} %collective-permute-done.other_ref) | copy-start | bytes 1769476
  10.9 1.5 copy-start
  12.4 17.5 %copy-start.18 = (bf16[128,8,192]{0,2,1:T(8,128)(2,1)S(1)}, bf16[128,8,192]{0,2,1:T(8,128)(2,1)}, u32[]{:S(2)}) copy-start(bf16[128,8,192]{0,2,1:T(8,128)(2,1)} %param.9) | copy-start | bytes 1179652
  12.4 86.6 %all-to-all-start = ((bf16[128,8,1280]{2,1,0:T(8,128)(2,1)}), bf16[128,8,1280]{2,1,0:T(8,128)(2,1)S(1)}, u32[]{:S(2)}, u32[]{:S(2)}) async-start(bf16[128,8,1280]{2,1,0:T(8,128)(2,1)} %bitcast.12), calls=%async_computation | async-start | bytes 5242880 | tf_op jit(solution)/shard_map/all_to_all | solution.py:269
  30.3 59.3 %collective-permute-start.6 = (bf16[192,4096]{1,0:T(8,128)(2,1)}, bf16[192,4096]{1,0:T(8,128)(2,1)S(1)}, u32[]{:S(2)}, u32[]{:S(2)}) collective-permute-start(bf16[192,4096]{1,0:T(8,128)(2,1)} %bitcast.19), channel_id=1, source_target_pairs={{0,3},{1,0},{2,1},{3,2},{4,7},{5,4},{6,5},{7,6},{8,11},{9,8},{10,9... | collective-permute-start | bytes 4718600 | tf_op jit(solution)/shard_map/ppermute | solution.py:255
  35.0 54.6 %collective-permute-start.5 = (bf16[192,4096]{1,0:T(8,128)(2,1)}, bf16[192,4096]{1,0:T(8,128)(2,1)S(1)}, u32[]{:S(2)}, u32[]{:S(2)}) collective-permute-start(bf16[192,4096]{1,0:T(8,128)(2,1)} %bitcast.20), channel_id=1, source_target_pairs={{0,1},{1,2},{2,3},{3,0},{4,5},{5,6},{6,7},{7,4},{8,9},{9,10},{10,1... | collective-permute-start | bytes 4718600 | tf_op jit(solution)/shard_map/ppermute | solution.py:255
  37.0 3.8 %collective-permute-start.1 = (bf16[1024,192]{1,0:T(8,128)(2,1)S(1)}, bf16[1024,192]{1,0:T(8,128)(2,1)S(1)}, u32[]{:S(2)}, u32[]{:S(2)}) collective-permute-start(bf16[1024,192]{1,0:T(8,128)(2,1)S(1)} %bitcast.13), channel_id=1, source_target_pairs={{0,4},{4,0},{8,12},{12,8},{16,20},{20,16},{24,28},{28,24},{32,36},... | collective-permute-start | bytes 1179656 | tf_op jit(solution)/shard_map/ppermute | solution.py:263
  40.8 1.1 copy-start.14
  44.7 38.2 %collective-permute-start.2 = (bf16[384,256]{1,0:T(8,128)(2,1)S(1)}, bf16[384,256]{1,0:T(8,128)(2,1)S(1)}, u32[]{:S(2)}, u32[]{:S(2)}) collective-permute-start(bf16[384,256]{1,0:T(8,128)(2,1)S(1)} %get-tuple-element.23), channel_id=1, source_target_pairs={{0,1},{1,2},{2,3},{3,0},{4,5},{5,6},{6,7},{7,4},{8,9},{9,10},{10,1... | collective-permute-start | bytes 589832 | tf_op jit(solution)/shard_map/ppermute | solution.py:255
  47.3 35.6 %collective-permute-start.3 = (bf16[384,256]{1,0:T(8,128)(2,1)S(1)}, bf16[384,256]{1,0:T(8,128)(2,1)S(1)}, u32[]{:S(2)}, u32[]{:S(2)}) collective-permute-start(bf16[384,256]{1,0:T(8,128)(2,1)S(1)} %get-tuple-element.24), channel_id=1, source_target_pairs={{0,2},{1,3},{2,0},{3,1},{4,6},{5,7},{6,4},{7,5},{8,10},{9,11},{10,... | collective-permute-start | bytes 589832 | tf_op jit(solution)/shard_map/ppermute | solution.py:255
  53.2 29.7 %collective-permute-start.4 = (bf16[384,256]{1,0:T(8,128)(2,1)S(1)}, bf16[384,256]{1,0:T(8,128)(2,1)S(1)}, u32[]{:S(2)}, u32[]{:S(2)}) collective-permute-start(bf16[384,256]{1,0:T(8,128)(2,1)S(1)} %get-tuple-element.25), channel_id=1, source_target_pairs={{0,3},{1,0},{2,1},{3,2},{4,7},{5,4},{6,5},{7,6},{8,11},{9,8},{10,9... | collective-permute-start | bytes 589832 | tf_op jit(solution)/shard_map/ppermute | solution.py:255
  89.6 2.3 %copy-start.5 = (bf16[192,4096]{1,0:T(8,128)(2,1)}, bf16[192,4096]{1,0:T(8,128)(2,1)S(1)}, u32[]{:S(2)}) copy-start(bf16[192,4096]{1,0:T(8,128)(2,1)S(1)} %collective-permute-done.6.right_ref) | copy-start | bytes 4718596
  89.6 2.3 %copy-start.7 = (bf16[192,4096]{1,0:T(8,128)(2,1)}, bf16[192,4096]{1,0:T(8,128)(2,1)S(1)}, u32[]{:S(2)}) copy-start(bf16[192,4096]{1,0:T(8,128)(2,1)S(1)} %collective-permute-done.5.left_ref) | copy-start | bytes 4718596
  91.9 21.0 %collective-permute-start.7 = (bf16[96,4096]{1,0:T(8,128)(2,1)}, bf16[96,4096]{1,0:T(8,128)(2,1)}, u32[]{:S(2)}, u32[]{:S(2)}) collective-permute-start(bf16[96,4096]{1,0:T(8,128)(2,1)} %slice.6), channel_id=1, source_target_pairs={{0,1},{1,2},{2,3},{3,0},{4,5},{5,6},{6,7},{7,4},{8,9},{9,10},{10,1... | collective-permute-start | bytes 2359304 | tf_op jit(solution)/shard_map/ppermute | solution.py:255
  93.8 20.2 %collective-permute-start.8 = (bf16[96,4096]{1,0:T(8,128)(2,1)}, bf16[96,4096]{1,0:T(8,128)(2,1)}, u32[]{:S(2)}, u32[]{:S(2)}) collective-permute-start(bf16[96,4096]{1,0:T(8,128)(2,1)} %slice.7), channel_id=1, source_target_pairs={{0,3},{1,0},{2,1},{3,2},{4,7},{5,4},{6,5},{7,6},{8,11},{9,8},{10,9... | collective-permute-start | bytes 2359304 | tf_op jit(solution)/shard_map/ppermute | solution.py:255
  99.0 42.7 %all-to-all-start.1 = ((bf16[128,8,256]{2,1,0:T(8,128)(2,1)}), bf16[128,8,256]{2,1,0:T(8,128)(2,1)S(1)}, u32[]{:S(2)}, u32[]{:S(2)}) async-start(bf16[128,8,256]{2,1,0:T(8,128)(2,1)} %bitcast.8), calls=%async_computation.1 | async-start | bytes 1048576 | tf_op jit(solution)/shard_map/all_to_all | solution.py:269
  114.0 1.4 copy-start.6
  115.4 1.4 copy-start.8
  116.9 1.4 copy-start.11
  118.3 1.2 copy-start.12
  129.0 0.8 copy-start.3
  129.8 1.0 copy-start.16
  130.8 28.8 %collective-permute-start.9 = (bf16[128,1024]{1,0:T(8,128)(2,1)}, bf16[128,1024]{1,0:T(8,128)(2,1)S(1)}, u32[]{:S(2)}, u32[]{:S(2)}) collective-permute-start(bf16[128,1024]{1,0:T(8,128)(2,1)} %get-tuple-element.29), channel_id=1, source_target_pairs={{0,1},{1,2},{2,3},{3,0},{4,5},{5,6},{6,7},{7,4},{8,9},{9,10},{10,1... | collective-permute-start | bytes 786440 | tf_op jit(solution)/shard_map/ppermute | solution.py:255
  133.7 25.9 %collective-permute-start.10 = (bf16[128,1024]{1,0:T(8,128)(2,1)}, bf16[128,1024]{1,0:T(8,128)(2,1)S(1)}, u32[]{:S(2)}, u32[]{:S(2)}) collective-permute-start(bf16[128,1024]{1,0:T(8,128)(2,1)} %get-tuple-element.30), channel_id=1, source_target_pairs={{0,2},{1,3},{2,0},{3,1},{4,6},{5,7},{6,4},{7,5},{8,10},{9,11},{10,... | collective-permute-start | bytes 786440 | tf_op jit(solution)/shard_map/ppermute | solution.py:255
  139.8 19.9 %collective-permute-start.11 = (bf16[128,1024]{1,0:T(8,128)(2,1)S(1)}, bf16[128,1024]{1,0:T(8,128)(2,1)S(1)}, u32[]{:S(2)}, u32[]{:S(2)}) collective-permute-start(bf16[128,1024]{1,0:T(8,128)(2,1)S(1)} %get-tuple-element.31), channel_id=1, source_target_pairs={{0,3},{1,0},{2,1},{3,2},{4,7},{5,4},{6,5},{7,6},{8,11},{9,8},{10,9... | collective-permute-start | bytes 786440 | tf_op jit(solution)/shard_map/ppermute | solution.py:255
  141.7 0.9 copy-start.15
  142.6 1.3 copy-start.17
  143.9 15.7 %copy-start.4 = (f32[128,1024]{1,0:T(8,128)S(1)}, f32[128,1024]{1,0:T(8,128)}, u32[]{:S(2)}) copy-start(f32[128,1024]{1,0:T(8,128)} %copy-done.3) | copy-start | bytes 1572868
  145.8 7.2 %collective-permute-start.12 = (bf16[192,128]{1,0:T(8,128)(2,1)S(1)}, bf16[192,128]{1,0:T(8,128)(2,1)S(1)}, u32[]{:S(2)}, u32[]{:S(2)}) collective-permute-start(bf16[192,128]{1,0:T(8,128)(2,1)S(1)} %get-tuple-element.35), channel_id=1, source_target_pairs={{0,1},{1,2},{2,3},{3,0},{4,5},{5,6},{6,7},{7,4},{8,9},{9,10},{10,1... | collective-permute-start | bytes 147464 | tf_op jit(solution)/shard_map/ppermute | solution.py:255
  149.7 7.5 %collective-permute-start.13 = (bf16[192,128]{1,0:T(8,128)(2,1)S(1)}, bf16[192,128]{1,0:T(8,128)(2,1)S(1)}, u32[]{:S(2)}, u32[]{:S(2)}) collective-permute-start(bf16[192,128]{1,0:T(8,128)(2,1)S(1)} %get-tuple-element.36), channel_id=1, source_target_pairs={{0,2},{1,3},{2,0},{3,1},{4,6},{5,7},{6,4},{7,5},{8,10},{9,11},{10,... | collective-permute-start | bytes 147464 | tf_op jit(solution)/shard_map/ppermute | solution.py:255
  153.0 6.0 %collective-permute-start.14 = (bf16[192,128]{1,0:T(8,128)(2,1)S(1)}, bf16[192,128]{1,0:T(8,128)(2,1)S(1)}, u32[]{:S(2)}, u32[]{:S(2)}) collective-permute-start(bf16[192,128]{1,0:T(8,128)(2,1)S(1)} %get-tuple-element.37), channel_id=1, source_target_pairs={{0,3},{1,0},{2,1},{3,2},{4,7},{5,4},{6,5},{7,6},{8,11},{9,8},{10,9... | collective-permute-start | bytes 147464 | tf_op jit(solution)/shard_map/ppermute | solution.py:255

commit v5 on v4

--- a/solution.py
+++ b/solution.py
@@ -59,6 +59,27 @@
     )
 
 
+def gridded_call(
+    body, out_shape, steps, in_specs, out_specs, bytes_accessed, scratch=(), aliases=None
+):
+    return pl.pallas_call(
+        body,
+        out_shape=out_shape,
+        grid_spec=pltpu.PrefetchScalarGridSpec(
+            num_scalar_prefetch=1,
+            grid=(steps,),
+            in_specs=in_specs,
+            out_specs=out_specs,
+            scratch_shapes=list(scratch),
+        ),
+        input_output_aliases=aliases or {},
+        compiler_params=pltpu.CompilerParams(vmem_limit_bytes=56 * MIB),
+        cost_estimate=pl.CostEstimate(
+            flops=1 << 30, bytes_accessed=bytes_accessed, transcendentals=0
+        ),
+    )
+
+
 def places(ids_t):
     experts = iota((OWNERS, TOK), 0)
     named = jnp.zeros((OWNERS, TOK), F32)
@@ -80,7 +101,7 @@
 
 
 def spread(table, times):
-    shape = (OWNERS * times, OWNERS)
+    shape = (table.shape[0] * times, table.shape[0])
     return dot(ones_where(iota(shape, 0) // times == iota(shape, 1)), table.astype(BF))
 
 
@@ -95,19 +116,28 @@
     return other_ref[TOK:, :TOK].astype(F32)[:TOP].astype(jnp.int32)
 
 
-def send_rows(pos_ref, ids_ref, tokens_ref, other_ref, out_ref, half_ref, half_ids_ref):
-    x, c = pos_ref[0], pos_ref[1]
-    mine = x // 2 == c
-    table = spread(places(ids_ref[...]), FOLD)
-    row = iota((ROWS, TOK), 0)
+def send_whole(pos_ref, ids_ref, tokens_ref, out_ref, table_ref):
+    step, x = pl.program_id(0), pos_ref[0]
+
+    @pl.when(step == 0)
+    def _():
+        table_ref[...] = places(ids_ref[...])
+
+    table = spread(table_ref[pl.ds(pl.multiple_of(step * 32, 32), 32), :], FOLD)
+    row = iota(table.shape, 0)
     whole = table == (2 * x + row % 8 // 4).astype(F32)
     picks = jnp.concatenate([ones_where(whole & (row % 4 == b)) for b in range(4)], 1)
     parts = jnp.concatenate([tokens_ref[:, b * SHARE : (b + 1) * SHARE] for b in range(4)], 0)
-    out_ref[:, :SHARE] = dot(picks, parts).astype(BF)
+    out_ref[...] = dot(picks, parts).astype(BF)
+
+
+def send_shared(pos_ref, ids_ref, tokens_ref, other_ref, _, out_ref, half_ref, half_ids_ref):
+    x, c = pos_ref[0], pos_ref[1]
+    mine = x // 2 == c
 
     @pl.when(mine)
     def _():
-        half_ref[...] = tokens_ref[:, pl.ds(pl.multiple_of(c * HALF, HALF), HALF)]
+        half_ref[...] = tokens_ref[...]
         half_ids_ref[...] = ids_ref[...]
 
     @pl.when(jnp.logical_not(mine))
@@ -116,10 +146,11 @@
         half_ids_ref[...] = other_ids(other_ref)
 
     table = spread(places(half_ids_ref[...]), FOLD)
+    row = iota(table.shape, 0)
     shared = table == (FIRST + x % 2).astype(F32)
     picks = jnp.concatenate([ones_where(shared & (row % 8 == b)) for b in range(8)], 1)
     parts = jnp.concatenate([half_ref[:, b * STRIP : (b + 1) * STRIP] for b in range(8)], 0)
-    out_ref[:, SHARE:] = dot(picks, parts).astype(BF)
+    out_ref[...] = dot(picks, parts).astype(BF)
 
 
 def pick_grads(pos_ref, ids_ref, other_ref, grads_ref, other_grads_ref, *outs):
@@ -171,41 +202,32 @@
             put(p, slice(g * size, (g + 1) * size), got[p * size : (p + 1) * size])
 
 
-def products(
-    pos_ref, rows_ref, probes_ref, own_ref, right_ref, top_ref, bottom_ref, left_ref,
-    gate_ref, i0, i1, i2, i3, rows_all_ref, sum_ref,
-):
+def input_products(pos_ref, rows_ref, probes_ref, all_ref, i0, i1, i2, i3, sum_ref):
     x = pos_ref[0]
 
     def put_whole(p, at, got):
-        rows_all_ref[at, p * SHARE : (p + 1) * SHARE] = got
+        all_ref[at, p * SHARE : (p + 1) * SHARE] = got
 
     def put_shared(p, at, got):
-        rows_all_ref[SLOTS + at.start : SLOTS + at.stop, p * STRIP : (p + 1) * STRIP] = got
+        all_ref[SLOTS + at.start : SLOTS + at.stop, p * STRIP : (p + 1) * STRIP] = got
 
     regroup(lambda at: rows_ref[at, :SHARE], 4, put_whole)
     regroup(lambda at: rows_ref[at, SHARE:], 16, put_shared)
-    rows_all_ref[SLOTS + PAIRS :, :] = jnp.zeros((ALL - SLOTS - PAIRS, D), BF)
-    rows = rows_all_ref[...]
+    all_ref[SLOTS + PAIRS :, :] = jnp.zeros((ALL - SLOTS - PAIRS, D), BF)
+    rows = all_ref[...]
     projected = dot(probes_ref[...], rows, NT).astype(BF)
     sum_ref[...] = dot(projected, rows)
     for k, out in enumerate((i0, i1, i2, i3)):
         base = lax.rem(x + k, REPS) * SHARE
         out[...] = sum_ref[:, pl.ds(pl.multiple_of(base, SHARE), SHARE)].astype(out.dtype)
-    half = UNITS // 2
-    for w, k, start, size in (
-        (own_ref, 0, 0, UNITS),
-        (right_ref, 1, 0, UNITS),
-        (top_ref, 2, 0, half),
-        (bottom_ref, 2, half, half),
-        (left_ref, 3, 0, UNITS),
-    ):
-        base = lax.rem(x + k, REPS) * UNITS + start
-        gate_ref[pl.ds(pl.multiple_of(base, half), size), :] = dot(w[...], rows, NT)
+
+
+def gate_products(rows_ref, weights_ref, gate_ref):
+    gate_ref[...] = dot(weights_ref[...], rows_ref[...], NT)
 
 
 def gate_part(
-    pos_ref, grad_probes_ref, gate_ref, got_ref, t0, t1, t2, t3,
+    pos_ref, grad_probes_ref, gate_ref, got_ref, own_ref, out_ref,
     whole_ref, shared_ref, sketch_ref,
 ):
     x = pos_ref[0]
@@ -236,9 +258,8 @@
     gate_grad = (grads * (s * (1.0 + gate * (1.0 - s)))).astype(BF)
     projected = dot(grad_probes_ref[...], gate_grad).astype(BF)
     sketch_ref[...] = dot(gate_grad, projected, NT)
-    for k, out in enumerate((t0, t1, t2, t3)):
-        base = lax.rem(x + k, REPS) * UNITS
-        out[...] = sketch_ref[pl.ds(pl.multiple_of(base, UNITS), UNITS), :].astype(out.dtype)
+    out_ref[...] = sketch_ref[...].astype(BF)
+    own_ref[...] = sketch_ref[pl.ds(pl.multiple_of(x * UNITS, UNITS), UNITS), :]
 
 
 def finish_input(inverse_ref, i0, i1, i2, i3, out_ref):
@@ -246,8 +267,10 @@
     out_ref[...] = (total * inverse_ref[0]).T
 
 
-def finish_grad(inverse_ref, t0, t1, t2, t3, out_ref):
-    total = t0[...] + (t1[...].astype(F32) + t2[...].astype(F32) + t3[...].astype(F32))
+def finish_grad(pos_ref, inverse_ref, own_ref, parts_ref, out_ref):
+    total = own_ref[...]
+    for k in range(1, REPS):
+        total += parts_ref[lax.rem(pos_ref[0] + k, REPS)].astype(F32)
     out_ref[...] = total * inverse_ref[0]
 
 
@@ -275,33 +298,38 @@
     inverse = 1.0 / window_counts.astype(F32)
     ids_t = expert_ids.T
 
-    packed = pl.pallas_call(
-        pack_half,
-        out_shape=sds((TOK + 16, HALF), BF),
-        grid_spec=pltpu.PrefetchScalarGridSpec(
-            num_scalar_prefetch=1,
-            grid=(1,),
-            in_specs=[VM, pl.BlockSpec((TOK, HALF), lambda i, pos: (0, 1 - pos[1]))],
-            out_specs=VM,
-        ),
-        compiler_params=pltpu.CompilerParams(vmem_limit_bytes=6 * MIB),
-        cost_estimate=pl.CostEstimate(flops=1000, bytes_accessed=MIB, transcendentals=0),
+    weights = lax.all_gather(gate_weight[0], "rep", axis=0, tiled=True)
+
+    half = lambda other: pl.BlockSpec(
+        (TOK, HALF), lambda i, pos: (0, 1 - pos[1] if other else pos[1])
+    )
+    packed = gridded_call(
+        pack_half, sds((TOK + 16, HALF), BF), 1, [VM, half(True)], VM, MIB
     )(pos, ids_t, tokens)
     other = swap(packed)
-    out_rows = kernel_call(
-        send_rows,
-        sds((ROWS, SHARE + STRIP), BF),
-        [SM] + [VM] * 3,
-        1 << 31,
-        5 * MIB,
-        20,
+    sent = sds((ROWS, SHARE + STRIP), BF)
+    out_rows = gridded_call(
+        send_whole,
+        sent,
+        4,
+        [VM, VM],
+        pl.BlockSpec((ROWS // 4, SHARE), lambda i, pos: (i, 0)),
+        3 * MIB,
+        [pltpu.VMEM((OWNERS, TOK), F32)],
+    )(pos, ids_t, tokens)
+    out_rows = gridded_call(
+        send_shared,
+        sent,
+        1,
+        [VM, half(False), VM, pl.BlockSpec(memory_space=pl.ANY)],
+        pl.BlockSpec((ROWS, STRIP), lambda i, pos: (0, SHARE // STRIP)),
+        2 * MIB,
         [pltpu.VMEM((TOK, HALF), BF), pltpu.VMEM((TOP, TOK), jnp.int32)],
-    )(pos, ids_t, tokens, other)
+        {4: 0},
+    )(pos, ids_t, tokens, other, out_rows)
     rows = to_owners(out_rows)
 
-    own, grads = gate_weight[0], hidden_grads.reshape(TOK * TOP, UNITS)
-    own, grads, _ = lax.optimization_barrier((own, grads, out_rows))
-    left, right = shift(own, 1), shift(own, REPS - 1)
+    grads, _ = lax.optimization_barrier((hidden_grads.reshape(TOK * TOP, UNITS), out_rows))
     other_grads = swap(grads)
     picked = kernel_call(
         pick_grads, [sds((SLOTS + OWNERS, 256), BF)] * REPS, [SM] + [VM] * 4, 5 << 30, 3 * MIB, 20
@@ -309,40 +337,51 @@
     out_grads = kernel_call(
         fold_grads, sds((ROWS, 256), BF), [SM] + [VM] * 4, 1 << 31, 3 * MIB, 12
     )(pos, *shifted(picked))
-    out_grads, left, right = lax.optimization_barrier((out_grads, left, right))
-    top = shift(left[: UNITS // 2], 1)
-    bottom = shift(right[UNITS // 2 :], REPS - 1)
     got = to_owners(out_grads)
 
     kinds = [F32, BF, BF, BF]
-    gate, *inputs = kernel_call(
-        products,
-        [sds((FFW, ALL), F32)] + [sds((R, SHARE), kind) for kind in kinds],
-        [SM] + [VM] * 7,
-        4 << 30,
-        12 * MIB,
+    rows_all, *inputs = kernel_call(
+        input_products,
+        [sds((ALL, D), BF)] + [sds((R, SHARE), kind) for kind in kinds],
+        [SM] + [VM] * 2,
+        1 << 30,
+        8 * MIB,
         16,
-        [pltpu.VMEM((ALL, D), BF), pltpu.VMEM((R, D), F32)],
-    )(pos, rows, probes, own, right, top, bottom, left)
+        [pltpu.VMEM((R, D), F32)],
+    )(pos, rows, probes)
     inputs = shifted(inputs)
-
-    sketches = kernel_call(
+    steps = 3
+    gate = pl.pallas_call(
+        gate_products,
+        out_shape=sds((FFW, ALL), F32),
+        grid=(steps,),
+        in_specs=[VM, pl.BlockSpec((FFW // steps, D), lambda i: (i, 0))],
+        out_specs=pl.BlockSpec((FFW // steps, ALL), lambda i: (i, 0)),
+        compiler_params=pltpu.CompilerParams(vmem_limit_bytes=24 * MIB),
+        cost_estimate=pl.CostEstimate(
+            flops=5 << 29, bytes_accessed=10 * MIB, transcendentals=0
+        ),
+    )(rows_all, weights)
+
+    own_sketch, sketch = kernel_call(
         gate_part,
-        [sds((UNITS, R), kind) for kind in kinds],
+        [sds((UNITS, R), F32), sds((FFW, R), BF)],
         [SM] + [VM] * 3,
         1 << 30,
         3 * MIB,
         14,
         [pltpu.VMEM((ROWS, 256), BF), pltpu.VMEM((ROWS, 256), BF), pltpu.VMEM((FFW, R), F32)],
     )(pos, grad_probes, gate, got)
-    sketches = shifted(sketches)
+    sketches = lax.all_to_all(
+        sketch.reshape(REPS, UNITS, R), "rep", split_axis=0, concat_axis=0, tiled=True
+    )
 
     input_sketch = kernel_call(
         finish_input, sds((SHARE, R), F32), [SM] + [VM] * 4, 1 << 20, 2 * MIB, 6
     )(inverse, *inputs)
     grad_sketch = kernel_call(
-        finish_grad, sds((UNITS, R), F32), [SM] + [VM] * 4, 1 << 18, MIB // 4, 4
-    )(inverse, *sketches)
+        finish_grad, sds((UNITS, R), F32), [SM] * 2 + [VM] * 2, 1 << 18, MIB // 4, 4
+    )(pos, inverse, own_sketch, sketches)
     return input_sketch[None], grad_sketch[None]
 
 

time: 162 us -> 166 us (1.025)
  starting transfers between devices: 79.5 us -> 54.4 us
  between operations: 1.61 us -> 14.9 us
  Pallas kernels: 26.9 us -> 36 us
  waiting for transfers between devices: 35.9 us -> 43.3 us
    all_to_all x2, waiting for transfers between devices: 0.01 us -> 22.6 us  [to_owners(): lax.all_to_all(rows, 'ep', split_axis=0, concat_axis=0, tiled=True)]
    ppermute x13 -> x6, starting transfers between devices: 44.3 us -> 22.8 us  [shift(): lax.ppermute(block, 'rep', [(i, (i + k) % REPS) for i in range(REPS)])]
    ppermute x13 -> x6, waiting for transfers between devices: 32.1 us -> 14.5 us  [shift(): lax.ppermute(block, 'rep', [(i, (i + k) % REPS) for i in range(REPS)])]
    pallas_call x5 -> x7, Pallas kernels: 16.4 us -> 24.5 us  [the longest x1 5.45 us: local(): gridded_call(send_whole, sent, 4, [VM, VM], pl.BlockSpec((ROWS // 4, SHAR...]
    all_to_all x2, starting transfers between devices: 31.4 us -> 24.3 us  [to_owners(): lax.all_to_all(rows, 'ep', split_axis=0, concat_axis=0, tiled=True)]
    all_to_all x0 -> x1, waiting for transfers between devices: none -> 3.5 us  [local(): lax.all_to_all(sketch.reshape(REPS, UNITS, R), 'rep', split_axis=0, conca...]
    all_to_all x0 -> x1, starting transfers between devices: none -> 3.36 us  [local(): lax.all_to_all(sketch.reshape(REPS, UNITS, R), 'rep', split_axis=0, conca...]
    slice x2 -> x0, local copies, waits for them, and re-layouts: 2.27 us -> none  [the longest x1 1.18 us: local(): top = shift(left[:UNITS // 2], 1)]
  transfers between devices with their start and end apart: 17 -> 12, of which waited for: 7 -> 6; matrix products, arithmetic and copies ran while one was open for 2% -> 2% of each run, Pallas kernels for 13% -> 21%
where the time goes in v5:
time: 166 us; the launch traced here: 165 us
  starting transfers between devices  54.4 us (33%)
  waiting for transfers between devices  43.3 us (26%)
  Pallas kernels  36 us (22%)
  local copies, waits for them, and re-layouts  15.3 us (9%)
  between operations  14.9 us (9%)
    all_to_all x2, starting transfers between devices, to_owners(): lax.all_to_all(rows, 'ep', split_axis=0, concat_axis=0, tiled=True)  24.3 us
    ppermute x6, starting transfers between devices, shift(): lax.ppermute(block, 'rep', [(i, (i + k) % REPS) for i in range(REPS)])  22.8 us
    all_to_all x2, waiting for transfers between devices, to_owners(): lax.all_to_all(rows, 'ep', split_axis=0, concat_axis=0, tiled=True)  22.6 us
    unnamed x29, local copies, waits for them, and re-layouts  15.3 us
    ppermute x6, waiting for transfers between devices, shift(): lax.ppermute(block, 'rep', [(i, (i + k) % REPS) for i in range(REPS)])  14.5 us
    pallas_call x1, Pallas kernels, local(): kernel_call(fold_grads, sds((ROWS, 256), BF), [SM] + [VM] * 4, 1 << 31, 3...  6.63 us
    pallas_call x1, Pallas kernels, local(): gridded_call(send_whole, sent, 4, [VM, VM], pl.BlockSpec((ROWS // 4, SHAR...  5.45 us
    pallas_call x1, Pallas kernels, local(): kernel_call(input_products, [sds((ALL, D), BF)] + [sds((R, SHARE), kind)...  4.57 us
  transfers between devices with their start and end apart: 12, of which 6 were waited for; matrix products, arithmetic and copies ran while one was open for 2% of the time, Pallas kernels for 21%

profile of v5, /device:TPU:8, one launch (start us, length us, event | category | flops | bytes accessed | tf_op | source)
XLA Modules:
  0.0 164.5 jit_solution(6212757054538323734)
XLA Ops:
  7.2 0.0 all-gather.3.cloned.1.call-start
  7.2 0.7 all-gather.3.cloned.1.call-update
  7.9 0.6 pad_add_fusion.pos_ref
  8.5 2.6 %shard_map.86 = bf16[144,2048]{1,0:T(8,128)(2,1)} custom-call(s32[2]{0:T(128)} %pad_add_fusion.pos_ref, s32[8,128]{1,0:T(8,128)} %bitcast.16, bf16[128,4096]{1,0:T(8,128)(2,1)} %tokens_ref.5), custom_call_target="tpu_custom_call" | custom-call | flops 1073741824 | bytes 1048576 | tf_op jit(solution)/shard_map/pallas_call | solution.py:306
  11.1 1.9 %collective-permute-start = (bf16[144,2048]{1,0:T(8,128)(2,1)}, bf16[144,2048]{1,0:T(8,128)(2,1)S(1)}, u32[]{:S(2)}, u32[]{:S(2)}) collective-permute-start(bf16[144,2048]{1,0:T(8,128)(2,1)} %shard_map.86), channel_id=1, source_target_pairs={{0,4},{4,0},{8,12},{12,8},{16,20},{20,16},{24,28},{28,24},{32,36},... | collective-permute-start | bytes 1769480 | tf_op jit(solution)/shard_map/ppermute | solution.py:286
  13.0 5.4 %shard_map.87._ = bf16[1024,1280]{1,0:T(8,128)(2,1)} custom-call(s32[2]{0:T(128)} %pad_add_fusion.pos_ref, s32[8,128]{1,0:T(8,128)} %bitcast.17, bf16[128,4096]{1,0:T(8,128)(2,1)} %tokens_ref.5), custom_call_target="tpu_custom_call" | custom-call | flops 1073741824 | bytes 3145728 | tf_op jit(solution)/shard_map/pallas_call | solution.py:311
  18.4 0.0 collective-permute-done.other_ref
  18.4 0.8 copy-done.5
  19.2 3.8 %shard_map.88 = bf16[1024,1280]{1,0:T(8,128)(2,1)} custom-call(s32[2]{0:T(128)} %pad_add_fusion.pos_ref, s32[8,128]{1,0:T(8,128)} %bitcast.18, bf16[128,4096]{1,0:T(8,128)(2,1)} %tokens_ref.5, bf16[144,2048]{1,0:T(8,128)(2,1)} %copy-done.5, bf16[1024,1280]{1,0:T(8,128)(2,1)} %shard_map.87._), custom_call_target="tpu_custom_call", output_to_operand_aliasing={{}: (4, {})} | custom-call | flops 1073741824 | bytes 2097152 | tf_op jit(solution)/shard_map/pallas_call | solution.py:320
  23.0 17.6 %all-to-all-start = ((bf16[128,8,1280]{2,1,0:T(8,128)(2,1)}), bf16[128,8,1280]{2,1,0:T(8,128)(2,1)S(1)}, u32[]{:S(2)}, u32[]{:S(2)}) async-start(bf16[128,8,1280]{2,1,0:T(8,128)(2,1)} %bitcast.20), calls=%async_computation | async-start | bytes 5242880 | tf_op jit(solution)/shard_map/all_to_all | solution.py:292
  40.6 2.2 %copy.10 = bf16[128,8,192]{2,1,0:T(8,128)(2,1)} copy(bf16[128,8,192]{0,2,1:T(8,128)(2,1)} %param.9) | data formatting | bytes 786432 | tf_op args[2]
  42.8 2.0 %collective-permute-start.4 = (bf16[1024,192]{1,0:T(8,128)(2,1)}, bf16[1024,192]{1,0:T(8,128)(2,1)S(1)}, u32[]{:S(2)}, u32[]{:S(2)}) collective-permute-start(bf16[1024,192]{1,0:T(8,128)(2,1)} %bitcast.14), channel_id=1, source_target_pairs={{0,4},{4,0},{8,12},{12,8},{16,20},{20,16},{24,28},{28,24},{32,36},... | collective-permute-start | bytes 1179656 | tf_op jit(solution)/shard_map/ppermute | solution.py:286
  44.8 1.9 %collective-permute-done.4.other_grads_ref = bf16[1024,192]{1,0:T(8,128)(2,1)S(1)} collective-permute-done((bf16[1024,192]{1,0:T(8,128)(2,1)}, bf16[1024,192]{1,0:T(8,128)(2,1)S(1)}, u32[]{:S(2)}, u32[]{:S(2)}) %collective-permute-start.4) | collective-permute-done | bytes 393248 | tf_op jit(solution)/shard_map/ppermute | solution.py:286
  46.8 0.0 copy-start.7
  46.8 1.0 copy-done.7
  47.9 2.8 %shard_map.92 = (bf16[384,256]{1,0:T(8,128)(2,1)S(1)}, bf16[384,256]{1,0:T(8,128)(2,1)S(1)}, bf16[384,256]{1,0:T(8,128)(2,1)S(1)}, bf16[384,256]{1,0:T(8,128)(2,1)S(1)}) custom-call(s32[2]{0:T(128)S(1)} %copy-done.11, s32[8,128]{1,0:T(8,128)S(1)} %bitcast.19, bf16[144,2048]{1,0:T(8,128)(2,1)S(1)} %copy-done.6, bf16[1024,192]{1,0:T(8,128)(2,1)S(1)} %bitcast.15, ...), custom_call_target="tpu_custom_call" | custom-call | flops 5368709120 | bytes 3145728 | tf_op jit(solution)/shard_map/pallas_call | solution.py:334
  50.7 3.4 %collective-permute-start.5 = (bf16[384,256]{1,0:T(8,128)(2,1)S(1)}, bf16[384,256]{1,0:T(8,128)(2,1)S(1)}, u32[]{:S(2)}, u32[]{:S(2)}) collective-permute-start(bf16[384,256]{1,0:T(8,128)(2,1)S(1)} %get-tuple-element.21), channel_id=1, source_target_pairs={{0,1},{1,2},{2,3},{3,0},{4,5},{5,6},{6,7},{7,4},{8,9},{9,10},{10,1... | collective-permute-start | bytes 589832 | tf_op jit(solution)/shard_map/ppermute | solution.py:278
  54.1 4.6 %collective-permute-start.6 = (bf16[384,256]{1,0:T(8,128)(2,1)S(1)}, bf16[384,256]{1,0:T(8,128)(2,1)S(1)}, u32[]{:S(2)}, u32[]{:S(2)}) collective-permute-start(bf16[384,256]{1,0:T(8,128)(2,1)S(1)} %get-tuple-element.22), channel_id=1, source_target_pairs={{0,2},{1,3},{2,0},{3,1},{4,6},{5,7},{6,4},{7,5},{8,10},{9,11},{10,... | collective-permute-start | bytes 589832 | tf_op jit(solution)/shard_map/ppermute | solution.py:278
  58.8 3.3 %collective-permute-start.7 = (bf16[384,256]{1,0:T(8,128)(2,1)S(1)}, bf16[384,256]{1,0:T(8,128)(2,1)S(1)}, u32[]{:S(2)}, u32[]{:S(2)}) collective-permute-start(bf16[384,256]{1,0:T(8,128)(2,1)S(1)} %get-tuple-element.23), channel_id=1, source_target_pairs={{0,3},{1,0},{2,1},{3,2},{4,7},{5,4},{6,5},{7,6},{8,11},{9,8},{10,9... | collective-permute-start | bytes 589832 | tf_op jit(solution)/shard_map/ppermute | solution.py:278
  62.1 3.4 %collective-permute-done.5.g1 = bf16[384,256]{1,0:T(8,128)(2,1)S(1)} collective-permute-done((bf16[384,256]{1,0:T(8,128)(2,1)S(1)}, bf16[384,256]{1,0:T(8,128)(2,1)S(1)}, u32[]{:S(2)}, u32[]{:S(2)}) %collective-permute-start.5) | collective-permute-done | bytes 196640 | tf_op jit(solution)/shard_map/ppermute | solution.py:278
  65.5 9.4 %collective-permute-done.6.g2 = bf16[384,256]{1,0:T(8,128)(2,1)S(1)} collective-permute-done((bf16[384,256]{1,0:T(8,128)(2,1)S(1)}, bf16[384,256]{1,0:T(8,128)(2,1)S(1)}, u32[]{:S(2)}, u32[]{:S(2)}) %collective-permute-start.6) | collective-permute-done | bytes 196640 | tf_op jit(solution)/shard_map/ppermute | solution.py:278
  74.9 1.7 %collective-permute-done.7.g3 = bf16[384,256]{1,0:T(8,128)(2,1)S(1)} collective-permute-done((bf16[384,256]{1,0:T(8,128)(2,1)S(1)}, bf16[384,256]{1,0:T(8,128)(2,1)S(1)}, u32[]{:S(2)}, u32[]{:S(2)}) %collective-permute-start.7) | collective-permute-done | bytes 196640 | tf_op jit(solution)/shard_map/ppermute | solution.py:278
  76.6 6.6 %shard_map.93 = bf16[1024,256]{1,0:T(8,128)(2,1)} custom-call(s32[2]{0:T(128)S(1)} %copy-done.11, bf16[384,256]{1,0:T(8,128)(2,1)S(1)} %get-tuple-element.20.g0, bf16[384,256]{1,0:T(8,128)(2,1)S(1)} %collective-permute-done.5.g1, bf16[384,256]{1,0:T(8,128)(2,1)S(1)} %collective-permute-done.6.g2, bf16[384,256]{1,0:T(8,128)(2,1)S(1)} %collective-permute-done.7.g3), custom_call_target="tpu_custom_call" | custom-call | flops 2147483648 | bytes 3145728 | tf_op jit(solution)/shard_map/pallas_call | solution.py:337
  83.2 22.6 %all-to-all-done = bf16[128,8,1280]{2,1,0:T(8,128)(2,1)S(1)} async-done(((bf16[128,8,1280]{2,1,0:T(8,128)(2,1)}), bf16[128,8,1280]{2,1,0:T(8,128)(2,1)S(1)}, u32[]{:S(2)}, u32[]{:S(2)}) %all-to-all-start) | async-done | bytes 2621472 | tf_op jit(solution)/shard_map/all_to_all | solution.py:292
  105.9 1.5 copy-done.1
  107.4 6.7 %all-to-all-start.1 = ((bf16[128,8,256]{2,1,0:T(8,128)(2,1)}), bf16[128,8,256]{2,1,0:T(8,128)(2,1)}, u32[]{:S(2)}, u32[]{:S(2)}) async-start(bf16[128,8,256]{2,1,0:T(8,128)(2,1)} %bitcast.8), calls=%async_computation.1 | async-start | bytes 1048576 | tf_op jit(solution)/shard_map/all_to_all | solution.py:292
  114.1 1.7 %copy-done.2 = bf16[128,8,1280]{2,1,0:T(8,128)(2,1)S(1)} copy-done((bf16[128,8,1280]{2,1,0:T(8,128)(2,1)S(1)}, bf16[128,8,1280]{2,1,0:T(8,128)(2,1)}, u32[]{:S(2)}) %copy-start.2) | copy-done | bytes 2621464
  115.9 1.2 copy-done.12
  117.1 4.6 %shard_map.89 = (bf16[384,4096]{1,0:T(8,128)(2,1)S(1)}, f32[128,1024]{1,0:T(8,128)S(1)}, bf16[128,1024]{1,0:T(8,128)(2,1)}, bf16[128,1024]{1,0:T(8,128)(2,1)}, bf16[128,1024]{1,0:T(8,128)(2,1)}) custom-call(s32[2]{0:T(128)S(1)} %copy-done.11, bf16[1024,1280]{1,0:T(8,128)(2,1)S(1)} %bitcast.13, bf16[128,4096]{1,0:T(8,128)(2,1)S(1)} %copy-done.12), custom_call_target="tpu_custom_call" | custom-call | flops 1073741824 | bytes 8388608 | tf_op jit(solution)/shard_map/pallas_call | solution.py:343
  121.7 0.8 copy-done.8
  122.5 3.4 %collective-permute-start.1 = (bf16[128,1024]{1,0:T(8,128)(2,1)}, bf16[128,1024]{1,0:T(8,128)(2,1)S(1)}, u32[]{:S(2)}, u32[]{:S(2)}) collective-permute-start(bf16[128,1024]{1,0:T(8,128)(2,1)} %get-tuple-element.15), channel_id=1, source_target_pairs={{0,1},{1,2},{2,3},{3,0},{4,5},{5,6},{6,7},{7,4},{8,9},{9,10},{10,1... | collective-permute-start | bytes 786440 | tf_op jit(solution)/shard_map/ppermute | solution.py:278
  125.9 4.6 %collective-permute-start.2 = (bf16[128,1024]{1,0:T(8,128)(2,1)}, bf16[128,1024]{1,0:T(8,128)(2,1)}, u32[]{:S(2)}, u32[]{:S(2)}) collective-permute-start(bf16[128,1024]{1,0:T(8,128)(2,1)} %get-tuple-element.16), channel_id=1, source_target_pairs={{0,2},{1,3},{2,0},{3,1},{4,6},{5,7},{6,4},{7,5},{8,10},{9,11},{10,... | collective-permute-start | bytes 786440 | tf_op jit(solution)/shard_map/ppermute | solution.py:278
  130.5 3.3 %collective-permute-start.3 = (bf16[128,1024]{1,0:T(8,128)(2,1)}, bf16[128,1024]{1,0:T(8,128)(2,1)}, u32[]{:S(2)}, u32[]{:S(2)}) collective-permute-start(bf16[128,1024]{1,0:T(8,128)(2,1)} %get-tuple-element.17), channel_id=1, source_target_pairs={{0,3},{1,0},{2,1},{3,2},{4,7},{5,4},{6,5},{7,6},{8,11},{9,8},{10,9... | collective-permute-start | bytes 786440 | tf_op jit(solution)/shard_map/ppermute | solution.py:278
  133.9 0.0 all-gather.3.cloned.1.call-done
  133.9 2.8 %copy-done = bf16[1,768,4096]{2,1,0:T(8,128)(2,1)S(1)} copy-done((bf16[1,768,4096]{2,1,0:T(8,128)(2,1)S(1)}, bf16[1,768,4096]{2,1,0:T(8,128)(2,1)}, u32[]{:S(2)}) %copy-start) | copy-done | bytes 6291480
  136.7 3.8 %shard_map.91.gate_ref = f32[768,384]{1,0:T(8,128)S(1)} custom-call(bf16[384,4096]{1,0:T(8,128)(2,1)S(1)} %get-tuple-element.18.rows_ref, bf16[768,4096]{1,0:T(8,128)(2,1)S(1)} %bitcast.12), custom_call_target="tpu_custom_call" | custom-call | flops 2684354560 | bytes 10485760 | tf_op jit(solution)/shard_map/pallas_call | solution.py:354
  140.5 1.0 copy-done.3
  141.5 0.0 all-to-all-done.1
  141.5 1.3 copy-done.4
  142.8 0.9 copy-done.13
  143.7 3.1 %shard_map.94 = (f32[192,128]{1,0:T(8,128)S(1)}, bf16[768,128]{1,0:T(8,128)(2,1)}) custom-call(s32[2]{0:T(128)S(1)} %copy-done.11, bf16[128,768]{1,0:T(8,128)(2,1)S(1)} %copy-done.13, f32[768,384]{1,0:T(8,128)S(1)} %copy-done.4, bf16[1024,256]{1,0:T(8,128)(2,1)} %bitcast.9.got_ref), custom_call_target="tpu_custom_call" | custom-call | flops 1073741824 | bytes 3145728 | tf_op jit(solution)/shard_map/pallas_call | solution.py:366
  146.8 3.4 %all-to-all-start.2 = ((bf16[4,192,128]{2,1,0:T(8,128)(2,1)}), bf16[4,192,128]{2,1,0:T(8,128)(2,1)S(1)}, u32[]{:S(2)}, u32[]{:S(2)}) async-start(bf16[4,192,128]{2,1,0:T(8,128)(2,1)} %bitcast.10), calls=%async_computation.2 | async-start | bytes 393216 | tf_op jit(solution)/shard_map/all_to_all | solution.py:375
  150.9 0.0 collective-permute-done.1.i1
  150.9 0.0 collective-permute-done.2.i2
  150.9 0.0 collective-permute-done.3.i3
  150.9 2.1 %shard_map.90 = f32[1024,128]{1,0:T(8,128)} custom-call(f32[1]{0:T(128)S(6)} %div.3.inverse_ref, f32[128,1024]{1,0:T(8,128)S(1)} %copy-done.9, bf16[128,1024]{1,0:T(8,128)(2,1)S(1)} %collective-permute-done.1.i1, bf16[128,1024]{1,0:T(8,128)(2,1)} %collective-permute-done.2.i2, bf16[128,1024]{1,0:T(8,128)(2,1)} %collective-permute-done.3.i3), custom_call_target="tpu_custom_call" | custom-call | flops 1048576 | bytes 2097152 | tf_op jit(solution)/shard_map/pallas_call | solution.py:379
  153.0 3.5 %all-to-all-done.2.parts_ref = bf16[4,192,128]{2,1,0:T(8,128)(2,1)S(1)} async-done(((bf16[4,192,128]{2,1,0:T(8,128)(2,1)}), bf16[4,192,128]{2,1,0:T(8,128)(2,1)S(1)}, u32[]{:S(2)}, u32[]{:S(2)}) %all-to-all-start.2) | async-done | bytes 196640 | tf_op jit(solution)/shard_map/all_to_all | solution.py:375
  156.5 1.2 shard_map.95
  (17 shorter events, 0.0 us)
Async XLA Ops:
  7.2 126.7 %all-gather.3.cloned.1.call-start = ((), (), s32[]{:S(2)}) async-start(), calls=%async_computation.3 | async-start | bytes 7864320 | tf_op jit(solution)/shard_map/all_gather | solution.py:301
  11.1 7.4 %collective-permute-start = (bf16[144,2048]{1,0:T(8,128)(2,1)}, bf16[144,2048]{1,0:T(8,128)(2,1)S(1)}, u32[]{:S(2)}, u32[]{:S(2)}) collective-permute-start(bf16[144,2048]{1,0:T(8,128)(2,1)} %shard_map.86), channel_id=1, source_target_pairs={{0,4},{4,0},{8,12},{12,8},{16,20},{20,16},{24,28},{28,24},{32,36},... | collective-permute-start | bytes 1769480 | tf_op jit(solution)/shard_map/ppermute | solution.py:286
  18.4 0.8 copy-start.5
  23.0 23.8 %copy-start.6 = (bf16[144,2048]{1,0:T(8,128)(2,1)S(1)}, bf16[144,2048]{1,0:T(8,128)(2,1)}, u32[]{:S(2)}) copy-start(bf16[144,2048]{1,0:T(8,128)(2,1)} %copy-done.5) | copy-start | bytes 1769476
  23.0 23.8 %copy-start.10 = (s32[128,8]{0,1:T(8,128)S(1)}, s32[128,8]{0,1:T(8,128)}, u32[]{:S(2)}) copy-start(s32[128,8]{0,1:T(8,128)} %param.8) | copy-start | bytes 12292
  23.0 23.8 %copy-start.11 = (s32[2]{0:T(128)S(1)}, s32[2]{0:T(128)}, u32[]{:S(2)}) copy-start(s32[2]{0:T(128)} %pad_add_fusion.pos_ref) | copy-start | bytes 28
  23.0 82.9 %all-to-all-start = ((bf16[128,8,1280]{2,1,0:T(8,128)(2,1)}), bf16[128,8,1280]{2,1,0:T(8,128)(2,1)S(1)}, u32[]{:S(2)}, u32[]{:S(2)}) async-start(bf16[128,8,1280]{2,1,0:T(8,128)(2,1)} %bitcast.20), calls=%async_computation | async-start | bytes 5242880 | tf_op jit(solution)/shard_map/all_to_all | solution.py:292
  42.8 4.0 %collective-permute-start.4 = (bf16[1024,192]{1,0:T(8,128)(2,1)}, bf16[1024,192]{1,0:T(8,128)(2,1)S(1)}, u32[]{:S(2)}, u32[]{:S(2)}) collective-permute-start(bf16[1024,192]{1,0:T(8,128)(2,1)} %bitcast.14), channel_id=1, source_target_pairs={{0,4},{4,0},{8,12},{12,8},{16,20},{20,16},{24,28},{28,24},{32,36},... | collective-permute-start | bytes 1179656 | tf_op jit(solution)/shard_map/ppermute | solution.py:286
  46.8 1.0 copy-start.7
  50.7 14.8 %collective-permute-start.5 = (bf16[384,256]{1,0:T(8,128)(2,1)S(1)}, bf16[384,256]{1,0:T(8,128)(2,1)S(1)}, u32[]{:S(2)}, u32[]{:S(2)}) collective-permute-start(bf16[384,256]{1,0:T(8,128)(2,1)S(1)} %get-tuple-element.21), channel_id=1, source_target_pairs={{0,1},{1,2},{2,3},{3,0},{4,5},{5,6},{6,7},{7,4},{8,9},{9,10},{10,1... | collective-permute-start | bytes 589832 | tf_op jit(solution)/shard_map/ppermute | solution.py:278
  54.1 20.8 %collective-permute-start.6 = (bf16[384,256]{1,0:T(8,128)(2,1)S(1)}, bf16[384,256]{1,0:T(8,128)(2,1)S(1)}, u32[]{:S(2)}, u32[]{:S(2)}) collective-permute-start(bf16[384,256]{1,0:T(8,128)(2,1)S(1)} %get-tuple-element.22), channel_id=1, source_target_pairs={{0,2},{1,3},{2,0},{3,1},{4,6},{5,7},{6,4},{7,5},{8,10},{9,11},{10,... | collective-permute-start | bytes 589832 | tf_op jit(solution)/shard_map/ppermute | solution.py:278
  58.8 17.8 %collective-permute-start.7 = (bf16[384,256]{1,0:T(8,128)(2,1)S(1)}, bf16[384,256]{1,0:T(8,128)(2,1)S(1)}, u32[]{:S(2)}, u32[]{:S(2)}) collective-permute-start(bf16[384,256]{1,0:T(8,128)(2,1)S(1)} %get-tuple-element.23), channel_id=1, source_target_pairs={{0,3},{1,0},{2,1},{3,2},{4,7},{5,4},{6,5},{7,6},{8,11},{9,8},{10,9... | collective-permute-start | bytes 589832 | tf_op jit(solution)/shard_map/ppermute | solution.py:278
  105.9 1.5 copy-start.1
  107.4 34.1 %all-to-all-start.1 = ((bf16[128,8,256]{2,1,0:T(8,128)(2,1)}), bf16[128,8,256]{2,1,0:T(8,128)(2,1)}, u32[]{:S(2)}, u32[]{:S(2)}) async-start(bf16[128,8,256]{2,1,0:T(8,128)(2,1)} %bitcast.8), calls=%async_computation.1 | async-start | bytes 1048576 | tf_op jit(solution)/shard_map/all_to_all | solution.py:292
  114.1 1.7 %copy-start.2 = (bf16[128,8,1280]{2,1,0:T(8,128)(2,1)S(1)}, bf16[128,8,1280]{2,1,0:T(8,128)(2,1)}, u32[]{:S(2)}) copy-start(bf16[128,8,1280]{2,1,0:T(8,128)(2,1)} %copy-done.1) | copy-start | bytes 7864324
  115.9 1.2 copy-start.12
  121.7 0.8 copy-start.8
  122.5 28.4 %collective-permute-start.1 = (bf16[128,1024]{1,0:T(8,128)(2,1)}, bf16[128,1024]{1,0:T(8,128)(2,1)S(1)}, u32[]{:S(2)}, u32[]{:S(2)}) collective-permute-start(bf16[128,1024]{1,0:T(8,128)(2,1)} %get-tuple-element.15), channel_id=1, source_target_pairs={{0,1},{1,2},{2,3},{3,0},{4,5},{5,6},{6,7},{7,4},{8,9},{9,10},{10,1... | collective-permute-start | bytes 786440 | tf_op jit(solution)/shard_map/ppermute | solution.py:278
  125.9 25.0 %collective-permute-start.2 = (bf16[128,1024]{1,0:T(8,128)(2,1)}, bf16[128,1024]{1,0:T(8,128)(2,1)}, u32[]{:S(2)}, u32[]{:S(2)}) collective-permute-start(bf16[128,1024]{1,0:T(8,128)(2,1)} %get-tuple-element.16), channel_id=1, source_target_pairs={{0,2},{1,3},{2,0},{3,1},{4,6},{5,7},{6,4},{7,5},{8,10},{9,11},{10,... | collective-permute-start | bytes 786440 | tf_op jit(solution)/shard_map/ppermute | solution.py:278
  130.5 20.4 %collective-permute-start.3 = (bf16[128,1024]{1,0:T(8,128)(2,1)}, bf16[128,1024]{1,0:T(8,128)(2,1)}, u32[]{:S(2)}, u32[]{:S(2)}) collective-permute-start(bf16[128,1024]{1,0:T(8,128)(2,1)} %get-tuple-element.17), channel_id=1, source_target_pairs={{0,3},{1,0},{2,1},{3,2},{4,7},{5,4},{6,5},{7,6},{8,11},{9,8},{10,9... | collective-permute-start | bytes 786440 | tf_op jit(solution)/shard_map/ppermute | solution.py:278
  133.9 2.8 %copy-start = (bf16[1,768,4096]{2,1,0:T(8,128)(2,1)S(1)}, bf16[1,768,4096]{2,1,0:T(8,128)(2,1)}, u32[]{:S(2)}) copy-start(bf16[1,768,4096]{2,1,0:T(8,128)(2,1)} %all-gather.3.cloned.1.call-done) | copy-start | bytes 18874372
  140.5 1.0 copy-start.3
  141.5 1.3 copy-start.4
  142.8 0.9 copy-start.13
  143.7 7.2 %copy-start.9 = (f32[128,1024]{1,0:T(8,128)S(1)}, f32[128,1024]{1,0:T(8,128)}, u32[]{:S(2)}) copy-start(f32[128,1024]{1,0:T(8,128)} %copy-done.8) | copy-start | bytes 1572868
  146.8 9.7 %all-to-all-start.2 = ((bf16[4,192,128]{2,1,0:T(8,128)(2,1)}), bf16[4,192,128]{2,1,0:T(8,128)(2,1)S(1)}, u32[]{:S(2)}, u32[]{:S(2)}) async-start(bf16[4,192,128]{2,1,0:T(8,128)(2,1)} %bitcast.10), calls=%async_computation.2 | async-start | bytes 393216 | tf_op jit(solution)/shard_map/all_to_all | solution.py:375
Sparse Core Ops, SparseCore 0:
  10.1 83.9 all-gather.2

commit v6 on v5

--- a/solution.py
+++ b/solution.py
@@ -116,22 +116,19 @@
     return other_ref[TOK:, :TOK].astype(F32)[:TOP].astype(jnp.int32)
 
 
-def send_whole(pos_ref, ids_ref, tokens_ref, out_ref, table_ref):
-    step, x = pl.program_id(0), pos_ref[0]
-
-    @pl.when(step == 0)
-    def _():
-        table_ref[...] = places(ids_ref[...])
-
-    table = spread(table_ref[pl.ds(pl.multiple_of(step * 32, 32), 32), :], FOLD)
-    row = iota(table.shape, 0)
+def send_whole(pos_ref, ids_ref, tokens_ref, out_ref):
+    x = pos_ref[0]
+    table = spread(places(ids_ref[...]), FOLD)
+    row = iota((ROWS, TOK), 0)
     whole = table == (2 * x + row % 8 // 4).astype(F32)
     picks = jnp.concatenate([ones_where(whole & (row % 4 == b)) for b in range(4)], 1)
     parts = jnp.concatenate([tokens_ref[:, b * SHARE : (b + 1) * SHARE] for b in range(4)], 0)
     out_ref[...] = dot(picks, parts).astype(BF)
 
 
-def send_shared(pos_ref, ids_ref, tokens_ref, other_ref, _, out_ref, half_ref, half_ids_ref):
+def send_shared(
+    pos_ref, ids_ref, tokens_ref, other_ref, _, out_ref, half_ref, half_ids_ref, fold_ref
+):
     x, c = pos_ref[0], pos_ref[1]
     mine = x // 2 == c
 
@@ -145,12 +142,14 @@
         half_ref[...] = other_ref[:TOK, :]
         half_ids_ref[...] = other_ids(other_ref)
 
-    table = spread(places(half_ids_ref[...]), FOLD)
-    row = iota(table.shape, 0)
-    shared = table == (FIRST + x % 2).astype(F32)
-    picks = jnp.concatenate([ones_where(shared & (row % 8 == b)) for b in range(8)], 1)
-    parts = jnp.concatenate([half_ref[:, b * STRIP : (b + 1) * STRIP] for b in range(8)], 0)
-    out_ref[...] = dot(picks, parts).astype(BF)
+    picks = ones_where(places(half_ids_ref[...]) == (FIRST + x % 2).astype(F32))
+    rows = dot(picks, half_ref[...])
+    for b in range(FOLD):
+        for h in range(STRIP // 128):
+            start = b * STRIP + h * 128
+            fold_ref[h, pl.ds(b, OWNERS, stride=FOLD), :] = rows[:, start : start + 128]
+    for h in range(STRIP // 128):
+        out_ref[:, h * 128 : (h + 1) * 128] = fold_ref[h].astype(BF)
 
 
 def pick_grads(pos_ref, ids_ref, other_ref, grads_ref, other_grads_ref, *outs):
@@ -202,9 +201,7 @@
             put(p, slice(g * size, (g + 1) * size), got[p * size : (p + 1) * size])
 
 
-def input_products(pos_ref, rows_ref, probes_ref, all_ref, i0, i1, i2, i3, sum_ref):
-    x = pos_ref[0]
-
+def gather_rows(rows_ref, all_ref):
     def put_whole(p, at, got):
         all_ref[at, p * SHARE : (p + 1) * SHARE] = got
 
@@ -214,7 +211,12 @@
     regroup(lambda at: rows_ref[at, :SHARE], 4, put_whole)
     regroup(lambda at: rows_ref[at, SHARE:], 16, put_shared)
     all_ref[SLOTS + PAIRS :, :] = jnp.zeros((ALL - SLOTS - PAIRS, D), BF)
-    rows = all_ref[...]
+    return all_ref[...]
+
+
+def input_products(pos_ref, rows_ref, probes_ref, i0, i1, i2, i3, all_ref, sum_ref):
+    x = pos_ref[0]
+    rows = gather_rows(rows_ref, all_ref)
     projected = dot(probes_ref[...], rows, NT).astype(BF)
     sum_ref[...] = dot(projected, rows)
     for k, out in enumerate((i0, i1, i2, i3)):
@@ -222,8 +224,27 @@
         out[...] = sum_ref[:, pl.ds(pl.multiple_of(base, SHARE), SHARE)].astype(out.dtype)
 
 
-def gate_products(rows_ref, weights_ref, gate_ref):
-    gate_ref[...] = dot(weights_ref[...], rows_ref[...], NT)
+def gate_products(pos_ref, rows_ref, w0, w1, w2, w3, w4, gate_ref, held_ref, all_ref, sems):
+    x = pos_ref[0]
+    half = UNITS // 2
+    blocks = []
+    for n, (w, k, start, size) in enumerate(
+        (
+            (w0, 0, 0, UNITS),
+            (w1, 1, 0, UNITS),
+            (w2, 2, 0, half),
+            (w3, 2, half, half),
+            (w4, 3, 0, UNITS),
+        )
+    ):
+        at = slice(k * UNITS + start, k * UNITS + start + size)
+        copy = pltpu.make_async_copy(w, held_ref.at[at, :], sems.at[n])
+        copy.start()
+        blocks.append((copy, at, lax.rem(x + k, REPS) * UNITS + start, size))
+    rows = gather_rows(rows_ref, all_ref)
+    for copy, at, base, size in blocks:
+        copy.wait()
+        gate_ref[pl.ds(pl.multiple_of(base, half), size), :] = dot(held_ref[at, :], rows, NT)
 
 
 def gate_part(
@@ -298,8 +319,6 @@
     inverse = 1.0 / window_counts.astype(F32)
     ids_t = expert_ids.T
 
-    weights = lax.all_gather(gate_weight[0], "rep", axis=0, tiled=True)
-
     half = lambda other: pl.BlockSpec(
         (TOK, HALF), lambda i, pos: (0, 1 - pos[1] if other else pos[1])
     )
@@ -311,11 +330,10 @@
     out_rows = gridded_call(
         send_whole,
         sent,
-        4,
+        1,
         [VM, VM],
-        pl.BlockSpec((ROWS // 4, SHARE), lambda i, pos: (i, 0)),
+        pl.BlockSpec((ROWS, SHARE), lambda i, pos: (0, 0)),
         3 * MIB,
-        [pltpu.VMEM((OWNERS, TOK), F32)],
     )(pos, ids_t, tokens)
     out_rows = gridded_call(
         send_shared,
@@ -324,44 +342,57 @@
         [VM, half(False), VM, pl.BlockSpec(memory_space=pl.ANY)],
         pl.BlockSpec((ROWS, STRIP), lambda i, pos: (0, SHARE // STRIP)),
         2 * MIB,
-        [pltpu.VMEM((TOK, HALF), BF), pltpu.VMEM((TOP, TOK), jnp.int32)],
+        [
+            pltpu.VMEM((TOK, HALF), BF),
+            pltpu.VMEM((TOP, TOK), jnp.int32),
+            pltpu.VMEM((STRIP // 128, ROWS, 128), F32),
+        ],
         {4: 0},
     )(pos, ids_t, tokens, other, out_rows)
     rows = to_owners(out_rows)
 
-    grads, _ = lax.optimization_barrier((hidden_grads.reshape(TOK * TOP, UNITS), out_rows))
+    own, grads, _ = lax.optimization_barrier(
+        (gate_weight[0], hidden_grads.reshape(TOK * TOP, UNITS), out_rows)
+    )
+    left, right = shift(own, 1), shift(own, REPS - 1)
     other_grads = swap(grads)
     picked = kernel_call(
         pick_grads, [sds((SLOTS + OWNERS, 256), BF)] * REPS, [SM] + [VM] * 4, 5 << 30, 3 * MIB, 20
     )(pos, ids_t, other, grads, other_grads)
+    top = shift(left[: UNITS // 2], 1)
+    bottom = shift(right[UNITS // 2 :], REPS - 1)
     out_grads = kernel_call(
         fold_grads, sds((ROWS, 256), BF), [SM] + [VM] * 4, 1 << 31, 3 * MIB, 12
     )(pos, *shifted(picked))
+    out_grads, left, right, top, bottom = lax.optimization_barrier(
+        (out_grads, left, right, top, bottom)
+    )
     got = to_owners(out_grads)
 
     kinds = [F32, BF, BF, BF]
-    rows_all, *inputs = kernel_call(
+    inputs = kernel_call(
         input_products,
-        [sds((ALL, D), BF)] + [sds((R, SHARE), kind) for kind in kinds],
+        [sds((R, SHARE), kind) for kind in kinds],
         [SM] + [VM] * 2,
         1 << 30,
         8 * MIB,
-        16,
-        [pltpu.VMEM((R, D), F32)],
+        56,
+        [pltpu.VMEM((ALL, D), BF), pltpu.VMEM((R, D), F32)],
     )(pos, rows, probes)
     inputs = shifted(inputs)
-    steps = 3
-    gate = pl.pallas_call(
+    gate = kernel_call(
         gate_products,
-        out_shape=sds((FFW, ALL), F32),
-        grid=(steps,),
-        in_specs=[VM, pl.BlockSpec((FFW // steps, D), lambda i: (i, 0))],
-        out_specs=pl.BlockSpec((FFW // steps, ALL), lambda i: (i, 0)),
-        compiler_params=pltpu.CompilerParams(vmem_limit_bytes=24 * MIB),
-        cost_estimate=pl.CostEstimate(
-            flops=5 << 29, bytes_accessed=10 * MIB, transcendentals=0
-        ),
-    )(rows_all, weights)
+        sds((FFW, ALL), F32),
+        [SM, VM] + [pl.BlockSpec(memory_space=pl.ANY)] * 5,
+        5 << 29,
+        10 * MIB,
+        56,
+        [
+            pltpu.VMEM((FFW, D), BF),
+            pltpu.VMEM((ALL, D), BF),
+            pltpu.SemaphoreType.DMA((5,)),
+        ],
+    )(pos, rows, own, right, top, bottom, left)
 
     own_sketch, sketch = kernel_call(
         gate_part,
@@ -369,7 +400,7 @@
         [SM] + [VM] * 3,
         1 << 30,
         3 * MIB,
-        14,
+        56,
         [pltpu.VMEM((ROWS, 256), BF), pltpu.VMEM((ROWS, 256), BF), pltpu.VMEM((FFW, R), F32)],
     )(pos, grad_probes, gate, got)
     sketches = lax.all_to_all(

time: 166 us -> 173 us (1.042)
  starting transfers between devices: 54.4 us -> 73.4 us
  between operations: 14.9 us -> 1.64 us
  local copies, waits for them, and re-layouts: 15.3 us -> 3.09 us
  waiting for transfers between devices: 43.3 us -> 50.6 us
  Pallas kernels: 36 us -> 42.9 us
    ppermute x6 -> x10, waiting for transfers between devices: 14.5 us -> 44.9 us  [shift(): lax.ppermute(block, 'rep', [(i, (i + k) % REPS) for i in range(REPS)])]
    all_to_all x2, waiting for transfers between devices: 22.6 us -> 0.01 us  [to_owners(): lax.all_to_all(rows, 'ep', split_axis=0, concat_axis=0, tiled=True)]
    unnamed x29, local copies, waits for them, and re-layouts: 15.3 us -> 2.99 us
    ppermute x6 -> x10, starting transfers between devices: 22.8 us -> 33.6 us  [shift(): lax.ppermute(block, 'rep', [(i, (i + k) % REPS) for i in range(REPS)])]
    pallas_call x3, Pallas kernels: 13.8 us -> 21.8 us  [the longest x1 10.7 us: local(): kernel_call(gate_products, sds((FFW, ALL), F32), [SM, VM] + [pl.BlockSpec...]
    all_to_all x2, starting transfers between devices: 24.3 us -> 31.7 us  [to_owners(): lax.all_to_all(rows, 'ep', split_axis=0, concat_axis=0, tiled=True)]
    all_to_all x1, waiting for transfers between devices: 3.5 us -> 5.64 us  [local(): lax.all_to_all(sketch.reshape(REPS, UNITS, R), 'rep', split_axis=0, conca...]
    ppermute x2, waiting for transfers between devices: 1.95 us -> 0.01 us  [swap(): return lax.ppermute(block, 'ep', [(i, i ^ 1) for i in range(OWNERS)])]
  transfers between devices with their start and end apart: 12 -> 15, of which waited for: 6 -> 3; matrix products, arithmetic and copies ran while one was open for 2% -> 0% of each run, Pallas kernels for 21% -> 21%
where the time goes in v6:
time: 173 us; the launch traced here: 172 us
  starting transfers between devices  73.4 us (42%)
  waiting for transfers between devices  50.6 us (29%)
  Pallas kernels  42.9 us (25%)
  local copies, waits for them, and re-layouts  3.09 us (2%)
    ppermute x10, waiting for transfers between devices, shift(): lax.ppermute(block, 'rep', [(i, (i + k) % REPS) for i in range(REPS)])  44.9 us
    ppermute x10, starting transfers between devices, shift(): lax.ppermute(block, 'rep', [(i, (i + k) % REPS) for i in range(REPS)])  33.6 us
    all_to_all x2, starting transfers between devices, to_owners(): lax.all_to_all(rows, 'ep', split_axis=0, concat_axis=0, tiled=True)  31.7 us
    pallas_call x1, Pallas kernels, local(): kernel_call(gate_products, sds((FFW, ALL), F32), [SM, VM] + [pl.BlockSpec...  10.7 us
    pallas_call x1, Pallas kernels, local(): kernel_call(fold_grads, sds((ROWS, 256), BF), [SM] + [VM] * 4, 1 << 31, 3...  6.67 us
    pallas_call x1, Pallas kernels, local(): kernel_call(input_products, [sds((R, SHARE), kind) for kind in kinds], [S...  6.18 us
    all_to_all x1, waiting for transfers between devices, local(): lax.all_to_all(sketch.reshape(REPS, UNITS, R), 'rep', split_axis=0, conca...  5.64 us
    pallas_call x1, Pallas kernels, local(): gridded_call(send_whole, sent, 1, [VM, VM], pl.BlockSpec((ROWS, SHARE), l...  4.91 us
  transfers between devices with their start and end apart: 15, of which 3 were waited for; matrix products, arithmetic and copies ran while one was open for 0% of the time, Pallas kernels for 21%

profile of v6, /device:TPU:8, one launch (start us, length us, event | category | flops | bytes accessed | tf_op | source)
XLA Modules:
  0.0 172.3 jit_solution(14957694249778554873)
XLA Ops:
  0.6 0.6 pad_add_fusion.pos_ref
  1.3 2.6 %shard_map.86 = bf16[144,2048]{1,0:T(8,128)(2,1)} custom-call(s32[2]{0:T(128)} %pad_add_fusion.pos_ref, s32[8,128]{1,0:T(8,128)} %bitcast.14, bf16[128,4096]{1,0:T(8,128)(2,1)} %tokens_ref.5), custom_call_target="tpu_custom_call" | custom-call | flops 1073741824 | bytes 1048576 | tf_op jit(solution)/shard_map/pallas_call | solution.py:325
  3.8 1.9 %collective-permute-start = (bf16[144,2048]{1,0:T(8,128)(2,1)}, bf16[144,2048]{1,0:T(8,128)(2,1)S(1)}, u32[]{:S(2)}, u32[]{:S(2)}) collective-permute-start(bf16[144,2048]{1,0:T(8,128)(2,1)} %shard_map.86), channel_id=1, source_target_pairs={{0,4},{4,0},{8,12},{12,8},{16,20},{20,16},{24,28},{28,24},{32,36},... | collective-permute-start | bytes 1769480 | tf_op jit(solution)/shard_map/ppermute | solution.py:307
  5.7 4.9 %shard_map.87._ = bf16[1024,1280]{1,0:T(8,128)(2,1)} custom-call(s32[2]{0:T(128)} %pad_add_fusion.pos_ref, s32[8,128]{1,0:T(8,128)} %bitcast.15, bf16[128,4096]{1,0:T(8,128)(2,1)} %tokens_ref.5), custom_call_target="tpu_custom_call" | custom-call | flops 1073741824 | bytes 3145728 | tf_op jit(solution)/shard_map/pallas_call | solution.py:330
  10.7 0.0 collective-permute-done.other_ref
  10.7 0.9 copy-done
  11.5 3.4 %shard_map.88 = bf16[1024,1280]{1,0:T(8,128)(2,1)} custom-call(s32[2]{0:T(128)} %pad_add_fusion.pos_ref, s32[8,128]{1,0:T(8,128)} %bitcast.16, bf16[128,4096]{1,0:T(8,128)(2,1)} %tokens_ref.5, bf16[144,2048]{1,0:T(8,128)(2,1)} %copy-done, bf16[1024,1280]{1,0:T(8,128)(2,1)} %shard_map.87._), custom_call_target="tpu_custom_call", output_to_operand_aliasing={{}: (4, {})} | custom-call | flops 1073741824 | bytes 2097152 | tf_op jit(solution)/shard_map/pallas_call | solution.py:338
  14.9 18.0 %all-to-all-start = ((bf16[128,8,1280]{2,1,0:T(8,128)(2,1)}), bf16[128,8,1280]{2,1,0:T(8,128)(2,1)}, u32[]{:S(2)}, u32[]{:S(2)}) async-start(bf16[128,8,1280]{2,1,0:T(8,128)(2,1)} %bitcast.18), calls=%async_computation | async-start | bytes 5242880 | tf_op jit(solution)/shard_map/all_to_all | solution.py:313
  32.9 0.4 copy.10
  33.3 0.0 copy-start.6
  33.4 4.8 %collective-permute-start.9 = (bf16[192,4096]{1,0:T(8,128)(2,1)S(1)}, bf16[192,4096]{1,0:T(8,128)(2,1)S(1)}, u32[]{:S(2)}, u32[]{:S(2)}) collective-permute-start(bf16[192,4096]{1,0:T(8,128)(2,1)S(1)} %bitcast.20), channel_id=1, source_target_pairs={{0,3},{1,0},{2,1},{3,2},{4,7},{5,4},{6,5},{7,6},{8,11},{9,8},{10,9... | collective-permute-start | bytes 4718600 | tf_op jit(solution)/shard_map/ppermute | solution.py:299
  38.2 1.9 %collective-permute-start.8 = (bf16[192,4096]{1,0:T(8,128)(2,1)S(1)}, bf16[192,4096]{1,0:T(8,128)(2,1)S(1)}, u32[]{:S(2)}, u32[]{:S(2)}) collective-permute-start(bf16[192,4096]{1,0:T(8,128)(2,1)S(1)} %bitcast.21), channel_id=1, source_target_pairs={{0,1},{1,2},{2,3},{3,0},{4,5},{5,6},{6,7},{7,4},{8,9},{9,10},{10,1... | collective-permute-start | bytes 4718600 | tf_op jit(solution)/shard_map/ppermute | solution.py:299
  40.1 1.9 %collective-permute-start.4 = (bf16[1024,192]{1,0:T(8,128)(2,1)S(1)}, bf16[1024,192]{1,0:T(8,128)(2,1)S(1)}, u32[]{:S(2)}, u32[]{:S(2)}) collective-permute-start(bf16[1024,192]{1,0:T(8,128)(2,1)S(1)} %bitcast.12), channel_id=1, source_target_pairs={{0,4},{4,0},{8,12},{12,8},{16,20},{20,16},{24,28},{28,24},{32,36},... | collective-permute-start | bytes 1179656 | tf_op jit(solution)/shard_map/ppermute | solution.py:307
  42.0 30.1 %collective-permute-done.9.w1 = bf16[192,4096]{1,0:T(8,128)(2,1)S(1)} collective-permute-done((bf16[192,4096]{1,0:T(8,128)(2,1)S(1)}, bf16[192,4096]{1,0:T(8,128)(2,1)S(1)}, u32[]{:S(2)}, u32[]{:S(2)}) %collective-permute-start.9) | collective-permute-done | bytes 1572896 | tf_op jit(solution)/shard_map/ppermute | solution.py:299
  72.1 0.1 slice.9
  72.2 5.6 %collective-permute-start.11 = (bf16[96,4096]{1,0:T(8,128)(2,1)S(1)}, bf16[96,4096]{1,0:T(8,128)(2,1)S(1)}, u32[]{:S(2)}, u32[]{:S(2)}) collective-permute-start(bf16[96,4096]{1,0:T(8,128)(2,1)S(1)} %slice.9), channel_id=1, source_target_pairs={{0,3},{1,0},{2,1},{3,2},{4,7},{5,4},{6,5},{7,6},{8,11},{9,8},{10,9... | collective-permute-start | bytes 2359304 | tf_op jit(solution)/shard_map/ppermute | solution.py:299
  77.8 0.0 collective-permute-done.8.w4
  77.8 0.1 slice.8
  77.9 1.9 %collective-permute-start.10 = (bf16[96,4096]{1,0:T(8,128)(2,1)S(1)}, bf16[96,4096]{1,0:T(8,128)(2,1)S(1)}, u32[]{:S(2)}, u32[]{:S(2)}) collective-permute-start(bf16[96,4096]{1,0:T(8,128)(2,1)S(1)} %slice.8), channel_id=1, source_target_pairs={{0,1},{1,2},{2,3},{3,0},{4,5},{5,6},{6,7},{7,4},{8,9},{9,10},{10,1... | collective-permute-start | bytes 2359304 | tf_op jit(solution)/shard_map/ppermute | solution.py:299
  79.8 0.0 collective-permute-done.4.other_grads_ref
  79.9 2.9 %shard_map.91 = (bf16[384,256]{1,0:T(8,128)(2,1)S(1)}, bf16[384,256]{1,0:T(8,128)(2,1)S(1)}, bf16[384,256]{1,0:T(8,128)(2,1)S(1)}, bf16[384,256]{1,0:T(8,128)(2,1)S(1)}) custom-call(s32[2]{0:T(128)S(1)} %copy-done.4, s32[8,128]{1,0:T(8,128)S(1)} %bitcast.17, bf16[144,2048]{1,0:T(8,128)(2,1)S(1)} %copy-done.1, bf16[1024,192]{1,0:T(8,128)(2,1)S(1)} %bitcast.13, ...), custom_call_target="tpu_custom_call" | custom-call | flops 5368709120 | bytes 3145728 | tf_op jit(solution)/shard_map/pallas_call | solution.py:359
  82.7 1.9 %collective-permute-start.5 = (bf16[384,256]{1,0:T(8,128)(2,1)S(1)}, bf16[384,256]{1,0:T(8,128)(2,1)S(1)}, u32[]{:S(2)}, u32[]{:S(2)}) collective-permute-start(bf16[384,256]{1,0:T(8,128)(2,1)S(1)} %get-tuple-element.26), channel_id=1, source_target_pairs={{0,1},{1,2},{2,3},{3,0},{4,5},{5,6},{6,7},{7,4},{8,9},{9,10},{10,1... | collective-permute-start | bytes 589832 | tf_op jit(solution)/shard_map/ppermute | solution.py:299
  84.6 6.6 %collective-permute-start.6 = (bf16[384,256]{1,0:T(8,128)(2,1)S(1)}, bf16[384,256]{1,0:T(8,128)(2,1)S(1)}, u32[]{:S(2)}, u32[]{:S(2)}) collective-permute-start(bf16[384,256]{1,0:T(8,128)(2,1)S(1)} %get-tuple-element.27), channel_id=1, source_target_pairs={{0,2},{1,3},{2,0},{3,1},{4,6},{5,7},{6,4},{7,5},{8,10},{9,11},{10,... | collective-permute-start | bytes 589832 | tf_op jit(solution)/shard_map/ppermute | solution.py:299
  91.2 1.9 %collective-permute-start.7 = (bf16[384,256]{1,0:T(8,128)(2,1)S(1)}, bf16[384,256]{1,0:T(8,128)(2,1)S(1)}, u32[]{:S(2)}, u32[]{:S(2)}) collective-permute-start(bf16[384,256]{1,0:T(8,128)(2,1)S(1)} %get-tuple-element.28), channel_id=1, source_target_pairs={{0,3},{1,0},{2,1},{3,2},{4,7},{5,4},{6,5},{7,6},{8,11},{9,8},{10,9... | collective-permute-start | bytes 589832 | tf_op jit(solution)/shard_map/ppermute | solution.py:299
  93.2 14.8 %collective-permute-done.5.g1 = bf16[384,256]{1,0:T(8,128)(2,1)S(1)} collective-permute-done((bf16[384,256]{1,0:T(8,128)(2,1)S(1)}, bf16[384,256]{1,0:T(8,128)(2,1)S(1)}, u32[]{:S(2)}, u32[]{:S(2)}) %collective-permute-start.5) | collective-permute-done | bytes 196640 | tf_op jit(solution)/shard_map/ppermute | solution.py:299
  108.0 0.0 collective-permute-done.6.g2
  108.0 0.0 collective-permute-done.7.g3
  108.0 6.7 %shard_map.92 = bf16[1024,256]{1,0:T(8,128)(2,1)} custom-call(s32[2]{0:T(128)S(1)} %copy-done.4, bf16[384,256]{1,0:T(8,128)(2,1)S(1)} %get-tuple-element.25.g0, bf16[384,256]{1,0:T(8,128)(2,1)S(1)} %collective-permute-done.5.g1, bf16[384,256]{1,0:T(8,128)(2,1)S(1)} %collective-permute-done.6.g2, bf16[384,256]{1,0:T(8,128)(2,1)S(1)} %collective-permute-done.7.g3), custom_call_target="tpu_custom_call" | custom-call | flops 2147483648 | bytes 3145728 | tf_op jit(solution)/shard_map/pallas_call | solution.py:364
  114.7 0.0 collective-permute-done.11.w3
  114.7 0.0 collective-permute-done.10.w2
  114.7 0.0 all-to-all-done
  114.7 13.7 %all-to-all-start.1 = ((bf16[128,8,256]{2,1,0:T(8,128)(2,1)}), bf16[128,8,256]{2,1,0:T(8,128)(2,1)S(1)}, u32[]{:S(2)}, u32[]{:S(2)}) async-start(bf16[128,8,256]{2,1,0:T(8,128)(2,1)} %bitcast.8), calls=%async_computation.1 | async-start | bytes 1048576 | tf_op jit(solution)/shard_map/all_to_all | solution.py:313
  128.4 6.2 %shard_map.89 = (f32[128,1024]{1,0:T(8,128)}, bf16[128,1024]{1,0:T(8,128)(2,1)}, bf16[128,1024]{1,0:T(8,128)(2,1)}, bf16[128,1024]{1,0:T(8,128)(2,1)}) custom-call(s32[2]{0:T(128)} %pad_add_fusion.pos_ref, bf16[1024,1280]{1,0:T(8,128)(2,1)} %bitcast.4.rows_ref, bf16[128,4096]{1,0:T(8,128)(2,1)} %probes_ref.1), custom_call_target="tpu_custom_call" | custom-call | flops 1073741824 | bytes 8388608 | tf_op jit(solution)/shard_map/pallas_call | solution.py:373
  134.6 1.9 %collective-permute-start.1 = (bf16[128,1024]{1,0:T(8,128)(2,1)}, bf16[128,1024]{1,0:T(8,128)(2,1)S(1)}, u32[]{:S(2)}, u32[]{:S(2)}) collective-permute-start(bf16[128,1024]{1,0:T(8,128)(2,1)} %get-tuple-element.20), channel_id=1, source_target_pairs={{0,1},{1,2},{2,3},{3,0},{4,5},{5,6},{6,7},{7,4},{8,9},{9,10},{10,1... | collective-permute-start | bytes 786440 | tf_op jit(solution)/shard_map/ppermute | solution.py:299
  136.6 2.9 %collective-permute-start.2 = (bf16[128,1024]{1,0:T(8,128)(2,1)}, bf16[128,1024]{1,0:T(8,128)(2,1)S(1)}, u32[]{:S(2)}, u32[]{:S(2)}) collective-permute-start(bf16[128,1024]{1,0:T(8,128)(2,1)} %get-tuple-element.21), channel_id=1, source_target_pairs={{0,2},{1,3},{2,0},{3,1},{4,6},{5,7},{6,4},{7,5},{8,10},{9,11},{10,... | collective-permute-start | bytes 786440 | tf_op jit(solution)/shard_map/ppermute | solution.py:299
  139.5 4.1 %collective-permute-start.3 = (bf16[128,1024]{1,0:T(8,128)(2,1)}, bf16[128,1024]{1,0:T(8,128)(2,1)S(1)}, u32[]{:S(2)}, u32[]{:S(2)}) collective-permute-start(bf16[128,1024]{1,0:T(8,128)(2,1)} %get-tuple-element.22), channel_id=1, source_target_pairs={{0,3},{1,0},{2,1},{3,2},{4,7},{5,4},{6,5},{7,6},{8,11},{9,8},{10,9... | collective-permute-start | bytes 786440 | tf_op jit(solution)/shard_map/ppermute | solution.py:299
  143.6 10.7 %shard_map.93.gate_ref = f32[768,384]{1,0:T(8,128)} custom-call(s32[2]{0:T(128)} %pad_add_fusion.pos_ref, bf16[1024,1280]{1,0:T(8,128)(2,1)} %bitcast.4.rows_ref, bf16[192,4096]{1,0:T(8,128)(2,1)} %bitcast.19, bf16[192,4096]{1,0:T(8,128)(2,1)} %copy-done.7, bf16[96,4096]{1,0:T(8,128)(2,1)} %copy-done.11, bf16[96,4096]{1,0:T(8,128)(2,1)} %copy-done.10, ...), custom_call_target="tpu_custom_call" | custom-call | flops 2684354560 | bytes 10485760 | tf_op jit(solution)/shard_map/pallas_call | solution.py:383
  154.3 0.0 all-to-all-done.1
  154.3 0.8 copy-done.12
  155.1 3.5 %shard_map.94 = (f32[192,128]{1,0:T(8,128)}, bf16[768,128]{1,0:T(8,128)(2,1)}) custom-call(s32[2]{0:T(128)} %pad_add_fusion.pos_ref, bf16[128,768]{1,0:T(8,128)(2,1)} %grad_probes_ref.1, f32[768,384]{1,0:T(8,128)} %shard_map.93.gate_ref, bf16[1024,256]{1,0:T(8,128)(2,1)} %bitcast.22), custom_call_target="tpu_custom_call" | custom-call | flops 1073741824 | bytes 3145728 | tf_op jit(solution)/shard_map/pallas_call | solution.py:397
  158.6 4.2 %all-to-all-start.2 = ((bf16[4,192,128]{2,1,0:T(8,128)(2,1)}), bf16[4,192,128]{2,1,0:T(8,128)(2,1)S(1)}, u32[]{:S(2)}, u32[]{:S(2)}) async-start(bf16[4,192,128]{2,1,0:T(8,128)(2,1)} %bitcast.24), calls=%async_computation.2 | async-start | bytes 393216 | tf_op jit(solution)/shard_map/all_to_all | solution.py:406
  163.5 5.6 %all-to-all-done.2.parts_ref = bf16[4,192,128]{2,1,0:T(8,128)(2,1)S(1)} async-done(((bf16[4,192,128]{2,1,0:T(8,128)(2,1)}), bf16[4,192,128]{2,1,0:T(8,128)(2,1)S(1)}, u32[]{:S(2)}, u32[]{:S(2)}) %all-to-all-start.2) | async-done | bytes 196640 | tf_op jit(solution)/shard_map/all_to_all | solution.py:406
  169.1 0.9 copy-done.3
  170.0 1.2 shard_map.95
  171.2 0.0 collective-permute-done.1.i1
  171.2 0.0 collective-permute-done.2.i2
  171.2 0.0 collective-permute-done.3.i3
  171.2 1.0 shard_map.90
  (24 shorter events, 0.0 us)
Async XLA Ops:
  3.8 6.8 %collective-permute-start = (bf16[144,2048]{1,0:T(8,128)(2,1)}, bf16[144,2048]{1,0:T(8,128)(2,1)S(1)}, u32[]{:S(2)}, u32[]{:S(2)}) collective-permute-start(bf16[144,2048]{1,0:T(8,128)(2,1)} %shard_map.86), channel_id=1, source_target_pairs={{0,4},{4,0},{8,12},{12,8},{16,20},{20,16},{24,28},{28,24},{32,36},... | collective-permute-start | bytes 1769480 | tf_op jit(solution)/shard_map/ppermute | solution.py:307
  10.7 0.9 copy-start
  14.9 18.0 %copy-start.13 = (bf16[128,8,192]{0,2,1:T(8,128)(2,1)S(1)}, bf16[128,8,192]{0,2,1:T(8,128)(2,1)}, u32[]{:S(2)}) copy-start(bf16[128,8,192]{0,2,1:T(8,128)(2,1)} %param.9) | copy-start | bytes 1179652
  14.9 18.4 %copy-start.9 = (bf16[1,192,4096]{2,1,0:T(8,128)(2,1)S(1)}, bf16[1,192,4096]{2,1,0:T(8,128)(2,1)}, u32[]{:S(2)}) copy-start(bf16[1,192,4096]{2,1,0:T(8,128)(2,1)} %param.10) | copy-start | bytes 4718596
  14.9 99.8 %all-to-all-start = ((bf16[128,8,1280]{2,1,0:T(8,128)(2,1)}), bf16[128,8,1280]{2,1,0:T(8,128)(2,1)}, u32[]{:S(2)}, u32[]{:S(2)}) async-start(bf16[128,8,1280]{2,1,0:T(8,128)(2,1)} %bitcast.18), calls=%async_computation | async-start | bytes 5242880 | tf_op jit(solution)/shard_map/all_to_all | solution.py:313
  33.3 46.5 %copy-start.1 = (bf16[144,2048]{1,0:T(8,128)(2,1)S(1)}, bf16[144,2048]{1,0:T(8,128)(2,1)}, u32[]{:S(2)}) copy-start(bf16[144,2048]{1,0:T(8,128)(2,1)} %copy-done) | copy-start | bytes 1769476
  33.3 46.5 %copy-start.4 = (s32[2]{0:T(128)S(1)}, s32[2]{0:T(128)}, u32[]{:S(2)}) copy-start(s32[2]{0:T(128)} %pad_add_fusion.pos_ref) | copy-start | bytes 28
  33.3 46.5 %copy-start.6 = (s32[128,8]{0,1:T(8,128)S(1)}, s32[128,8]{0,1:T(8,128)}, u32[]{:S(2)}) copy-start(s32[128,8]{0,1:T(8,128)} %param.8) | copy-start | bytes 12292
  33.4 38.8 %collective-permute-start.9 = (bf16[192,4096]{1,0:T(8,128)(2,1)S(1)}, bf16[192,4096]{1,0:T(8,128)(2,1)S(1)}, u32[]{:S(2)}, u32[]{:S(2)}) collective-permute-start(bf16[192,4096]{1,0:T(8,128)(2,1)S(1)} %bitcast.20), channel_id=1, source_target_pairs={{0,3},{1,0},{2,1},{3,2},{4,7},{5,4},{6,5},{7,6},{8,11},{9,8},{10,9... | collective-permute-start | bytes 4718600 | tf_op jit(solution)/shard_map/ppermute | solution.py:299
  38.2 39.6 %collective-permute-start.8 = (bf16[192,4096]{1,0:T(8,128)(2,1)S(1)}, bf16[192,4096]{1,0:T(8,128)(2,1)S(1)}, u32[]{:S(2)}, u32[]{:S(2)}) collective-permute-start(bf16[192,4096]{1,0:T(8,128)(2,1)S(1)} %bitcast.21), channel_id=1, source_target_pairs={{0,1},{1,2},{2,3},{3,0},{4,5},{5,6},{6,7},{7,4},{8,9},{9,10},{10,1... | collective-permute-start | bytes 4718600 | tf_op jit(solution)/shard_map/ppermute | solution.py:299
  40.1 39.7 %collective-permute-start.4 = (bf16[1024,192]{1,0:T(8,128)(2,1)S(1)}, bf16[1024,192]{1,0:T(8,128)(2,1)S(1)}, u32[]{:S(2)}, u32[]{:S(2)}) collective-permute-start(bf16[1024,192]{1,0:T(8,128)(2,1)S(1)} %bitcast.12), channel_id=1, source_target_pairs={{0,4},{4,0},{8,12},{12,8},{16,20},{20,16},{24,28},{28,24},{32,36},... | collective-permute-start | bytes 1179656 | tf_op jit(solution)/shard_map/ppermute | solution.py:307
  72.1 5.8 %copy-start.7 = (bf16[192,4096]{1,0:T(8,128)(2,1)}, bf16[192,4096]{1,0:T(8,128)(2,1)S(1)}, u32[]{:S(2)}) copy-start(bf16[192,4096]{1,0:T(8,128)(2,1)S(1)} %collective-permute-done.9.w1) | copy-start | bytes 4718596
  72.2 42.5 %collective-permute-start.11 = (bf16[96,4096]{1,0:T(8,128)(2,1)S(1)}, bf16[96,4096]{1,0:T(8,128)(2,1)S(1)}, u32[]{:S(2)}, u32[]{:S(2)}) collective-permute-start(bf16[96,4096]{1,0:T(8,128)(2,1)S(1)} %slice.9), channel_id=1, source_target_pairs={{0,3},{1,0},{2,1},{3,2},{4,7},{5,4},{6,5},{7,6},{8,11},{9,8},{10,9... | collective-permute-start | bytes 2359304 | tf_op jit(solution)/shard_map/ppermute | solution.py:299
  77.8 2.0 %copy-start.8 = (bf16[192,4096]{1,0:T(8,128)(2,1)}, bf16[192,4096]{1,0:T(8,128)(2,1)S(1)}, u32[]{:S(2)}) copy-start(bf16[192,4096]{1,0:T(8,128)(2,1)S(1)} %collective-permute-done.8.w4) | copy-start | bytes 4718596
  77.9 36.8 %collective-permute-start.10 = (bf16[96,4096]{1,0:T(8,128)(2,1)S(1)}, bf16[96,4096]{1,0:T(8,128)(2,1)S(1)}, u32[]{:S(2)}, u32[]{:S(2)}) collective-permute-start(bf16[96,4096]{1,0:T(8,128)(2,1)S(1)} %slice.8), channel_id=1, source_target_pairs={{0,1},{1,2},{2,3},{3,0},{4,5},{5,6},{6,7},{7,4},{8,9},{9,10},{10,1... | collective-permute-start | bytes 2359304 | tf_op jit(solution)/shard_map/ppermute | solution.py:299
  82.7 25.3 %collective-permute-start.5 = (bf16[384,256]{1,0:T(8,128)(2,1)S(1)}, bf16[384,256]{1,0:T(8,128)(2,1)S(1)}, u32[]{:S(2)}, u32[]{:S(2)}) collective-permute-start(bf16[384,256]{1,0:T(8,128)(2,1)S(1)} %get-tuple-element.26), channel_id=1, source_target_pairs={{0,1},{1,2},{2,3},{3,0},{4,5},{5,6},{6,7},{7,4},{8,9},{9,10},{10,1... | collective-permute-start | bytes 589832 | tf_op jit(solution)/shard_map/ppermute | solution.py:299
  84.6 23.4 %collective-permute-start.6 = (bf16[384,256]{1,0:T(8,128)(2,1)S(1)}, bf16[384,256]{1,0:T(8,128)(2,1)S(1)}, u32[]{:S(2)}, u32[]{:S(2)}) collective-permute-start(bf16[384,256]{1,0:T(8,128)(2,1)S(1)} %get-tuple-element.27), channel_id=1, source_target_pairs={{0,2},{1,3},{2,0},{3,1},{4,6},{5,7},{6,4},{7,5},{8,10},{9,11},{10,... | collective-permute-start | bytes 589832 | tf_op jit(solution)/shard_map/ppermute | solution.py:299
  91.2 16.8 %collective-permute-start.7 = (bf16[384,256]{1,0:T(8,128)(2,1)S(1)}, bf16[384,256]{1,0:T(8,128)(2,1)S(1)}, u32[]{:S(2)}, u32[]{:S(2)}) collective-permute-start(bf16[384,256]{1,0:T(8,128)(2,1)S(1)} %get-tuple-element.28), channel_id=1, source_target_pairs={{0,3},{1,0},{2,1},{3,2},{4,7},{5,4},{6,5},{7,6},{8,11},{9,8},{10,9... | collective-permute-start | bytes 589832 | tf_op jit(solution)/shard_map/ppermute | solution.py:299
  114.7 20.0 %copy-start.10 = (bf16[96,4096]{1,0:T(8,128)(2,1)}, bf16[96,4096]{1,0:T(8,128)(2,1)S(1)}, u32[]{:S(2)}) copy-start(bf16[96,4096]{1,0:T(8,128)(2,1)S(1)} %collective-permute-done.11.w3) | copy-start | bytes 2359300
  114.7 20.0 %copy-start.11 = (bf16[96,4096]{1,0:T(8,128)(2,1)}, bf16[96,4096]{1,0:T(8,128)(2,1)S(1)}, u32[]{:S(2)}) copy-start(bf16[96,4096]{1,0:T(8,128)(2,1)S(1)} %collective-permute-done.10.w2) | copy-start | bytes 2359300
  114.7 39.6 %all-to-all-start.1 = ((bf16[128,8,256]{2,1,0:T(8,128)(2,1)}), bf16[128,8,256]{2,1,0:T(8,128)(2,1)S(1)}, u32[]{:S(2)}, u32[]{:S(2)}) async-start(bf16[128,8,256]{2,1,0:T(8,128)(2,1)} %bitcast.8), calls=%async_computation.1 | async-start | bytes 1048576 | tf_op jit(solution)/shard_map/all_to_all | solution.py:313
  134.6 36.6 %collective-permute-start.1 = (bf16[128,1024]{1,0:T(8,128)(2,1)}, bf16[128,1024]{1,0:T(8,128)(2,1)S(1)}, u32[]{:S(2)}, u32[]{:S(2)}) collective-permute-start(bf16[128,1024]{1,0:T(8,128)(2,1)} %get-tuple-element.20), channel_id=1, source_target_pairs={{0,1},{1,2},{2,3},{3,0},{4,5},{5,6},{6,7},{7,4},{8,9},{9,10},{10,1... | collective-permute-start | bytes 786440 | tf_op jit(solution)/shard_map/ppermute | solution.py:299
  136.6 34.7 %collective-permute-start.2 = (bf16[128,1024]{1,0:T(8,128)(2,1)}, bf16[128,1024]{1,0:T(8,128)(2,1)S(1)}, u32[]{:S(2)}, u32[]{:S(2)}) collective-permute-start(bf16[128,1024]{1,0:T(8,128)(2,1)} %get-tuple-element.21), channel_id=1, source_target_pairs={{0,2},{1,3},{2,0},{3,1},{4,6},{5,7},{6,4},{7,5},{8,10},{9,11},{10,... | collective-permute-start | bytes 786440 | tf_op jit(solution)/shard_map/ppermute | solution.py:299
  139.5 31.8 %collective-permute-start.3 = (bf16[128,1024]{1,0:T(8,128)(2,1)}, bf16[128,1024]{1,0:T(8,128)(2,1)S(1)}, u32[]{:S(2)}, u32[]{:S(2)}) collective-permute-start(bf16[128,1024]{1,0:T(8,128)(2,1)} %get-tuple-element.22), channel_id=1, source_target_pairs={{0,3},{1,0},{2,1},{3,2},{4,7},{5,4},{6,5},{7,6},{8,11},{9,8},{10,9... | collective-permute-start | bytes 786440 | tf_op jit(solution)/shard_map/ppermute | solution.py:299
  154.3 0.8 copy-start.12
  155.1 14.0 %copy-start.5 = (s32[2]{0:T(128)S(1)}, s32[2]{0:T(128)}, u32[]{:S(2)}) copy-start(s32[2]{0:T(128)} %pad_add_fusion.pos_ref) | copy-start | bytes 28
  155.1 16.1 %copy-start.2 = (f32[128,1024]{1,0:T(8,128)S(1)}, f32[128,1024]{1,0:T(8,128)}, u32[]{:S(2)}) copy-start(f32[128,1024]{1,0:T(8,128)} %get-tuple-element.19.i0) | copy-start | bytes 1572868
  158.6 10.5 %all-to-all-start.2 = ((bf16[4,192,128]{2,1,0:T(8,128)(2,1)}), bf16[4,192,128]{2,1,0:T(8,128)(2,1)S(1)}, u32[]{:S(2)}, u32[]{:S(2)}) async-start(bf16[4,192,128]{2,1,0:T(8,128)(2,1)} %bitcast.24), calls=%async_computation.2 | async-start | bytes 393216 | tf_op jit(solution)/shard_map/all_to_all | solution.py:406
  169.1 0.9 copy-start.3

commit v7 on v3

--- a/solution.py
+++ b/solution.py
@@ -19,7 +19,6 @@
 ROWS = OWNERS * FOLD
 SLOTS = OWNERS * 2
 STRIP = SHARE // 4
-LIMIT = 30 * 1024 * 1024
 
 BF = jnp.bfloat16
 F32 = jnp.float32
@@ -42,15 +41,14 @@
     return jnp.where(mask, 1.0, 0.0).astype(BF)
 
 
-def kernel_call(body, out_shape, in_specs, flops, bytes_accessed, scratch=(), grid=()):
+def kernel_call(body, out_shape, in_specs, flops, bytes_accessed, limit, scratch=()):
     return pl.pallas_call(
         body,
-        grid=grid,
         out_shape=out_shape,
         in_specs=in_specs,
         out_specs=jax.tree.map(lambda _: VM, out_shape),
         scratch_shapes=list(scratch),
-        compiler_params=pltpu.CompilerParams(vmem_limit_bytes=LIMIT),
+        compiler_params=pltpu.CompilerParams(vmem_limit_bytes=limit << 20),
         cost_estimate=pl.CostEstimate(
             flops=flops, bytes_accessed=bytes_accessed, transcendentals=0
         ),
@@ -159,35 +157,36 @@
             put(b, slice(g * 64, (g + 1) * 64), got[b * 64 : (b + 1) * 64])
 
 
-def cut_products(pos_ref, rows_ref, weights_ref, cut_ref, o0, o1, o2, o3):
+def products(
+    pos_ref, rows_ref, weights_ref, gate_ref, cut_ref, own_ref, own_sum_ref, o1, o2, o3,
+    whole_ref, sum_ref,
+):
     x = pos_ref[0]
 
     def put(b, at, got):
-        cut_ref[at, b * STRIP : (b + 1) * STRIP] = got
+        whole_ref[at, b * SHARE : (b + 1) * SHARE] = got[:, :SHARE]
+        cut_ref[at, b * STRIP : (b + 1) * STRIP] = got[:, SHARE:]
 
     unfold(rows_ref, put)
     cut = cut_ref[...]
-    projected = dot(weights_ref[FFW:, :], cut, NT)
-    for k, out in enumerate((o0, o1, o2, o3)):
+    share = pl.ds(pl.multiple_of(x * SHARE, SHARE), SHARE)
+    projected = dot(weights_ref[FFW:, share], cut, NT)
+    for k, out in enumerate((own_ref, o1, o2, o3)):
         base = lax.rem(x + k, REPS) * UNITS
-        weights = weights_ref[pl.ds(pl.multiple_of(base, UNITS), UNITS), :]
+        weights = weights_ref[pl.ds(pl.multiple_of(base, UNITS), UNITS), share]
         out[:UNITS, :] = dot(weights, cut, NT).astype(out.dtype)
-        out[UNITS:, :] = projected.astype(out.dtype)
-
-
-def whole_products(pos_ref, rows_ref, weights_ref, gate_ref, partial_ref, own_ref, whole_ref, sum_ref):
-    x = pos_ref[0]
-
-    def put(b, at, got):
-        whole_ref[at, b * SHARE : (b + 1) * SHARE] = got
-
-    unfold(rows_ref, put)
+        out[UNITS : UNITS + R, :] = projected.astype(out.dtype)
     whole = whole_ref[...]
     both = dot(weights_ref[...], whole, NT)
     gate_ref[...] = both[:FFW]
     sum_ref[...] = dot(both[FFW:].astype(BF), whole)
-    partial_ref[...] = sum_ref[...].astype(BF)
-    own_ref[...] = sum_ref[:, pl.ds(pl.multiple_of(x * SHARE, SHARE), SHARE)]
+    own_sum_ref[...] = sum_ref[:, share]
+    for k, out in enumerate((o1, o2, o3)):
+        base = lax.rem(x + k + 1, REPS) * SHARE
+        for j in range(4):
+            columns = pl.ds(pl.multiple_of(base + j * 256, 256), 256)
+            start = UNITS + (1 + j) * R
+            out[start : start + R, :] = sum_ref[:, columns].astype(BF)
 
 
 def gate_gradient(gate, grads):
@@ -196,8 +195,8 @@
 
 
 def gate_part(
-    pos_ref, grad_probes_ref, probe_share_ref, gate_ref, partial_ref, got_ref, s0, s1, s2, s3,
-    cut_grad_ref, t0, t1, t2, t3, grads_ref, sketch_ref,
+    pos_ref, grad_probes_ref, gate_ref, got_ref, s0, s1, s2, s3,
+    cut_grad_ref, own_ref, out_ref, grads_ref, sketch_ref, padded_ref,
 ):
     x = pos_ref[0]
 
@@ -213,50 +212,45 @@
     )
     cut_grad = gate_gradient(cut_gate, jnp.concatenate([p[UNITS:] for p in parts[:3]], 0))
     cut_grad_ref[...] = cut_grad
-    cut_projected = dot(probe_share_ref[...], cut_grad)
+    mine = pl.ds(pl.multiple_of(x * UNITS, UNITS), UNITS)
+    padded_ref[...] = jnp.zeros((FFW, SLOTS), BF)
+    padded_ref[mine, :] = cut_grad
+    cut_projected = dot(grad_probes_ref[...], padded_ref[...])
     whole = jnp.concatenate([p[:UNITS] for p in parts], 0)
     gate_grad = gate_gradient(gate_ref[...], whole)
     projected = dot(grad_probes_ref[...], gate_grad).astype(BF)
     sketch_ref[...] = dot(gate_grad, projected, NT)
-    for k, out in enumerate((t0, t1, t2, t3)):
-        base = lax.rem(x + k, REPS) * UNITS
-        sketch = sketch_ref[pl.ds(pl.multiple_of(base, UNITS), UNITS), :]
-        out[:UNITS, :] = sketch.astype(out.dtype)
-        out[UNITS : UNITS + R, :] = cut_projected[:, :128].astype(out.dtype)
-        out[UNITS + R : UNITS + 2 * R, :] = cut_projected[:, 128:].astype(out.dtype)
-        if k > 0:
-            base = lax.rem(x + k, REPS) * SHARE
-            for j in range(SHARE // 128):
-                start = UNITS + (2 + j) * R
-                columns = pl.ds(pl.multiple_of(base + j * 128, 128), 128)
-                out[start : start + R, :] = partial_ref[:, columns]
-
-
-def finish(
-    inverse_ref, cut_ref, own_ref, s0, s1, s2, s3, cut_grad_ref, t0, t1, t2, t3,
-    input_ref, grad_ref,
-):
-    inverse = inverse_ref[0]
-    others = (t1, t2, t3)
-    mixed = UNITS + 2 * R
-    total = t0[...] + (
-        t1[:mixed, :].astype(F32) + t2[:mixed, :].astype(F32) + t3[:mixed, :].astype(F32)
-    )
+    own_ref[:UNITS, :] = sketch_ref[mine, :]
+    own_ref[UNITS : UNITS + R, :] = cut_projected[:, :128]
+    own_ref[UNITS + R :, :] = cut_projected[:, 128:]
+    for to in range(REPS):
+        out_ref[to, :UNITS, :] = sketch_ref[to * UNITS : (to + 1) * UNITS, :].astype(BF)
+        out_ref[to, UNITS : UNITS + R, :] = cut_projected[:, :128].astype(BF)
+        out_ref[to, UNITS + R :, :] = cut_projected[:, 128:].astype(BF)
+
+
+def finish_input(inverse_ref, cut_ref, own_sum_ref, s0, s1, s2, s3, out_ref):
+    at = slice(UNITS, UNITS + R)
+    projected = s0[at, :] + (
+        s1[at, :].astype(F32) + s2[at, :].astype(F32) + s3[at, :].astype(F32)
+    )
+    total = own_sum_ref[...] + dot(projected.astype(BF), cut_ref[...])
+    for j in range(4):
+        block = total[:, j * 256 : (j + 1) * 256]
+        start = UNITS + (1 + j) * R
+        for other in (s1, s2, s3):
+            block += other[start : start + R, :].astype(F32)
+        out_ref[j * 256 : (j + 1) * 256, :] = (block * inverse_ref[0]).T
+
+
+def finish_grad(pos_ref, inverse_ref, cut_grad_ref, own_ref, parts_ref, out_ref):
+    total = own_ref[...]
+    for k in range(1, REPS):
+        total += parts_ref[lax.rem(pos_ref[0] + k, REPS)].astype(F32)
     projected = total[UNITS:].astype(BF)
     sketch = total[:UNITS] + dot(cut_grad_ref[:, :128], projected[:R], NT)
     sketch += dot(cut_grad_ref[:, 128:], projected[R:], NT)
-    grad_ref[...] = sketch * inverse
-
-    projected = s0[UNITS:, :] + (
-        s1[UNITS:, :].astype(F32) + s2[UNITS:, :].astype(F32) + s3[UNITS:, :].astype(F32)
-    )
-    total = own_ref[...] + dot(projected.astype(BF), cut_ref[...])
-    for j in range(SHARE // 128):
-        start = mixed + j * R
-        block = total[:, j * 128 : (j + 1) * 128]
-        for other in others:
-            block += other[start : start + R, :].astype(F32)
-        input_ref[j * 128 : (j + 1) * 128, :] = (block * inverse).T
+    out_ref[...] = sketch * inverse_ref[0]
 
 
 def shift(block, k):
@@ -280,10 +274,9 @@
     inverse = 1.0 / window_counts.astype(F32)
     ids_t = expert_ids.T
     flat_ids = expert_ids.reshape(1, TOK * TOP)
-    probe_share = lax.dynamic_slice_in_dim(grad_probes, x * UNITS, UNITS, 1)
 
     out_rows = kernel_call(
-        send_rows, sds((ROWS, SHARE + STRIP), BF), [SM] + [VM] * 2, 1 << 31, 4 << 20
+        send_rows, sds((ROWS, SHARE + STRIP), BF), [SM] + [VM] * 2, 1 << 31, 4 << 20, 20
     )(pos, ids_t, tokens)
     rows = to_owners(out_rows)
 
@@ -297,67 +290,59 @@
         [SM] + [VM] * 3,
         4 << 30,
         3 << 20,
+        20,
     )(pos, ids_t, flat_ids, hidden_grads.reshape(TOK * TOP, UNITS))
     picked = shifted(picked)
     out_grads = kernel_call(
-        fold_grads, sds((ROWS, STRIP), BF), [SM] + [VM] * 5, 1 << 29, 3 << 20
+        fold_grads, sds((ROWS, STRIP), BF), [SM] + [VM] * 5, 1 << 29, 3 << 20, 12
     )(pos, tail, *picked)
     out_grads, left, right = lax.optimization_barrier((out_grads, left, right))
     top = shift(left[: UNITS // 2], 1)
     bottom = shift(right[UNITS // 2 :], REPS - 1)
     weights = kernel_call(
-        stack_weights, sds((FFW + R, D), BF), [SM] + [VM] * 6, 1000, 14 << 20
+        stack_weights, sds((FFW + R, D), BF), [SM] + [VM] * 6, 1000, 14 << 20, 8
     )(pos, probes, own, right, top, bottom, left)
     got = to_owners(out_grads)
 
-    kinds = [F32, BF, BF, BF]
-    cut, *cut_sums = pl.pallas_call(
-        cut_products,
-        out_shape=[sds((SLOTS, SHARE), BF)] + [sds((UNITS + R, SLOTS), kind) for kind in kinds],
-        grid_spec=pltpu.PrefetchScalarGridSpec(
-            num_scalar_prefetch=1,
-            grid=(1,),
-            in_specs=[
-                pl.BlockSpec((ROWS, STRIP), lambda i, pos: (0, SHARE // STRIP)),
-                pl.BlockSpec((FFW + R, SHARE), lambda i, pos: (0, pos[0])),
-            ],
-            out_specs=[VM] * 5,
-        ),
-        compiler_params=pltpu.CompilerParams(vmem_limit_bytes=LIMIT),
-        cost_estimate=pl.CostEstimate(
-            flops=1 << 29, bytes_accessed=4 << 20, transcendentals=0
-        ),
-    )(pos, rows, weights)
-    cut_sums = shifted(cut_sums)
-    gate, partial, own_partial = kernel_call(
-        whole_products,
-        [sds((FFW, SLOTS), F32), sds((R, D), BF), sds((R, SHARE), F32)],
-        [SM, pl.BlockSpec((ROWS, SHARE), lambda i: (0, 0)), VM],
+    gate, cut, own_sums, own_inputs, *sums = kernel_call(
+        products,
+        [
+            sds((FFW, SLOTS), F32),
+            sds((SLOTS, SHARE), BF),
+            sds((UNITS + R, SLOTS), F32),
+            sds((R, SHARE), F32),
+        ]
+        + [sds((UNITS + 5 * R, SLOTS), BF)] * (REPS - 1),
+        [SM] + [VM] * 2,
         3 << 30,
         14 << 20,
+        20,
         [pltpu.VMEM((SLOTS, D), BF), pltpu.VMEM((R, D), F32)],
-        (1,),
     )(pos, rows, weights)
+    sums = shifted([own_sums] + sums)
 
     mixed = UNITS + 2 * R
-    cut_grad, *sums = kernel_call(
+    cut_grad, own_sketch, sketch = kernel_call(
         gate_part,
-        [sds((UNITS, SLOTS), BF), sds((mixed, 128), F32)]
-        + [sds((mixed + SHARE, 128), BF)] * (REPS - 1),
-        [SM] + [VM] * 9,
+        [sds((UNITS, SLOTS), BF), sds((mixed, R), F32), sds((REPS, mixed, R), BF)],
+        [SM] + [VM] * 7,
         2 << 30,
         4 << 20,
-        [pltpu.VMEM((ROWS, STRIP), BF), pltpu.VMEM((FFW, R), F32)],
-    )(pos, grad_probes, probe_share, gate, partial, got, *cut_sums)
-    sums = shifted(sums)
-
-    input_sketch, grad_sketch = kernel_call(
-        finish,
-        [sds((SHARE, R), F32), sds((UNITS, R), F32)],
-        [SM] + [VM] * 11,
-        1 << 28,
-        4 << 20,
-    )(inverse, cut, own_partial, *cut_sums, cut_grad, *sums)
+        16,
+        [
+            pltpu.VMEM((ROWS, STRIP), BF),
+            pltpu.VMEM((FFW, R), F32),
+            pltpu.VMEM((FFW, SLOTS), BF),
+        ],
+    )(pos, grad_probes, gate, got, *sums)
+    parts = lax.all_to_all(sketch, "rep", split_axis=0, concat_axis=0, tiled=True)
+
+    input_sketch = kernel_call(
+        finish_input, sds((SHARE, R), F32), [SM] + [VM] * 6, 1 << 27, 3 << 20, 8
+    )(inverse, cut, own_inputs, *sums)
+    grad_sketch = kernel_call(
+        finish_grad, sds((UNITS, R), F32), [SM] * 2 + [VM] * 3, 1 << 24, 1 << 20, 6
+    )(pos, inverse, cut_grad, own_sketch, parts)
     return input_sketch[None], grad_sketch[None]
 
 

time: 155 us -> 154 us (level)
  the two profiles are of different devices: /device:TPU:8 before, /device:TPU:16 now
where the time goes in v7:
time: 154 us; the launch traced here: 153 us
  starting transfers between devices  65.9 us (43%)
  waiting for transfers between devices  50.1 us (33%)
  Pallas kernels  22.6 us (15%)
  local copies, waits for them, and re-layouts  12.8 us (8%)
    ppermute x10, waiting for transfers between devices, shift(): lax.ppermute(block, 'rep', [(i, (i + k) % REPS) for i in range(REPS)])  37.8 us
    ppermute x10, starting transfers between devices, shift(): lax.ppermute(block, 'rep', [(i, (i + k) % REPS) for i in range(REPS)])  35.6 us
    all_to_all x2, starting transfers between devices, to_owners(): lax.all_to_all(rows, 'ep', split_axis=0, concat_axis=0, tiled=True)  26.1 us
    unnamed x22, local copies, waits for them, and re-layouts  9.84 us
    pallas_call x1, Pallas kernels, local(): kernel_call(products, [sds((FFW, SLOTS), F32), sds((SLOTS, SHARE), BF), s...  7.18 us
    all_to_all x1, waiting for transfers between devices, local(): lax.all_to_all(sketch, 'rep', split_axis=0, concat_axis=0, tiled=True)  6.44 us
    all_to_all x2, waiting for transfers between devices, to_owners(): lax.all_to_all(rows, 'ep', split_axis=0, concat_axis=0, tiled=True)  5.91 us
    all_to_all x1, starting transfers between devices, local(): lax.all_to_all(sketch, 'rep', split_axis=0, concat_axis=0, tiled=True)  4.21 us
  transfers between devices with their start and end apart: 13, of which 9 were waited for; matrix products, arithmetic and copies ran while one was open for 3% of the time, Pallas kernels for 10%

profile of v7, /device:TPU:16, one launch (start us, length us, event | category | flops | bytes accessed | tf_op | source)
XLA Modules:
  0.0 152.9 jit_solution(386715805342752786)
XLA Ops:
  0.6 0.0 copy-start.3
  0.6 0.7 copy-done.3
  1.3 1.2 copy-done.5
  2.5 3.5 %shard_map.86 = bf16[1024,1280]{1,0:T(8,128)(2,1)} custom-call(s32[1]{0:T(128)} %bitcast.pos_ref, s32[8,128]{1,0:T(8,128)S(1)} %bitcast.12, bf16[128,4096]{1,0:T(8,128)(2,1)S(1)} %copy-done.5), custom_call_target="tpu_custom_call" | custom-call | flops 2147483648 | bytes 4194304 | tf_op jit(solution)/shard_map/pallas_call | solution.py:278
  6.0 17.8 %all-to-all-start = ((bf16[128,8,1280]{2,1,0:T(8,128)(2,1)}), bf16[128,8,1280]{2,1,0:T(8,128)(2,1)}, u32[]{:S(2)}, u32[]{:S(2)}) async-start(bf16[128,8,1280]{2,1,0:T(8,128)(2,1)} %bitcast.2), calls=%async_computation | async-start | bytes 5242880 | tf_op jit(solution)/shard_map/all_to_all | solution.py:267
  23.8 3.4 %collective-permute-start.3 = (bf16[192,4096]{1,0:T(8,128)(2,1)}, bf16[192,4096]{1,0:T(8,128)(2,1)S(1)}, u32[]{:S(2)}, u32[]{:S(2)}) collective-permute-start(bf16[192,4096]{1,0:T(8,128)(2,1)} %bitcast.4.own_ref), channel_id=1, source_target_pairs={{0,1},{1,2},{2,3},{3,0},{4,5},{5,6},{6,7},{7,4},{8,9},{9,10},{10,1... | collective-permute-start | bytes 4718600 | tf_op jit(solution)/shard_map/ppermute | solution.py:257
  27.2 3.7 %collective-permute-start.4 = (bf16[192,4096]{1,0:T(8,128)(2,1)}, bf16[192,4096]{1,0:T(8,128)(2,1)S(1)}, u32[]{:S(2)}, u32[]{:S(2)}) collective-permute-start(bf16[192,4096]{1,0:T(8,128)(2,1)} %bitcast.4.own_ref), channel_id=1, source_target_pairs={{0,3},{1,0},{2,1},{3,2},{4,7},{5,4},{6,5},{7,6},{8,11},{9,8},{10,9... | collective-permute-start | bytes 4718600 | tf_op jit(solution)/shard_map/ppermute | solution.py:257
  30.9 0.7 copy.11
  31.6 1.2 copy.12
  32.8 0.9 reshape.28.flat_ref
  33.8 1.0 copy-done.1
  34.8 3.9 %shard_map.87 = (bf16[1024,256]{1,0:T(8,128)(2,1)S(1)}, bf16[256,256]{1,0:T(8,128)(2,1)S(1)}, bf16[256,256]{1,0:T(8,128)(2,1)S(1)}, bf16[256,256]{1,0:T(8,128)(2,1)S(1)}, bf16[256,256]{1,0:T(8,128)(2,1)S(1)}) custom-call(s32[1]{0:T(128)} %bitcast.pos_ref, s32[8,128]{1,0:T(8,128)S(1)} %bitcast.13, s32[1,1024]{1,0:T(1,128)S(1)} %reshape.28.flat_ref, ...), custom_call_target="tpu_custom_call" | custom-call | flops 4294967296 | bytes 3145728 | tf_op jit(solution)/shard_map/pallas_call | solution.py:287
  38.7 2.2 %collective-permute-start = (bf16[256,256]{1,0:T(8,128)(2,1)S(1)}, bf16[256,256]{1,0:T(8,128)(2,1)S(1)}, u32[]{:S(2)}, u32[]{:S(2)}) collective-permute-start(bf16[256,256]{1,0:T(8,128)(2,1)S(1)} %get-tuple-element.24), channel_id=1, source_target_pairs={{0,1},{1,2},{2,3},{3,0},{4,5},{5,6},{6,7},{7,4},{8,9},{9,10},{10,1... | collective-permute-start | bytes 393224 | tf_op jit(solution)/shard_map/ppermute | solution.py:257
  40.9 4.6 %collective-permute-start.1 = (bf16[256,256]{1,0:T(8,128)(2,1)S(1)}, bf16[256,256]{1,0:T(8,128)(2,1)S(1)}, u32[]{:S(2)}, u32[]{:S(2)}) collective-permute-start(bf16[256,256]{1,0:T(8,128)(2,1)S(1)} %get-tuple-element.25), channel_id=1, source_target_pairs={{0,2},{1,3},{2,0},{3,1},{4,6},{5,7},{6,4},{7,5},{8,10},{9,11},{10,... | collective-permute-start | bytes 393224 | tf_op jit(solution)/shard_map/ppermute | solution.py:257
  45.6 3.3 %collective-permute-start.2 = (bf16[256,256]{1,0:T(8,128)(2,1)S(1)}, bf16[256,256]{1,0:T(8,128)(2,1)S(1)}, u32[]{:S(2)}, u32[]{:S(2)}) collective-permute-start(bf16[256,256]{1,0:T(8,128)(2,1)S(1)} %get-tuple-element.26), channel_id=1, source_target_pairs={{0,3},{1,0},{2,1},{3,2},{4,7},{5,4},{6,5},{7,6},{8,11},{9,8},{10,9... | collective-permute-start | bytes 393224 | tf_op jit(solution)/shard_map/ppermute | solution.py:257
  48.9 17.5 %collective-permute-done.g1 = bf16[256,256]{1,0:T(8,128)(2,1)S(1)} collective-permute-done((bf16[256,256]{1,0:T(8,128)(2,1)S(1)}, bf16[256,256]{1,0:T(8,128)(2,1)S(1)}, u32[]{:S(2)}, u32[]{:S(2)}) %collective-permute-start) | collective-permute-done | bytes 131104 | tf_op jit(solution)/shard_map/ppermute | solution.py:257
  66.4 3.8 %collective-permute-done.1.g2 = bf16[256,256]{1,0:T(8,128)(2,1)S(1)} collective-permute-done((bf16[256,256]{1,0:T(8,128)(2,1)S(1)}, bf16[256,256]{1,0:T(8,128)(2,1)S(1)}, u32[]{:S(2)}, u32[]{:S(2)}) %collective-permute-start.1) | collective-permute-done | bytes 131104 | tf_op jit(solution)/shard_map/ppermute | solution.py:257
  70.2 0.9 collective-permute-done.2.g3
  71.1 0.7 shard_map.88
  71.8 0.0 copy-start.2
  71.9 0.8 copy-done.2
  72.6 0.0 collective-permute-done.3.left_ref
  72.6 0.0 collective-permute-done.4.right_ref
  72.6 1.0 slice.6
  73.6 3.4 %collective-permute-start.5 = (bf16[96,4096]{1,0:T(8,128)(2,1)}, bf16[96,4096]{1,0:T(8,128)(2,1)}, u32[]{:S(2)}, u32[]{:S(2)}) collective-permute-start(bf16[96,4096]{1,0:T(8,128)(2,1)} %slice.6), channel_id=1, source_target_pairs={{0,1},{1,2},{2,3},{3,0},{4,5},{5,6},{6,7},{7,4},{8,9},{9,10},{10,1... | collective-permute-start | bytes 2359304 | tf_op jit(solution)/shard_map/ppermute | solution.py:257
  77.0 1.0 slice.7
  78.0 3.6 %collective-permute-start.6 = (bf16[96,4096]{1,0:T(8,128)(2,1)}, bf16[96,4096]{1,0:T(8,128)(2,1)}, u32[]{:S(2)}, u32[]{:S(2)}) collective-permute-start(bf16[96,4096]{1,0:T(8,128)(2,1)} %slice.7), channel_id=1, source_target_pairs={{0,3},{1,0},{2,1},{3,2},{4,7},{5,4},{6,5},{7,6},{8,11},{9,8},{10,9... | collective-permute-start | bytes 2359304 | tf_op jit(solution)/shard_map/ppermute | solution.py:257
  81.7 5.9 %all-to-all-done = bf16[128,8,1280]{2,1,0:T(8,128)(2,1)} async-done(((bf16[128,8,1280]{2,1,0:T(8,128)(2,1)}), bf16[128,8,1280]{2,1,0:T(8,128)(2,1)}, u32[]{:S(2)}, u32[]{:S(2)}) %all-to-all-start) | async-done | bytes 2621472 | tf_op jit(solution)/shard_map/all_to_all | solution.py:267
  87.6 8.3 %all-to-all-start.1 = ((bf16[128,8,256]{2,1,0:T(8,128)(2,1)}), bf16[128,8,256]{2,1,0:T(8,128)(2,1)}, u32[]{:S(2)}, u32[]{:S(2)}) async-start(bf16[128,8,256]{2,1,0:T(8,128)(2,1)} %bitcast.11), calls=%async_computation.1 | async-start | bytes 1048576 | tf_op jit(solution)/shard_map/all_to_all | solution.py:267
  95.9 2.5 %collective-permute-done.6.bottom_ref = bf16[96,4096]{1,0:T(8,128)(2,1)} collective-permute-done((bf16[96,4096]{1,0:T(8,128)(2,1)}, bf16[96,4096]{1,0:T(8,128)(2,1)}, u32[]{:S(2)}, u32[]{:S(2)}) %collective-permute-start.6) | collective-permute-done | bytes 786464 | tf_op jit(solution)/shard_map/ppermute | solution.py:257
  98.5 1.2 copy-done
  99.7 2.3 %shard_map.89.weights_ref = bf16[896,4096]{1,0:T(8,128)(2,1)S(1)} custom-call(s32[1]{0:T(128)} %bitcast.pos_ref, bf16[128,4096]{1,0:T(8,128)(2,1)S(1)} %copy-done, bf16[192,4096]{1,0:T(8,128)(2,1)} %bitcast.4.own_ref, bf16[192,4096]{1,0:T(8,128)(2,1)S(1)} %collective-permute-done.4.right_ref, bf16[96,4096]{1,0:T(8,128)(2,1)} %collective-permute-done.5.top_ref, ...), custom_call_target="tpu_custom_call" | custom-call | flops 1000 | bytes 14680064 | tf_op jit(solution)/shard_map/pallas_call | solution.py:302
  102.0 7.2 %shard_map.90 = (f32[768,256]{1,0:T(8,128)S(1)}, bf16[256,1024]{1,0:T(8,128)(2,1)S(1)}, f32[320,256]{1,0:T(8,128)S(1)}, f32[128,1024]{1,0:T(8,128)S(1)}, bf16[83...) custom-call(s32[1]{0:T(128)} %bitcast.pos_ref, bf16[1024,1280]{1,0:T(8,128)(2,1)} %bitcast.3.rows_ref, ...), custom_call_target="tpu_custom_call" | custom-call | flops 3221225472 | bytes 14680064 | tf_op jit(solution)/shard_map/pallas_call | solution.py:307
  109.2 0.9 copy-done.7
  110.1 3.1 %collective-permute-start.7 = (bf16[832,256]{1,0:T(8,128)(2,1)}, bf16[832,256]{1,0:T(8,128)(2,1)S(1)}, u32[]{:S(2)}, u32[]{:S(2)}) collective-permute-start(bf16[832,256]{1,0:T(8,128)(2,1)} %get-tuple-element.32), channel_id=1, source_target_pairs={{0,1},{1,2},{2,3},{3,0},{4,5},{5,6},{6,7},{7,4},{8,9},{9,10},{10,1... | collective-permute-start | bytes 1277960 | tf_op jit(solution)/shard_map/ppermute | solution.py:257
  113.2 5.1 %collective-permute-start.8 = (bf16[832,256]{1,0:T(8,128)(2,1)S(1)}, bf16[832,256]{1,0:T(8,128)(2,1)S(1)}, u32[]{:S(2)}, u32[]{:S(2)}) collective-permute-start(bf16[832,256]{1,0:T(8,128)(2,1)S(1)} %get-tuple-element.33), channel_id=1, source_target_pairs={{0,2},{1,3},{2,0},{3,1},{4,6},{5,7},{6,4},{7,5},{8,10},{9,11},{10,... | collective-permute-start | bytes 1277960 | tf_op jit(solution)/shard_map/ppermute | solution.py:257
  118.3 3.1 %collective-permute-start.9 = (bf16[832,256]{1,0:T(8,128)(2,1)S(1)}, bf16[832,256]{1,0:T(8,128)(2,1)S(1)}, u32[]{:S(2)}, u32[]{:S(2)}) collective-permute-start(bf16[832,256]{1,0:T(8,128)(2,1)S(1)} %get-tuple-element.34), channel_id=1, source_target_pairs={{0,3},{1,0},{2,1},{3,2},{4,7},{5,4},{6,5},{7,6},{8,11},{9,8},{10,9... | collective-permute-start | bytes 1277960 | tf_op jit(solution)/shard_map/ppermute | solution.py:257
  121.4 0.0 all-to-all-done.1
  121.4 3.6 %collective-permute-done.7.s1 = bf16[832,256]{1,0:T(8,128)(2,1)S(1)} collective-permute-done((bf16[832,256]{1,0:T(8,128)(2,1)}, bf16[832,256]{1,0:T(8,128)(2,1)S(1)}, u32[]{:S(2)}, u32[]{:S(2)}) %collective-permute-start.7) | collective-permute-done | bytes 426016 | tf_op jit(solution)/shard_map/ppermute | solution.py:257
  125.0 8.4 %collective-permute-done.8.s2 = bf16[832,256]{1,0:T(8,128)(2,1)S(1)} collective-permute-done((bf16[832,256]{1,0:T(8,128)(2,1)S(1)}, bf16[832,256]{1,0:T(8,128)(2,1)S(1)}, u32[]{:S(2)}, u32[]{:S(2)}) %collective-permute-start.8) | collective-permute-done | bytes 426016 | tf_op jit(solution)/shard_map/ppermute | solution.py:257
  133.3 1.2 collective-permute-done.9.s3
  134.5 0.9 copy-done.6
  135.4 1.1 copy-done.8
  136.6 3.0 %shard_map.92 = (bf16[192,256]{1,0:T(8,128)(2,1)S(1)}, f32[448,128]{1,0:T(8,128)S(1)}, bf16[4,448,128]{2,1,0:T(8,128)(2,1)}) custom-call(s32[1]{0:T(128)} %bitcast.pos_ref, bf16[128,768]{1,0:T(8,128)(2,1)S(1)} %copy-done.6, f32[768,256]{1,0:T(8,128)S(1)} %copy-done.8, bf16[1024,256]{1,0:T(8,128)(2,1)} %bitcast.8.got_ref, ...), custom_call_target="tpu_custom_call" | custom-call | flops 2147483648 | bytes 4194304 | tf_op jit(solution)/shard_map/pallas_call | solution.py:325
  139.5 4.2 %all-to-all-start.2 = ((bf16[4,448,128]{2,1,0:T(8,128)(2,1)}), bf16[4,448,128]{2,1,0:T(8,128)(2,1)S(1)}, u32[]{:S(2)}, u32[]{:S(2)}) async-start(bf16[4,448,128]{2,1,0:T(8,128)(2,1)} %get-tuple-element.39), calls=%async_computation.2 | async-start | bytes 917504 | tf_op jit(solution)/shard_map/all_to_all | solution.py:338
  144.4 1.2 shard_map.91
  145.6 6.4 %all-to-all-done.2.parts_ref = bf16[4,448,128]{2,1,0:T(8,128)(2,1)S(1)} async-done(((bf16[4,448,128]{2,1,0:T(8,128)(2,1)}), bf16[4,448,128]{2,1,0:T(8,128)(2,1)S(1)}, u32[]{:S(2)}, u32[]{:S(2)}) %all-to-all-start.2) | async-done | bytes 458784 | tf_op jit(solution)/shard_map/all_to_all | solution.py:338
  152.1 0.8 shard_map.93
  (11 shorter events, 0.0 us)
Async XLA Ops:
  0.6 0.7 copy-start.3
  1.3 1.2 copy-start.5
  6.0 24.9 %copy-start.4 = (s32[128,8]{0,1:T(8,128)S(1)}, s32[128,8]{0,1:T(8,128)}, u32[]{:S(2)}) copy-start(s32[128,8]{0,1:T(8,128)} %param.8) | copy-start | bytes 12292
  6.0 25.6 %copy-start.9 = (bf16[128,8,192]{0,2,1:T(8,128)(2,1)S(1)}, bf16[128,8,192]{0,2,1:T(8,128)(2,1)}, u32[]{:S(2)}) copy-start(bf16[128,8,192]{0,2,1:T(8,128)(2,1)} %param.9) | copy-start | bytes 1179652
  6.0 81.6 %all-to-all-start = ((bf16[128,8,1280]{2,1,0:T(8,128)(2,1)}), bf16[128,8,1280]{2,1,0:T(8,128)(2,1)}, u32[]{:S(2)}, u32[]{:S(2)}) async-start(bf16[128,8,1280]{2,1,0:T(8,128)(2,1)} %bitcast.2), calls=%async_computation | async-start | bytes 5242880 | tf_op jit(solution)/shard_map/all_to_all | solution.py:267
  23.8 48.8 %collective-permute-start.3 = (bf16[192,4096]{1,0:T(8,128)(2,1)}, bf16[192,4096]{1,0:T(8,128)(2,1)S(1)}, u32[]{:S(2)}, u32[]{:S(2)}) collective-permute-start(bf16[192,4096]{1,0:T(8,128)(2,1)} %bitcast.4.own_ref), channel_id=1, source_target_pairs={{0,1},{1,2},{2,3},{3,0},{4,5},{5,6},{6,7},{7,4},{8,9},{9,10},{10,1... | collective-permute-start | bytes 4718600 | tf_op jit(solution)/shard_map/ppermute | solution.py:257
  27.2 45.4 %collective-permute-start.4 = (bf16[192,4096]{1,0:T(8,128)(2,1)}, bf16[192,4096]{1,0:T(8,128)(2,1)S(1)}, u32[]{:S(2)}, u32[]{:S(2)}) collective-permute-start(bf16[192,4096]{1,0:T(8,128)(2,1)} %bitcast.4.own_ref), channel_id=1, source_target_pairs={{0,3},{1,0},{2,1},{3,2},{4,7},{5,4},{6,5},{7,6},{8,11},{9,8},{10,9... | collective-permute-start | bytes 4718600 | tf_op jit(solution)/shard_map/ppermute | solution.py:257
  33.8 1.0 copy-start.1
  38.7 27.7 %collective-permute-start = (bf16[256,256]{1,0:T(8,128)(2,1)S(1)}, bf16[256,256]{1,0:T(8,128)(2,1)S(1)}, u32[]{:S(2)}, u32[]{:S(2)}) collective-permute-start(bf16[256,256]{1,0:T(8,128)(2,1)S(1)} %get-tuple-element.24), channel_id=1, source_target_pairs={{0,1},{1,2},{2,3},{3,0},{4,5},{5,6},{6,7},{7,4},{8,9},{9,10},{10,1... | collective-permute-start | bytes 393224 | tf_op jit(solution)/shard_map/ppermute | solution.py:257
  40.9 29.3 %collective-permute-start.1 = (bf16[256,256]{1,0:T(8,128)(2,1)S(1)}, bf16[256,256]{1,0:T(8,128)(2,1)S(1)}, u32[]{:S(2)}, u32[]{:S(2)}) collective-permute-start(bf16[256,256]{1,0:T(8,128)(2,1)S(1)} %get-tuple-element.25), channel_id=1, source_target_pairs={{0,2},{1,3},{2,0},{3,1},{4,6},{5,7},{6,4},{7,5},{8,10},{9,11},{10,... | collective-permute-start | bytes 393224 | tf_op jit(solution)/shard_map/ppermute | solution.py:257
  45.6 25.6 %collective-permute-start.2 = (bf16[256,256]{1,0:T(8,128)(2,1)S(1)}, bf16[256,256]{1,0:T(8,128)(2,1)S(1)}, u32[]{:S(2)}, u32[]{:S(2)}) collective-permute-start(bf16[256,256]{1,0:T(8,128)(2,1)S(1)} %get-tuple-element.26), channel_id=1, source_target_pairs={{0,3},{1,0},{2,1},{3,2},{4,7},{5,4},{6,5},{7,6},{8,11},{9,8},{10,9... | collective-permute-start | bytes 393224 | tf_op jit(solution)/shard_map/ppermute | solution.py:257
  71.8 0.8 copy-start.2
  73.6 22.3 %collective-permute-start.5 = (bf16[96,4096]{1,0:T(8,128)(2,1)}, bf16[96,4096]{1,0:T(8,128)(2,1)}, u32[]{:S(2)}, u32[]{:S(2)}) collective-permute-start(bf16[96,4096]{1,0:T(8,128)(2,1)} %slice.6), channel_id=1, source_target_pairs={{0,1},{1,2},{2,3},{3,0},{4,5},{5,6},{6,7},{7,4},{8,9},{9,10},{10,1... | collective-permute-start | bytes 2359304 | tf_op jit(solution)/shard_map/ppermute | solution.py:257
  78.0 20.4 %collective-permute-start.6 = (bf16[96,4096]{1,0:T(8,128)(2,1)}, bf16[96,4096]{1,0:T(8,128)(2,1)}, u32[]{:S(2)}, u32[]{:S(2)}) collective-permute-start(bf16[96,4096]{1,0:T(8,128)(2,1)} %slice.7), channel_id=1, source_target_pairs={{0,3},{1,0},{2,1},{3,2},{4,7},{5,4},{6,5},{7,6},{8,11},{9,8},{10,9... | collective-permute-start | bytes 2359304 | tf_op jit(solution)/shard_map/ppermute | solution.py:257
  87.6 33.8 %all-to-all-start.1 = ((bf16[128,8,256]{2,1,0:T(8,128)(2,1)}), bf16[128,8,256]{2,1,0:T(8,128)(2,1)}, u32[]{:S(2)}, u32[]{:S(2)}) async-start(bf16[128,8,256]{2,1,0:T(8,128)(2,1)} %bitcast.11), calls=%async_computation.1 | async-start | bytes 1048576 | tf_op jit(solution)/shard_map/all_to_all | solution.py:267
  98.5 1.2 copy-start
  109.2 0.9 copy-start.7
  110.1 14.9 %collective-permute-start.7 = (bf16[832,256]{1,0:T(8,128)(2,1)}, bf16[832,256]{1,0:T(8,128)(2,1)S(1)}, u32[]{:S(2)}, u32[]{:S(2)}) collective-permute-start(bf16[832,256]{1,0:T(8,128)(2,1)} %get-tuple-element.32), channel_id=1, source_target_pairs={{0,1},{1,2},{2,3},{3,0},{4,5},{5,6},{6,7},{7,4},{8,9},{9,10},{10,1... | collective-permute-start | bytes 1277960 | tf_op jit(solution)/shard_map/ppermute | solution.py:257
  113.2 20.1 %collective-permute-start.8 = (bf16[832,256]{1,0:T(8,128)(2,1)S(1)}, bf16[832,256]{1,0:T(8,128)(2,1)S(1)}, u32[]{:S(2)}, u32[]{:S(2)}) collective-permute-start(bf16[832,256]{1,0:T(8,128)(2,1)S(1)} %get-tuple-element.33), channel_id=1, source_target_pairs={{0,2},{1,3},{2,0},{3,1},{4,6},{5,7},{6,4},{7,5},{8,10},{9,11},{10,... | collective-permute-start | bytes 1277960 | tf_op jit(solution)/shard_map/ppermute | solution.py:257
  118.3 16.2 %collective-permute-start.9 = (bf16[832,256]{1,0:T(8,128)(2,1)S(1)}, bf16[832,256]{1,0:T(8,128)(2,1)S(1)}, u32[]{:S(2)}, u32[]{:S(2)}) collective-permute-start(bf16[832,256]{1,0:T(8,128)(2,1)S(1)} %get-tuple-element.34), channel_id=1, source_target_pairs={{0,3},{1,0},{2,1},{3,2},{4,7},{5,4},{6,5},{7,6},{8,11},{9,8},{10,9... | collective-permute-start | bytes 1277960 | tf_op jit(solution)/shard_map/ppermute | solution.py:257
  134.5 0.9 copy-start.6
  135.4 1.1 copy-start.8
  139.5 12.5 %all-to-all-start.2 = ((bf16[4,448,128]{2,1,0:T(8,128)(2,1)}), bf16[4,448,128]{2,1,0:T(8,128)(2,1)S(1)}, u32[]{:S(2)}, u32[]{:S(2)}) async-start(bf16[4,448,128]{2,1,0:T(8,128)(2,1)} %get-tuple-element.39), calls=%async_computation.2 | async-start | bytes 917504 | tf_op jit(solution)/shard_map/all_to_all | solution.py:338

commit v8 on v7

--- a/solution.py
+++ b/solution.py
@@ -152,22 +152,18 @@
     shape = (256, 256)
     order = ones_where(iota(shape, 1) == 4 * (iota(shape, 0) % 64) + iota(shape, 0) // 64)
     for g in range(4):
-        got = dot(order, source[g * 256 : (g + 1) * 256, :]).astype(BF)
+        got = dot(order, source(slice(g * 256, (g + 1) * 256))).astype(BF)
         for b in range(4):
             put(b, slice(g * 64, (g + 1) * 64), got[b * 64 : (b + 1) * 64])
 
 
-def products(
-    pos_ref, rows_ref, weights_ref, gate_ref, cut_ref, own_ref, own_sum_ref, o1, o2, o3,
-    whole_ref, sum_ref,
-):
+def cut_products(pos_ref, rows_ref, weights_ref, cut_ref, own_ref, o1, o2, o3):
     x = pos_ref[0]
 
     def put(b, at, got):
-        whole_ref[at, b * SHARE : (b + 1) * SHARE] = got[:, :SHARE]
-        cut_ref[at, b * STRIP : (b + 1) * STRIP] = got[:, SHARE:]
-
-    unfold(rows_ref, put)
+        cut_ref[at, b * STRIP : (b + 1) * STRIP] = got
+
+    unfold(lambda at: rows_ref[at, SHARE:], put)
     cut = cut_ref[...]
     share = pl.ds(pl.multiple_of(x * SHARE, SHARE), SHARE)
     projected = dot(weights_ref[FFW:, share], cut, NT)
@@ -175,18 +171,25 @@
         base = lax.rem(x + k, REPS) * UNITS
         weights = weights_ref[pl.ds(pl.multiple_of(base, UNITS), UNITS), share]
         out[:UNITS, :] = dot(weights, cut, NT).astype(out.dtype)
-        out[UNITS : UNITS + R, :] = projected.astype(out.dtype)
+        out[UNITS:, :] = projected.astype(out.dtype)
+
+
+def whole_products(
+    pos_ref, rows_ref, weights_ref, gate_ref, own_ref, o1, o2, o3, whole_ref, sum_ref
+):
+    x = pos_ref[0]
+
+    def put(b, at, got):
+        whole_ref[at, b * SHARE : (b + 1) * SHARE] = got
+
+    unfold(lambda at: rows_ref[at, :SHARE], put)
     whole = whole_ref[...]
     both = dot(weights_ref[...], whole, NT)
     gate_ref[...] = both[:FFW]
     sum_ref[...] = dot(both[FFW:].astype(BF), whole)
-    own_sum_ref[...] = sum_ref[:, share]
-    for k, out in enumerate((o1, o2, o3)):
-        base = lax.rem(x + k + 1, REPS) * SHARE
-        for j in range(4):
-            columns = pl.ds(pl.multiple_of(base + j * 256, 256), 256)
-            start = UNITS + (1 + j) * R
-            out[start : start + R, :] = sum_ref[:, columns].astype(BF)
+    for k, out in enumerate((own_ref, o1, o2, o3)):
+        base = lax.rem(x + k, REPS) * SHARE
+        out[...] = sum_ref[:, pl.ds(pl.multiple_of(base, SHARE), SHARE)].astype(out.dtype)
 
 
 def gate_gradient(gate, grads):
@@ -203,7 +206,7 @@
     def put(b, at, got):
         grads_ref[b * SLOTS + at.start : b * SLOTS + at.stop, :] = got
 
-    unfold(got_ref, put)
+    unfold(lambda at: got_ref[at, :], put)
     same = ones_where(iota((STRIP, STRIP), 0) == iota((STRIP, STRIP), 1))
     turned = dot(same, grads_ref[...], NT)
     parts = [turned[:, b * SLOTS : (b + 1) * SLOTS] for b in range(4)]
@@ -229,18 +232,14 @@
         out_ref[to, UNITS + R :, :] = cut_projected[:, 128:].astype(BF)
 
 
-def finish_input(inverse_ref, cut_ref, own_sum_ref, s0, s1, s2, s3, out_ref):
+def finish_input(inverse_ref, cut_ref, s0, s1, s2, s3, i0, i1, i2, i3, out_ref):
     at = slice(UNITS, UNITS + R)
     projected = s0[at, :] + (
         s1[at, :].astype(F32) + s2[at, :].astype(F32) + s3[at, :].astype(F32)
     )
-    total = own_sum_ref[...] + dot(projected.astype(BF), cut_ref[...])
-    for j in range(4):
-        block = total[:, j * 256 : (j + 1) * 256]
-        start = UNITS + (1 + j) * R
-        for other in (s1, s2, s3):
-            block += other[start : start + R, :].astype(F32)
-        out_ref[j * 256 : (j + 1) * 256, :] = (block * inverse_ref[0]).T
+    total = i0[...] + dot(projected.astype(BF), cut_ref[...])
+    total += i1[...].astype(F32) + i2[...].astype(F32) + i3[...].astype(F32)
+    out_ref[...] = (total * inverse_ref[0]).T
 
 
 def finish_grad(pos_ref, inverse_ref, cut_grad_ref, own_ref, parts_ref, out_ref):
@@ -304,22 +303,25 @@
     )(pos, probes, own, right, top, bottom, left)
     got = to_owners(out_grads)
 
-    gate, cut, own_sums, own_inputs, *sums = kernel_call(
-        products,
-        [
-            sds((FFW, SLOTS), F32),
-            sds((SLOTS, SHARE), BF),
-            sds((UNITS + R, SLOTS), F32),
-            sds((R, SHARE), F32),
-        ]
-        + [sds((UNITS + 5 * R, SLOTS), BF)] * (REPS - 1),
+    kinds = [F32, BF, BF, BF]
+    cut, *sums = kernel_call(
+        cut_products,
+        [sds((SLOTS, SHARE), BF)] + [sds((UNITS + R, SLOTS), kind) for kind in kinds],
+        [SM] + [VM] * 2,
+        1 << 29,
+        4 << 20,
+        12,
+    )(pos, rows, weights)
+    sums = shifted(sums)
+    gate, *inputs = kernel_call(
+        whole_products,
+        [sds((FFW, SLOTS), F32)] + [sds((R, SHARE), kind) for kind in kinds],
         [SM] + [VM] * 2,
         3 << 30,
         14 << 20,
-        20,
+        16,
         [pltpu.VMEM((SLOTS, D), BF), pltpu.VMEM((R, D), F32)],
     )(pos, rows, weights)
-    sums = shifted([own_sums] + sums)
 
     mixed = UNITS + 2 * R
     cut_grad, own_sketch, sketch = kernel_call(
@@ -335,11 +337,13 @@
             pltpu.VMEM((FFW, SLOTS), BF),
         ],
     )(pos, grad_probes, gate, got, *sums)
+    *inputs, sketch = lax.optimization_barrier((*inputs, sketch))
+    inputs = shifted(inputs)
     parts = lax.all_to_all(sketch, "rep", split_axis=0, concat_axis=0, tiled=True)
 
     input_sketch = kernel_call(
-        finish_input, sds((SHARE, R), F32), [SM] + [VM] * 6, 1 << 27, 3 << 20, 8
-    )(inverse, cut, own_inputs, *sums)
+        finish_input, sds((SHARE, R), F32), [SM] + [VM] * 9, 1 << 27, 3 << 20, 8
+    )(inverse, cut, *sums, *inputs)
     grad_sketch = kernel_call(
         finish_grad, sds((UNITS, R), F32), [SM] * 2 + [VM] * 3, 1 << 24, 1 << 20, 6
     )(pos, inverse, cut_grad, own_sketch, parts)

time: 154 us -> 157 us (1.019)
  the two profiles are of different devices: /device:TPU:16 before, /device:TPU:10 now
where the time goes in v8:
time: 157 us; the launch traced here: 156 us
  starting transfers between devices  73.5 us (47%)
  waiting for transfers between devices  41 us (26%)
  Pallas kernels  21.8 us (14%)
  local copies, waits for them, and re-layouts  18.3 us (12%)
  between operations  1.57 us (1%)
    ppermute x13, starting transfers between devices, shift(): lax.ppermute(block, 'rep', [(i, (i + k) % REPS) for i in range(REPS)])  43.5 us
    ppermute x13, waiting for transfers between devices, shift(): lax.ppermute(block, 'rep', [(i, (i + k) % REPS) for i in range(REPS)])  34.7 us
    all_to_all x2, starting transfers between devices, to_owners(): lax.all_to_all(rows, 'ep', split_axis=0, concat_axis=0, tiled=True)  25.4 us
    unnamed x36, local copies, waits for them, and re-layouts  13.1 us
    all_to_all x2, waiting for transfers between devices, to_owners(): lax.all_to_all(rows, 'ep', split_axis=0, concat_axis=0, tiled=True)  6.32 us
    all_to_all x1, starting transfers between devices, local(): lax.all_to_all(sketch, 'rep', split_axis=0, concat_axis=0, tiled=True)  4.56 us
    pallas_call x1, Pallas kernels, local(): kernel_call(whole_products, [sds((FFW, SLOTS), F32)] + [sds((R, SHARE), k...  4.49 us
    pallas_call x1, Pallas kernels, local(): kernel_call(pick_grads, [sds((ROWS, STRIP), BF)] + [sds((SLOTS, STRIP), B...  3.91 us
  transfers between devices with their start and end apart: 16, of which 8 were waited for; matrix products, arithmetic and copies ran while one was open for 4% of the time, Pallas kernels for 10%

profile of v8, /device:TPU:10, one launch (start us, length us, event | category | flops | bytes accessed | tf_op | source)
XLA Modules:
  0.0 156.2 jit_solution(1815962409339033348)
XLA Ops:
  1.3 1.2 copy-done.8
  2.5 1.9 %shard_map.86 = bf16[1024,1280]{1,0:T(8,128)(2,1)S(1)} custom-call(s32[1]{0:T(128)} %bitcast.pos_ref, s32[8,128]{1,0:T(8,128)S(1)} %bitcast.18, bf16[128,4096]{1,0:T(8,128)(2,1)S(1)} %copy-done.8), custom_call_target="tpu_custom_call" | custom-call | flops 2147483648 | bytes 4194304 | tf_op jit(solution)/shard_map/pallas_call | solution.py:277
  4.5 1.5 copy-done
  6.0 17.5 %all-to-all-start = ((bf16[128,8,1280]{2,1,0:T(8,128)(2,1)}), bf16[128,8,1280]{2,1,0:T(8,128)(2,1)S(1)}, u32[]{:S(2)}, u32[]{:S(2)}) async-start(bf16[128,8,1280]{2,1,0:T(8,128)(2,1)} %bitcast.12), calls=%async_computation | async-start | bytes 5242880 | tf_op jit(solution)/shard_map/all_to_all | solution.py:266
  23.5 3.4 %collective-permute-start.3 = (bf16[192,4096]{1,0:T(8,128)(2,1)}, bf16[192,4096]{1,0:T(8,128)(2,1)}, u32[]{:S(2)}, u32[]{:S(2)}) collective-permute-start(bf16[192,4096]{1,0:T(8,128)(2,1)} %bitcast.13), channel_id=1, source_target_pairs={{0,1},{1,2},{2,3},{3,0},{4,5},{5,6},{6,7},{7,4},{8,9},{9,10},{10,1... | collective-permute-start | bytes 4718600 | tf_op jit(solution)/shard_map/ppermute | solution.py:256
  26.9 2.4 %collective-permute-start.4 = (bf16[192,4096]{1,0:T(8,128)(2,1)}, bf16[192,4096]{1,0:T(8,128)(2,1)}, u32[]{:S(2)}, u32[]{:S(2)}) collective-permute-start(bf16[192,4096]{1,0:T(8,128)(2,1)} %bitcast.14), channel_id=1, source_target_pairs={{0,3},{1,0},{2,1},{3,2},{4,7},{5,4},{6,5},{7,6},{8,11},{9,8},{10,9... | collective-permute-start | bytes 4718600 | tf_op jit(solution)/shard_map/ppermute | solution.py:256
  29.4 0.7 copy.11
  30.5 0.9 reshape.28.flat_ref
  31.4 3.9 %shard_map.87 = (bf16[1024,256]{1,0:T(8,128)(2,1)S(1)}, bf16[256,256]{1,0:T(8,128)(2,1)S(1)}, bf16[256,256]{1,0:T(8,128)(2,1)S(1)}, bf16[256,256]{1,0:T(8,128)(2,1)S(1)}, bf16[256,256]{1,0:T(8,128)(2,1)S(1)}) custom-call(s32[1]{0:T(128)} %bitcast.pos_ref, s32[8,128]{1,0:T(8,128)S(1)} %bitcast.19, s32[1,1024]{1,0:T(1,128)S(1)} %reshape.28.flat_ref, ...), custom_call_target="tpu_custom_call" | custom-call | flops 4294967296 | bytes 3145728 | tf_op jit(solution)/shard_map/pallas_call | solution.py:286
  35.4 3.4 %collective-permute-start = (bf16[256,256]{1,0:T(8,128)(2,1)S(1)}, bf16[256,256]{1,0:T(8,128)(2,1)S(1)}, u32[]{:S(2)}, u32[]{:S(2)}) collective-permute-start(bf16[256,256]{1,0:T(8,128)(2,1)S(1)} %get-tuple-element.32), channel_id=1, source_target_pairs={{0,1},{1,2},{2,3},{3,0},{4,5},{5,6},{6,7},{7,4},{8,9},{9,10},{10,1... | collective-permute-start | bytes 393224 | tf_op jit(solution)/shard_map/ppermute | solution.py:256
  38.8 4.2 %collective-permute-start.1 = (bf16[256,256]{1,0:T(8,128)(2,1)S(1)}, bf16[256,256]{1,0:T(8,128)(2,1)S(1)}, u32[]{:S(2)}, u32[]{:S(2)}) collective-permute-start(bf16[256,256]{1,0:T(8,128)(2,1)S(1)} %get-tuple-element.33), channel_id=1, source_target_pairs={{0,2},{1,3},{2,0},{3,1},{4,6},{5,7},{6,4},{7,5},{8,10},{9,11},{10,... | collective-permute-start | bytes 393224 | tf_op jit(solution)/shard_map/ppermute | solution.py:256
  43.0 2.8 %collective-permute-start.2 = (bf16[256,256]{1,0:T(8,128)(2,1)S(1)}, bf16[256,256]{1,0:T(8,128)(2,1)S(1)}, u32[]{:S(2)}, u32[]{:S(2)}) collective-permute-start(bf16[256,256]{1,0:T(8,128)(2,1)S(1)} %get-tuple-element.34), channel_id=1, source_target_pairs={{0,3},{1,0},{2,1},{3,2},{4,7},{5,4},{6,5},{7,6},{8,11},{9,8},{10,9... | collective-permute-start | bytes 393224 | tf_op jit(solution)/shard_map/ppermute | solution.py:256
  45.9 19.8 %collective-permute-done.g1 = bf16[256,256]{1,0:T(8,128)(2,1)S(1)} collective-permute-done((bf16[256,256]{1,0:T(8,128)(2,1)S(1)}, bf16[256,256]{1,0:T(8,128)(2,1)S(1)}, u32[]{:S(2)}, u32[]{:S(2)}) %collective-permute-start) | collective-permute-done | bytes 131104 | tf_op jit(solution)/shard_map/ppermute | solution.py:256
  65.6 4.1 %collective-permute-done.1.g2 = bf16[256,256]{1,0:T(8,128)(2,1)S(1)} collective-permute-done((bf16[256,256]{1,0:T(8,128)(2,1)S(1)}, bf16[256,256]{1,0:T(8,128)(2,1)S(1)}, u32[]{:S(2)}, u32[]{:S(2)}) %collective-permute-start.1) | collective-permute-done | bytes 131104 | tf_op jit(solution)/shard_map/ppermute | solution.py:256
  69.7 1.1 collective-permute-done.2.g3
  70.8 0.7 shard_map.88
  71.5 0.8 copy-done.3
  72.4 2.1 %slice.6 = bf16[96,4096]{1,0:T(8,128)(2,1)} slice(bf16[192,4096]{1,0:T(8,128)(2,1)} %collective-permute-done.3.left_ref), slice={[0:96], [0:4096]} | slice | bytes 1572864 | tf_op jit(solution)/shard_map/slice | solution.py:299
  74.4 3.1 %collective-permute-start.5 = (bf16[96,4096]{1,0:T(8,128)(2,1)}, bf16[96,4096]{1,0:T(8,128)(2,1)S(1)}, u32[]{:S(2)}, u32[]{:S(2)}) collective-permute-start(bf16[96,4096]{1,0:T(8,128)(2,1)} %slice.6), channel_id=1, source_target_pairs={{0,1},{1,2},{2,3},{3,0},{4,5},{5,6},{6,7},{7,4},{8,9},{9,10},{10,1... | collective-permute-start | bytes 2359304 | tf_op jit(solution)/shard_map/ppermute | solution.py:256
  77.5 2.2 %slice.7 = bf16[96,4096]{1,0:T(8,128)(2,1)} slice(bf16[192,4096]{1,0:T(8,128)(2,1)} %collective-permute-done.4.right_ref), slice={[96:192], [0:4096]} | slice | bytes 1572864 | tf_op jit(solution)/shard_map/slice | solution.py:300
  79.7 2.7 %collective-permute-start.6 = (bf16[96,4096]{1,0:T(8,128)(2,1)}, bf16[96,4096]{1,0:T(8,128)(2,1)}, u32[]{:S(2)}, u32[]{:S(2)}) collective-permute-start(bf16[96,4096]{1,0:T(8,128)(2,1)} %slice.7), channel_id=1, source_target_pairs={{0,3},{1,0},{2,1},{3,2},{4,7},{5,4},{6,5},{7,6},{8,11},{9,8},{10,9... | collective-permute-start | bytes 2359304 | tf_op jit(solution)/shard_map/ppermute | solution.py:256
  82.4 6.3 %all-to-all-done = bf16[128,8,1280]{2,1,0:T(8,128)(2,1)S(1)} async-done(((bf16[128,8,1280]{2,1,0:T(8,128)(2,1)}), bf16[128,8,1280]{2,1,0:T(8,128)(2,1)S(1)}, u32[]{:S(2)}, u32[]{:S(2)}) %all-to-all-start) | async-done | bytes 2621472 | tf_op jit(solution)/shard_map/all_to_all | solution.py:266
  88.7 7.9 %all-to-all-start.1 = ((bf16[128,8,256]{2,1,0:T(8,128)(2,1)}), bf16[128,8,256]{2,1,0:T(8,128)(2,1)}, u32[]{:S(2)}, u32[]{:S(2)}) async-start(bf16[128,8,256]{2,1,0:T(8,128)(2,1)} %bitcast.17), calls=%async_computation.1 | async-start | bytes 1048576 | tf_op jit(solution)/shard_map/all_to_all | solution.py:266
  96.6 3.4 %collective-permute-done.6.bottom_ref = bf16[96,4096]{1,0:T(8,128)(2,1)} collective-permute-done((bf16[96,4096]{1,0:T(8,128)(2,1)}, bf16[96,4096]{1,0:T(8,128)(2,1)}, u32[]{:S(2)}, u32[]{:S(2)}) %collective-permute-start.6) | collective-permute-done | bytes 786464 | tf_op jit(solution)/shard_map/ppermute | solution.py:256
  100.0 1.4 copy-done.1
  101.5 1.2 copy-done.2
  102.7 2.6 %shard_map.89.weights_ref = bf16[896,4096]{1,0:T(8,128)(2,1)S(1)} custom-call(s32[1]{0:T(128)} %bitcast.pos_ref, bf16[128,4096]{1,0:T(8,128)(2,1)S(1)} %copy-done.2, bf16[192,4096]{1,0:T(8,128)(2,1)S(1)} %bitcast.15, bf16[192,4096]{1,0:T(8,128)(2,1)} %collective-permute-done.4.right_ref, bf16[96,4096]{1,0:T(8,128)(2,1)S(1)} %collective-permute-done.5.top_ref, ...), custom_call_target="tpu_custom_call" | custom-call | flops 1000 | bytes 14680064 | tf_op jit(solution)/shard_map/pallas_call | solution.py:301
  105.3 1.9 %shard_map.90 = (bf16[256,1024]{1,0:T(8,128)(2,1)S(1)}, f32[320,256]{1,0:T(8,128)S(1)}, bf16[320,256]{1,0:T(8,128)(2,1)}, bf16[320,256]{1,0:T(8,128)(2,1)}, bf16[320,256]{1,0:T(8,128)(2,1)}) custom-call(s32[1]{0:T(128)} %bitcast.pos_ref, bf16[1024,1280]{1,0:T(8,128)(2,1)S(1)} %bitcast.10, bf16[896,4096]{1,0:T(8,128)(2,1)S(1)} %shard_map.89.weights_ref), custom_call_target="tpu_custom_call" | custom-call | flops 536870912 | bytes 4194304 | tf_op jit(solution)/shard_map/pallas_call | solution.py:307
  107.2 3.6 %collective-permute-start.7 = (bf16[320,256]{1,0:T(8,128)(2,1)}, bf16[320,256]{1,0:T(8,128)(2,1)}, u32[]{:S(2)}, u32[]{:S(2)}) collective-permute-start(bf16[320,256]{1,0:T(8,128)(2,1)} %get-tuple-element.39), channel_id=1, source_target_pairs={{0,1},{1,2},{2,3},{3,0},{4,5},{5,6},{6,7},{7,4},{8,9},{9,10},{10,1... | collective-permute-start | bytes 491528 | tf_op jit(solution)/shard_map/ppermute | solution.py:256
  110.8 3.1 %collective-permute-start.8 = (bf16[320,256]{1,0:T(8,128)(2,1)}, bf16[320,256]{1,0:T(8,128)(2,1)}, u32[]{:S(2)}, u32[]{:S(2)}) collective-permute-start(bf16[320,256]{1,0:T(8,128)(2,1)} %get-tuple-element.40), channel_id=1, source_target_pairs={{0,2},{1,3},{2,0},{3,1},{4,6},{5,7},{6,4},{7,5},{8,10},{9,11},{10,... | collective-permute-start | bytes 491528 | tf_op jit(solution)/shard_map/ppermute | solution.py:256
  113.8 4.3 %collective-permute-start.9 = (bf16[320,256]{1,0:T(8,128)(2,1)}, bf16[320,256]{1,0:T(8,128)(2,1)}, u32[]{:S(2)}, u32[]{:S(2)}) collective-permute-start(bf16[320,256]{1,0:T(8,128)(2,1)} %get-tuple-element.41), channel_id=1, source_target_pairs={{0,3},{1,0},{2,1},{3,2},{4,7},{5,4},{6,5},{7,6},{8,11},{9,8},{10,9... | collective-permute-start | bytes 491528 | tf_op jit(solution)/shard_map/ppermute | solution.py:256
  118.2 4.5 %shard_map.91 = (f32[768,256]{1,0:T(8,128)S(1)}, f32[128,1024]{1,0:T(8,128)S(1)}, bf16[128,1024]{1,0:T(8,128)(2,1)}, bf16[128,1024]{1,0:T(8,128)(2,1)S(1)}, bf16[128,1024]{1,0:T(8,128)(2,1)S(1)}) custom-call(s32[1]{0:T(128)} %bitcast.pos_ref, bf16[1024,1280]{1,0:T(8,128)(2,1)S(1)} %bitcast.11, bf16[896,4096]{1,0:T(8,128)(2,1)S(1)} %shard_map.89.weights_ref), custom_call_target="tpu_custom_call" | custom-call | flops 3221225472 | bytes 14680064 | tf_op jit(solution)/shard_map/pallas_call | solution.py:316
  122.7 0.8 copy-done.4
  123.4 0.7 copy-done.9
  124.1 0.7 copy-done.11
  124.8 0.9 copy-done.14
  125.8 0.9 copy-done.13
  126.7 1.1 copy-done.15
  127.8 3.2 %shard_map.92 = (bf16[192,256]{1,0:T(8,128)(2,1)S(1)}, f32[448,128]{1,0:T(8,128)S(1)}, bf16[4,448,128]{2,1,0:T(8,128)(2,1)}) custom-call(s32[1]{0:T(128)} %bitcast.pos_ref, bf16[128,768]{1,0:T(8,128)(2,1)S(1)} %copy-done.13, f32[768,256]{1,0:T(8,128)S(1)} %copy-done.15, bf16[1024,256]{1,0:T(8,128)(2,1)} %bitcast.7.got_ref, ...), custom_call_target="tpu_custom_call" | custom-call | flops 2147483648 | bytes 4194304 | tf_op jit(solution)/shard_map/pallas_call | solution.py:327
  131.0 4.6 %all-to-all-start.2 = ((bf16[4,448,128]{2,1,0:T(8,128)(2,1)}), bf16[4,448,128]{2,1,0:T(8,128)(2,1)S(1)}, u32[]{:S(2)}, u32[]{:S(2)}) async-start(bf16[4,448,128]{2,1,0:T(8,128)(2,1)} %get-tuple-element.55), calls=%async_computation.2 | async-start | bytes 917504 | tf_op jit(solution)/shard_map/all_to_all | solution.py:342
  135.6 3.4 %collective-permute-start.10 = (bf16[128,1024]{1,0:T(8,128)(2,1)}, bf16[128,1024]{1,0:T(8,128)(2,1)S(1)}, u32[]{:S(2)}, u32[]{:S(2)}) collective-permute-start(bf16[128,1024]{1,0:T(8,128)(2,1)} %get-tuple-element.50), channel_id=1, source_target_pairs={{0,1},{1,2},{2,3},{3,0},{4,5},{5,6},{6,7},{7,4},{8,9},{9,10},{10,1... | collective-permute-start | bytes 786440 | tf_op jit(solution)/shard_map/ppermute | solution.py:256
  139.0 2.6 %collective-permute-start.11 = (bf16[128,1024]{1,0:T(8,128)(2,1)S(1)}, bf16[128,1024]{1,0:T(8,128)(2,1)S(1)}, u32[]{:S(2)}, u32[]{:S(2)}) collective-permute-start(bf16[128,1024]{1,0:T(8,128)(2,1)S(1)} %copy-done.12), channel_id=1, source_target_pairs={{0,2},{1,3},{2,0},{3,1},{4,6},{5,7},{6,4},{7,5},{8,10},{9,11},{10,... | collective-permute-start | bytes 786440 | tf_op jit(solution)/shard_map/ppermute | solution.py:256
  141.5 4.5 %collective-permute-start.12 = (bf16[128,1024]{1,0:T(8,128)(2,1)S(1)}, bf16[128,1024]{1,0:T(8,128)(2,1)S(1)}, u32[]{:S(2)}, u32[]{:S(2)}) collective-permute-start(bf16[128,1024]{1,0:T(8,128)(2,1)S(1)} %copy-done.10), channel_id=1, source_target_pairs={{0,3},{1,0},{2,1},{3,2},{4,7},{5,4},{6,5},{7,6},{8,11},{9,8},{10,9... | collective-permute-start | bytes 786440 | tf_op jit(solution)/shard_map/ppermute | solution.py:256
  146.7 1.1 collective-permute-done.10.i1
  147.8 2.6 %collective-permute-done.11.i2 = bf16[128,1024]{1,0:T(8,128)(2,1)S(1)} collective-permute-done((bf16[128,1024]{1,0:T(8,128)(2,1)S(1)}, bf16[128,1024]{1,0:T(8,128)(2,1)S(1)}, u32[]{:S(2)}, u32[]{:S(2)}) %collective-permute-start.11) | collective-permute-done | bytes 262176 | tf_op jit(solution)/shard_map/ppermute | solution.py:256
  150.4 2.7 %collective-permute-done.12.i3 = bf16[128,1024]{1,0:T(8,128)(2,1)S(1)} collective-permute-done((bf16[128,1024]{1,0:T(8,128)(2,1)S(1)}, bf16[128,1024]{1,0:T(8,128)(2,1)S(1)}, u32[]{:S(2)}, u32[]{:S(2)}) %collective-permute-start.12) | collective-permute-done | bytes 262176 | tf_op jit(solution)/shard_map/ppermute | solution.py:256
  153.1 2.2 %shard_map.93 = f32[1024,128]{1,0:T(8,128)} custom-call(f32[1]{0:T(128)S(6)} %div.3.inverse_ref, bf16[256,1024]{1,0:T(8,128)(2,1)S(1)} %get-tuple-element.37.cut_ref, f32[320,256]{1,0:T(8,128)S(1)} %get-tuple-element.38.s0, bf16[320,256]{1,0:T(8,128)(2,1)} %collective-permute-done.7.s1, bf16[320,256]{1,0:T(8,128)(2,1)} %collective-permute-done.8.s2, ...), custom_call_target="tpu_custom_call" | custom-call | flops 134217728 | bytes 3145728 | tf_op jit(solution)/shard_map/pallas_call | solution.py:344
  155.3 0.8 shard_map.94
  (32 shorter events, 1.1 us)
Async XLA Ops:
  0.6 0.7 copy-start.6
  1.3 1.2 copy-start.8
  4.5 1.5 copy-start
  6.0 23.4 %copy-start.7 = (s32[128,8]{0,1:T(8,128)S(1)}, s32[128,8]{0,1:T(8,128)}, u32[]{:S(2)}) copy-start(s32[128,8]{0,1:T(8,128)} %param.8) | copy-start | bytes 12292
  6.0 24.1 %copy-start.16 = (bf16[128,8,192]{0,2,1:T(8,128)(2,1)S(1)}, bf16[128,8,192]{0,2,1:T(8,128)(2,1)}, u32[]{:S(2)}) copy-start(bf16[128,8,192]{0,2,1:T(8,128)(2,1)} %param.9) | copy-start | bytes 1179652
  6.0 82.8 %all-to-all-start = ((bf16[128,8,1280]{2,1,0:T(8,128)(2,1)}), bf16[128,8,1280]{2,1,0:T(8,128)(2,1)S(1)}, u32[]{:S(2)}, u32[]{:S(2)}) async-start(bf16[128,8,1280]{2,1,0:T(8,128)(2,1)} %bitcast.12), calls=%async_computation | async-start | bytes 5242880 | tf_op jit(solution)/shard_map/all_to_all | solution.py:266
  23.5 48.9 %collective-permute-start.3 = (bf16[192,4096]{1,0:T(8,128)(2,1)}, bf16[192,4096]{1,0:T(8,128)(2,1)}, u32[]{:S(2)}, u32[]{:S(2)}) collective-permute-start(bf16[192,4096]{1,0:T(8,128)(2,1)} %bitcast.13), channel_id=1, source_target_pairs={{0,1},{1,2},{2,3},{3,0},{4,5},{5,6},{6,7},{7,4},{8,9},{9,10},{10,1... | collective-permute-start | bytes 4718600 | tf_op jit(solution)/shard_map/ppermute | solution.py:256
  26.9 45.5 %collective-permute-start.4 = (bf16[192,4096]{1,0:T(8,128)(2,1)}, bf16[192,4096]{1,0:T(8,128)(2,1)}, u32[]{:S(2)}, u32[]{:S(2)}) collective-permute-start(bf16[192,4096]{1,0:T(8,128)(2,1)} %bitcast.14), channel_id=1, source_target_pairs={{0,3},{1,0},{2,1},{3,2},{4,7},{5,4},{6,5},{7,6},{8,11},{9,8},{10,9... | collective-permute-start | bytes 4718600 | tf_op jit(solution)/shard_map/ppermute | solution.py:256
  35.4 30.3 %collective-permute-start = (bf16[256,256]{1,0:T(8,128)(2,1)S(1)}, bf16[256,256]{1,0:T(8,128)(2,1)S(1)}, u32[]{:S(2)}, u32[]{:S(2)}) collective-permute-start(bf16[256,256]{1,0:T(8,128)(2,1)S(1)} %get-tuple-element.32), channel_id=1, source_target_pairs={{0,1},{1,2},{2,3},{3,0},{4,5},{5,6},{6,7},{7,4},{8,9},{9,10},{10,1... | collective-permute-start | bytes 393224 | tf_op jit(solution)/shard_map/ppermute | solution.py:256
  38.8 31.0 %collective-permute-start.1 = (bf16[256,256]{1,0:T(8,128)(2,1)S(1)}, bf16[256,256]{1,0:T(8,128)(2,1)S(1)}, u32[]{:S(2)}, u32[]{:S(2)}) collective-permute-start(bf16[256,256]{1,0:T(8,128)(2,1)S(1)} %get-tuple-element.33), channel_id=1, source_target_pairs={{0,2},{1,3},{2,0},{3,1},{4,6},{5,7},{6,4},{7,5},{8,10},{9,11},{10,... | collective-permute-start | bytes 393224 | tf_op jit(solution)/shard_map/ppermute | solution.py:256
  43.0 27.8 %collective-permute-start.2 = (bf16[256,256]{1,0:T(8,128)(2,1)S(1)}, bf16[256,256]{1,0:T(8,128)(2,1)S(1)}, u32[]{:S(2)}, u32[]{:S(2)}) collective-permute-start(bf16[256,256]{1,0:T(8,128)(2,1)S(1)} %get-tuple-element.34), channel_id=1, source_target_pairs={{0,3},{1,0},{2,1},{3,2},{4,7},{5,4},{6,5},{7,6},{8,11},{9,8},{10,9... | collective-permute-start | bytes 393224 | tf_op jit(solution)/shard_map/ppermute | solution.py:256
  71.5 0.9 copy-start.3
  74.4 22.2 %collective-permute-start.5 = (bf16[96,4096]{1,0:T(8,128)(2,1)}, bf16[96,4096]{1,0:T(8,128)(2,1)S(1)}, u32[]{:S(2)}, u32[]{:S(2)}) collective-permute-start(bf16[96,4096]{1,0:T(8,128)(2,1)} %slice.6), channel_id=1, source_target_pairs={{0,1},{1,2},{2,3},{3,0},{4,5},{5,6},{6,7},{7,4},{8,9},{9,10},{10,1... | collective-permute-start | bytes 2359304 | tf_op jit(solution)/shard_map/ppermute | solution.py:256
  79.7 20.4 %collective-permute-start.6 = (bf16[96,4096]{1,0:T(8,128)(2,1)}, bf16[96,4096]{1,0:T(8,128)(2,1)}, u32[]{:S(2)}, u32[]{:S(2)}) collective-permute-start(bf16[96,4096]{1,0:T(8,128)(2,1)} %slice.7), channel_id=1, source_target_pairs={{0,3},{1,0},{2,1},{3,2},{4,7},{5,4},{6,5},{7,6},{8,11},{9,8},{10,9... | collective-permute-start | bytes 2359304 | tf_op jit(solution)/shard_map/ppermute | solution.py:256
  88.7 37.0 %all-to-all-start.1 = ((bf16[128,8,256]{2,1,0:T(8,128)(2,1)}), bf16[128,8,256]{2,1,0:T(8,128)(2,1)}, u32[]{:S(2)}, u32[]{:S(2)}) async-start(bf16[128,8,256]{2,1,0:T(8,128)(2,1)} %bitcast.17), calls=%async_computation.1 | async-start | bytes 1048576 | tf_op jit(solution)/shard_map/all_to_all | solution.py:266
  100.0 1.4 copy-start.1
  101.4 1.2 copy-start.2
  107.2 18.6 %collective-permute-start.7 = (bf16[320,256]{1,0:T(8,128)(2,1)}, bf16[320,256]{1,0:T(8,128)(2,1)}, u32[]{:S(2)}, u32[]{:S(2)}) collective-permute-start(bf16[320,256]{1,0:T(8,128)(2,1)} %get-tuple-element.39), channel_id=1, source_target_pairs={{0,1},{1,2},{2,3},{3,0},{4,5},{5,6},{6,7},{7,4},{8,9},{9,10},{10,1... | collective-permute-start | bytes 491528 | tf_op jit(solution)/shard_map/ppermute | solution.py:256
  110.8 15.0 %collective-permute-start.8 = (bf16[320,256]{1,0:T(8,128)(2,1)}, bf16[320,256]{1,0:T(8,128)(2,1)}, u32[]{:S(2)}, u32[]{:S(2)}) collective-permute-start(bf16[320,256]{1,0:T(8,128)(2,1)} %get-tuple-element.40), channel_id=1, source_target_pairs={{0,2},{1,3},{2,0},{3,1},{4,6},{5,7},{6,4},{7,5},{8,10},{9,11},{10,... | collective-permute-start | bytes 491528 | tf_op jit(solution)/shard_map/ppermute | solution.py:256
  113.8 11.9 %collective-permute-start.9 = (bf16[320,256]{1,0:T(8,128)(2,1)}, bf16[320,256]{1,0:T(8,128)(2,1)}, u32[]{:S(2)}, u32[]{:S(2)}) collective-permute-start(bf16[320,256]{1,0:T(8,128)(2,1)} %get-tuple-element.41), channel_id=1, source_target_pairs={{0,3},{1,0},{2,1},{3,2},{4,7},{5,4},{6,5},{7,6},{8,11},{9,8},{10,9... | collective-permute-start | bytes 491528 | tf_op jit(solution)/shard_map/ppermute | solution.py:256
  122.7 0.8 copy-start.4
  123.4 0.7 copy-start.9
  124.1 0.7 copy-start.11
  124.8 0.9 copy-start.14
  125.8 0.9 copy-start.13
  126.7 1.1 copy-start.15
  127.8 11.1 %copy-start.12 = (bf16[128,1024]{1,0:T(8,128)(2,1)S(1)}, bf16[128,1024]{1,0:T(8,128)(2,1)}, u32[]{:S(2)}) copy-start(bf16[128,1024]{1,0:T(8,128)(2,1)} %copy-done.11) | copy-start | bytes 786436
  127.8 13.7 %copy-start.10 = (bf16[128,1024]{1,0:T(8,128)(2,1)S(1)}, bf16[128,1024]{1,0:T(8,128)(2,1)}, u32[]{:S(2)}) copy-start(bf16[128,1024]{1,0:T(8,128)(2,1)} %copy-done.9) | copy-start | bytes 786436
  127.8 25.3 %copy-start.5 = (f32[128,1024]{1,0:T(8,128)S(1)}, f32[128,1024]{1,0:T(8,128)}, u32[]{:S(2)}) copy-start(f32[128,1024]{1,0:T(8,128)} %copy-done.4) | copy-start | bytes 1572868
  131.0 24.3 %all-to-all-start.2 = ((bf16[4,448,128]{2,1,0:T(8,128)(2,1)}), bf16[4,448,128]{2,1,0:T(8,128)(2,1)S(1)}, u32[]{:S(2)}, u32[]{:S(2)}) async-start(bf16[4,448,128]{2,1,0:T(8,128)(2,1)} %get-tuple-element.55), calls=%async_computation.2 | async-start | bytes 917504 | tf_op jit(solution)/shard_map/all_to_all | solution.py:342
  135.6 12.2 %collective-permute-start.10 = (bf16[128,1024]{1,0:T(8,128)(2,1)}, bf16[128,1024]{1,0:T(8,128)(2,1)S(1)}, u32[]{:S(2)}, u32[]{:S(2)}) collective-permute-start(bf16[128,1024]{1,0:T(8,128)(2,1)} %get-tuple-element.50), channel_id=1, source_target_pairs={{0,1},{1,2},{2,3},{3,0},{4,5},{5,6},{6,7},{7,4},{8,9},{9,10},{10,1... | collective-permute-start | bytes 786440 | tf_op jit(solution)/shard_map/ppermute | solution.py:256
  139.0 11.5 %collective-permute-start.11 = (bf16[128,1024]{1,0:T(8,128)(2,1)S(1)}, bf16[128,1024]{1,0:T(8,128)(2,1)S(1)}, u32[]{:S(2)}, u32[]{:S(2)}) collective-permute-start(bf16[128,1024]{1,0:T(8,128)(2,1)S(1)} %copy-done.12), channel_id=1, source_target_pairs={{0,2},{1,3},{2,0},{3,1},{4,6},{5,7},{6,4},{7,5},{8,10},{9,11},{10,... | collective-permute-start | bytes 786440 | tf_op jit(solution)/shard_map/ppermute | solution.py:256
  141.5 11.6 %collective-permute-start.12 = (bf16[128,1024]{1,0:T(8,128)(2,1)S(1)}, bf16[128,1024]{1,0:T(8,128)(2,1)S(1)}, u32[]{:S(2)}, u32[]{:S(2)}) collective-permute-start(bf16[128,1024]{1,0:T(8,128)(2,1)S(1)} %copy-done.10), channel_id=1, source_target_pairs={{0,3},{1,0},{2,1},{3,2},{4,7},{5,4},{6,5},{7,6},{8,11},{9,8},{10,9... | collective-permute-start | bytes 786440 | tf_op jit(solution)/shard_map/ppermute | solution.py:256

commit v9 on v4

--- a/solution.py
+++ b/solution.py
@@ -95,7 +95,7 @@
     return other_ref[TOK:, :TOK].astype(F32)[:TOP].astype(jnp.int32)
 
 
-def send_rows(pos_ref, ids_ref, tokens_ref, other_ref, out_ref, half_ref, half_ids_ref):
+def send_rows(pos_ref, ids_ref, tokens_ref, other_ref, out_ref, half_ref, half_ids_ref, fold_ref):
     x, c = pos_ref[0], pos_ref[1]
     mine = x // 2 == c
     table = spread(places(ids_ref[...]), FOLD)
@@ -115,11 +115,14 @@
         half_ref[...] = other_ref[:TOK, :]
         half_ids_ref[...] = other_ids(other_ref)
 
-    table = spread(places(half_ids_ref[...]), FOLD)
-    shared = table == (FIRST + x % 2).astype(F32)
-    picks = jnp.concatenate([ones_where(shared & (row % 8 == b)) for b in range(8)], 1)
-    parts = jnp.concatenate([half_ref[:, b * STRIP : (b + 1) * STRIP] for b in range(8)], 0)
-    out_ref[:, SHARE:] = dot(picks, parts).astype(BF)
+    picks = ones_where(places(half_ids_ref[...]) == (FIRST + x % 2).astype(F32))
+    rows = dot(picks, half_ref[...])
+    for b in range(FOLD):
+        for h in range(2):
+            start = b * STRIP + h * 128
+            fold_ref[h, pl.ds(b, OWNERS, stride=FOLD), :] = rows[:, start : start + 128]
+    for h in range(2):
+        out_ref[:, SHARE + h * 128 : SHARE + (h + 1) * 128] = fold_ref[h].astype(BF)
 
 
 def pick_grads(pos_ref, ids_ref, other_ref, grads_ref, other_grads_ref, *outs):
@@ -143,21 +146,26 @@
         ).astype(BF)
 
 
-def fold_grads(pos_ref, g0, g1, g2, g3, out_ref):
+def fold_grads(pos_ref, g0, g1, g2, g3, out_ref, fold_ref):
     x, c = pos_ref[0], pos_ref[1]
-    row, column = iota((ROWS, SLOTS), 0), iota((ROWS, SLOTS), 1)
-    total = jnp.zeros((ROWS, 256), F32)
     for k, got in enumerate((g0, g1, g2, g3)):
         unit = lax.rem(x - k + REPS, REPS)
-        total += dot(ones_where((row // 4 == column) & (row % 4 == unit)), got[:SLOTS, :])
-        for u in range(3):
-            at = jnp.where(unit // 2 == c, unit % 2 * 3 + u, -1)
-            source, lane = iota((256, 256), 0), iota((256, 256), 1)
-            move = ones_where((source // 64 == u) & (lane == UNITS + source % 64))
-            moved = dot(got[SLOTS:, :], move).astype(BF)
-            row5, column5 = iota((ROWS, OWNERS), 0), iota((ROWS, OWNERS), 1)
-            total += dot(ones_where((row5 // 8 == column5) & (row5 % 8 == at)), moved)
-    out_ref[...] = total.astype(BF)
+        for h in range(2):
+            block = got[:SLOTS, h * 128 : (h + 1) * 128].astype(F32)
+            fold_ref[h, pl.ds(unit, SLOTS, stride=4), :] = block
+    for k, got in enumerate((g0, g1, g2, g3)):
+        unit = lax.rem(x - k + REPS, REPS)
+
+        @pl.when(unit // 2 == c)
+        def _():
+            source, lane = iota((256, 128), 0), iota((256, 128), 1)
+            for u in range(3):
+                move = ones_where((source // 64 == u) & (lane == 64 + source % 64))
+                at = pl.ds(unit % 2 * 3 + u, OWNERS, stride=FOLD)
+                fold_ref[1, at, :] = fold_ref[1, at, :] + dot(got[SLOTS:, :], move)
+
+    for h in range(2):
+        out_ref[:, h * 128 : (h + 1) * 128] = fold_ref[h].astype(BF)
 
 
 def regroup(source, many, put):
@@ -171,27 +179,8 @@
             put(p, slice(g * size, (g + 1) * size), got[p * size : (p + 1) * size])
 
 
-def products(
-    pos_ref, rows_ref, probes_ref, own_ref, right_ref, top_ref, bottom_ref, left_ref,
-    gate_ref, i0, i1, i2, i3, rows_all_ref, sum_ref,
-):
+def stack_weights(pos_ref, probes_ref, own_ref, right_ref, top_ref, bottom_ref, left_ref, out_ref):
     x = pos_ref[0]
-
-    def put_whole(p, at, got):
-        rows_all_ref[at, p * SHARE : (p + 1) * SHARE] = got
-
-    def put_shared(p, at, got):
-        rows_all_ref[SLOTS + at.start : SLOTS + at.stop, p * STRIP : (p + 1) * STRIP] = got
-
-    regroup(lambda at: rows_ref[at, :SHARE], 4, put_whole)
-    regroup(lambda at: rows_ref[at, SHARE:], 16, put_shared)
-    rows_all_ref[SLOTS + PAIRS :, :] = jnp.zeros((ALL - SLOTS - PAIRS, D), BF)
-    rows = rows_all_ref[...]
-    projected = dot(probes_ref[...], rows, NT).astype(BF)
-    sum_ref[...] = dot(projected, rows)
-    for k, out in enumerate((i0, i1, i2, i3)):
-        base = lax.rem(x + k, REPS) * SHARE
-        out[...] = sum_ref[:, pl.ds(pl.multiple_of(base, SHARE), SHARE)].astype(out.dtype)
     half = UNITS // 2
     for w, k, start, size in (
         (own_ref, 0, 0, UNITS),
@@ -201,11 +190,35 @@
         (left_ref, 3, 0, UNITS),
     ):
         base = lax.rem(x + k, REPS) * UNITS + start
-        gate_ref[pl.ds(pl.multiple_of(base, half), size), :] = dot(w[...], rows, NT)
+        out_ref[pl.ds(pl.multiple_of(base, half), size), :] = w[...]
+    out_ref[FFW:, :] = probes_ref[...]
+
+
+def products(
+    pos_ref, rows_ref, weights_ref, gate_ref, i0, i1, i2, i3, rows_all_ref, sum_ref
+):
+    x = pos_ref[0]
+
+    def put_whole(p, at, got):
+        rows_all_ref[at, p * SHARE : (p + 1) * SHARE] = got
+
+    def put_shared(p, at, got):
+        rows_all_ref[SLOTS + at.start : SLOTS + at.stop, p * STRIP : (p + 1) * STRIP] = got
+
+    regroup(lambda at: rows_ref[at, :SHARE], 4, put_whole)
+    regroup(lambda at: rows_ref[at, SHARE:], 16, put_shared)
+    rows_all_ref[SLOTS + PAIRS :, :] = jnp.zeros((ALL - SLOTS - PAIRS, D), BF)
+    rows = rows_all_ref[...]
+    both = dot(weights_ref[...], rows, NT)
+    gate_ref[...] = both[:FFW]
+    sum_ref[...] = dot(both[FFW:].astype(BF), rows)
+    for k, out in enumerate((i0, i1, i2, i3)):
+        base = lax.rem(x + k, REPS) * SHARE
+        out[...] = sum_ref[:, pl.ds(pl.multiple_of(base, SHARE), SHARE)].astype(out.dtype)
 
 
 def gate_part(
-    pos_ref, grad_probes_ref, gate_ref, got_ref, t0, t1, t2, t3,
+    pos_ref, grad_probes_ref, gate_ref, got_ref, own_ref, out_ref,
     whole_ref, shared_ref, sketch_ref,
 ):
     x = pos_ref[0]
@@ -236,9 +249,8 @@
     gate_grad = (grads * (s * (1.0 + gate * (1.0 - s)))).astype(BF)
     projected = dot(grad_probes_ref[...], gate_grad).astype(BF)
     sketch_ref[...] = dot(gate_grad, projected, NT)
-    for k, out in enumerate((t0, t1, t2, t3)):
-        base = lax.rem(x + k, REPS) * UNITS
-        out[...] = sketch_ref[pl.ds(pl.multiple_of(base, UNITS), UNITS), :].astype(out.dtype)
+    out_ref[...] = sketch_ref[...].astype(BF)
+    own_ref[...] = sketch_ref[pl.ds(pl.multiple_of(x * UNITS, UNITS), UNITS), :]
 
 
 def finish_input(inverse_ref, i0, i1, i2, i3, out_ref):
@@ -246,8 +258,10 @@
     out_ref[...] = (total * inverse_ref[0]).T
 
 
-def finish_grad(inverse_ref, t0, t1, t2, t3, out_ref):
-    total = t0[...] + (t1[...].astype(F32) + t2[...].astype(F32) + t3[...].astype(F32))
+def finish_grad(pos_ref, inverse_ref, own_ref, parts_ref, out_ref):
+    total = own_ref[...]
+    for k in range(1, REPS):
+        total += parts_ref[lax.rem(pos_ref[0] + k, REPS)].astype(F32)
     out_ref[...] = total * inverse_ref[0]
 
 
@@ -295,7 +309,11 @@
         1 << 31,
         5 * MIB,
         20,
-        [pltpu.VMEM((TOK, HALF), BF), pltpu.VMEM((TOP, TOK), jnp.int32)],
+        [
+            pltpu.VMEM((TOK, HALF), BF),
+            pltpu.VMEM((TOP, TOK), jnp.int32),
+            pltpu.VMEM((2, ROWS, 128), F32),
+        ],
     )(pos, ids_t, tokens, other)
     rows = to_owners(out_rows)
 
@@ -306,43 +324,54 @@
     picked = kernel_call(
         pick_grads, [sds((SLOTS + OWNERS, 256), BF)] * REPS, [SM] + [VM] * 4, 5 << 30, 3 * MIB, 20
     )(pos, ids_t, other, grads, other_grads)
-    out_grads = kernel_call(
-        fold_grads, sds((ROWS, 256), BF), [SM] + [VM] * 4, 1 << 31, 3 * MIB, 12
-    )(pos, *shifted(picked))
-    out_grads, left, right = lax.optimization_barrier((out_grads, left, right))
+    left, right, _ = lax.optimization_barrier((left, right, picked[1]))
     top = shift(left[: UNITS // 2], 1)
     bottom = shift(right[UNITS // 2 :], REPS - 1)
+    out_grads = kernel_call(
+        fold_grads,
+        sds((ROWS, 256), BF),
+        [SM] + [VM] * 4,
+        1 << 27,
+        3 * MIB,
+        8,
+        [pltpu.VMEM((2, ROWS, 128), F32)],
+    )(pos, *shifted(picked))
+    weights = kernel_call(
+        stack_weights, sds((FFW + R, D), BF), [SM] + [VM] * 6, 1000, 14 * MIB, 8
+    )(pos, probes, own, right, top, bottom, left)
     got = to_owners(out_grads)
 
     kinds = [F32, BF, BF, BF]
     gate, *inputs = kernel_call(
         products,
         [sds((FFW, ALL), F32)] + [sds((R, SHARE), kind) for kind in kinds],
-        [SM] + [VM] * 7,
+        [SM] + [VM] * 2,
         4 << 30,
         12 * MIB,
-        16,
+        20,
         [pltpu.VMEM((ALL, D), BF), pltpu.VMEM((R, D), F32)],
-    )(pos, rows, probes, own, right, top, bottom, left)
+    )(pos, rows, weights)
     inputs = shifted(inputs)
 
-    sketches = kernel_call(
+    own_sketch, sketch = kernel_call(
         gate_part,
-        [sds((UNITS, R), kind) for kind in kinds],
+        [sds((UNITS, R), F32), sds((FFW, R), BF)],
         [SM] + [VM] * 3,
         1 << 30,
         3 * MIB,
         14,
         [pltpu.VMEM((ROWS, 256), BF), pltpu.VMEM((ROWS, 256), BF), pltpu.VMEM((FFW, R), F32)],
     )(pos, grad_probes, gate, got)
-    sketches = shifted(sketches)
+    sketches = lax.all_to_all(
+        sketch.reshape(REPS, UNITS, R), "rep", split_axis=0, concat_axis=0, tiled=True
+    )
 
     input_sketch = kernel_call(
         finish_input, sds((SHARE, R), F32), [SM] + [VM] * 4, 1 << 20, 2 * MIB, 6
     )(inverse, *inputs)
     grad_sketch = kernel_call(
-        finish_grad, sds((UNITS, R), F32), [SM] + [VM] * 4, 1 << 18, MIB // 4, 4
-    )(inverse, *sketches)
+        finish_grad, sds((UNITS, R), F32), [SM] * 2 + [VM] * 2, 1 << 18, MIB // 4, 4
+    )(pos, inverse, own_sketch, sketches)
     return input_sketch[None], grad_sketch[None]
 
 

time: 162 us -> 141 us (0.87)
  starting transfers between devices: 79.5 us -> 67.5 us
  local copies, waits for them, and re-layouts: 16.6 us -> 11.5 us
  Pallas kernels: 26.9 us -> 23.6 us
    ppermute x13 -> x10, waiting for transfers between devices: 32.1 us -> 20.5 us  [shift(): lax.ppermute(block, 'rep', [(i, (i + k) % REPS) for i in range(REPS)])]
    ppermute x13 -> x10, starting transfers between devices: 44.3 us -> 34.2 us  [shift(): lax.ppermute(block, 'rep', [(i, (i + k) % REPS) for i in range(REPS)])]
    all_to_all x2, waiting for transfers between devices: 0.01 us -> 6 us  [to_owners(): lax.all_to_all(rows, 'ep', split_axis=0, concat_axis=0, tiled=True)]
    all_to_all x0 -> x1, waiting for transfers between devices: none -> 5.6 us  [local(): lax.all_to_all(sketch.reshape(REPS, UNITS, R), 'rep', split_axis=0, conca...]
    all_to_all x2, starting transfers between devices: 31.4 us -> 26.1 us  [to_owners(): lax.all_to_all(rows, 'ep', split_axis=0, concat_axis=0, tiled=True)]
    unnamed x39 -> x27, local copies, waits for them, and re-layouts: 14.4 us -> 9.53 us
    all_to_all x0 -> x1, starting transfers between devices: none -> 3.37 us  [local(): lax.all_to_all(sketch.reshape(REPS, UNITS, R), 'rep', split_axis=0, conca...]
    pallas_call x1, Pallas kernels: 9.48 us -> 7.23 us  [local(): kernel_call(products, [sds((FFW, ALL), F32)] + [sds((R, SHARE), kind) for...]
  transfers between devices with their start and end apart: 17 -> 15, of which waited for: 7 -> 6; matrix products, arithmetic and copies ran while one was open for 2% -> 2% of each run, Pallas kernels for 13% -> 13%
where the time goes in v9:
time: 141 us; the launch traced here: 140 us
  starting transfers between devices  67.5 us (48%)
  waiting for transfers between devices  36.1 us (26%)
  Pallas kernels  23.6 us (17%)
  local copies, waits for them, and re-layouts  11.5 us (8%)
  between operations  1.61 us (1%)
    ppermute x10, starting transfers between devices, shift(): lax.ppermute(block, 'rep', [(i, (i + k) % REPS) for i in range(REPS)])  34.2 us
    all_to_all x2, starting transfers between devices, to_owners(): lax.all_to_all(rows, 'ep', split_axis=0, concat_axis=0, tiled=True)  26.1 us
    ppermute x10, waiting for transfers between devices, shift(): lax.ppermute(block, 'rep', [(i, (i + k) % REPS) for i in range(REPS)])  20.5 us
    unnamed x27, local copies, waits for them, and re-layouts  9.53 us
    pallas_call x1, Pallas kernels, local(): kernel_call(products, [sds((FFW, ALL), F32)] + [sds((R, SHARE), kind) for...  7.23 us
    all_to_all x2, waiting for transfers between devices, to_owners(): lax.all_to_all(rows, 'ep', split_axis=0, concat_axis=0, tiled=True)  6 us
    all_to_all x1, waiting for transfers between devices, local(): lax.all_to_all(sketch.reshape(REPS, UNITS, R), 'rep', split_axis=0, conca...  5.6 us
    pallas_call x1, Pallas kernels, local(): kernel_call(send_rows, sds((ROWS, SHARE + STRIP), BF), [SM] + [VM] * 3, 1...  4.26 us
  transfers between devices with their start and end apart: 15, of which 6 were waited for; matrix products, arithmetic and copies ran while one was open for 2% of the time, Pallas kernels for 13%

profile of v9, /device:TPU:8, one launch (start us, length us, event | category | flops | bytes accessed | tf_op | source)
XLA Modules:
  0.0 140.4 jit_solution(8242931621601164072)
XLA Ops:
  0.6 0.0 copy-start.6
  0.7 0.1 pad_add_fusion.pos_ref
  0.7 1.2 copy-done.2
  2.0 0.7 copy-done.5
  2.6 0.6 shard_map.86
  3.2 1.9 %collective-permute-start = (bf16[144,2048]{1,0:T(8,128)(2,1)S(1)}, bf16[144,2048]{1,0:T(8,128)(2,1)S(1)}, u32[]{:S(2)}, u32[]{:S(2)}) collective-permute-start(bf16[144,2048]{1,0:T(8,128)(2,1)S(1)} %shard_map.86), channel_id=1, source_target_pairs={{0,4},{4,0},{8,12},{12,8},{16,20},{20,16},{24,28},{28,24},{32,36},... | collective-permute-start | bytes 1769480 | tf_op jit(solution)/shard_map/ppermute | solution.py:277
  5.2 2.0 %collective-permute-done.other_ref = bf16[144,2048]{1,0:T(8,128)(2,1)S(1)} collective-permute-done((bf16[144,2048]{1,0:T(8,128)(2,1)S(1)}, bf16[144,2048]{1,0:T(8,128)(2,1)S(1)}, u32[]{:S(2)}, u32[]{:S(2)}) %collective-permute-start) | collective-permute-done | bytes 589856 | tf_op jit(solution)/shard_map/ppermute | solution.py:277
  7.1 4.3 %shard_map.87 = bf16[1024,1280]{1,0:T(8,128)(2,1)} custom-call(s32[2]{0:T(128)S(1)} %pad_add_fusion.pos_ref, s32[8,128]{1,0:T(8,128)S(1)} %bitcast.16, bf16[128,4096]{1,0:T(8,128)(2,1)S(1)} %copy-done.3, bf16[144,2048]{1,0:T(8,128)(2,1)S(1)} %collective-permute-done.other_ref), custom_call_target="tpu_custom_call" | custom-call | flops 2147483648 | bytes 5242880 | tf_op jit(solution)/shard_map/pallas_call | solution.py:305
  11.4 17.9 %all-to-all-start = ((bf16[128,8,1280]{2,1,0:T(8,128)(2,1)}), bf16[128,8,1280]{2,1,0:T(8,128)(2,1)}, u32[]{:S(2)}, u32[]{:S(2)}) async-start(bf16[128,8,1280]{2,1,0:T(8,128)(2,1)} %bitcast.3), calls=%async_computation | async-start | bytes 5242880 | tf_op jit(solution)/shard_map/all_to_all | solution.py:283
  29.3 1.2 copy.9
  30.5 3.4 %collective-permute-start.1 = (bf16[192,4096]{1,0:T(8,128)(2,1)}, bf16[192,4096]{1,0:T(8,128)(2,1)S(1)}, u32[]{:S(2)}, u32[]{:S(2)}) collective-permute-start(bf16[192,4096]{1,0:T(8,128)(2,1)} %bitcast.5.own_ref), channel_id=1, source_target_pairs={{0,1},{1,2},{2,3},{3,0},{4,5},{5,6},{6,7},{7,4},{8,9},{9,10},{10,1... | collective-permute-start | bytes 4718600 | tf_op jit(solution)/shard_map/ppermute | solution.py:269
  33.9 3.6 %collective-permute-start.2 = (bf16[192,4096]{1,0:T(8,128)(2,1)}, bf16[192,4096]{1,0:T(8,128)(2,1)S(1)}, u32[]{:S(2)}, u32[]{:S(2)}) collective-permute-start(bf16[192,4096]{1,0:T(8,128)(2,1)} %bitcast.5.own_ref), channel_id=1, source_target_pairs={{0,3},{1,0},{2,1},{3,2},{4,7},{5,4},{6,5},{7,6},{8,11},{9,8},{10,9... | collective-permute-start | bytes 4718600 | tf_op jit(solution)/shard_map/ppermute | solution.py:269
  37.6 1.9 %collective-permute-start.3 = (bf16[1024,192]{1,0:T(8,128)(2,1)}, bf16[1024,192]{1,0:T(8,128)(2,1)S(1)}, u32[]{:S(2)}, u32[]{:S(2)}) collective-permute-start(bf16[1024,192]{1,0:T(8,128)(2,1)} %bitcast.13), channel_id=1, source_target_pairs={{0,4},{4,0},{8,12},{12,8},{16,20},{20,16},{24,28},{28,24},{32,36},... | collective-permute-start | bytes 1179656 | tf_op jit(solution)/shard_map/ppermute | solution.py:277
  39.5 2.1 %collective-permute-done.3.other_grads_ref = bf16[1024,192]{1,0:T(8,128)(2,1)S(1)} collective-permute-done((bf16[1024,192]{1,0:T(8,128)(2,1)}, bf16[1024,192]{1,0:T(8,128)(2,1)S(1)}, u32[]{:S(2)}, u32[]{:S(2)}) %collective-permute-start.3) | collective-permute-done | bytes 393248 | tf_op jit(solution)/shard_map/ppermute | solution.py:277
  41.6 1.0 copy-done.4
  42.6 1.1 copy-done.8
  43.7 2.8 %shard_map.88 = (bf16[384,256]{1,0:T(8,128)(2,1)S(1)}, bf16[384,256]{1,0:T(8,128)(2,1)S(1)}, bf16[384,256]{1,0:T(8,128)(2,1)S(1)}, bf16[384,256]{1,0:T(8,128)(2,1)S(1)}) custom-call(s32[2]{0:T(128)S(1)} %pad_add_fusion.pos_ref, s32[8,128]{1,0:T(8,128)S(1)} %bitcast.17, bf16[144,2048]{1,0:T(8,128)(2,1)S(1)} %copy-done.8, bf16[1024,192]{1,0:T(8,128)(2,1)S(1)} %bitcast.14, ...), custom_call_target="tpu_custom_call" | custom-call | flops 5368709120 | bytes 3145728 | tf_op jit(solution)/shard_map/pallas_call | solution.py:324
  46.5 3.7 %collective-permute-start.10 = (bf16[384,256]{1,0:T(8,128)(2,1)S(1)}, bf16[384,256]{1,0:T(8,128)(2,1)S(1)}, u32[]{:S(2)}, u32[]{:S(2)}) collective-permute-start(bf16[384,256]{1,0:T(8,128)(2,1)S(1)} %get-tuple-element.28), channel_id=1, source_target_pairs={{0,2},{1,3},{2,0},{3,1},{4,6},{5,7},{6,4},{7,5},{8,10},{9,11},{10,... | collective-permute-start | bytes 589832 | tf_op jit(solution)/shard_map/ppermute | solution.py:269
  50.3 3.0 %collective-permute-start.11 = (bf16[384,256]{1,0:T(8,128)(2,1)S(1)}, bf16[384,256]{1,0:T(8,128)(2,1)S(1)}, u32[]{:S(2)}, u32[]{:S(2)}) collective-permute-start(bf16[384,256]{1,0:T(8,128)(2,1)S(1)} %get-tuple-element.29), channel_id=1, source_target_pairs={{0,3},{1,0},{2,1},{3,2},{4,7},{5,4},{6,5},{7,6},{8,11},{9,8},{10,9... | collective-permute-start | bytes 589832 | tf_op jit(solution)/shard_map/ppermute | solution.py:269
  53.3 2.8 %collective-permute-start.9 = (bf16[384,256]{1,0:T(8,128)(2,1)S(1)}, bf16[384,256]{1,0:T(8,128)(2,1)S(1)}, u32[]{:S(2)}, u32[]{:S(2)}) collective-permute-start(bf16[384,256]{1,0:T(8,128)(2,1)S(1)} %get-tuple-element.19), channel_id=1, source_target_pairs={{0,1},{1,2},{2,3},{3,0},{4,5},{5,6},{6,7},{7,4},{8,9},{9,10},{10,1... | collective-permute-start | bytes 589832 | tf_op jit(solution)/shard_map/ppermute | solution.py:269
  56.1 15.5 %collective-permute-done.1.left_ref = bf16[192,4096]{1,0:T(8,128)(2,1)S(1)} collective-permute-done((bf16[192,4096]{1,0:T(8,128)(2,1)}, bf16[192,4096]{1,0:T(8,128)(2,1)S(1)}, u32[]{:S(2)}, u32[]{:S(2)}) %collective-permute-start.1) | collective-permute-done | bytes 1572896 | tf_op jit(solution)/shard_map/ppermute | solution.py:269
  71.6 5.0 %collective-permute-done.2.right_ref = bf16[192,4096]{1,0:T(8,128)(2,1)S(1)} collective-permute-done((bf16[192,4096]{1,0:T(8,128)(2,1)}, bf16[192,4096]{1,0:T(8,128)(2,1)S(1)}, u32[]{:S(2)}, u32[]{:S(2)}) %collective-permute-start.2) | collective-permute-done | bytes 1572896 | tf_op jit(solution)/shard_map/ppermute | solution.py:269
  76.6 1.0 slice.6
  77.6 3.6 %collective-permute-start.4 = (bf16[96,4096]{1,0:T(8,128)(2,1)}, bf16[96,4096]{1,0:T(8,128)(2,1)}, u32[]{:S(2)}, u32[]{:S(2)}) collective-permute-start(bf16[96,4096]{1,0:T(8,128)(2,1)} %slice.6), channel_id=1, source_target_pairs={{0,1},{1,2},{2,3},{3,0},{4,5},{5,6},{6,7},{7,4},{8,9},{9,10},{10,1... | collective-permute-start | bytes 2359304 | tf_op jit(solution)/shard_map/ppermute | solution.py:269
  81.2 1.0 slice.7
  82.2 4.1 %collective-permute-start.5 = (bf16[96,4096]{1,0:T(8,128)(2,1)}, bf16[96,4096]{1,0:T(8,128)(2,1)}, u32[]{:S(2)}, u32[]{:S(2)}) collective-permute-start(bf16[96,4096]{1,0:T(8,128)(2,1)} %slice.7), channel_id=1, source_target_pairs={{0,3},{1,0},{2,1},{3,2},{4,7},{5,4},{6,5},{7,6},{8,11},{9,8},{10,9... | collective-permute-start | bytes 2359304 | tf_op jit(solution)/shard_map/ppermute | solution.py:269
  86.3 0.0 collective-permute-done.9.g1
  86.3 1.2 shard_map.92
  87.5 0.0 copy-start
  87.5 0.8 copy-done
  88.3 6.0 %all-to-all-done = bf16[128,8,1280]{2,1,0:T(8,128)(2,1)} async-done(((bf16[128,8,1280]{2,1,0:T(8,128)(2,1)}), bf16[128,8,1280]{2,1,0:T(8,128)(2,1)}, u32[]{:S(2)}, u32[]{:S(2)}) %all-to-all-start) | async-done | bytes 2621472 | tf_op jit(solution)/shard_map/all_to_all | solution.py:283
  94.2 8.2 %all-to-all-start.1 = ((bf16[128,8,256]{2,1,0:T(8,128)(2,1)}), bf16[128,8,256]{2,1,0:T(8,128)(2,1)}, u32[]{:S(2)}, u32[]{:S(2)}) async-start(bf16[128,8,256]{2,1,0:T(8,128)(2,1)} %bitcast.12), calls=%async_computation.1 | async-start | bytes 1048576 | tf_op jit(solution)/shard_map/all_to_all | solution.py:283
  102.5 0.0 collective-permute-done.4.top_ref
  102.5 0.0 copy-start.1
  102.5 1.2 copy-done.1
  103.7 2.3 %shard_map.89.weights_ref = bf16[896,4096]{1,0:T(8,128)(2,1)S(1)} custom-call(s32[2]{0:T(128)S(1)} %pad_add_fusion.pos_ref, bf16[128,4096]{1,0:T(8,128)(2,1)S(1)} %copy-done.1, bf16[192,4096]{1,0:T(8,128)(2,1)} %bitcast.5.own_ref, bf16[192,4096]{1,0:T(8,128)(2,1)S(1)} %collective-permute-done.2.right_ref, bf16[96,4096]{1,0:T(8,128)(2,1)} %collective-permute-done.4.top_ref, ...), custom_call_target="tpu_custom_call" | custom-call | flops 1000 | bytes 14680064 | tf_op jit(solution)/shard_map/pallas_call | solution.py:339
  106.1 0.0 copy-start.9
  106.1 7.2 %shard_map.90 = (f32[768,384]{1,0:T(8,128)S(1)}, f32[128,1024]{1,0:T(8,128)S(1)}, bf16[128,1024]{1,0:T(8,128)(2,1)S(1)}, bf16[128,1024]{1,0:T(8,128)(2,1)S(1)}, bf16[128,1024]{1,0:T(8,128)(2,1)S(1)}) custom-call(s32[2]{0:T(128)S(1)} %pad_add_fusion.pos_ref, bf16[1024,1280]{1,0:T(8,128)(2,1)} %bitcast.4.rows_ref, bf16[896,4096]{1,0:T(8,128)(2,1)S(1)} %shard_map.89.weights_ref), custom_call_target="tpu_custom_call" | custom-call | flops 4294967296 | bytes 12582912 | tf_op jit(solution)/shard_map/pallas_call | solution.py:345
  113.3 1.0 copy-done.10
  114.3 1.9 %collective-permute-start.6 = (bf16[128,1024]{1,0:T(8,128)(2,1)S(1)}, bf16[128,1024]{1,0:T(8,128)(2,1)S(1)}, u32[]{:S(2)}, u32[]{:S(2)}) collective-permute-start(bf16[128,1024]{1,0:T(8,128)(2,1)S(1)} %get-tuple-element.23), channel_id=1, source_target_pairs={{0,1},{1,2},{2,3},{3,0},{4,5},{5,6},{6,7},{7,4},{8,9},{9,10},{10,1... | collective-permute-start | bytes 786440 | tf_op jit(solution)/shard_map/ppermute | solution.py:269
  116.3 5.4 %collective-permute-start.7 = (bf16[128,1024]{1,0:T(8,128)(2,1)S(1)}, bf16[128,1024]{1,0:T(8,128)(2,1)S(1)}, u32[]{:S(2)}, u32[]{:S(2)}) collective-permute-start(bf16[128,1024]{1,0:T(8,128)(2,1)S(1)} %get-tuple-element.24), channel_id=1, source_target_pairs={{0,2},{1,3},{2,0},{3,1},{4,6},{5,7},{6,4},{7,5},{8,10},{9,11},{10,... | collective-permute-start | bytes 786440 | tf_op jit(solution)/shard_map/ppermute | solution.py:269
  121.6 2.6 %collective-permute-start.8 = (bf16[128,1024]{1,0:T(8,128)(2,1)S(1)}, bf16[128,1024]{1,0:T(8,128)(2,1)S(1)}, u32[]{:S(2)}, u32[]{:S(2)}) collective-permute-start(bf16[128,1024]{1,0:T(8,128)(2,1)S(1)} %get-tuple-element.25), channel_id=1, source_target_pairs={{0,3},{1,0},{2,1},{3,2},{4,7},{5,4},{6,5},{7,6},{8,11},{9,8},{10,9... | collective-permute-start | bytes 786440 | tf_op jit(solution)/shard_map/ppermute | solution.py:269
  124.3 1.3 copy-done.11
  125.5 3.0 %shard_map.93 = (f32[192,128]{1,0:T(8,128)S(1)}, bf16[768,128]{1,0:T(8,128)(2,1)}) custom-call(s32[2]{0:T(128)S(1)} %pad_add_fusion.pos_ref, bf16[128,768]{1,0:T(8,128)(2,1)S(1)} %copy-done.9, f32[768,384]{1,0:T(8,128)S(1)} %copy-done.11, bf16[1024,256]{1,0:T(8,128)(2,1)} %bitcast.9.got_ref), custom_call_target="tpu_custom_call" | custom-call | flops 1073741824 | bytes 3145728 | tf_op jit(solution)/shard_map/pallas_call | solution.py:356
  128.5 3.4 %all-to-all-start.2 = ((bf16[4,192,128]{2,1,0:T(8,128)(2,1)}), bf16[4,192,128]{2,1,0:T(8,128)(2,1)S(1)}, u32[]{:S(2)}, u32[]{:S(2)}) async-start(bf16[4,192,128]{2,1,0:T(8,128)(2,1)} %bitcast.10), calls=%async_computation.2 | async-start | bytes 393216 | tf_op jit(solution)/shard_map/all_to_all | solution.py:365
  132.6 5.6 %all-to-all-done.2.parts_ref = bf16[4,192,128]{2,1,0:T(8,128)(2,1)S(1)} async-done(((bf16[4,192,128]{2,1,0:T(8,128)(2,1)}), bf16[4,192,128]{2,1,0:T(8,128)(2,1)S(1)}, u32[]{:S(2)}, u32[]{:S(2)}) %all-to-all-start.2) | async-done | bytes 196640 | tf_op jit(solution)/shard_map/all_to_all | solution.py:365
  138.2 1.2 shard_map.94
  139.4 1.0 shard_map.91
  (21 shorter events, 0.0 us)
Async XLA Ops:
  0.6 6.5 %copy-start.6 = (s32[128,8]{0,1:T(8,128)S(1)}, s32[128,8]{0,1:T(8,128)}, u32[]{:S(2)}) copy-start(s32[128,8]{0,1:T(8,128)} %param.8) | copy-start | bytes 12292
  0.7 1.2 copy-start.2
  2.0 0.7 copy-start.5
  2.6 4.5 %copy-start.3 = (bf16[128,4096]{1,0:T(8,128)(2,1)S(1)}, bf16[128,4096]{1,0:T(8,128)(2,1)}, u32[]{:S(2)}) copy-start(bf16[128,4096]{1,0:T(8,128)(2,1)} %tokens_ref.3) | copy-start | bytes 3145732
  3.2 3.9 %collective-permute-start = (bf16[144,2048]{1,0:T(8,128)(2,1)S(1)}, bf16[144,2048]{1,0:T(8,128)(2,1)S(1)}, u32[]{:S(2)}, u32[]{:S(2)}) collective-permute-start(bf16[144,2048]{1,0:T(8,128)(2,1)S(1)} %shard_map.86), channel_id=1, source_target_pairs={{0,4},{4,0},{8,12},{12,8},{16,20},{20,16},{24,28},{28,24},{32,36},... | collective-permute-start | bytes 1769480 | tf_op jit(solution)/shard_map/ppermute | solution.py:277
  7.1 4.3 %copy-start.7 = (bf16[144,2048]{1,0:T(8,128)(2,1)}, bf16[144,2048]{1,0:T(8,128)(2,1)S(1)}, u32[]{:S(2)}) copy-start(bf16[144,2048]{1,0:T(8,128)(2,1)S(1)} %collective-permute-done.other_ref) | copy-start | bytes 1769476
  11.4 17.9 %copy-start.12 = (bf16[128,8,192]{0,2,1:T(8,128)(2,1)S(1)}, bf16[128,8,192]{0,2,1:T(8,128)(2,1)}, u32[]{:S(2)}) copy-start(bf16[128,8,192]{0,2,1:T(8,128)(2,1)} %param.9) | copy-start | bytes 1179652
  11.4 82.9 %all-to-all-start = ((bf16[128,8,1280]{2,1,0:T(8,128)(2,1)}), bf16[128,8,1280]{2,1,0:T(8,128)(2,1)}, u32[]{:S(2)}, u32[]{:S(2)}) async-start(bf16[128,8,1280]{2,1,0:T(8,128)(2,1)} %bitcast.3), calls=%async_computation | async-start | bytes 5242880 | tf_op jit(solution)/shard_map/all_to_all | solution.py:283
  30.5 41.1 %collective-permute-start.1 = (bf16[192,4096]{1,0:T(8,128)(2,1)}, bf16[192,4096]{1,0:T(8,128)(2,1)S(1)}, u32[]{:S(2)}, u32[]{:S(2)}) collective-permute-start(bf16[192,4096]{1,0:T(8,128)(2,1)} %bitcast.5.own_ref), channel_id=1, source_target_pairs={{0,1},{1,2},{2,3},{3,0},{4,5},{5,6},{6,7},{7,4},{8,9},{9,10},{10,1... | collective-permute-start | bytes 4718600 | tf_op jit(solution)/shard_map/ppermute | solution.py:269
  33.9 42.7 %collective-permute-start.2 = (bf16[192,4096]{1,0:T(8,128)(2,1)}, bf16[192,4096]{1,0:T(8,128)(2,1)S(1)}, u32[]{:S(2)}, u32[]{:S(2)}) collective-permute-start(bf16[192,4096]{1,0:T(8,128)(2,1)} %bitcast.5.own_ref), channel_id=1, source_target_pairs={{0,3},{1,0},{2,1},{3,2},{4,7},{5,4},{6,5},{7,6},{8,11},{9,8},{10,9... | collective-permute-start | bytes 4718600 | tf_op jit(solution)/shard_map/ppermute | solution.py:269
  37.6 4.0 %collective-permute-start.3 = (bf16[1024,192]{1,0:T(8,128)(2,1)}, bf16[1024,192]{1,0:T(8,128)(2,1)S(1)}, u32[]{:S(2)}, u32[]{:S(2)}) collective-permute-start(bf16[1024,192]{1,0:T(8,128)(2,1)} %bitcast.13), channel_id=1, source_target_pairs={{0,4},{4,0},{8,12},{12,8},{16,20},{20,16},{24,28},{28,24},{32,36},... | collective-permute-start | bytes 1179656 | tf_op jit(solution)/shard_map/ppermute | solution.py:277
  41.6 1.0 copy-start.4
  42.6 1.1 copy-start.8
  46.5 39.7 %collective-permute-start.10 = (bf16[384,256]{1,0:T(8,128)(2,1)S(1)}, bf16[384,256]{1,0:T(8,128)(2,1)S(1)}, u32[]{:S(2)}, u32[]{:S(2)}) collective-permute-start(bf16[384,256]{1,0:T(8,128)(2,1)S(1)} %get-tuple-element.28), channel_id=1, source_target_pairs={{0,2},{1,3},{2,0},{3,1},{4,6},{5,7},{6,4},{7,5},{8,10},{9,11},{10,... | collective-permute-start | bytes 589832 | tf_op jit(solution)/shard_map/ppermute | solution.py:269
  50.3 36.0 %collective-permute-start.11 = (bf16[384,256]{1,0:T(8,128)(2,1)S(1)}, bf16[384,256]{1,0:T(8,128)(2,1)S(1)}, u32[]{:S(2)}, u32[]{:S(2)}) collective-permute-start(bf16[384,256]{1,0:T(8,128)(2,1)S(1)} %get-tuple-element.29), channel_id=1, source_target_pairs={{0,3},{1,0},{2,1},{3,2},{4,7},{5,4},{6,5},{7,6},{8,11},{9,8},{10,9... | collective-permute-start | bytes 589832 | tf_op jit(solution)/shard_map/ppermute | solution.py:269
  53.3 33.0 %collective-permute-start.9 = (bf16[384,256]{1,0:T(8,128)(2,1)S(1)}, bf16[384,256]{1,0:T(8,128)(2,1)S(1)}, u32[]{:S(2)}, u32[]{:S(2)}) collective-permute-start(bf16[384,256]{1,0:T(8,128)(2,1)S(1)} %get-tuple-element.19), channel_id=1, source_target_pairs={{0,1},{1,2},{2,3},{3,0},{4,5},{5,6},{6,7},{7,4},{8,9},{9,10},{10,1... | collective-permute-start | bytes 589832 | tf_op jit(solution)/shard_map/ppermute | solution.py:269
  77.6 24.9 %collective-permute-start.4 = (bf16[96,4096]{1,0:T(8,128)(2,1)}, bf16[96,4096]{1,0:T(8,128)(2,1)}, u32[]{:S(2)}, u32[]{:S(2)}) collective-permute-start(bf16[96,4096]{1,0:T(8,128)(2,1)} %slice.6), channel_id=1, source_target_pairs={{0,1},{1,2},{2,3},{3,0},{4,5},{5,6},{6,7},{7,4},{8,9},{9,10},{10,1... | collective-permute-start | bytes 2359304 | tf_op jit(solution)/shard_map/ppermute | solution.py:269
  82.2 20.3 %collective-permute-start.5 = (bf16[96,4096]{1,0:T(8,128)(2,1)}, bf16[96,4096]{1,0:T(8,128)(2,1)}, u32[]{:S(2)}, u32[]{:S(2)}) collective-permute-start(bf16[96,4096]{1,0:T(8,128)(2,1)} %slice.7), channel_id=1, source_target_pairs={{0,3},{1,0},{2,1},{3,2},{4,7},{5,4},{6,5},{7,6},{8,11},{9,8},{10,9... | collective-permute-start | bytes 2359304 | tf_op jit(solution)/shard_map/ppermute | solution.py:269
  87.5 0.8 copy-start
  94.2 30.0 %all-to-all-start.1 = ((bf16[128,8,256]{2,1,0:T(8,128)(2,1)}), bf16[128,8,256]{2,1,0:T(8,128)(2,1)}, u32[]{:S(2)}, u32[]{:S(2)}) async-start(bf16[128,8,256]{2,1,0:T(8,128)(2,1)} %bitcast.12), calls=%async_computation.1 | async-start | bytes 1048576 | tf_op jit(solution)/shard_map/all_to_all | solution.py:283
  102.5 1.2 copy-start.1
  106.1 18.2 %copy-start.9 = (bf16[128,768]{1,0:T(8,128)(2,1)S(1)}, bf16[128,768]{1,0:T(8,128)(2,1)}, u32[]{:S(2)}) copy-start(bf16[128,768]{1,0:T(8,128)(2,1)} %grad_probes_ref.1) | copy-start | bytes 589828
  113.3 1.0 copy-start.10
  114.3 25.0 %collective-permute-start.6 = (bf16[128,1024]{1,0:T(8,128)(2,1)S(1)}, bf16[128,1024]{1,0:T(8,128)(2,1)S(1)}, u32[]{:S(2)}, u32[]{:S(2)}) collective-permute-start(bf16[128,1024]{1,0:T(8,128)(2,1)S(1)} %get-tuple-element.23), channel_id=1, source_target_pairs={{0,1},{1,2},{2,3},{3,0},{4,5},{5,6},{6,7},{7,4},{8,9},{9,10},{10,1... | collective-permute-start | bytes 786440 | tf_op jit(solution)/shard_map/ppermute | solution.py:269
  116.3 23.1 %collective-permute-start.7 = (bf16[128,1024]{1,0:T(8,128)(2,1)S(1)}, bf16[128,1024]{1,0:T(8,128)(2,1)S(1)}, u32[]{:S(2)}, u32[]{:S(2)}) collective-permute-start(bf16[128,1024]{1,0:T(8,128)(2,1)S(1)} %get-tuple-element.24), channel_id=1, source_target_pairs={{0,2},{1,3},{2,0},{3,1},{4,6},{5,7},{6,4},{7,5},{8,10},{9,11},{10,... | collective-permute-start | bytes 786440 | tf_op jit(solution)/shard_map/ppermute | solution.py:269
  121.6 17.8 %collective-permute-start.8 = (bf16[128,1024]{1,0:T(8,128)(2,1)S(1)}, bf16[128,1024]{1,0:T(8,128)(2,1)S(1)}, u32[]{:S(2)}, u32[]{:S(2)}) collective-permute-start(bf16[128,1024]{1,0:T(8,128)(2,1)S(1)} %get-tuple-element.25), channel_id=1, source_target_pairs={{0,3},{1,0},{2,1},{3,2},{4,7},{5,4},{6,5},{7,6},{8,11},{9,8},{10,9... | collective-permute-start | bytes 786440 | tf_op jit(solution)/shard_map/ppermute | solution.py:269
  124.2 1.3 copy-start.11
  128.5 9.7 %all-to-all-start.2 = ((bf16[4,192,128]{2,1,0:T(8,128)(2,1)}), bf16[4,192,128]{2,1,0:T(8,128)(2,1)S(1)}, u32[]{:S(2)}, u32[]{:S(2)}) async-start(bf16[4,192,128]{2,1,0:T(8,128)(2,1)} %bitcast.10), calls=%async_computation.2 | async-start | bytes 393216 | tf_op jit(solution)/shard_map/all_to_all | solution.py:365

commit v10 on v9

--- a/solution.py
+++ b/solution.py
@@ -95,15 +95,29 @@
     return other_ref[TOK:, :TOK].astype(F32)[:TOP].astype(jnp.int32)
 
 
-def send_rows(pos_ref, ids_ref, tokens_ref, other_ref, out_ref, half_ref, half_ids_ref, fold_ref):
+def fold(picked, many, put):
+    size = 256 // many
+    width = picked.shape[1] // many
+    shape = (256, 256)
+    to = iota(shape, 0)
+    order = ones_where(iota(shape, 1) == to % many * size + to // many)
+    for g in range(ROWS // 256):
+        at = slice(g * size, (g + 1) * size)
+        parts = [picked[at, p * width : (p + 1) * width] for p in range(many)]
+        put(slice(g * 256, (g + 1) * 256), dot(order, jnp.concatenate(parts, 0)).astype(BF))
+
+
+def send_rows(pos_ref, ids_ref, tokens_ref, other_ref, out_ref, half_ref, half_ids_ref):
     x, c = pos_ref[0], pos_ref[1]
     mine = x // 2 == c
-    table = spread(places(ids_ref[...]), FOLD)
-    row = iota((ROWS, TOK), 0)
-    whole = table == (2 * x + row % 8 // 4).astype(F32)
-    picks = jnp.concatenate([ones_where(whole & (row % 4 == b)) for b in range(4)], 1)
-    parts = jnp.concatenate([tokens_ref[:, b * SHARE : (b + 1) * SHARE] for b in range(4)], 0)
-    out_ref[:, :SHARE] = dot(picks, parts).astype(BF)
+    table = spread(places(ids_ref[...]), 2)
+    place = 2 * x + iota(table.shape, 0) % 2
+    picked = dot(ones_where(table == place.astype(F32)), tokens_ref[...]).astype(BF)
+
+    def put_whole(at, got):
+        out_ref[at, :SHARE] = got
+
+    fold(picked, 4, put_whole)
 
     @pl.when(mine)
     def _():
@@ -115,14 +129,13 @@
         half_ref[...] = other_ref[:TOK, :]
         half_ids_ref[...] = other_ids(other_ref)
 
-    picks = ones_where(places(half_ids_ref[...]) == (FIRST + x % 2).astype(F32))
-    rows = dot(picks, half_ref[...])
-    for b in range(FOLD):
-        for h in range(2):
-            start = b * STRIP + h * 128
-            fold_ref[h, pl.ds(b, OWNERS, stride=FOLD), :] = rows[:, start : start + 128]
-    for h in range(2):
-        out_ref[:, SHARE + h * 128 : SHARE + (h + 1) * 128] = fold_ref[h].astype(BF)
+    table = places(half_ids_ref[...])
+    picked = dot(ones_where(table == (FIRST + x % 2).astype(F32)), half_ref[...]).astype(BF)
+
+    def put_shared(at, got):
+        out_ref[at, SHARE:] = got
+
+    fold(picked, FOLD, put_shared)
 
 
 def pick_grads(pos_ref, ids_ref, other_ref, grads_ref, other_grads_ref, *outs):
@@ -306,14 +319,10 @@
         send_rows,
         sds((ROWS, SHARE + STRIP), BF),
         [SM] + [VM] * 3,
-        1 << 31,
+        1 << 30,
         5 * MIB,
         20,
-        [
-            pltpu.VMEM((TOK, HALF), BF),
-            pltpu.VMEM((TOP, TOK), jnp.int32),
-            pltpu.VMEM((2, ROWS, 128), F32),
-        ],
+        [pltpu.VMEM((TOK, HALF), BF), pltpu.VMEM((TOP, TOK), jnp.int32)],
     )(pos, ids_t, tokens, other)
     rows = to_owners(out_rows)
 
@@ -369,6 +378,7 @@
     input_sketch = kernel_call(
         finish_input, sds((SHARE, R), F32), [SM] + [VM] * 4, 1 << 20, 2 * MIB, 6
     )(inverse, *inputs)
+    own_sketch, input_sketch = lax.optimization_barrier((own_sketch, input_sketch))
     grad_sketch = kernel_call(
         finish_grad, sds((UNITS, R), F32), [SM] * 2 + [VM] * 2, 1 << 18, MIB // 4, 4
     )(pos, inverse, own_sketch, sketches)

time: 141 us -> 143 us (1.014)
  starting transfers between devices: 67.5 us -> 69.5 us
    ppermute x10, waiting for transfers between devices: 20.5 us -> 25.6 us  [shift(): lax.ppermute(block, 'rep', [(i, (i + k) % REPS) for i in range(REPS)])]
    all_to_all x2, starting transfers between devices: 26.1 us -> 28.9 us  [to_owners(): lax.all_to_all(rows, 'ep', split_axis=0, concat_axis=0, tiled=True)]
    all_to_all x2, waiting for transfers between devices: 6 us -> 3.24 us  [to_owners(): lax.all_to_all(rows, 'ep', split_axis=0, concat_axis=0, tiled=True)]
    all_to_all x1, waiting for transfers between devices: 5.6 us -> 2.9 us  [local(): lax.all_to_all(sketch.reshape(REPS, UNITS, R), 'rep', split_axis=0, conca...]
    ppermute x10, starting transfers between devices: 34.2 us -> 32.6 us  [shift(): lax.ppermute(block, 'rep', [(i, (i + k) % REPS) for i in range(REPS)])]
  transfers between devices with their start and end apart: 15 -> 15, of which waited for: 6 -> 7; matrix products, arithmetic and copies ran while one was open for 2% -> 2% of each run, Pallas kernels for 13% -> 12%
where the time goes in v10:
time: 143 us; the launch traced here: 142 us
  starting transfers between devices  69.5 us (49%)
  waiting for transfers between devices  35.8 us (25%)
  Pallas kernels  23.7 us (17%)
  local copies, waits for them, and re-layouts  11.5 us (8%)
  between operations  1.62 us (1%)
    ppermute x10, starting transfers between devices, shift(): lax.ppermute(block, 'rep', [(i, (i + k) % REPS) for i in range(REPS)])  32.6 us
    all_to_all x2, starting transfers between devices, to_owners(): lax.all_to_all(rows, 'ep', split_axis=0, concat_axis=0, tiled=True)  28.9 us
    ppermute x10, waiting for transfers between devices, shift(): lax.ppermute(block, 'rep', [(i, (i + k) % REPS) for i in range(REPS)])  25.6 us
    unnamed x27, local copies, waits for them, and re-layouts  9.53 us
    pallas_call x1, Pallas kernels, local(): kernel_call(products, [sds((FFW, ALL), F32)] + [sds((R, SHARE), kind) for...  7.23 us
    pallas_call x1, Pallas kernels, local(): kernel_call(send_rows, sds((ROWS, SHARE + STRIP), BF), [SM] + [VM] * 3, 1...  4.32 us
    all_to_all x1, starting transfers between devices, local(): lax.all_to_all(sketch.reshape(REPS, UNITS, R), 'rep', split_axis=0, conca...  4.18 us
    ppermute x2, waiting for transfers between devices, swap(): return lax.ppermute(block, 'ep', [(i, i ^ 1) for i in range(OWNERS)])  4.06 us
  transfers between devices with their start and end apart: 15, of which 7 were waited for; matrix products, arithmetic and copies ran while one was open for 2% of the time, Pallas kernels for 12%

profile of v10, /device:TPU:8, one launch (start us, length us, event | category | flops | bytes accessed | tf_op | source)
XLA Modules:
  0.0 142.1 jit_solution(3521662452145730275)
XLA Ops:
  0.6 0.0 copy-start.8
  0.7 0.1 pad_add_fusion.pos_ref
  0.7 1.2 copy-done
  2.0 0.7 copy-done.7
  2.6 0.6 shard_map.86
  3.2 1.9 %collective-permute-start = (bf16[144,2048]{1,0:T(8,128)(2,1)S(1)}, bf16[144,2048]{1,0:T(8,128)(2,1)S(1)}, u32[]{:S(2)}, u32[]{:S(2)}) collective-permute-start(bf16[144,2048]{1,0:T(8,128)(2,1)S(1)} %shard_map.86), channel_id=1, source_target_pairs={{0,4},{4,0},{8,12},{12,8},{16,20},{20,16},{24,28},{28,24},{32,36},... | collective-permute-start | bytes 1769480 | tf_op jit(solution)/shard_map/ppermute | solution.py:290
  5.2 2.0 %collective-permute-done.other_ref = bf16[144,2048]{1,0:T(8,128)(2,1)S(1)} collective-permute-done((bf16[144,2048]{1,0:T(8,128)(2,1)S(1)}, bf16[144,2048]{1,0:T(8,128)(2,1)S(1)}, u32[]{:S(2)}, u32[]{:S(2)}) %collective-permute-start) | collective-permute-done | bytes 589856 | tf_op jit(solution)/shard_map/ppermute | solution.py:290
  7.1 4.3 %shard_map.87 = bf16[1024,1280]{1,0:T(8,128)(2,1)} custom-call(s32[2]{0:T(128)S(1)} %pad_add_fusion.pos_ref, s32[8,128]{1,0:T(8,128)S(1)} %bitcast.16, bf16[128,4096]{1,0:T(8,128)(2,1)S(1)} %copy-done.1, bf16[144,2048]{1,0:T(8,128)(2,1)S(1)} %collective-permute-done.other_ref), custom_call_target="tpu_custom_call" | custom-call | flops 1073741824 | bytes 5242880 | tf_op jit(solution)/shard_map/pallas_call | solution.py:318
  11.5 17.9 %all-to-all-start = ((bf16[128,8,1280]{2,1,0:T(8,128)(2,1)}), bf16[128,8,1280]{2,1,0:T(8,128)(2,1)}, u32[]{:S(2)}, u32[]{:S(2)}) async-start(bf16[128,8,1280]{2,1,0:T(8,128)(2,1)} %bitcast.3), calls=%async_computation | async-start | bytes 5242880 | tf_op jit(solution)/shard_map/all_to_all | solution.py:296
  29.4 1.2 copy.9
  30.6 4.7 %collective-permute-start.2 = (bf16[192,4096]{1,0:T(8,128)(2,1)}, bf16[192,4096]{1,0:T(8,128)(2,1)S(1)}, u32[]{:S(2)}, u32[]{:S(2)}) collective-permute-start(bf16[192,4096]{1,0:T(8,128)(2,1)} %bitcast.5.own_ref), channel_id=1, source_target_pairs={{0,3},{1,0},{2,1},{3,2},{4,7},{5,4},{6,5},{7,6},{8,11},{9,8},{10,9... | collective-permute-start | bytes 4718600 | tf_op jit(solution)/shard_map/ppermute | solution.py:282
  35.2 1.9 %collective-permute-start.1 = (bf16[192,4096]{1,0:T(8,128)(2,1)}, bf16[192,4096]{1,0:T(8,128)(2,1)S(1)}, u32[]{:S(2)}, u32[]{:S(2)}) collective-permute-start(bf16[192,4096]{1,0:T(8,128)(2,1)} %bitcast.5.own_ref), channel_id=1, source_target_pairs={{0,1},{1,2},{2,3},{3,0},{4,5},{5,6},{6,7},{7,4},{8,9},{9,10},{10,1... | collective-permute-start | bytes 4718600 | tf_op jit(solution)/shard_map/ppermute | solution.py:282
  37.2 1.9 %collective-permute-start.3 = (bf16[1024,192]{1,0:T(8,128)(2,1)}, bf16[1024,192]{1,0:T(8,128)(2,1)S(1)}, u32[]{:S(2)}, u32[]{:S(2)}) collective-permute-start(bf16[1024,192]{1,0:T(8,128)(2,1)} %bitcast.13), channel_id=1, source_target_pairs={{0,4},{4,0},{8,12},{12,8},{16,20},{20,16},{24,28},{28,24},{32,36},... | collective-permute-start | bytes 1179656 | tf_op jit(solution)/shard_map/ppermute | solution.py:290
  39.1 2.1 %collective-permute-done.3.other_grads_ref = bf16[1024,192]{1,0:T(8,128)(2,1)S(1)} collective-permute-done((bf16[1024,192]{1,0:T(8,128)(2,1)}, bf16[1024,192]{1,0:T(8,128)(2,1)S(1)}, u32[]{:S(2)}, u32[]{:S(2)}) %collective-permute-start.3) | collective-permute-done | bytes 393248 | tf_op jit(solution)/shard_map/ppermute | solution.py:290
  41.2 1.1 copy-done.5
  42.3 1.0 copy-done.6
  43.3 2.8 %shard_map.88 = (bf16[384,256]{1,0:T(8,128)(2,1)S(1)}, bf16[384,256]{1,0:T(8,128)(2,1)S(1)}, bf16[384,256]{1,0:T(8,128)(2,1)S(1)}, bf16[384,256]{1,0:T(8,128)(2,1)S(1)}) custom-call(s32[2]{0:T(128)S(1)} %pad_add_fusion.pos_ref, s32[8,128]{1,0:T(8,128)S(1)} %bitcast.17, bf16[144,2048]{1,0:T(8,128)(2,1)S(1)} %copy-done.5, bf16[1024,192]{1,0:T(8,128)(2,1)S(1)} %bitcast.14, ...), custom_call_target="tpu_custom_call" | custom-call | flops 5368709120 | bytes 3145728 | tf_op jit(solution)/shard_map/pallas_call | solution.py:333
  46.2 4.2 %collective-permute-start.7 = (bf16[384,256]{1,0:T(8,128)(2,1)S(1)}, bf16[384,256]{1,0:T(8,128)(2,1)S(1)}, u32[]{:S(2)}, u32[]{:S(2)}) collective-permute-start(bf16[384,256]{1,0:T(8,128)(2,1)S(1)} %get-tuple-element.26), channel_id=1, source_target_pairs={{0,2},{1,3},{2,0},{3,1},{4,6},{5,7},{6,4},{7,5},{8,10},{9,11},{10,... | collective-permute-start | bytes 589832 | tf_op jit(solution)/shard_map/ppermute | solution.py:282
  50.3 3.0 %collective-permute-start.8 = (bf16[384,256]{1,0:T(8,128)(2,1)S(1)}, bf16[384,256]{1,0:T(8,128)(2,1)S(1)}, u32[]{:S(2)}, u32[]{:S(2)}) collective-permute-start(bf16[384,256]{1,0:T(8,128)(2,1)S(1)} %get-tuple-element.27), channel_id=1, source_target_pairs={{0,3},{1,0},{2,1},{3,2},{4,7},{5,4},{6,5},{7,6},{8,11},{9,8},{10,9... | collective-permute-start | bytes 589832 | tf_op jit(solution)/shard_map/ppermute | solution.py:282
  53.4 2.8 %collective-permute-start.6 = (bf16[384,256]{1,0:T(8,128)(2,1)S(1)}, bf16[384,256]{1,0:T(8,128)(2,1)S(1)}, u32[]{:S(2)}, u32[]{:S(2)}) collective-permute-start(bf16[384,256]{1,0:T(8,128)(2,1)S(1)} %get-tuple-element.21), channel_id=1, source_target_pairs={{0,1},{1,2},{2,3},{3,0},{4,5},{5,6},{6,7},{7,4},{8,9},{9,10},{10,1... | collective-permute-start | bytes 589832 | tf_op jit(solution)/shard_map/ppermute | solution.py:282
  56.2 18.2 %collective-permute-done.2.right_ref = bf16[192,4096]{1,0:T(8,128)(2,1)S(1)} collective-permute-done((bf16[192,4096]{1,0:T(8,128)(2,1)}, bf16[192,4096]{1,0:T(8,128)(2,1)S(1)}, u32[]{:S(2)}, u32[]{:S(2)}) %collective-permute-start.2) | collective-permute-done | bytes 1572896 | tf_op jit(solution)/shard_map/ppermute | solution.py:282
  74.4 5.7 %collective-permute-done.1.left_ref = bf16[192,4096]{1,0:T(8,128)(2,1)S(1)} collective-permute-done((bf16[192,4096]{1,0:T(8,128)(2,1)}, bf16[192,4096]{1,0:T(8,128)(2,1)S(1)}, u32[]{:S(2)}, u32[]{:S(2)}) %collective-permute-start.1) | collective-permute-done | bytes 1572896 | tf_op jit(solution)/shard_map/ppermute | solution.py:282
  80.1 0.9 slice.7
  81.0 1.0 slice.6
  82.0 1.9 %collective-permute-start.4 = (bf16[96,4096]{1,0:T(8,128)(2,1)}, bf16[96,4096]{1,0:T(8,128)(2,1)}, u32[]{:S(2)}, u32[]{:S(2)}) collective-permute-start(bf16[96,4096]{1,0:T(8,128)(2,1)} %slice.6), channel_id=1, source_target_pairs={{0,1},{1,2},{2,3},{3,0},{4,5},{5,6},{6,7},{7,4},{8,9},{9,10},{10,1... | collective-permute-start | bytes 2359304 | tf_op jit(solution)/shard_map/ppermute | solution.py:282
  83.9 5.1 %collective-permute-start.5 = (bf16[96,4096]{1,0:T(8,128)(2,1)}, bf16[96,4096]{1,0:T(8,128)(2,1)}, u32[]{:S(2)}, u32[]{:S(2)}) collective-permute-start(bf16[96,4096]{1,0:T(8,128)(2,1)} %slice.7), channel_id=1, source_target_pairs={{0,3},{1,0},{2,1},{3,2},{4,7},{5,4},{6,5},{7,6},{8,11},{9,8},{10,9... | collective-permute-start | bytes 2359304 | tf_op jit(solution)/shard_map/ppermute | solution.py:282
  89.1 0.0 collective-permute-done.8.g3
  89.1 1.2 shard_map.91
  90.3 0.0 copy-start.2
  90.3 0.8 copy-done.2
  91.1 3.2 %all-to-all-done = bf16[128,8,1280]{2,1,0:T(8,128)(2,1)} async-done(((bf16[128,8,1280]{2,1,0:T(8,128)(2,1)}), bf16[128,8,1280]{2,1,0:T(8,128)(2,1)}, u32[]{:S(2)}, u32[]{:S(2)}) %all-to-all-start) | async-done | bytes 2621472 | tf_op jit(solution)/shard_map/all_to_all | solution.py:296
  94.3 11.0 %all-to-all-start.1 = ((bf16[128,8,256]{2,1,0:T(8,128)(2,1)}), bf16[128,8,256]{2,1,0:T(8,128)(2,1)}, u32[]{:S(2)}, u32[]{:S(2)}) async-start(bf16[128,8,256]{2,1,0:T(8,128)(2,1)} %bitcast.12), calls=%async_computation.1 | async-start | bytes 1048576 | tf_op jit(solution)/shard_map/all_to_all | solution.py:296
  105.3 0.0 copy-start.3
  105.3 1.2 copy-done.3
  106.5 2.3 %shard_map.89.weights_ref = bf16[896,4096]{1,0:T(8,128)(2,1)S(1)} custom-call(s32[2]{0:T(128)S(1)} %pad_add_fusion.pos_ref, bf16[128,4096]{1,0:T(8,128)(2,1)S(1)} %copy-done.3, bf16[192,4096]{1,0:T(8,128)(2,1)} %bitcast.5.own_ref, bf16[192,4096]{1,0:T(8,128)(2,1)S(1)} %collective-permute-done.2.right_ref, bf16[96,4096]{1,0:T(8,128)(2,1)} %collective-permute-done.4.top_ref, ...), custom_call_target="tpu_custom_call" | custom-call | flops 1000 | bytes 14680064 | tf_op jit(solution)/shard_map/pallas_call | solution.py:348
  108.9 0.0 copy-start.9
  108.9 7.2 %shard_map.90 = (f32[768,384]{1,0:T(8,128)S(1)}, f32[128,1024]{1,0:T(8,128)S(1)}, bf16[128,1024]{1,0:T(8,128)(2,1)S(1)}, bf16[128,1024]{1,0:T(8,128)(2,1)S(1)}, bf16[128,1024]{1,0:T(8,128)(2,1)S(1)}) custom-call(s32[2]{0:T(128)S(1)} %pad_add_fusion.pos_ref, bf16[1024,1280]{1,0:T(8,128)(2,1)} %bitcast.4.rows_ref, bf16[896,4096]{1,0:T(8,128)(2,1)S(1)} %shard_map.89.weights_ref), custom_call_target="tpu_custom_call" | custom-call | flops 4294967296 | bytes 12582912 | tf_op jit(solution)/shard_map/pallas_call | solution.py:354
  116.1 1.0 copy-done.10
  117.2 1.9 %collective-permute-start.9 = (bf16[128,1024]{1,0:T(8,128)(2,1)S(1)}, bf16[128,1024]{1,0:T(8,128)(2,1)S(1)}, u32[]{:S(2)}, u32[]{:S(2)}) collective-permute-start(bf16[128,1024]{1,0:T(8,128)(2,1)S(1)} %get-tuple-element.30), channel_id=1, source_target_pairs={{0,1},{1,2},{2,3},{3,0},{4,5},{5,6},{6,7},{7,4},{8,9},{9,10},{10,1... | collective-permute-start | bytes 786440 | tf_op jit(solution)/shard_map/ppermute | solution.py:282
  119.1 3.4 %collective-permute-start.10 = (bf16[128,1024]{1,0:T(8,128)(2,1)S(1)}, bf16[128,1024]{1,0:T(8,128)(2,1)S(1)}, u32[]{:S(2)}, u32[]{:S(2)}) collective-permute-start(bf16[128,1024]{1,0:T(8,128)(2,1)S(1)} %get-tuple-element.31), channel_id=1, source_target_pairs={{0,2},{1,3},{2,0},{3,1},{4,6},{5,7},{6,4},{7,5},{8,10},{9,11},{10,... | collective-permute-start | bytes 786440 | tf_op jit(solution)/shard_map/ppermute | solution.py:282
  122.5 3.7 %collective-permute-start.11 = (bf16[128,1024]{1,0:T(8,128)(2,1)S(1)}, bf16[128,1024]{1,0:T(8,128)(2,1)S(1)}, u32[]{:S(2)}, u32[]{:S(2)}) collective-permute-start(bf16[128,1024]{1,0:T(8,128)(2,1)S(1)} %get-tuple-element.32), channel_id=1, source_target_pairs={{0,3},{1,0},{2,1},{3,2},{4,7},{5,4},{6,5},{7,6},{8,11},{9,8},{10,9... | collective-permute-start | bytes 786440 | tf_op jit(solution)/shard_map/ppermute | solution.py:282
  126.2 1.3 copy-done.11
  127.4 3.0 %shard_map.92 = (f32[192,128]{1,0:T(8,128)S(1)}, bf16[768,128]{1,0:T(8,128)(2,1)}) custom-call(s32[2]{0:T(128)S(1)} %pad_add_fusion.pos_ref, bf16[128,768]{1,0:T(8,128)(2,1)S(1)} %copy-done.9, f32[768,384]{1,0:T(8,128)S(1)} %copy-done.11, bf16[1024,256]{1,0:T(8,128)(2,1)} %bitcast.8.got_ref), custom_call_target="tpu_custom_call" | custom-call | flops 1073741824 | bytes 3145728 | tf_op jit(solution)/shard_map/pallas_call | solution.py:365
  130.4 4.2 %all-to-all-start.2 = ((bf16[4,192,128]{2,1,0:T(8,128)(2,1)}), bf16[4,192,128]{2,1,0:T(8,128)(2,1)S(1)}, u32[]{:S(2)}, u32[]{:S(2)}) async-start(bf16[4,192,128]{2,1,0:T(8,128)(2,1)} %bitcast.10), calls=%async_computation.2 | async-start | bytes 393216 | tf_op jit(solution)/shard_map/all_to_all | solution.py:374
  135.3 1.7 %collective-permute-done.11.i3 = bf16[128,1024]{1,0:T(8,128)(2,1)S(1)} collective-permute-done((bf16[128,1024]{1,0:T(8,128)(2,1)S(1)}, bf16[128,1024]{1,0:T(8,128)(2,1)S(1)}, u32[]{:S(2)}, u32[]{:S(2)}) %collective-permute-start.11) | collective-permute-done | bytes 262176 | tf_op jit(solution)/shard_map/ppermute | solution.py:282
  137.0 1.0 shard_map.93
  138.0 2.9 %all-to-all-done.2.parts_ref = bf16[4,192,128]{2,1,0:T(8,128)(2,1)S(1)} async-done(((bf16[4,192,128]{2,1,0:T(8,128)(2,1)}), bf16[4,192,128]{2,1,0:T(8,128)(2,1)S(1)}, u32[]{:S(2)}, u32[]{:S(2)}) %all-to-all-start.2) | async-done | bytes 196640 | tf_op jit(solution)/shard_map/all_to_all | solution.py:374
  140.9 1.2 shard_map.94
  (21 shorter events, 0.0 us)
Async XLA Ops:
  0.6 6.5 %copy-start.8 = (s32[128,8]{0,1:T(8,128)S(1)}, s32[128,8]{0,1:T(8,128)}, u32[]{:S(2)}) copy-start(s32[128,8]{0,1:T(8,128)} %param.8) | copy-start | bytes 12292
  0.7 1.2 copy-start
  2.0 0.7 copy-start.7
  2.6 4.5 %copy-start.1 = (bf16[128,4096]{1,0:T(8,128)(2,1)S(1)}, bf16[128,4096]{1,0:T(8,128)(2,1)}, u32[]{:S(2)}) copy-start(bf16[128,4096]{1,0:T(8,128)(2,1)} %tokens_ref.3) | copy-start | bytes 3145732
  3.2 3.9 %collective-permute-start = (bf16[144,2048]{1,0:T(8,128)(2,1)S(1)}, bf16[144,2048]{1,0:T(8,128)(2,1)S(1)}, u32[]{:S(2)}, u32[]{:S(2)}) collective-permute-start(bf16[144,2048]{1,0:T(8,128)(2,1)S(1)} %shard_map.86), channel_id=1, source_target_pairs={{0,4},{4,0},{8,12},{12,8},{16,20},{20,16},{24,28},{28,24},{32,36},... | collective-permute-start | bytes 1769480 | tf_op jit(solution)/shard_map/ppermute | solution.py:290
  7.1 4.3 %copy-start.4 = (bf16[144,2048]{1,0:T(8,128)(2,1)}, bf16[144,2048]{1,0:T(8,128)(2,1)S(1)}, u32[]{:S(2)}) copy-start(bf16[144,2048]{1,0:T(8,128)(2,1)S(1)} %collective-permute-done.other_ref) | copy-start | bytes 1769476
  11.5 17.9 %copy-start.12 = (bf16[128,8,192]{0,2,1:T(8,128)(2,1)S(1)}, bf16[128,8,192]{0,2,1:T(8,128)(2,1)}, u32[]{:S(2)}) copy-start(bf16[128,8,192]{0,2,1:T(8,128)(2,1)} %param.9) | copy-start | bytes 1179652
  11.5 82.9 %all-to-all-start = ((bf16[128,8,1280]{2,1,0:T(8,128)(2,1)}), bf16[128,8,1280]{2,1,0:T(8,128)(2,1)}, u32[]{:S(2)}, u32[]{:S(2)}) async-start(bf16[128,8,1280]{2,1,0:T(8,128)(2,1)} %bitcast.3), calls=%async_computation | async-start | bytes 5242880 | tf_op jit(solution)/shard_map/all_to_all | solution.py:296
  30.6 43.8 %collective-permute-start.2 = (bf16[192,4096]{1,0:T(8,128)(2,1)}, bf16[192,4096]{1,0:T(8,128)(2,1)S(1)}, u32[]{:S(2)}, u32[]{:S(2)}) collective-permute-start(bf16[192,4096]{1,0:T(8,128)(2,1)} %bitcast.5.own_ref), channel_id=1, source_target_pairs={{0,3},{1,0},{2,1},{3,2},{4,7},{5,4},{6,5},{7,6},{8,11},{9,8},{10,9... | collective-permute-start | bytes 4718600 | tf_op jit(solution)/shard_map/ppermute | solution.py:282
  35.2 44.8 %collective-permute-start.1 = (bf16[192,4096]{1,0:T(8,128)(2,1)}, bf16[192,4096]{1,0:T(8,128)(2,1)S(1)}, u32[]{:S(2)}, u32[]{:S(2)}) collective-permute-start(bf16[192,4096]{1,0:T(8,128)(2,1)} %bitcast.5.own_ref), channel_id=1, source_target_pairs={{0,1},{1,2},{2,3},{3,0},{4,5},{5,6},{6,7},{7,4},{8,9},{9,10},{10,1... | collective-permute-start | bytes 4718600 | tf_op jit(solution)/shard_map/ppermute | solution.py:282
  37.2 4.0 %collective-permute-start.3 = (bf16[1024,192]{1,0:T(8,128)(2,1)}, bf16[1024,192]{1,0:T(8,128)(2,1)S(1)}, u32[]{:S(2)}, u32[]{:S(2)}) collective-permute-start(bf16[1024,192]{1,0:T(8,128)(2,1)} %bitcast.13), channel_id=1, source_target_pairs={{0,4},{4,0},{8,12},{12,8},{16,20},{20,16},{24,28},{28,24},{32,36},... | collective-permute-start | bytes 1179656 | tf_op jit(solution)/shard_map/ppermute | solution.py:290
  41.2 1.1 copy-start.5
  42.3 1.0 copy-start.6
  46.2 42.9 %collective-permute-start.7 = (bf16[384,256]{1,0:T(8,128)(2,1)S(1)}, bf16[384,256]{1,0:T(8,128)(2,1)S(1)}, u32[]{:S(2)}, u32[]{:S(2)}) collective-permute-start(bf16[384,256]{1,0:T(8,128)(2,1)S(1)} %get-tuple-element.26), channel_id=1, source_target_pairs={{0,2},{1,3},{2,0},{3,1},{4,6},{5,7},{6,4},{7,5},{8,10},{9,11},{10,... | collective-permute-start | bytes 589832 | tf_op jit(solution)/shard_map/ppermute | solution.py:282
  50.3 38.7 %collective-permute-start.8 = (bf16[384,256]{1,0:T(8,128)(2,1)S(1)}, bf16[384,256]{1,0:T(8,128)(2,1)S(1)}, u32[]{:S(2)}, u32[]{:S(2)}) collective-permute-start(bf16[384,256]{1,0:T(8,128)(2,1)S(1)} %get-tuple-element.27), channel_id=1, source_target_pairs={{0,3},{1,0},{2,1},{3,2},{4,7},{5,4},{6,5},{7,6},{8,11},{9,8},{10,9... | collective-permute-start | bytes 589832 | tf_op jit(solution)/shard_map/ppermute | solution.py:282
  53.4 35.7 %collective-permute-start.6 = (bf16[384,256]{1,0:T(8,128)(2,1)S(1)}, bf16[384,256]{1,0:T(8,128)(2,1)S(1)}, u32[]{:S(2)}, u32[]{:S(2)}) collective-permute-start(bf16[384,256]{1,0:T(8,128)(2,1)S(1)} %get-tuple-element.21), channel_id=1, source_target_pairs={{0,1},{1,2},{2,3},{3,0},{4,5},{5,6},{6,7},{7,4},{8,9},{9,10},{10,1... | collective-permute-start | bytes 589832 | tf_op jit(solution)/shard_map/ppermute | solution.py:282
  82.0 23.3 %collective-permute-start.4 = (bf16[96,4096]{1,0:T(8,128)(2,1)}, bf16[96,4096]{1,0:T(8,128)(2,1)}, u32[]{:S(2)}, u32[]{:S(2)}) collective-permute-start(bf16[96,4096]{1,0:T(8,128)(2,1)} %slice.6), channel_id=1, source_target_pairs={{0,1},{1,2},{2,3},{3,0},{4,5},{5,6},{6,7},{7,4},{8,9},{9,10},{10,1... | collective-permute-start | bytes 2359304 | tf_op jit(solution)/shard_map/ppermute | solution.py:282
  83.9 21.4 %collective-permute-start.5 = (bf16[96,4096]{1,0:T(8,128)(2,1)}, bf16[96,4096]{1,0:T(8,128)(2,1)}, u32[]{:S(2)}, u32[]{:S(2)}) collective-permute-start(bf16[96,4096]{1,0:T(8,128)(2,1)} %slice.7), channel_id=1, source_target_pairs={{0,3},{1,0},{2,1},{3,2},{4,7},{5,4},{6,5},{7,6},{8,11},{9,8},{10,9... | collective-permute-start | bytes 2359304 | tf_op jit(solution)/shard_map/ppermute | solution.py:282
  90.3 0.8 copy-start.2
  94.3 31.8 %all-to-all-start.1 = ((bf16[128,8,256]{2,1,0:T(8,128)(2,1)}), bf16[128,8,256]{2,1,0:T(8,128)(2,1)}, u32[]{:S(2)}, u32[]{:S(2)}) async-start(bf16[128,8,256]{2,1,0:T(8,128)(2,1)} %bitcast.12), calls=%async_computation.1 | async-start | bytes 1048576 | tf_op jit(solution)/shard_map/all_to_all | solution.py:296
  105.3 1.2 copy-start.3
  108.9 17.3 %copy-start.9 = (bf16[128,768]{1,0:T(8,128)(2,1)S(1)}, bf16[128,768]{1,0:T(8,128)(2,1)}, u32[]{:S(2)}) copy-start(bf16[128,768]{1,0:T(8,128)(2,1)} %grad_probes_ref.1) | copy-start | bytes 589828
  116.1 1.0 copy-start.10
  117.2 18.1 %collective-permute-start.9 = (bf16[128,1024]{1,0:T(8,128)(2,1)S(1)}, bf16[128,1024]{1,0:T(8,128)(2,1)S(1)}, u32[]{:S(2)}, u32[]{:S(2)}) collective-permute-start(bf16[128,1024]{1,0:T(8,128)(2,1)S(1)} %get-tuple-element.30), channel_id=1, source_target_pairs={{0,1},{1,2},{2,3},{3,0},{4,5},{5,6},{6,7},{7,4},{8,9},{9,10},{10,1... | collective-permute-start | bytes 786440 | tf_op jit(solution)/shard_map/ppermute | solution.py:282
  119.1 16.2 %collective-permute-start.10 = (bf16[128,1024]{1,0:T(8,128)(2,1)S(1)}, bf16[128,1024]{1,0:T(8,128)(2,1)S(1)}, u32[]{:S(2)}, u32[]{:S(2)}) collective-permute-start(bf16[128,1024]{1,0:T(8,128)(2,1)S(1)} %get-tuple-element.31), channel_id=1, source_target_pairs={{0,2},{1,3},{2,0},{3,1},{4,6},{5,7},{6,4},{7,5},{8,10},{9,11},{10,... | collective-permute-start | bytes 786440 | tf_op jit(solution)/shard_map/ppermute | solution.py:282
  122.5 14.6 %collective-permute-start.11 = (bf16[128,1024]{1,0:T(8,128)(2,1)S(1)}, bf16[128,1024]{1,0:T(8,128)(2,1)S(1)}, u32[]{:S(2)}, u32[]{:S(2)}) collective-permute-start(bf16[128,1024]{1,0:T(8,128)(2,1)S(1)} %get-tuple-element.32), channel_id=1, source_target_pairs={{0,3},{1,0},{2,1},{3,2},{4,7},{5,4},{6,5},{7,6},{8,11},{9,8},{10,9... | collective-permute-start | bytes 786440 | tf_op jit(solution)/shard_map/ppermute | solution.py:282
  126.2 1.3 copy-start.11
  130.4 10.5 %all-to-all-start.2 = ((bf16[4,192,128]{2,1,0:T(8,128)(2,1)}), bf16[4,192,128]{2,1,0:T(8,128)(2,1)S(1)}, u32[]{:S(2)}, u32[]{:S(2)}) async-start(bf16[4,192,128]{2,1,0:T(8,128)(2,1)} %bitcast.10), calls=%async_computation.2 | async-start | bytes 393216 | tf_op jit(solution)/shard_map/all_to_all | solution.py:374

commit v11 on v10

--- a/solution.py
+++ b/solution.py
@@ -45,12 +45,12 @@
     return jnp.where(mask, 1.0, 0.0).astype(BF)
 
 
-def kernel_call(body, out_shape, in_specs, flops, bytes_accessed, limit, scratch=()):
+def kernel_call(body, out_shape, in_specs, flops, bytes_accessed, limit, scratch=(), out_specs=None):
     return pl.pallas_call(
         body,
         out_shape=out_shape,
         in_specs=in_specs,
-        out_specs=jax.tree.map(lambda _: VM, out_shape),
+        out_specs=out_specs or jax.tree.map(lambda _: VM, out_shape),
         scratch_shapes=list(scratch),
         compiler_params=pltpu.CompilerParams(vmem_limit_bytes=limit * MIB),
         cost_estimate=pl.CostEstimate(
@@ -95,29 +95,22 @@
     return other_ref[TOK:, :TOK].astype(F32)[:TOP].astype(jnp.int32)
 
 
-def fold(picked, many, put):
+def fold(picked, many, g):
     size = 256 // many
     width = picked.shape[1] // many
     shape = (256, 256)
     to = iota(shape, 0)
     order = ones_where(iota(shape, 1) == to % many * size + to // many)
-    for g in range(ROWS // 256):
-        at = slice(g * size, (g + 1) * size)
-        parts = [picked[at, p * width : (p + 1) * width] for p in range(many)]
-        put(slice(g * 256, (g + 1) * 256), dot(order, jnp.concatenate(parts, 0)).astype(BF))
-
-
-def send_rows(pos_ref, ids_ref, tokens_ref, other_ref, out_ref, half_ref, half_ids_ref):
+    at = slice(g * size, (g + 1) * size)
+    parts = [picked[at, p * width : (p + 1) * width] for p in range(many)]
+    return dot(order, jnp.concatenate(parts, 0)).astype(BF)
+
+
+def send_rows(
+    pos_ref, ids_ref, tokens_ref, other_ref, out_ref, made_ref, half_ref, half_ids_ref, sems
+):
     x, c = pos_ref[0], pos_ref[1]
     mine = x // 2 == c
-    table = spread(places(ids_ref[...]), 2)
-    place = 2 * x + iota(table.shape, 0) % 2
-    picked = dot(ones_where(table == place.astype(F32)), tokens_ref[...]).astype(BF)
-
-    def put_whole(at, got):
-        out_ref[at, :SHARE] = got
-
-    fold(picked, 4, put_whole)
 
     @pl.when(mine)
     def _():
@@ -130,12 +123,21 @@
         half_ids_ref[...] = other_ids(other_ref)
 
     table = places(half_ids_ref[...])
-    picked = dot(ones_where(table == (FIRST + x % 2).astype(F32)), half_ref[...]).astype(BF)
-
-    def put_shared(at, got):
-        out_ref[at, SHARE:] = got
-
-    fold(picked, FOLD, put_shared)
+    shared = dot(ones_where(table == (FIRST + x % 2).astype(F32)), half_ref[...]).astype(BF)
+    table = spread(places(ids_ref[...]), 2)
+    place = 2 * x + iota(table.shape, 0) % 2
+    picks = ones_where(table == place.astype(F32))
+    copies = []
+    for g in range(ROWS // 256):
+        at = slice(g * 256, (g + 1) * 256)
+        whole = dot(picks[g * 64 : (g + 1) * 64], tokens_ref[...]).astype(BF)
+        made_ref[at, :SHARE] = fold(whole, 4, 0)
+        made_ref[at, SHARE:] = fold(shared, FOLD, g)
+        copy = pltpu.make_async_copy(made_ref.at[at, :], out_ref.at[at, :], sems.at[g])
+        copy.start()
+        copies.append(copy)
+    for copy in copies:
+        copy.wait()
 
 
 def pick_grads(pos_ref, ids_ref, other_ref, grads_ref, other_grads_ref, *outs):
@@ -208,7 +210,7 @@
 
 
 def products(
-    pos_ref, rows_ref, weights_ref, gate_ref, i0, i1, i2, i3, rows_all_ref, sum_ref
+    pos_ref, rows_ref, weights_ref, slope_ref, i0, i1, i2, i3, rows_all_ref, sum_ref
 ):
     x = pos_ref[0]
 
@@ -223,7 +225,9 @@
     rows_all_ref[SLOTS + PAIRS :, :] = jnp.zeros((ALL - SLOTS - PAIRS, D), BF)
     rows = rows_all_ref[...]
     both = dot(weights_ref[...], rows, NT)
-    gate_ref[...] = both[:FFW]
+    gate = both[:FFW]
+    sigmoid = 1.0 / (1.0 + jnp.exp(-gate))
+    slope_ref[...] = sigmoid * (1.0 + gate * (1.0 - sigmoid))
     sum_ref[...] = dot(both[FFW:].astype(BF), rows)
     for k, out in enumerate((i0, i1, i2, i3)):
         base = lax.rem(x + k, REPS) * SHARE
@@ -231,10 +235,12 @@
 
 
 def gate_part(
-    pos_ref, grad_probes_ref, gate_ref, got_ref, own_ref, out_ref,
-    whole_ref, shared_ref, sketch_ref,
+    pos_ref, grad_probes_ref, slope_ref, got_ref, own_ref, out_ref,
+    whole_ref, shared_ref, sketch_ref, held_ref, sem,
 ):
     x = pos_ref[0]
+    copy = pltpu.make_async_copy(slope_ref, held_ref, sem)
+    copy.start()
 
     def put_whole(p, at, got):
         whole_ref[p * SLOTS + at.start : p * SLOTS + at.stop, :] = got
@@ -257,9 +263,8 @@
     late = jnp.where(iota((FFW, 128), 1) < PAIRS, late, 0.0)
     early = jnp.concatenate([whole[:, b * SLOTS : (b + 1) * SLOTS] for b in range(4)], 0)
     grads = jnp.concatenate([early, late], 1)
-    gate = gate_ref[...]
-    s = 1.0 / (1.0 + jnp.exp(-gate))
-    gate_grad = (grads * (s * (1.0 + gate * (1.0 - s)))).astype(BF)
+    copy.wait()
+    gate_grad = (grads * held_ref[...]).astype(BF)
     projected = dot(grad_probes_ref[...], gate_grad).astype(BF)
     sketch_ref[...] = dot(gate_grad, projected, NT)
     out_ref[...] = sketch_ref[...].astype(BF)
@@ -322,7 +327,13 @@
         1 << 30,
         5 * MIB,
         20,
-        [pltpu.VMEM((TOK, HALF), BF), pltpu.VMEM((TOP, TOK), jnp.int32)],
+        [
+            pltpu.VMEM((ROWS, SHARE + STRIP), BF),
+            pltpu.VMEM((TOK, HALF), BF),
+            pltpu.VMEM((TOP, TOK), jnp.int32),
+            pltpu.SemaphoreType.DMA((ROWS // 256,)),
+        ],
+        pl.BlockSpec(memory_space=pl.ANY),
     )(pos, ids_t, tokens, other)
     rows = to_owners(out_rows)
 
@@ -351,7 +362,7 @@
     got = to_owners(out_grads)
 
     kinds = [F32, BF, BF, BF]
-    gate, *inputs = kernel_call(
+    slope, *inputs = kernel_call(
         products,
         [sds((FFW, ALL), F32)] + [sds((R, SHARE), kind) for kind in kinds],
         [SM] + [VM] * 2,
@@ -365,12 +376,18 @@
     own_sketch, sketch = kernel_call(
         gate_part,
         [sds((UNITS, R), F32), sds((FFW, R), BF)],
-        [SM] + [VM] * 3,
+        [SM, VM, pl.BlockSpec(memory_space=pl.ANY), VM],
         1 << 30,
         3 * MIB,
-        14,
-        [pltpu.VMEM((ROWS, 256), BF), pltpu.VMEM((ROWS, 256), BF), pltpu.VMEM((FFW, R), F32)],
-    )(pos, grad_probes, gate, got)
+        16,
+        [
+            pltpu.VMEM((ROWS, 256), BF),
+            pltpu.VMEM((ROWS, 256), BF),
+            pltpu.VMEM((FFW, R), F32),
+            pltpu.VMEM((FFW, ALL), F32),
+            pltpu.SemaphoreType.DMA,
+        ],
+    )(pos, grad_probes, slope, got)
     sketches = lax.all_to_all(
         sketch.reshape(REPS, UNITS, R), "rep", split_axis=0, concat_axis=0, tiled=True
     )

time: 143 us -> 143 us (level)
  transfers between devices with their start and end apart: 15 -> 15, of which waited for: 7 -> 7; matrix products, arithmetic and copies ran while one was open for 2% -> 2% of each run, Pallas kernels for 12% -> 13%
where the time goes in v11:
time: 143 us; the launch traced here: 142 us
  starting transfers between devices  69.5 us (49%)
  waiting for transfers between devices  35.8 us (25%)
  Pallas kernels  23.7 us (17%)
  local copies, waits for them, and re-layouts  11.5 us (8%)
  between operations  1.65 us (1%)
    ppermute x10, starting transfers between devices, shift(): lax.ppermute(block, 'rep', [(i, (i + k) % REPS) for i in range(REPS)])  32.6 us
    all_to_all x2, starting transfers between devices, to_owners(): lax.all_to_all(rows, 'ep', split_axis=0, concat_axis=0, tiled=True)  28.8 us
    ppermute x10, waiting for transfers between devices, shift(): lax.ppermute(block, 'rep', [(i, (i + k) % REPS) for i in range(REPS)])  25 us
    unnamed x27, local copies, waits for them, and re-layouts  9.53 us
    pallas_call x1, Pallas kernels, local(): kernel_call(products, [sds((FFW, ALL), F32)] + [sds((R, SHARE), kind) for...  7.32 us
    all_to_all x1, starting transfers between devices, local(): lax.all_to_all(sketch.reshape(REPS, UNITS, R), 'rep', split_axis=0, conca...  4.19 us
    ppermute x2, waiting for transfers between devices, swap(): return lax.ppermute(block, 'ep', [(i, i ^ 1) for i in range(OWNERS)])  4.06 us
    pallas_call x1, Pallas kernels, local(): kernel_call(send_rows, sds((ROWS, SHARE + STRIP), BF), [SM] + [VM] * 3, 1...  3.94 us
  transfers between devices with their start and end apart: 15, of which 7 were waited for; matrix products, arithmetic and copies ran while one was open for 2% of the time, Pallas kernels for 13%

profile of v11, /device:TPU:8, one launch (start us, length us, event | category | flops | bytes accessed | tf_op | source)
XLA Modules:
  0.0 142.2 jit_solution(5034408953261447278)
XLA Ops:
  0.6 0.0 copy-start.8
  0.7 0.1 pad_add_fusion.pos_ref
  0.7 1.2 copy-done
  2.0 0.7 copy-done.7
  2.6 0.6 shard_map.86
  3.2 1.9 %collective-permute-start = (bf16[144,2048]{1,0:T(8,128)(2,1)S(1)}, bf16[144,2048]{1,0:T(8,128)(2,1)S(1)}, u32[]{:S(2)}, u32[]{:S(2)}) collective-permute-start(bf16[144,2048]{1,0:T(8,128)(2,1)S(1)} %shard_map.86), channel_id=1, source_target_pairs={{0,4},{4,0},{8,12},{12,8},{16,20},{20,16},{24,28},{28,24},{32,36},... | collective-permute-start | bytes 1769480 | tf_op jit(solution)/shard_map/ppermute | solution.py:295
  5.2 2.0 %collective-permute-done.other_ref = bf16[144,2048]{1,0:T(8,128)(2,1)S(1)} collective-permute-done((bf16[144,2048]{1,0:T(8,128)(2,1)S(1)}, bf16[144,2048]{1,0:T(8,128)(2,1)S(1)}, u32[]{:S(2)}, u32[]{:S(2)}) %collective-permute-start) | collective-permute-done | bytes 589856 | tf_op jit(solution)/shard_map/ppermute | solution.py:295
  7.1 3.9 %shard_map.87 = bf16[1024,1280]{1,0:T(8,128)(2,1)} custom-call(s32[2]{0:T(128)S(1)} %pad_add_fusion.pos_ref, s32[8,128]{1,0:T(8,128)S(1)} %bitcast.16, bf16[128,4096]{1,0:T(8,128)(2,1)S(1)} %copy-done.1, bf16[144,2048]{1,0:T(8,128)(2,1)S(1)} %collective-permute-done.other_ref), custom_call_target="tpu_custom_call" | custom-call | flops 1073741824 | bytes 5242880 | tf_op jit(solution)/shard_map/pallas_call | solution.py:323
  11.1 0.0 copy-start.12
  11.1 17.9 %all-to-all-start = ((bf16[128,8,1280]{2,1,0:T(8,128)(2,1)}), bf16[128,8,1280]{2,1,0:T(8,128)(2,1)}, u32[]{:S(2)}, u32[]{:S(2)}) async-start(bf16[128,8,1280]{2,1,0:T(8,128)(2,1)} %bitcast.3), calls=%async_computation | async-start | bytes 5242880 | tf_op jit(solution)/shard_map/all_to_all | solution.py:301
  29.0 1.2 copy.9
  30.2 4.6 %collective-permute-start.2 = (bf16[192,4096]{1,0:T(8,128)(2,1)}, bf16[192,4096]{1,0:T(8,128)(2,1)S(1)}, u32[]{:S(2)}, u32[]{:S(2)}) collective-permute-start(bf16[192,4096]{1,0:T(8,128)(2,1)} %bitcast.5.own_ref), channel_id=1, source_target_pairs={{0,3},{1,0},{2,1},{3,2},{4,7},{5,4},{6,5},{7,6},{8,11},{9,8},{10,9... | collective-permute-start | bytes 4718600 | tf_op jit(solution)/shard_map/ppermute | solution.py:287
  34.9 1.9 %collective-permute-start.1 = (bf16[192,4096]{1,0:T(8,128)(2,1)}, bf16[192,4096]{1,0:T(8,128)(2,1)S(1)}, u32[]{:S(2)}, u32[]{:S(2)}) collective-permute-start(bf16[192,4096]{1,0:T(8,128)(2,1)} %bitcast.5.own_ref), channel_id=1, source_target_pairs={{0,1},{1,2},{2,3},{3,0},{4,5},{5,6},{6,7},{7,4},{8,9},{9,10},{10,1... | collective-permute-start | bytes 4718600 | tf_op jit(solution)/shard_map/ppermute | solution.py:287
  36.8 1.9 %collective-permute-start.3 = (bf16[1024,192]{1,0:T(8,128)(2,1)}, bf16[1024,192]{1,0:T(8,128)(2,1)S(1)}, u32[]{:S(2)}, u32[]{:S(2)}) collective-permute-start(bf16[1024,192]{1,0:T(8,128)(2,1)} %bitcast.13), channel_id=1, source_target_pairs={{0,4},{4,0},{8,12},{12,8},{16,20},{20,16},{24,28},{28,24},{32,36},... | collective-permute-start | bytes 1179656 | tf_op jit(solution)/shard_map/ppermute | solution.py:295
  38.7 2.1 %collective-permute-done.3.other_grads_ref = bf16[1024,192]{1,0:T(8,128)(2,1)S(1)} collective-permute-done((bf16[1024,192]{1,0:T(8,128)(2,1)}, bf16[1024,192]{1,0:T(8,128)(2,1)S(1)}, u32[]{:S(2)}, u32[]{:S(2)}) %collective-permute-start.3) | collective-permute-done | bytes 393248 | tf_op jit(solution)/shard_map/ppermute | solution.py:295
  40.8 1.1 copy-done.5
  41.9 1.0 copy-done.6
  42.9 2.8 %shard_map.88 = (bf16[384,256]{1,0:T(8,128)(2,1)S(1)}, bf16[384,256]{1,0:T(8,128)(2,1)S(1)}, bf16[384,256]{1,0:T(8,128)(2,1)S(1)}, bf16[384,256]{1,0:T(8,128)(2,1)S(1)}) custom-call(s32[2]{0:T(128)S(1)} %pad_add_fusion.pos_ref, s32[8,128]{1,0:T(8,128)S(1)} %bitcast.17, bf16[144,2048]{1,0:T(8,128)(2,1)S(1)} %copy-done.5, bf16[1024,192]{1,0:T(8,128)(2,1)S(1)} %bitcast.14, ...), custom_call_target="tpu_custom_call" | custom-call | flops 5368709120 | bytes 3145728 | tf_op jit(solution)/shard_map/pallas_call | solution.py:344
  45.8 4.2 %collective-permute-start.7 = (bf16[384,256]{1,0:T(8,128)(2,1)S(1)}, bf16[384,256]{1,0:T(8,128)(2,1)S(1)}, u32[]{:S(2)}, u32[]{:S(2)}) collective-permute-start(bf16[384,256]{1,0:T(8,128)(2,1)S(1)} %get-tuple-element.26), channel_id=1, source_target_pairs={{0,2},{1,3},{2,0},{3,1},{4,6},{5,7},{6,4},{7,5},{8,10},{9,11},{10,... | collective-permute-start | bytes 589832 | tf_op jit(solution)/shard_map/ppermute | solution.py:287
  50.0 3.1 %collective-permute-start.8 = (bf16[384,256]{1,0:T(8,128)(2,1)S(1)}, bf16[384,256]{1,0:T(8,128)(2,1)S(1)}, u32[]{:S(2)}, u32[]{:S(2)}) collective-permute-start(bf16[384,256]{1,0:T(8,128)(2,1)S(1)} %get-tuple-element.27), channel_id=1, source_target_pairs={{0,3},{1,0},{2,1},{3,2},{4,7},{5,4},{6,5},{7,6},{8,11},{9,8},{10,9... | collective-permute-start | bytes 589832 | tf_op jit(solution)/shard_map/ppermute | solution.py:287
  53.0 2.8 %collective-permute-start.6 = (bf16[384,256]{1,0:T(8,128)(2,1)S(1)}, bf16[384,256]{1,0:T(8,128)(2,1)S(1)}, u32[]{:S(2)}, u32[]{:S(2)}) collective-permute-start(bf16[384,256]{1,0:T(8,128)(2,1)S(1)} %get-tuple-element.21), channel_id=1, source_target_pairs={{0,1},{1,2},{2,3},{3,0},{4,5},{5,6},{6,7},{7,4},{8,9},{9,10},{10,1... | collective-permute-start | bytes 589832 | tf_op jit(solution)/shard_map/ppermute | solution.py:287
  55.8 18.2 %collective-permute-done.2.right_ref = bf16[192,4096]{1,0:T(8,128)(2,1)S(1)} collective-permute-done((bf16[192,4096]{1,0:T(8,128)(2,1)}, bf16[192,4096]{1,0:T(8,128)(2,1)S(1)}, u32[]{:S(2)}, u32[]{:S(2)}) %collective-permute-start.2) | collective-permute-done | bytes 1572896 | tf_op jit(solution)/shard_map/ppermute | solution.py:287
  74.0 5.7 %collective-permute-done.1.left_ref = bf16[192,4096]{1,0:T(8,128)(2,1)S(1)} collective-permute-done((bf16[192,4096]{1,0:T(8,128)(2,1)}, bf16[192,4096]{1,0:T(8,128)(2,1)S(1)}, u32[]{:S(2)}, u32[]{:S(2)}) %collective-permute-start.1) | collective-permute-done | bytes 1572896 | tf_op jit(solution)/shard_map/ppermute | solution.py:287
  79.7 0.9 slice.7
  80.6 1.0 slice.6
  81.6 1.9 %collective-permute-start.4 = (bf16[96,4096]{1,0:T(8,128)(2,1)}, bf16[96,4096]{1,0:T(8,128)(2,1)}, u32[]{:S(2)}, u32[]{:S(2)}) collective-permute-start(bf16[96,4096]{1,0:T(8,128)(2,1)} %slice.6), channel_id=1, source_target_pairs={{0,1},{1,2},{2,3},{3,0},{4,5},{5,6},{6,7},{7,4},{8,9},{9,10},{10,1... | collective-permute-start | bytes 2359304 | tf_op jit(solution)/shard_map/ppermute | solution.py:287
  83.6 5.1 %collective-permute-start.5 = (bf16[96,4096]{1,0:T(8,128)(2,1)}, bf16[96,4096]{1,0:T(8,128)(2,1)}, u32[]{:S(2)}, u32[]{:S(2)}) collective-permute-start(bf16[96,4096]{1,0:T(8,128)(2,1)} %slice.7), channel_id=1, source_target_pairs={{0,3},{1,0},{2,1},{3,2},{4,7},{5,4},{6,5},{7,6},{8,11},{9,8},{10,9... | collective-permute-start | bytes 2359304 | tf_op jit(solution)/shard_map/ppermute | solution.py:287
  88.7 1.2 shard_map.91
  89.9 0.0 copy-start.2
  89.9 0.8 copy-done.2
  90.7 3.3 %all-to-all-done = bf16[128,8,1280]{2,1,0:T(8,128)(2,1)} async-done(((bf16[128,8,1280]{2,1,0:T(8,128)(2,1)}), bf16[128,8,1280]{2,1,0:T(8,128)(2,1)}, u32[]{:S(2)}, u32[]{:S(2)}) %all-to-all-start) | async-done | bytes 2621472 | tf_op jit(solution)/shard_map/all_to_all | solution.py:301
  94.0 10.9 %all-to-all-start.1 = ((bf16[128,8,256]{2,1,0:T(8,128)(2,1)}), bf16[128,8,256]{2,1,0:T(8,128)(2,1)}, u32[]{:S(2)}, u32[]{:S(2)}) async-start(bf16[128,8,256]{2,1,0:T(8,128)(2,1)} %bitcast.12), calls=%async_computation.1 | async-start | bytes 1048576 | tf_op jit(solution)/shard_map/all_to_all | solution.py:301
  104.9 0.0 copy-start.3
  105.0 1.2 copy-done.3
  106.2 2.3 %shard_map.89.weights_ref = bf16[896,4096]{1,0:T(8,128)(2,1)S(1)} custom-call(s32[2]{0:T(128)S(1)} %pad_add_fusion.pos_ref, bf16[128,4096]{1,0:T(8,128)(2,1)S(1)} %copy-done.3, bf16[192,4096]{1,0:T(8,128)(2,1)} %bitcast.5.own_ref, bf16[192,4096]{1,0:T(8,128)(2,1)S(1)} %collective-permute-done.2.right_ref, bf16[96,4096]{1,0:T(8,128)(2,1)} %collective-permute-done.4.top_ref, ...), custom_call_target="tpu_custom_call" | custom-call | flops 1000 | bytes 14680064 | tf_op jit(solution)/shard_map/pallas_call | solution.py:359
  108.5 0.0 copy-start.9
  108.5 7.3 %shard_map.90 = (f32[768,384]{1,0:T(8,128)S(1)}, f32[128,1024]{1,0:T(8,128)S(1)}, bf16[128,1024]{1,0:T(8,128)(2,1)S(1)}, bf16[128,1024]{1,0:T(8,128)(2,1)S(1)}, bf16[128,1024]{1,0:T(8,128)(2,1)S(1)}) custom-call(s32[2]{0:T(128)S(1)} %pad_add_fusion.pos_ref, bf16[1024,1280]{1,0:T(8,128)(2,1)} %bitcast.4.rows_ref, bf16[896,4096]{1,0:T(8,128)(2,1)S(1)} %shard_map.89.weights_ref), custom_call_target="tpu_custom_call" | custom-call | flops 4294967296 | bytes 12582912 | tf_op jit(solution)/shard_map/pallas_call | solution.py:365
  115.9 1.0 copy-done.10
  116.9 1.9 %collective-permute-start.9 = (bf16[128,1024]{1,0:T(8,128)(2,1)S(1)}, bf16[128,1024]{1,0:T(8,128)(2,1)S(1)}, u32[]{:S(2)}, u32[]{:S(2)}) collective-permute-start(bf16[128,1024]{1,0:T(8,128)(2,1)S(1)} %get-tuple-element.30), channel_id=1, source_target_pairs={{0,1},{1,2},{2,3},{3,0},{4,5},{5,6},{6,7},{7,4},{8,9},{9,10},{10,1... | collective-permute-start | bytes 786440 | tf_op jit(solution)/shard_map/ppermute | solution.py:287
  118.8 3.4 %collective-permute-start.10 = (bf16[128,1024]{1,0:T(8,128)(2,1)S(1)}, bf16[128,1024]{1,0:T(8,128)(2,1)S(1)}, u32[]{:S(2)}, u32[]{:S(2)}) collective-permute-start(bf16[128,1024]{1,0:T(8,128)(2,1)S(1)} %get-tuple-element.31), channel_id=1, source_target_pairs={{0,2},{1,3},{2,0},{3,1},{4,6},{5,7},{6,4},{7,5},{8,10},{9,11},{10,... | collective-permute-start | bytes 786440 | tf_op jit(solution)/shard_map/ppermute | solution.py:287
  122.2 3.7 %collective-permute-start.11 = (bf16[128,1024]{1,0:T(8,128)(2,1)S(1)}, bf16[128,1024]{1,0:T(8,128)(2,1)S(1)}, u32[]{:S(2)}, u32[]{:S(2)}) collective-permute-start(bf16[128,1024]{1,0:T(8,128)(2,1)S(1)} %get-tuple-element.32), channel_id=1, source_target_pairs={{0,3},{1,0},{2,1},{3,2},{4,7},{5,4},{6,5},{7,6},{8,11},{9,8},{10,9... | collective-permute-start | bytes 786440 | tf_op jit(solution)/shard_map/ppermute | solution.py:287
  125.9 1.3 copy-done.11
  127.2 3.3 %shard_map.92 = (f32[192,128]{1,0:T(8,128)S(1)}, bf16[768,128]{1,0:T(8,128)(2,1)}) custom-call(s32[2]{0:T(128)S(1)} %pad_add_fusion.pos_ref, bf16[128,768]{1,0:T(8,128)(2,1)S(1)} %copy-done.9, f32[768,384]{1,0:T(8,128)S(1)} %copy-done.11, bf16[1024,256]{1,0:T(8,128)(2,1)} %bitcast.8.got_ref), custom_call_target="tpu_custom_call" | custom-call | flops 1073741824 | bytes 3145728 | tf_op jit(solution)/shard_map/pallas_call | solution.py:376
  130.5 4.2 %all-to-all-start.2 = ((bf16[4,192,128]{2,1,0:T(8,128)(2,1)}), bf16[4,192,128]{2,1,0:T(8,128)(2,1)S(1)}, u32[]{:S(2)}, u32[]{:S(2)}) async-start(bf16[4,192,128]{2,1,0:T(8,128)(2,1)} %bitcast.10), calls=%async_computation.2 | async-start | bytes 393216 | tf_op jit(solution)/shard_map/all_to_all | solution.py:391
  135.4 1.1 collective-permute-done.11.i3
  136.5 1.0 shard_map.93
  137.5 3.5 %all-to-all-done.2.parts_ref = bf16[4,192,128]{2,1,0:T(8,128)(2,1)S(1)} async-done(((bf16[4,192,128]{2,1,0:T(8,128)(2,1)}), bf16[4,192,128]{2,1,0:T(8,128)(2,1)S(1)}, u32[]{:S(2)}, u32[]{:S(2)}) %all-to-all-start.2) | async-done | bytes 196640 | tf_op jit(solution)/shard_map/all_to_all | solution.py:391
  141.0 1.2 shard_map.94
  (21 shorter events, 0.0 us)
Async XLA Ops:
  0.6 6.5 %copy-start.8 = (s32[128,8]{0,1:T(8,128)S(1)}, s32[128,8]{0,1:T(8,128)}, u32[]{:S(2)}) copy-start(s32[128,8]{0,1:T(8,128)} %param.8) | copy-start | bytes 12292
  0.7 1.2 copy-start
  2.0 0.7 copy-start.7
  2.6 4.5 %copy-start.1 = (bf16[128,4096]{1,0:T(8,128)(2,1)S(1)}, bf16[128,4096]{1,0:T(8,128)(2,1)}, u32[]{:S(2)}) copy-start(bf16[128,4096]{1,0:T(8,128)(2,1)} %tokens_ref.3) | copy-start | bytes 3145732
  3.2 3.9 %collective-permute-start = (bf16[144,2048]{1,0:T(8,128)(2,1)S(1)}, bf16[144,2048]{1,0:T(8,128)(2,1)S(1)}, u32[]{:S(2)}, u32[]{:S(2)}) collective-permute-start(bf16[144,2048]{1,0:T(8,128)(2,1)S(1)} %shard_map.86), channel_id=1, source_target_pairs={{0,4},{4,0},{8,12},{12,8},{16,20},{20,16},{24,28},{28,24},{32,36},... | collective-permute-start | bytes 1769480 | tf_op jit(solution)/shard_map/ppermute | solution.py:295
  7.1 4.0 %copy-start.4 = (bf16[144,2048]{1,0:T(8,128)(2,1)}, bf16[144,2048]{1,0:T(8,128)(2,1)S(1)}, u32[]{:S(2)}) copy-start(bf16[144,2048]{1,0:T(8,128)(2,1)S(1)} %collective-permute-done.other_ref) | copy-start | bytes 1769476
  11.1 17.9 %copy-start.12 = (bf16[128,8,192]{0,2,1:T(8,128)(2,1)S(1)}, bf16[128,8,192]{0,2,1:T(8,128)(2,1)}, u32[]{:S(2)}) copy-start(bf16[128,8,192]{0,2,1:T(8,128)(2,1)} %param.9) | copy-start | bytes 1179652
  11.1 82.9 %all-to-all-start = ((bf16[128,8,1280]{2,1,0:T(8,128)(2,1)}), bf16[128,8,1280]{2,1,0:T(8,128)(2,1)}, u32[]{:S(2)}, u32[]{:S(2)}) async-start(bf16[128,8,1280]{2,1,0:T(8,128)(2,1)} %bitcast.3), calls=%async_computation | async-start | bytes 5242880 | tf_op jit(solution)/shard_map/all_to_all | solution.py:301
  30.2 43.8 %collective-permute-start.2 = (bf16[192,4096]{1,0:T(8,128)(2,1)}, bf16[192,4096]{1,0:T(8,128)(2,1)S(1)}, u32[]{:S(2)}, u32[]{:S(2)}) collective-permute-start(bf16[192,4096]{1,0:T(8,128)(2,1)} %bitcast.5.own_ref), channel_id=1, source_target_pairs={{0,3},{1,0},{2,1},{3,2},{4,7},{5,4},{6,5},{7,6},{8,11},{9,8},{10,9... | collective-permute-start | bytes 4718600 | tf_op jit(solution)/shard_map/ppermute | solution.py:287
  34.9 44.8 %collective-permute-start.1 = (bf16[192,4096]{1,0:T(8,128)(2,1)}, bf16[192,4096]{1,0:T(8,128)(2,1)S(1)}, u32[]{:S(2)}, u32[]{:S(2)}) collective-permute-start(bf16[192,4096]{1,0:T(8,128)(2,1)} %bitcast.5.own_ref), channel_id=1, source_target_pairs={{0,1},{1,2},{2,3},{3,0},{4,5},{5,6},{6,7},{7,4},{8,9},{9,10},{10,1... | collective-permute-start | bytes 4718600 | tf_op jit(solution)/shard_map/ppermute | solution.py:287
  36.8 4.0 %collective-permute-start.3 = (bf16[1024,192]{1,0:T(8,128)(2,1)}, bf16[1024,192]{1,0:T(8,128)(2,1)S(1)}, u32[]{:S(2)}, u32[]{:S(2)}) collective-permute-start(bf16[1024,192]{1,0:T(8,128)(2,1)} %bitcast.13), channel_id=1, source_target_pairs={{0,4},{4,0},{8,12},{12,8},{16,20},{20,16},{24,28},{28,24},{32,36},... | collective-permute-start | bytes 1179656 | tf_op jit(solution)/shard_map/ppermute | solution.py:295
  40.8 1.1 copy-start.5
  41.9 1.0 copy-start.6
  45.8 42.9 %collective-permute-start.7 = (bf16[384,256]{1,0:T(8,128)(2,1)S(1)}, bf16[384,256]{1,0:T(8,128)(2,1)S(1)}, u32[]{:S(2)}, u32[]{:S(2)}) collective-permute-start(bf16[384,256]{1,0:T(8,128)(2,1)S(1)} %get-tuple-element.26), channel_id=1, source_target_pairs={{0,2},{1,3},{2,0},{3,1},{4,6},{5,7},{6,4},{7,5},{8,10},{9,11},{10,... | collective-permute-start | bytes 589832 | tf_op jit(solution)/shard_map/ppermute | solution.py:287
  50.0 38.7 %collective-permute-start.8 = (bf16[384,256]{1,0:T(8,128)(2,1)S(1)}, bf16[384,256]{1,0:T(8,128)(2,1)S(1)}, u32[]{:S(2)}, u32[]{:S(2)}) collective-permute-start(bf16[384,256]{1,0:T(8,128)(2,1)S(1)} %get-tuple-element.27), channel_id=1, source_target_pairs={{0,3},{1,0},{2,1},{3,2},{4,7},{5,4},{6,5},{7,6},{8,11},{9,8},{10,9... | collective-permute-start | bytes 589832 | tf_op jit(solution)/shard_map/ppermute | solution.py:287
  53.0 35.7 %collective-permute-start.6 = (bf16[384,256]{1,0:T(8,128)(2,1)S(1)}, bf16[384,256]{1,0:T(8,128)(2,1)S(1)}, u32[]{:S(2)}, u32[]{:S(2)}) collective-permute-start(bf16[384,256]{1,0:T(8,128)(2,1)S(1)} %get-tuple-element.21), channel_id=1, source_target_pairs={{0,1},{1,2},{2,3},{3,0},{4,5},{5,6},{6,7},{7,4},{8,9},{9,10},{10,1... | collective-permute-start | bytes 589832 | tf_op jit(solution)/shard_map/ppermute | solution.py:287
  81.6 23.3 %collective-permute-start.4 = (bf16[96,4096]{1,0:T(8,128)(2,1)}, bf16[96,4096]{1,0:T(8,128)(2,1)}, u32[]{:S(2)}, u32[]{:S(2)}) collective-permute-start(bf16[96,4096]{1,0:T(8,128)(2,1)} %slice.6), channel_id=1, source_target_pairs={{0,1},{1,2},{2,3},{3,0},{4,5},{5,6},{6,7},{7,4},{8,9},{9,10},{10,1... | collective-permute-start | bytes 2359304 | tf_op jit(solution)/shard_map/ppermute | solution.py:287
  83.6 21.4 %collective-permute-start.5 = (bf16[96,4096]{1,0:T(8,128)(2,1)}, bf16[96,4096]{1,0:T(8,128)(2,1)}, u32[]{:S(2)}, u32[]{:S(2)}) collective-permute-start(bf16[96,4096]{1,0:T(8,128)(2,1)} %slice.7), channel_id=1, source_target_pairs={{0,3},{1,0},{2,1},{3,2},{4,7},{5,4},{6,5},{7,6},{8,11},{9,8},{10,9... | collective-permute-start | bytes 2359304 | tf_op jit(solution)/shard_map/ppermute | solution.py:287
  89.9 0.8 copy-start.2
  94.0 31.9 %all-to-all-start.1 = ((bf16[128,8,256]{2,1,0:T(8,128)(2,1)}), bf16[128,8,256]{2,1,0:T(8,128)(2,1)}, u32[]{:S(2)}, u32[]{:S(2)}) async-start(bf16[128,8,256]{2,1,0:T(8,128)(2,1)} %bitcast.12), calls=%async_computation.1 | async-start | bytes 1048576 | tf_op jit(solution)/shard_map/all_to_all | solution.py:301
  104.9 1.2 copy-start.3
  108.5 17.4 %copy-start.9 = (bf16[128,768]{1,0:T(8,128)(2,1)S(1)}, bf16[128,768]{1,0:T(8,128)(2,1)}, u32[]{:S(2)}) copy-start(bf16[128,768]{1,0:T(8,128)(2,1)} %grad_probes_ref.1) | copy-start | bytes 589828
  115.8 1.0 copy-start.10
  116.9 18.5 %collective-permute-start.9 = (bf16[128,1024]{1,0:T(8,128)(2,1)S(1)}, bf16[128,1024]{1,0:T(8,128)(2,1)S(1)}, u32[]{:S(2)}, u32[]{:S(2)}) collective-permute-start(bf16[128,1024]{1,0:T(8,128)(2,1)S(1)} %get-tuple-element.30), channel_id=1, source_target_pairs={{0,1},{1,2},{2,3},{3,0},{4,5},{5,6},{6,7},{7,4},{8,9},{9,10},{10,1... | collective-permute-start | bytes 786440 | tf_op jit(solution)/shard_map/ppermute | solution.py:287
  118.8 16.6 %collective-permute-start.10 = (bf16[128,1024]{1,0:T(8,128)(2,1)S(1)}, bf16[128,1024]{1,0:T(8,128)(2,1)S(1)}, u32[]{:S(2)}, u32[]{:S(2)}) collective-permute-start(bf16[128,1024]{1,0:T(8,128)(2,1)S(1)} %get-tuple-element.31), channel_id=1, source_target_pairs={{0,2},{1,3},{2,0},{3,1},{4,6},{5,7},{6,4},{7,5},{8,10},{9,11},{10,... | collective-permute-start | bytes 786440 | tf_op jit(solution)/shard_map/ppermute | solution.py:287
  122.2 14.3 %collective-permute-start.11 = (bf16[128,1024]{1,0:T(8,128)(2,1)S(1)}, bf16[128,1024]{1,0:T(8,128)(2,1)S(1)}, u32[]{:S(2)}, u32[]{:S(2)}) collective-permute-start(bf16[128,1024]{1,0:T(8,128)(2,1)S(1)} %get-tuple-element.32), channel_id=1, source_target_pairs={{0,3},{1,0},{2,1},{3,2},{4,7},{5,4},{6,5},{7,6},{8,11},{9,8},{10,9... | collective-permute-start | bytes 786440 | tf_op jit(solution)/shard_map/ppermute | solution.py:287
  125.9 1.3 copy-start.11
  130.5 10.5 %all-to-all-start.2 = ((bf16[4,192,128]{2,1,0:T(8,128)(2,1)}), bf16[4,192,128]{2,1,0:T(8,128)(2,1)S(1)}, u32[]{:S(2)}, u32[]{:S(2)}) async-start(bf16[4,192,128]{2,1,0:T(8,128)(2,1)} %bitcast.10), calls=%async_computation.2 | async-start | bytes 393216 | tf_op jit(solution)/shard_map/all_to_all | solution.py:391

commit v12 on v11

--- a/solution.py
+++ b/solution.py
@@ -84,17 +84,6 @@
     return dot(ones_where(iota(shape, 0) // times == iota(shape, 1)), table.astype(BF))
 
 
-def pack_half(pos_ref, ids_ref, tokens_ref, out_ref):
-    out_ref[:TOK, :] = tokens_ref[...]
-    out_ref[TOK:, :] = jnp.zeros((16, HALF), BF)
-    ids = jnp.concatenate([ids_ref[...].astype(F32), jnp.zeros((8, TOK), F32)], 0)
-    out_ref[TOK:, :TOK] = ids.astype(BF)
-
-
-def other_ids(other_ref):
-    return other_ref[TOK:, :TOK].astype(F32)[:TOP].astype(jnp.int32)
-
-
 def fold(picked, many, g):
     size = 256 // many
     width = picked.shape[1] // many
@@ -107,20 +96,22 @@
 
 
 def send_rows(
-    pos_ref, ids_ref, tokens_ref, other_ref, out_ref, made_ref, half_ref, half_ids_ref, sems
+    pos_ref, ids_ref, tokens_ref, other_ids_ref, other_ref,
+    out_ref, made_ref, half_ref, half_ids_ref, sems,
 ):
     x, c = pos_ref[0], pos_ref[1]
     mine = x // 2 == c
+    columns = pl.ds(pl.multiple_of(c * HALF, HALF), HALF)
 
     @pl.when(mine)
     def _():
-        half_ref[...] = tokens_ref[:, pl.ds(pl.multiple_of(c * HALF, HALF), HALF)]
+        half_ref[...] = tokens_ref[:, columns]
         half_ids_ref[...] = ids_ref[...]
 
     @pl.when(jnp.logical_not(mine))
     def _():
-        half_ref[...] = other_ref[:TOK, :]
-        half_ids_ref[...] = other_ids(other_ref)
+        half_ref[...] = other_ref[:, columns]
+        half_ids_ref[...] = other_ids_ref[...]
 
     table = places(half_ids_ref[...])
     shared = dot(ones_where(table == (FIRST + x % 2).astype(F32)), half_ref[...]).astype(BF)
@@ -140,10 +131,10 @@
         copy.wait()
 
 
-def pick_grads(pos_ref, ids_ref, other_ref, grads_ref, other_grads_ref, *outs):
+def pick_grads(pos_ref, ids_ref, other_ids_ref, grads_ref, other_grads_ref, *outs):
     x, c = pos_ref[0], pos_ref[1]
     pairs = TOK * TOP
-    table, other_table = pair_places(ids_ref[...]), pair_places(other_ids(other_ref))
+    table, other_table = pair_places(ids_ref[...]), pair_places(other_ids_ref[...])
     embed = ones_where(iota((UNITS, 256), 0) == iota((UNITS, 256), 1))
     grads = dot(grads_ref[...], embed).astype(BF)
     other_grads = dot(other_grads_ref[...], embed).astype(BF)
@@ -307,23 +298,11 @@
     inverse = 1.0 / window_counts.astype(F32)
     ids_t = expert_ids.T
 
-    packed = pl.pallas_call(
-        pack_half,
-        out_shape=sds((TOK + 16, HALF), BF),
-        grid_spec=pltpu.PrefetchScalarGridSpec(
-            num_scalar_prefetch=1,
-            grid=(1,),
-            in_specs=[VM, pl.BlockSpec((TOK, HALF), lambda i, pos: (0, 1 - pos[1]))],
-            out_specs=VM,
-        ),
-        compiler_params=pltpu.CompilerParams(vmem_limit_bytes=6 * MIB),
-        cost_estimate=pl.CostEstimate(flops=1000, bytes_accessed=MIB, transcendentals=0),
-    )(pos, ids_t, tokens)
-    other = swap(packed)
+    other, other_ids = swap(tokens), swap(ids_t)
     out_rows = kernel_call(
         send_rows,
         sds((ROWS, SHARE + STRIP), BF),
-        [SM] + [VM] * 3,
+        [SM] + [VM] * 4,
         1 << 30,
         5 * MIB,
         20,
@@ -334,7 +313,7 @@
             pltpu.SemaphoreType.DMA((ROWS // 256,)),
         ],
         pl.BlockSpec(memory_space=pl.ANY),
-    )(pos, ids_t, tokens, other)
+    )(pos, ids_t, tokens, other_ids, other)
     rows = to_owners(out_rows)
 
     own, grads = gate_weight[0], hidden_grads.reshape(TOK * TOP, UNITS)
@@ -343,7 +322,7 @@
     other_grads = swap(grads)
     picked = kernel_call(
         pick_grads, [sds((SLOTS + OWNERS, 256), BF)] * REPS, [SM] + [VM] * 4, 5 << 30, 3 * MIB, 20
-    )(pos, ids_t, other, grads, other_grads)
+    )(pos, ids_t, other_ids, grads, other_grads)
     left, right, _ = lax.optimization_barrier((left, right, picked[1]))
     top = shift(left[: UNITS // 2], 1)
     bottom = shift(right[UNITS // 2 :], REPS - 1)

time: 143 us -> 144 us (level)
  starting transfers between devices: 69.5 us -> 71.9 us
    ppermute x2 -> x3, starting transfers between devices: 3.84 us -> 6.25 us  [swap(): return lax.ppermute(block, 'ep', [(i, i ^ 1) for i in range(OWNERS)])]
    unnamed x27 -> x21, local copies, waits for them, and re-layouts: 9.53 us -> 8.45 us
    ppermute x2 -> x3, waiting for transfers between devices: 4.06 us -> 3.01 us  [swap(): return lax.ppermute(block, 'ep', [(i, i ^ 1) for i in range(OWNERS)])]
    pallas_call x2 -> x1, Pallas kernels: 4.52 us -> 3.92 us  [local(): kernel_call(send_rows, sds((ROWS, SHARE + STRIP), BF), [SM] + [VM] * 4, 1...]
  transfers between devices with their start and end apart: 15 -> 16, of which waited for: 7 -> 7; matrix products, arithmetic and copies ran while one was open for 2% -> 2% of each run, Pallas kernels for 13% -> 13%
where the time goes in v12:
time: 144 us; the launch traced here: 143 us
  starting transfers between devices  71.9 us (50%)
  waiting for transfers between devices  35.8 us (25%)
  Pallas kernels  23.1 us (16%)
  local copies, waits for them, and re-layouts  10.4 us (7%)
  between operations  1.64 us (1%)
    ppermute x10, starting transfers between devices, shift(): lax.ppermute(block, 'rep', [(i, (i + k) % REPS) for i in range(REPS)])  32.6 us
    all_to_all x2, starting transfers between devices, to_owners(): lax.all_to_all(rows, 'ep', split_axis=0, concat_axis=0, tiled=True)  28.8 us
    ppermute x10, waiting for transfers between devices, shift(): lax.ppermute(block, 'rep', [(i, (i + k) % REPS) for i in range(REPS)])  26 us
    unnamed x21, local copies, waits for them, and re-layouts  8.45 us
    pallas_call x1, Pallas kernels, local(): kernel_call(products, [sds((FFW, ALL), F32)] + [sds((R, SHARE), kind) for...  7.32 us
    ppermute x3, starting transfers between devices, swap(): return lax.ppermute(block, 'ep', [(i, i ^ 1) for i in range(OWNERS)])  6.25 us
    all_to_all x1, starting transfers between devices, local(): lax.all_to_all(sketch.reshape(REPS, UNITS, R), 'rep', split_axis=0, conca...  4.19 us
    pallas_call x1, Pallas kernels, local(): kernel_call(send_rows, sds((ROWS, SHARE + STRIP), BF), [SM] + [VM] * 4, 1...  3.92 us
  transfers between devices with their start and end apart: 16, of which 7 were waited for; matrix products, arithmetic and copies ran while one was open for 2% of the time, Pallas kernels for 13%

profile of v12, /device:TPU:8, one launch (start us, length us, event | category | flops | bytes accessed | tf_op | source)
XLA Modules:
  0.0 143.0 jit_solution(18303087632041346092)
XLA Ops:
  0.6 1.9 %collective-permute-start.1 = (bf16[128,4096]{1,0:T(8,128)(2,1)}, bf16[128,4096]{1,0:T(8,128)(2,1)S(1)}, u32[]{:S(2)}, u32[]{:S(2)}) collective-permute-start(bf16[128,4096]{1,0:T(8,128)(2,1)} %tokens_ref.1), channel_id=1, source_target_pairs={{0,4},{4,0},{8,12},{12,8},{16,20},{20,16},{24,28},{28,24},{32,36},... | collective-permute-start | bytes 3145736 | tf_op jit(solution)/shard_map/ppermute | solution.py:286
  2.6 2.4 %collective-permute-start = (s32[8,128]{1,0:T(8,128)}, s32[8,128]{1,0:T(8,128)S(1)}, u32[]{:S(2)}, u32[]{:S(2)}) collective-permute-start(s32[8,128]{1,0:T(8,128)} %bitcast.15), channel_id=1, source_target_pairs={{0,4},{4,0},{8,12},{12,8},{16,20},{20,16},{24,28},{28,24},{32,36},... | collective-permute-start | bytes 12296 | tf_op jit(solution)/shard_map/ppermute | solution.py:286
  5.0 0.1 pad_add_fusion.pos_ref
  5.1 0.9 collective-permute-done.other_ids_ref
  6.0 0.0 collective-permute-done.1.other_ref
  6.0 1.2 copy-done.1
  7.2 0.7 copy-done.4
  7.9 3.9 %shard_map.86 = bf16[1024,1280]{1,0:T(8,128)(2,1)} custom-call(s32[2]{0:T(128)S(1)} %pad_add_fusion.pos_ref, s32[8,128]{1,0:T(8,128)S(1)} %bitcast.16, bf16[128,4096]{1,0:T(8,128)(2,1)S(1)} %copy-done.1, s32[8,128]{1,0:T(8,128)S(1)} %collective-permute-done.other_ids_ref, bf16[128,4096]{1,0:T(8,128)(2,1)S(1)} %collective-permute-done.1.other_ref), custom_call_target="tpu_custom_call" | custom-call | flops 1073741824 | bytes 5242880 | tf_op jit(solution)/shard_map/pallas_call | solution.py:302
  11.8 0.0 copy-start.9
  11.8 0.0 copy-start.5
  11.9 17.9 %all-to-all-start = ((bf16[128,8,1280]{2,1,0:T(8,128)(2,1)}), bf16[128,8,1280]{2,1,0:T(8,128)(2,1)}, u32[]{:S(2)}, u32[]{:S(2)}) async-start(bf16[128,8,1280]{2,1,0:T(8,128)(2,1)} %bitcast.3), calls=%async_computation | async-start | bytes 5242880 | tf_op jit(solution)/shard_map/all_to_all | solution.py:292
  29.8 1.2 copy.9
  31.0 4.7 %collective-permute-start.3 = (bf16[192,4096]{1,0:T(8,128)(2,1)}, bf16[192,4096]{1,0:T(8,128)(2,1)S(1)}, u32[]{:S(2)}, u32[]{:S(2)}) collective-permute-start(bf16[192,4096]{1,0:T(8,128)(2,1)} %bitcast.5.own_ref), channel_id=1, source_target_pairs={{0,3},{1,0},{2,1},{3,2},{4,7},{5,4},{6,5},{7,6},{8,11},{9,8},{10,9... | collective-permute-start | bytes 4718600 | tf_op jit(solution)/shard_map/ppermute | solution.py:278
  35.7 1.9 %collective-permute-start.2 = (bf16[192,4096]{1,0:T(8,128)(2,1)}, bf16[192,4096]{1,0:T(8,128)(2,1)S(1)}, u32[]{:S(2)}, u32[]{:S(2)}) collective-permute-start(bf16[192,4096]{1,0:T(8,128)(2,1)} %bitcast.5.own_ref), channel_id=1, source_target_pairs={{0,1},{1,2},{2,3},{3,0},{4,5},{5,6},{6,7},{7,4},{8,9},{9,10},{10,1... | collective-permute-start | bytes 4718600 | tf_op jit(solution)/shard_map/ppermute | solution.py:278
  37.6 1.9 %collective-permute-start.4 = (bf16[1024,192]{1,0:T(8,128)(2,1)}, bf16[1024,192]{1,0:T(8,128)(2,1)S(1)}, u32[]{:S(2)}, u32[]{:S(2)}) collective-permute-start(bf16[1024,192]{1,0:T(8,128)(2,1)} %bitcast.13), channel_id=1, source_target_pairs={{0,4},{4,0},{8,12},{12,8},{16,20},{20,16},{24,28},{28,24},{32,36},... | collective-permute-start | bytes 1179656 | tf_op jit(solution)/shard_map/ppermute | solution.py:286
  39.5 2.1 %collective-permute-done.4.other_grads_ref = bf16[1024,192]{1,0:T(8,128)(2,1)S(1)} collective-permute-done((bf16[1024,192]{1,0:T(8,128)(2,1)}, bf16[1024,192]{1,0:T(8,128)(2,1)S(1)}, u32[]{:S(2)}, u32[]{:S(2)}) %collective-permute-start.4) | collective-permute-done | bytes 393248 | tf_op jit(solution)/shard_map/ppermute | solution.py:286
  41.6 1.0 copy-done.3
  42.6 2.8 %shard_map.87 = (bf16[384,256]{1,0:T(8,128)(2,1)S(1)}, bf16[384,256]{1,0:T(8,128)(2,1)S(1)}, bf16[384,256]{1,0:T(8,128)(2,1)S(1)}, bf16[384,256]{1,0:T(8,128)(2,1)S(1)}) custom-call(s32[2]{0:T(128)S(1)} %pad_add_fusion.pos_ref, s32[8,128]{1,0:T(8,128)S(1)} %bitcast.17, s32[8,128]{1,0:T(8,128)S(1)} %collective-permute-done.other_ids_ref, ...), custom_call_target="tpu_custom_call" | custom-call | flops 5368709120 | bytes 3145728 | tf_op jit(solution)/shard_map/pallas_call | solution.py:323
  45.5 4.2 %collective-permute-start.8 = (bf16[384,256]{1,0:T(8,128)(2,1)S(1)}, bf16[384,256]{1,0:T(8,128)(2,1)S(1)}, u32[]{:S(2)}, u32[]{:S(2)}) collective-permute-start(bf16[384,256]{1,0:T(8,128)(2,1)S(1)} %get-tuple-element.26), channel_id=1, source_target_pairs={{0,2},{1,3},{2,0},{3,1},{4,6},{5,7},{6,4},{7,5},{8,10},{9,11},{10,... | collective-permute-start | bytes 589832 | tf_op jit(solution)/shard_map/ppermute | solution.py:278
  49.7 3.0 %collective-permute-start.9 = (bf16[384,256]{1,0:T(8,128)(2,1)S(1)}, bf16[384,256]{1,0:T(8,128)(2,1)S(1)}, u32[]{:S(2)}, u32[]{:S(2)}) collective-permute-start(bf16[384,256]{1,0:T(8,128)(2,1)S(1)} %get-tuple-element.27), channel_id=1, source_target_pairs={{0,3},{1,0},{2,1},{3,2},{4,7},{5,4},{6,5},{7,6},{8,11},{9,8},{10,9... | collective-permute-start | bytes 589832 | tf_op jit(solution)/shard_map/ppermute | solution.py:278
  52.8 2.8 %collective-permute-start.7 = (bf16[384,256]{1,0:T(8,128)(2,1)S(1)}, bf16[384,256]{1,0:T(8,128)(2,1)S(1)}, u32[]{:S(2)}, u32[]{:S(2)}) collective-permute-start(bf16[384,256]{1,0:T(8,128)(2,1)S(1)} %get-tuple-element.21), channel_id=1, source_target_pairs={{0,1},{1,2},{2,3},{3,0},{4,5},{5,6},{6,7},{7,4},{8,9},{9,10},{10,1... | collective-permute-start | bytes 589832 | tf_op jit(solution)/shard_map/ppermute | solution.py:278
  55.6 19.2 %collective-permute-done.3.right_ref = bf16[192,4096]{1,0:T(8,128)(2,1)S(1)} collective-permute-done((bf16[192,4096]{1,0:T(8,128)(2,1)}, bf16[192,4096]{1,0:T(8,128)(2,1)S(1)}, u32[]{:S(2)}, u32[]{:S(2)}) %collective-permute-start.3) | collective-permute-done | bytes 1572896 | tf_op jit(solution)/shard_map/ppermute | solution.py:278
  74.8 5.7 %collective-permute-done.2.left_ref = bf16[192,4096]{1,0:T(8,128)(2,1)S(1)} collective-permute-done((bf16[192,4096]{1,0:T(8,128)(2,1)}, bf16[192,4096]{1,0:T(8,128)(2,1)S(1)}, u32[]{:S(2)}, u32[]{:S(2)}) %collective-permute-start.2) | collective-permute-done | bytes 1572896 | tf_op jit(solution)/shard_map/ppermute | solution.py:278
  80.5 0.9 slice.7
  81.4 1.0 slice.6
  82.4 1.9 %collective-permute-start.5 = (bf16[96,4096]{1,0:T(8,128)(2,1)}, bf16[96,4096]{1,0:T(8,128)(2,1)}, u32[]{:S(2)}, u32[]{:S(2)}) collective-permute-start(bf16[96,4096]{1,0:T(8,128)(2,1)} %slice.6), channel_id=1, source_target_pairs={{0,1},{1,2},{2,3},{3,0},{4,5},{5,6},{6,7},{7,4},{8,9},{9,10},{10,1... | collective-permute-start | bytes 2359304 | tf_op jit(solution)/shard_map/ppermute | solution.py:278
  84.3 5.1 %collective-permute-start.6 = (bf16[96,4096]{1,0:T(8,128)(2,1)}, bf16[96,4096]{1,0:T(8,128)(2,1)}, u32[]{:S(2)}, u32[]{:S(2)}) collective-permute-start(bf16[96,4096]{1,0:T(8,128)(2,1)} %slice.7), channel_id=1, source_target_pairs={{0,3},{1,0},{2,1},{3,2},{4,7},{5,4},{6,5},{7,6},{8,11},{9,8},{10,9... | collective-permute-start | bytes 2359304 | tf_op jit(solution)/shard_map/ppermute | solution.py:278
  89.5 1.2 shard_map.90
  90.7 0.0 copy-start
  90.7 0.8 copy-done
  91.5 3.3 %all-to-all-done = bf16[128,8,1280]{2,1,0:T(8,128)(2,1)} async-done(((bf16[128,8,1280]{2,1,0:T(8,128)(2,1)}), bf16[128,8,1280]{2,1,0:T(8,128)(2,1)}, u32[]{:S(2)}, u32[]{:S(2)}) %all-to-all-start) | async-done | bytes 2621472 | tf_op jit(solution)/shard_map/all_to_all | solution.py:292
  94.7 10.9 %all-to-all-start.1 = ((bf16[128,8,256]{2,1,0:T(8,128)(2,1)}), bf16[128,8,256]{2,1,0:T(8,128)(2,1)}, u32[]{:S(2)}, u32[]{:S(2)}) async-start(bf16[128,8,256]{2,1,0:T(8,128)(2,1)} %bitcast.12), calls=%async_computation.1 | async-start | bytes 1048576 | tf_op jit(solution)/shard_map/all_to_all | solution.py:292
  105.7 0.0 copy-start.2
  105.7 1.2 copy-done.2
  106.9 2.3 %shard_map.88.weights_ref = bf16[896,4096]{1,0:T(8,128)(2,1)S(1)} custom-call(s32[2]{0:T(128)S(1)} %pad_add_fusion.pos_ref, bf16[128,4096]{1,0:T(8,128)(2,1)S(1)} %copy-done.2, bf16[192,4096]{1,0:T(8,128)(2,1)} %bitcast.5.own_ref, bf16[192,4096]{1,0:T(8,128)(2,1)S(1)} %collective-permute-done.3.right_ref, bf16[96,4096]{1,0:T(8,128)(2,1)} %collective-permute-done.5.top_ref, ...), custom_call_target="tpu_custom_call" | custom-call | flops 1000 | bytes 14680064 | tf_op jit(solution)/shard_map/pallas_call | solution.py:338
  109.3 0.0 copy-start.6
  109.3 7.3 %shard_map.89 = (f32[768,384]{1,0:T(8,128)S(1)}, f32[128,1024]{1,0:T(8,128)S(1)}, bf16[128,1024]{1,0:T(8,128)(2,1)S(1)}, bf16[128,1024]{1,0:T(8,128)(2,1)S(1)}, bf16[128,1024]{1,0:T(8,128)(2,1)S(1)}) custom-call(s32[2]{0:T(128)S(1)} %pad_add_fusion.pos_ref, bf16[1024,1280]{1,0:T(8,128)(2,1)} %bitcast.4.rows_ref, bf16[896,4096]{1,0:T(8,128)(2,1)S(1)} %shard_map.88.weights_ref), custom_call_target="tpu_custom_call" | custom-call | flops 4294967296 | bytes 12582912 | tf_op jit(solution)/shard_map/pallas_call | solution.py:344
  116.6 1.0 copy-done.7
  117.6 1.9 %collective-permute-start.10 = (bf16[128,1024]{1,0:T(8,128)(2,1)S(1)}, bf16[128,1024]{1,0:T(8,128)(2,1)S(1)}, u32[]{:S(2)}, u32[]{:S(2)}) collective-permute-start(bf16[128,1024]{1,0:T(8,128)(2,1)S(1)} %get-tuple-element.30), channel_id=1, source_target_pairs={{0,1},{1,2},{2,3},{3,0},{4,5},{5,6},{6,7},{7,4},{8,9},{9,10},{10,1... | collective-permute-start | bytes 786440 | tf_op jit(solution)/shard_map/ppermute | solution.py:278
  119.5 3.4 %collective-permute-start.11 = (bf16[128,1024]{1,0:T(8,128)(2,1)S(1)}, bf16[128,1024]{1,0:T(8,128)(2,1)S(1)}, u32[]{:S(2)}, u32[]{:S(2)}) collective-permute-start(bf16[128,1024]{1,0:T(8,128)(2,1)S(1)} %get-tuple-element.31), channel_id=1, source_target_pairs={{0,2},{1,3},{2,0},{3,1},{4,6},{5,7},{6,4},{7,5},{8,10},{9,11},{10,... | collective-permute-start | bytes 786440 | tf_op jit(solution)/shard_map/ppermute | solution.py:278
  122.9 3.7 %collective-permute-start.12 = (bf16[128,1024]{1,0:T(8,128)(2,1)S(1)}, bf16[128,1024]{1,0:T(8,128)(2,1)S(1)}, u32[]{:S(2)}, u32[]{:S(2)}) collective-permute-start(bf16[128,1024]{1,0:T(8,128)(2,1)S(1)} %get-tuple-element.32), channel_id=1, source_target_pairs={{0,3},{1,0},{2,1},{3,2},{4,7},{5,4},{6,5},{7,6},{8,11},{9,8},{10,9... | collective-permute-start | bytes 786440 | tf_op jit(solution)/shard_map/ppermute | solution.py:278
  126.6 1.3 copy-done.8
  127.9 3.3 %shard_map.91 = (f32[192,128]{1,0:T(8,128)S(1)}, bf16[768,128]{1,0:T(8,128)(2,1)}) custom-call(s32[2]{0:T(128)S(1)} %pad_add_fusion.pos_ref, bf16[128,768]{1,0:T(8,128)(2,1)S(1)} %copy-done.6, f32[768,384]{1,0:T(8,128)S(1)} %copy-done.8, bf16[1024,256]{1,0:T(8,128)(2,1)} %bitcast.8.got_ref), custom_call_target="tpu_custom_call" | custom-call | flops 1073741824 | bytes 3145728 | tf_op jit(solution)/shard_map/pallas_call | solution.py:355
  131.2 4.2 %all-to-all-start.2 = ((bf16[4,192,128]{2,1,0:T(8,128)(2,1)}), bf16[4,192,128]{2,1,0:T(8,128)(2,1)S(1)}, u32[]{:S(2)}, u32[]{:S(2)}) async-start(bf16[4,192,128]{2,1,0:T(8,128)(2,1)} %bitcast.10), calls=%async_computation.2 | async-start | bytes 393216 | tf_op jit(solution)/shard_map/all_to_all | solution.py:370
  136.1 1.1 collective-permute-done.12.i3
  137.2 1.0 shard_map.92
  138.2 3.5 %all-to-all-done.2.parts_ref = bf16[4,192,128]{2,1,0:T(8,128)(2,1)S(1)} async-done(((bf16[4,192,128]{2,1,0:T(8,128)(2,1)}), bf16[4,192,128]{2,1,0:T(8,128)(2,1)S(1)}, u32[]{:S(2)}, u32[]{:S(2)}) %all-to-all-start.2) | async-done | bytes 196640 | tf_op jit(solution)/shard_map/all_to_all | solution.py:370
  141.8 1.2 shard_map.93
  (16 shorter events, 0.0 us)
Async XLA Ops:
  0.6 5.4 %collective-permute-start.1 = (bf16[128,4096]{1,0:T(8,128)(2,1)}, bf16[128,4096]{1,0:T(8,128)(2,1)S(1)}, u32[]{:S(2)}, u32[]{:S(2)}) collective-permute-start(bf16[128,4096]{1,0:T(8,128)(2,1)} %tokens_ref.1), channel_id=1, source_target_pairs={{0,4},{4,0},{8,12},{12,8},{16,20},{20,16},{24,28},{28,24},{32,36},... | collective-permute-start | bytes 3145736 | tf_op jit(solution)/shard_map/ppermute | solution.py:286
  2.6 3.4 %collective-permute-start = (s32[8,128]{1,0:T(8,128)}, s32[8,128]{1,0:T(8,128)S(1)}, u32[]{:S(2)}, u32[]{:S(2)}) collective-permute-start(s32[8,128]{1,0:T(8,128)} %bitcast.15), channel_id=1, source_target_pairs={{0,4},{4,0},{8,12},{12,8},{16,20},{20,16},{24,28},{28,24},{32,36},... | collective-permute-start | bytes 12296 | tf_op jit(solution)/shard_map/ppermute | solution.py:286
  6.0 1.2 copy-start.1
  7.2 0.7 copy-start.4
  11.8 17.9 %copy-start.9 = (bf16[128,8,192]{0,2,1:T(8,128)(2,1)S(1)}, bf16[128,8,192]{0,2,1:T(8,128)(2,1)}, u32[]{:S(2)}) copy-start(bf16[128,8,192]{0,2,1:T(8,128)(2,1)} %param.9) | copy-start | bytes 1179652
  11.8 29.8 %copy-start.5 = (s32[128,8]{0,1:T(8,128)S(1)}, s32[128,8]{0,1:T(8,128)}, u32[]{:S(2)}) copy-start(s32[128,8]{0,1:T(8,128)} %param.8) | copy-start | bytes 12292
  11.9 82.9 %all-to-all-start = ((bf16[128,8,1280]{2,1,0:T(8,128)(2,1)}), bf16[128,8,1280]{2,1,0:T(8,128)(2,1)}, u32[]{:S(2)}, u32[]{:S(2)}) async-start(bf16[128,8,1280]{2,1,0:T(8,128)(2,1)} %bitcast.3), calls=%async_computation | async-start | bytes 5242880 | tf_op jit(solution)/shard_map/all_to_all | solution.py:292
  31.0 43.8 %collective-permute-start.3 = (bf16[192,4096]{1,0:T(8,128)(2,1)}, bf16[192,4096]{1,0:T(8,128)(2,1)S(1)}, u32[]{:S(2)}, u32[]{:S(2)}) collective-permute-start(bf16[192,4096]{1,0:T(8,128)(2,1)} %bitcast.5.own_ref), channel_id=1, source_target_pairs={{0,3},{1,0},{2,1},{3,2},{4,7},{5,4},{6,5},{7,6},{8,11},{9,8},{10,9... | collective-permute-start | bytes 4718600 | tf_op jit(solution)/shard_map/ppermute | solution.py:278
  35.7 44.8 %collective-permute-start.2 = (bf16[192,4096]{1,0:T(8,128)(2,1)}, bf16[192,4096]{1,0:T(8,128)(2,1)S(1)}, u32[]{:S(2)}, u32[]{:S(2)}) collective-permute-start(bf16[192,4096]{1,0:T(8,128)(2,1)} %bitcast.5.own_ref), channel_id=1, source_target_pairs={{0,1},{1,2},{2,3},{3,0},{4,5},{5,6},{6,7},{7,4},{8,9},{9,10},{10,1... | collective-permute-start | bytes 4718600 | tf_op jit(solution)/shard_map/ppermute | solution.py:278
  37.6 4.0 %collective-permute-start.4 = (bf16[1024,192]{1,0:T(8,128)(2,1)}, bf16[1024,192]{1,0:T(8,128)(2,1)S(1)}, u32[]{:S(2)}, u32[]{:S(2)}) collective-permute-start(bf16[1024,192]{1,0:T(8,128)(2,1)} %bitcast.13), channel_id=1, source_target_pairs={{0,4},{4,0},{8,12},{12,8},{16,20},{20,16},{24,28},{28,24},{32,36},... | collective-permute-start | bytes 1179656 | tf_op jit(solution)/shard_map/ppermute | solution.py:286
  41.6 1.0 copy-start.3
  45.5 44.0 %collective-permute-start.8 = (bf16[384,256]{1,0:T(8,128)(2,1)S(1)}, bf16[384,256]{1,0:T(8,128)(2,1)S(1)}, u32[]{:S(2)}, u32[]{:S(2)}) collective-permute-start(bf16[384,256]{1,0:T(8,128)(2,1)S(1)} %get-tuple-element.26), channel_id=1, source_target_pairs={{0,2},{1,3},{2,0},{3,1},{4,6},{5,7},{6,4},{7,5},{8,10},{9,11},{10,... | collective-permute-start | bytes 589832 | tf_op jit(solution)/shard_map/ppermute | solution.py:278
  49.7 39.8 %collective-permute-start.9 = (bf16[384,256]{1,0:T(8,128)(2,1)S(1)}, bf16[384,256]{1,0:T(8,128)(2,1)S(1)}, u32[]{:S(2)}, u32[]{:S(2)}) collective-permute-start(bf16[384,256]{1,0:T(8,128)(2,1)S(1)} %get-tuple-element.27), channel_id=1, source_target_pairs={{0,3},{1,0},{2,1},{3,2},{4,7},{5,4},{6,5},{7,6},{8,11},{9,8},{10,9... | collective-permute-start | bytes 589832 | tf_op jit(solution)/shard_map/ppermute | solution.py:278
  52.8 36.7 %collective-permute-start.7 = (bf16[384,256]{1,0:T(8,128)(2,1)S(1)}, bf16[384,256]{1,0:T(8,128)(2,1)S(1)}, u32[]{:S(2)}, u32[]{:S(2)}) collective-permute-start(bf16[384,256]{1,0:T(8,128)(2,1)S(1)} %get-tuple-element.21), channel_id=1, source_target_pairs={{0,1},{1,2},{2,3},{3,0},{4,5},{5,6},{6,7},{7,4},{8,9},{9,10},{10,1... | collective-permute-start | bytes 589832 | tf_op jit(solution)/shard_map/ppermute | solution.py:278
  82.4 23.3 %collective-permute-start.5 = (bf16[96,4096]{1,0:T(8,128)(2,1)}, bf16[96,4096]{1,0:T(8,128)(2,1)}, u32[]{:S(2)}, u32[]{:S(2)}) collective-permute-start(bf16[96,4096]{1,0:T(8,128)(2,1)} %slice.6), channel_id=1, source_target_pairs={{0,1},{1,2},{2,3},{3,0},{4,5},{5,6},{6,7},{7,4},{8,9},{9,10},{10,1... | collective-permute-start | bytes 2359304 | tf_op jit(solution)/shard_map/ppermute | solution.py:278
  84.3 21.4 %collective-permute-start.6 = (bf16[96,4096]{1,0:T(8,128)(2,1)}, bf16[96,4096]{1,0:T(8,128)(2,1)}, u32[]{:S(2)}, u32[]{:S(2)}) collective-permute-start(bf16[96,4096]{1,0:T(8,128)(2,1)} %slice.7), channel_id=1, source_target_pairs={{0,3},{1,0},{2,1},{3,2},{4,7},{5,4},{6,5},{7,6},{8,11},{9,8},{10,9... | collective-permute-start | bytes 2359304 | tf_op jit(solution)/shard_map/ppermute | solution.py:278
  90.7 0.8 copy-start
  94.7 31.9 %all-to-all-start.1 = ((bf16[128,8,256]{2,1,0:T(8,128)(2,1)}), bf16[128,8,256]{2,1,0:T(8,128)(2,1)}, u32[]{:S(2)}, u32[]{:S(2)}) async-start(bf16[128,8,256]{2,1,0:T(8,128)(2,1)} %bitcast.12), calls=%async_computation.1 | async-start | bytes 1048576 | tf_op jit(solution)/shard_map/all_to_all | solution.py:292
  105.7 1.2 copy-start.2
  109.3 17.4 %copy-start.6 = (bf16[128,768]{1,0:T(8,128)(2,1)S(1)}, bf16[128,768]{1,0:T(8,128)(2,1)}, u32[]{:S(2)}) copy-start(bf16[128,768]{1,0:T(8,128)(2,1)} %grad_probes_ref.1) | copy-start | bytes 589828
  116.6 1.0 copy-start.7
  117.6 18.5 %collective-permute-start.10 = (bf16[128,1024]{1,0:T(8,128)(2,1)S(1)}, bf16[128,1024]{1,0:T(8,128)(2,1)S(1)}, u32[]{:S(2)}, u32[]{:S(2)}) collective-permute-start(bf16[128,1024]{1,0:T(8,128)(2,1)S(1)} %get-tuple-element.30), channel_id=1, source_target_pairs={{0,1},{1,2},{2,3},{3,0},{4,5},{5,6},{6,7},{7,4},{8,9},{9,10},{10,1... | collective-permute-start | bytes 786440 | tf_op jit(solution)/shard_map/ppermute | solution.py:278
  119.5 16.6 %collective-permute-start.11 = (bf16[128,1024]{1,0:T(8,128)(2,1)S(1)}, bf16[128,1024]{1,0:T(8,128)(2,1)S(1)}, u32[]{:S(2)}, u32[]{:S(2)}) collective-permute-start(bf16[128,1024]{1,0:T(8,128)(2,1)S(1)} %get-tuple-element.31), channel_id=1, source_target_pairs={{0,2},{1,3},{2,0},{3,1},{4,6},{5,7},{6,4},{7,5},{8,10},{9,11},{10,... | collective-permute-start | bytes 786440 | tf_op jit(solution)/shard_map/ppermute | solution.py:278
  122.9 14.3 %collective-permute-start.12 = (bf16[128,1024]{1,0:T(8,128)(2,1)S(1)}, bf16[128,1024]{1,0:T(8,128)(2,1)S(1)}, u32[]{:S(2)}, u32[]{:S(2)}) collective-permute-start(bf16[128,1024]{1,0:T(8,128)(2,1)S(1)} %get-tuple-element.32), channel_id=1, source_target_pairs={{0,3},{1,0},{2,1},{3,2},{4,7},{5,4},{6,5},{7,6},{8,11},{9,8},{10,9... | collective-permute-start | bytes 786440 | tf_op jit(solution)/shard_map/ppermute | solution.py:278
  126.6 1.3 copy-start.8
  131.2 10.5 %all-to-all-start.2 = ((bf16[4,192,128]{2,1,0:T(8,128)(2,1)}), bf16[4,192,128]{2,1,0:T(8,128)(2,1)S(1)}, u32[]{:S(2)}, u32[]{:S(2)}) async-start(bf16[4,192,128]{2,1,0:T(8,128)(2,1)} %bitcast.10), calls=%async_computation.2 | async-start | bytes 393216 | tf_op jit(solution)/shard_map/all_to_all | solution.py:370

commit v13 on v11

--- a/solution.py
+++ b/solution.py
@@ -236,11 +236,13 @@
 
 def gate_part(
     pos_ref, grad_probes_ref, slope_ref, got_ref, own_ref, out_ref,
-    whole_ref, shared_ref, sketch_ref, held_ref, sem,
+    whole_ref, shared_ref, sketch_ref, held_ref, probes_ref, sems,
 ):
     x = pos_ref[0]
-    copy = pltpu.make_async_copy(slope_ref, held_ref, sem)
+    copy = pltpu.make_async_copy(slope_ref, held_ref, sems.at[0])
     copy.start()
+    second_copy = pltpu.make_async_copy(grad_probes_ref, probes_ref, sems.at[1])
+    second_copy.start()
 
     def put_whole(p, at, got):
         whole_ref[p * SLOTS + at.start : p * SLOTS + at.stop, :] = got
@@ -265,7 +267,8 @@
     grads = jnp.concatenate([early, late], 1)
     copy.wait()
     gate_grad = (grads * held_ref[...]).astype(BF)
-    projected = dot(grad_probes_ref[...], gate_grad).astype(BF)
+    second_copy.wait()
+    projected = dot(probes_ref[...], gate_grad).astype(BF)
     sketch_ref[...] = dot(gate_grad, projected, NT)
     out_ref[...] = sketch_ref[...].astype(BF)
     own_ref[...] = sketch_ref[pl.ds(pl.multiple_of(x * UNITS, UNITS), UNITS), :]
@@ -376,7 +379,7 @@
     own_sketch, sketch = kernel_call(
         gate_part,
         [sds((UNITS, R), F32), sds((FFW, R), BF)],
-        [SM, VM, pl.BlockSpec(memory_space=pl.ANY), VM],
+        [SM] + [pl.BlockSpec(memory_space=pl.ANY)] * 2 + [VM],
         1 << 30,
         3 * MIB,
         16,
@@ -385,7 +388,8 @@
             pltpu.VMEM((ROWS, 256), BF),
             pltpu.VMEM((FFW, R), F32),
             pltpu.VMEM((FFW, ALL), F32),
-            pltpu.SemaphoreType.DMA,
+            pltpu.VMEM((R, FFW), BF),
+            pltpu.SemaphoreType.DMA((2,)),
         ],
     )(pos, grad_probes, slope, got)
     sketches = lax.all_to_all(

time: 143 us -> 144 us (level)
  no operation moved by 1% of the time
where the time goes in v13:
time: 144 us; the launch traced here: 143 us
  starting transfers between devices  69.5 us (48%)
  waiting for transfers between devices  35.8 us (25%)
  Pallas kernels  24.1 us (17%)
  local copies, waits for them, and re-layouts  11.5 us (8%)
  between operations  1.65 us (1%)
    ppermute x10, starting transfers between devices, shift(): lax.ppermute(block, 'rep', [(i, (i + k) % REPS) for i in range(REPS)])  32.6 us
    all_to_all x2, starting transfers between devices, to_owners(): lax.all_to_all(rows, 'ep', split_axis=0, concat_axis=0, tiled=True)  28.8 us
    ppermute x10, waiting for transfers between devices, shift(): lax.ppermute(block, 'rep', [(i, (i + k) % REPS) for i in range(REPS)])  24.6 us
    unnamed x27, local copies, waits for them, and re-layouts  9.53 us
    pallas_call x1, Pallas kernels, local(): kernel_call(products, [sds((FFW, ALL), F32)] + [sds((R, SHARE), kind) for...  7.32 us
    all_to_all x1, starting transfers between devices, local(): lax.all_to_all(sketch.reshape(REPS, UNITS, R), 'rep', split_axis=0, conca...  4.19 us
    ppermute x2, waiting for transfers between devices, swap(): return lax.ppermute(block, 'ep', [(i, i ^ 1) for i in range(OWNERS)])  4.06 us
    pallas_call x1, Pallas kernels, local(): kernel_call(send_rows, sds((ROWS, SHARE + STRIP), BF), [SM] + [VM] * 3, 1...  3.94 us
  transfers between devices with their start and end apart: 15, of which 7 were waited for; matrix products, arithmetic and copies ran while one was open for 2% of the time, Pallas kernels for 13%

profile of v13, /device:TPU:8, one launch (start us, length us, event | category | flops | bytes accessed | tf_op | source)
XLA Modules:
  0.0 142.6 jit_solution(16613387383207272876)
XLA Ops:
  0.6 0.0 copy-start.8
  0.7 0.1 pad_add_fusion.pos_ref
  0.7 1.2 copy-done
  2.0 0.7 copy-done.7
  2.6 0.6 shard_map.86
  3.2 1.9 %collective-permute-start = (bf16[144,2048]{1,0:T(8,128)(2,1)S(1)}, bf16[144,2048]{1,0:T(8,128)(2,1)S(1)}, u32[]{:S(2)}, u32[]{:S(2)}) collective-permute-start(bf16[144,2048]{1,0:T(8,128)(2,1)S(1)} %shard_map.86), channel_id=1, source_target_pairs={{0,4},{4,0},{8,12},{12,8},{16,20},{20,16},{24,28},{28,24},{32,36},... | collective-permute-start | bytes 1769480 | tf_op jit(solution)/shard_map/ppermute | solution.py:298
  5.2 2.0 %collective-permute-done.other_ref = bf16[144,2048]{1,0:T(8,128)(2,1)S(1)} collective-permute-done((bf16[144,2048]{1,0:T(8,128)(2,1)S(1)}, bf16[144,2048]{1,0:T(8,128)(2,1)S(1)}, u32[]{:S(2)}, u32[]{:S(2)}) %collective-permute-start) | collective-permute-done | bytes 589856 | tf_op jit(solution)/shard_map/ppermute | solution.py:298
  7.1 3.9 %shard_map.87 = bf16[1024,1280]{1,0:T(8,128)(2,1)} custom-call(s32[2]{0:T(128)S(1)} %pad_add_fusion.pos_ref, s32[8,128]{1,0:T(8,128)S(1)} %bitcast.16, bf16[128,4096]{1,0:T(8,128)(2,1)S(1)} %copy-done.1, bf16[144,2048]{1,0:T(8,128)(2,1)S(1)} %collective-permute-done.other_ref), custom_call_target="tpu_custom_call" | custom-call | flops 1073741824 | bytes 5242880 | tf_op jit(solution)/shard_map/pallas_call | solution.py:326
  11.1 0.0 copy-start.12
  11.1 17.9 %all-to-all-start = ((bf16[128,8,1280]{2,1,0:T(8,128)(2,1)}), bf16[128,8,1280]{2,1,0:T(8,128)(2,1)}, u32[]{:S(2)}, u32[]{:S(2)}) async-start(bf16[128,8,1280]{2,1,0:T(8,128)(2,1)} %bitcast.3), calls=%async_computation | async-start | bytes 5242880 | tf_op jit(solution)/shard_map/all_to_all | solution.py:304
  29.0 1.2 copy.9
  30.2 4.6 %collective-permute-start.2 = (bf16[192,4096]{1,0:T(8,128)(2,1)}, bf16[192,4096]{1,0:T(8,128)(2,1)S(1)}, u32[]{:S(2)}, u32[]{:S(2)}) collective-permute-start(bf16[192,4096]{1,0:T(8,128)(2,1)} %bitcast.5.own_ref), channel_id=1, source_target_pairs={{0,3},{1,0},{2,1},{3,2},{4,7},{5,4},{6,5},{7,6},{8,11},{9,8},{10,9... | collective-permute-start | bytes 4718600 | tf_op jit(solution)/shard_map/ppermute | solution.py:290
  34.9 1.9 %collective-permute-start.1 = (bf16[192,4096]{1,0:T(8,128)(2,1)}, bf16[192,4096]{1,0:T(8,128)(2,1)S(1)}, u32[]{:S(2)}, u32[]{:S(2)}) collective-permute-start(bf16[192,4096]{1,0:T(8,128)(2,1)} %bitcast.5.own_ref), channel_id=1, source_target_pairs={{0,1},{1,2},{2,3},{3,0},{4,5},{5,6},{6,7},{7,4},{8,9},{9,10},{10,1... | collective-permute-start | bytes 4718600 | tf_op jit(solution)/shard_map/ppermute | solution.py:290
  36.8 1.9 %collective-permute-start.3 = (bf16[1024,192]{1,0:T(8,128)(2,1)}, bf16[1024,192]{1,0:T(8,128)(2,1)S(1)}, u32[]{:S(2)}, u32[]{:S(2)}) collective-permute-start(bf16[1024,192]{1,0:T(8,128)(2,1)} %bitcast.13), channel_id=1, source_target_pairs={{0,4},{4,0},{8,12},{12,8},{16,20},{20,16},{24,28},{28,24},{32,36},... | collective-permute-start | bytes 1179656 | tf_op jit(solution)/shard_map/ppermute | solution.py:298
  38.7 2.1 %collective-permute-done.3.other_grads_ref = bf16[1024,192]{1,0:T(8,128)(2,1)S(1)} collective-permute-done((bf16[1024,192]{1,0:T(8,128)(2,1)}, bf16[1024,192]{1,0:T(8,128)(2,1)S(1)}, u32[]{:S(2)}, u32[]{:S(2)}) %collective-permute-start.3) | collective-permute-done | bytes 393248 | tf_op jit(solution)/shard_map/ppermute | solution.py:298
  40.8 1.1 copy-done.5
  41.9 1.0 copy-done.6
  42.9 2.8 %shard_map.88 = (bf16[384,256]{1,0:T(8,128)(2,1)S(1)}, bf16[384,256]{1,0:T(8,128)(2,1)S(1)}, bf16[384,256]{1,0:T(8,128)(2,1)S(1)}, bf16[384,256]{1,0:T(8,128)(2,1)S(1)}) custom-call(s32[2]{0:T(128)S(1)} %pad_add_fusion.pos_ref, s32[8,128]{1,0:T(8,128)S(1)} %bitcast.17, bf16[144,2048]{1,0:T(8,128)(2,1)S(1)} %copy-done.5, bf16[1024,192]{1,0:T(8,128)(2,1)S(1)} %bitcast.14, ...), custom_call_target="tpu_custom_call" | custom-call | flops 5368709120 | bytes 3145728 | tf_op jit(solution)/shard_map/pallas_call | solution.py:347
  45.8 4.2 %collective-permute-start.7 = (bf16[384,256]{1,0:T(8,128)(2,1)S(1)}, bf16[384,256]{1,0:T(8,128)(2,1)S(1)}, u32[]{:S(2)}, u32[]{:S(2)}) collective-permute-start(bf16[384,256]{1,0:T(8,128)(2,1)S(1)} %get-tuple-element.26), channel_id=1, source_target_pairs={{0,2},{1,3},{2,0},{3,1},{4,6},{5,7},{6,4},{7,5},{8,10},{9,11},{10,... | collective-permute-start | bytes 589832 | tf_op jit(solution)/shard_map/ppermute | solution.py:290
  50.0 3.1 %collective-permute-start.8 = (bf16[384,256]{1,0:T(8,128)(2,1)S(1)}, bf16[384,256]{1,0:T(8,128)(2,1)S(1)}, u32[]{:S(2)}, u32[]{:S(2)}) collective-permute-start(bf16[384,256]{1,0:T(8,128)(2,1)S(1)} %get-tuple-element.27), channel_id=1, source_target_pairs={{0,3},{1,0},{2,1},{3,2},{4,7},{5,4},{6,5},{7,6},{8,11},{9,8},{10,9... | collective-permute-start | bytes 589832 | tf_op jit(solution)/shard_map/ppermute | solution.py:290
  53.0 2.8 %collective-permute-start.6 = (bf16[384,256]{1,0:T(8,128)(2,1)S(1)}, bf16[384,256]{1,0:T(8,128)(2,1)S(1)}, u32[]{:S(2)}, u32[]{:S(2)}) collective-permute-start(bf16[384,256]{1,0:T(8,128)(2,1)S(1)} %get-tuple-element.21), channel_id=1, source_target_pairs={{0,1},{1,2},{2,3},{3,0},{4,5},{5,6},{6,7},{7,4},{8,9},{9,10},{10,1... | collective-permute-start | bytes 589832 | tf_op jit(solution)/shard_map/ppermute | solution.py:290
  55.8 18.2 %collective-permute-done.2.right_ref = bf16[192,4096]{1,0:T(8,128)(2,1)S(1)} collective-permute-done((bf16[192,4096]{1,0:T(8,128)(2,1)}, bf16[192,4096]{1,0:T(8,128)(2,1)S(1)}, u32[]{:S(2)}, u32[]{:S(2)}) %collective-permute-start.2) | collective-permute-done | bytes 1572896 | tf_op jit(solution)/shard_map/ppermute | solution.py:290
  74.0 5.7 %collective-permute-done.1.left_ref = bf16[192,4096]{1,0:T(8,128)(2,1)S(1)} collective-permute-done((bf16[192,4096]{1,0:T(8,128)(2,1)}, bf16[192,4096]{1,0:T(8,128)(2,1)S(1)}, u32[]{:S(2)}, u32[]{:S(2)}) %collective-permute-start.1) | collective-permute-done | bytes 1572896 | tf_op jit(solution)/shard_map/ppermute | solution.py:290
  79.7 0.9 slice.7
  80.6 1.0 slice.6
  81.6 1.9 %collective-permute-start.4 = (bf16[96,4096]{1,0:T(8,128)(2,1)}, bf16[96,4096]{1,0:T(8,128)(2,1)}, u32[]{:S(2)}, u32[]{:S(2)}) collective-permute-start(bf16[96,4096]{1,0:T(8,128)(2,1)} %slice.6), channel_id=1, source_target_pairs={{0,1},{1,2},{2,3},{3,0},{4,5},{5,6},{6,7},{7,4},{8,9},{9,10},{10,1... | collective-permute-start | bytes 2359304 | tf_op jit(solution)/shard_map/ppermute | solution.py:290
  83.6 5.1 %collective-permute-start.5 = (bf16[96,4096]{1,0:T(8,128)(2,1)}, bf16[96,4096]{1,0:T(8,128)(2,1)}, u32[]{:S(2)}, u32[]{:S(2)}) collective-permute-start(bf16[96,4096]{1,0:T(8,128)(2,1)} %slice.7), channel_id=1, source_target_pairs={{0,3},{1,0},{2,1},{3,2},{4,7},{5,4},{6,5},{7,6},{8,11},{9,8},{10,9... | collective-permute-start | bytes 2359304 | tf_op jit(solution)/shard_map/ppermute | solution.py:290
  88.7 1.2 shard_map.91
  89.9 0.0 copy-start.2
  89.9 0.8 copy-done.2
  90.7 3.3 %all-to-all-done = bf16[128,8,1280]{2,1,0:T(8,128)(2,1)} async-done(((bf16[128,8,1280]{2,1,0:T(8,128)(2,1)}), bf16[128,8,1280]{2,1,0:T(8,128)(2,1)}, u32[]{:S(2)}, u32[]{:S(2)}) %all-to-all-start) | async-done | bytes 2621472 | tf_op jit(solution)/shard_map/all_to_all | solution.py:304
  94.0 10.9 %all-to-all-start.1 = ((bf16[128,8,256]{2,1,0:T(8,128)(2,1)}), bf16[128,8,256]{2,1,0:T(8,128)(2,1)}, u32[]{:S(2)}, u32[]{:S(2)}) async-start(bf16[128,8,256]{2,1,0:T(8,128)(2,1)} %bitcast.12), calls=%async_computation.1 | async-start | bytes 1048576 | tf_op jit(solution)/shard_map/all_to_all | solution.py:304
  104.9 0.0 copy-start.3
  105.0 1.2 copy-done.3
  106.2 2.3 %shard_map.89.weights_ref = bf16[896,4096]{1,0:T(8,128)(2,1)S(1)} custom-call(s32[2]{0:T(128)S(1)} %pad_add_fusion.pos_ref, bf16[128,4096]{1,0:T(8,128)(2,1)S(1)} %copy-done.3, bf16[192,4096]{1,0:T(8,128)(2,1)} %bitcast.5.own_ref, bf16[192,4096]{1,0:T(8,128)(2,1)S(1)} %collective-permute-done.2.right_ref, bf16[96,4096]{1,0:T(8,128)(2,1)} %collective-permute-done.4.top_ref, ...), custom_call_target="tpu_custom_call" | custom-call | flops 1000 | bytes 14680064 | tf_op jit(solution)/shard_map/pallas_call | solution.py:362
  108.5 0.0 copy-start.9
  108.5 7.3 %shard_map.90 = (f32[768,384]{1,0:T(8,128)S(1)}, f32[128,1024]{1,0:T(8,128)S(1)}, bf16[128,1024]{1,0:T(8,128)(2,1)S(1)}, bf16[128,1024]{1,0:T(8,128)(2,1)S(1)}, bf16[128,1024]{1,0:T(8,128)(2,1)S(1)}) custom-call(s32[2]{0:T(128)S(1)} %pad_add_fusion.pos_ref, bf16[1024,1280]{1,0:T(8,128)(2,1)} %bitcast.4.rows_ref, bf16[896,4096]{1,0:T(8,128)(2,1)S(1)} %shard_map.89.weights_ref), custom_call_target="tpu_custom_call" | custom-call | flops 4294967296 | bytes 12582912 | tf_op jit(solution)/shard_map/pallas_call | solution.py:368
  115.9 1.0 copy-done.10
  116.9 1.9 %collective-permute-start.9 = (bf16[128,1024]{1,0:T(8,128)(2,1)S(1)}, bf16[128,1024]{1,0:T(8,128)(2,1)S(1)}, u32[]{:S(2)}, u32[]{:S(2)}) collective-permute-start(bf16[128,1024]{1,0:T(8,128)(2,1)S(1)} %get-tuple-element.30), channel_id=1, source_target_pairs={{0,1},{1,2},{2,3},{3,0},{4,5},{5,6},{6,7},{7,4},{8,9},{9,10},{10,1... | collective-permute-start | bytes 786440 | tf_op jit(solution)/shard_map/ppermute | solution.py:290
  118.8 3.4 %collective-permute-start.10 = (bf16[128,1024]{1,0:T(8,128)(2,1)S(1)}, bf16[128,1024]{1,0:T(8,128)(2,1)S(1)}, u32[]{:S(2)}, u32[]{:S(2)}) collective-permute-start(bf16[128,1024]{1,0:T(8,128)(2,1)S(1)} %get-tuple-element.31), channel_id=1, source_target_pairs={{0,2},{1,3},{2,0},{3,1},{4,6},{5,7},{6,4},{7,5},{8,10},{9,11},{10,... | collective-permute-start | bytes 786440 | tf_op jit(solution)/shard_map/ppermute | solution.py:290
  122.2 3.7 %collective-permute-start.11 = (bf16[128,1024]{1,0:T(8,128)(2,1)S(1)}, bf16[128,1024]{1,0:T(8,128)(2,1)S(1)}, u32[]{:S(2)}, u32[]{:S(2)}) collective-permute-start(bf16[128,1024]{1,0:T(8,128)(2,1)S(1)} %get-tuple-element.32), channel_id=1, source_target_pairs={{0,3},{1,0},{2,1},{3,2},{4,7},{5,4},{6,5},{7,6},{8,11},{9,8},{10,9... | collective-permute-start | bytes 786440 | tf_op jit(solution)/shard_map/ppermute | solution.py:290
  125.9 1.3 copy-done.11
  127.2 3.7 %shard_map.92 = (f32[192,128]{1,0:T(8,128)S(1)}, bf16[768,128]{1,0:T(8,128)(2,1)}) custom-call(s32[2]{0:T(128)S(1)} %pad_add_fusion.pos_ref, bf16[128,768]{1,0:T(8,128)(2,1)S(1)} %copy-done.9, f32[768,384]{1,0:T(8,128)S(1)} %copy-done.11, bf16[1024,256]{1,0:T(8,128)(2,1)} %bitcast.8.got_ref), custom_call_target="tpu_custom_call" | custom-call | flops 1073741824 | bytes 3145728 | tf_op jit(solution)/shard_map/pallas_call | solution.py:379
  130.9 4.2 %all-to-all-start.2 = ((bf16[4,192,128]{2,1,0:T(8,128)(2,1)}), bf16[4,192,128]{2,1,0:T(8,128)(2,1)S(1)}, u32[]{:S(2)}, u32[]{:S(2)}) async-start(bf16[4,192,128]{2,1,0:T(8,128)(2,1)} %bitcast.10), calls=%async_computation.2 | async-start | bytes 393216 | tf_op jit(solution)/shard_map/all_to_all | solution.py:395
  135.8 0.7 collective-permute-done.11.i3
  136.5 1.0 shard_map.93
  137.5 3.9 %all-to-all-done.2.parts_ref = bf16[4,192,128]{2,1,0:T(8,128)(2,1)S(1)} async-done(((bf16[4,192,128]{2,1,0:T(8,128)(2,1)}), bf16[4,192,128]{2,1,0:T(8,128)(2,1)S(1)}, u32[]{:S(2)}, u32[]{:S(2)}) %all-to-all-start.2) | async-done | bytes 196640 | tf_op jit(solution)/shard_map/all_to_all | solution.py:395
  141.4 1.2 shard_map.94
  (21 shorter events, 0.0 us)
Async XLA Ops:
  0.6 6.5 %copy-start.8 = (s32[128,8]{0,1:T(8,128)S(1)}, s32[128,8]{0,1:T(8,128)}, u32[]{:S(2)}) copy-start(s32[128,8]{0,1:T(8,128)} %param.8) | copy-start | bytes 12292
  0.7 1.2 copy-start
  2.0 0.7 copy-start.7
  2.6 4.5 %copy-start.1 = (bf16[128,4096]{1,0:T(8,128)(2,1)S(1)}, bf16[128,4096]{1,0:T(8,128)(2,1)}, u32[]{:S(2)}) copy-start(bf16[128,4096]{1,0:T(8,128)(2,1)} %tokens_ref.3) | copy-start | bytes 3145732
  3.2 3.9 %collective-permute-start = (bf16[144,2048]{1,0:T(8,128)(2,1)S(1)}, bf16[144,2048]{1,0:T(8,128)(2,1)S(1)}, u32[]{:S(2)}, u32[]{:S(2)}) collective-permute-start(bf16[144,2048]{1,0:T(8,128)(2,1)S(1)} %shard_map.86), channel_id=1, source_target_pairs={{0,4},{4,0},{8,12},{12,8},{16,20},{20,16},{24,28},{28,24},{32,36},... | collective-permute-start | bytes 1769480 | tf_op jit(solution)/shard_map/ppermute | solution.py:298
  7.1 4.0 %copy-start.4 = (bf16[144,2048]{1,0:T(8,128)(2,1)}, bf16[144,2048]{1,0:T(8,128)(2,1)S(1)}, u32[]{:S(2)}) copy-start(bf16[144,2048]{1,0:T(8,128)(2,1)S(1)} %collective-permute-done.other_ref) | copy-start | bytes 1769476
  11.1 17.9 %copy-start.12 = (bf16[128,8,192]{0,2,1:T(8,128)(2,1)S(1)}, bf16[128,8,192]{0,2,1:T(8,128)(2,1)}, u32[]{:S(2)}) copy-start(bf16[128,8,192]{0,2,1:T(8,128)(2,1)} %param.9) | copy-start | bytes 1179652
  11.1 82.9 %all-to-all-start = ((bf16[128,8,1280]{2,1,0:T(8,128)(2,1)}), bf16[128,8,1280]{2,1,0:T(8,128)(2,1)}, u32[]{:S(2)}, u32[]{:S(2)}) async-start(bf16[128,8,1280]{2,1,0:T(8,128)(2,1)} %bitcast.3), calls=%async_computation | async-start | bytes 5242880 | tf_op jit(solution)/shard_map/all_to_all | solution.py:304
  30.2 43.8 %collective-permute-start.2 = (bf16[192,4096]{1,0:T(8,128)(2,1)}, bf16[192,4096]{1,0:T(8,128)(2,1)S(1)}, u32[]{:S(2)}, u32[]{:S(2)}) collective-permute-start(bf16[192,4096]{1,0:T(8,128)(2,1)} %bitcast.5.own_ref), channel_id=1, source_target_pairs={{0,3},{1,0},{2,1},{3,2},{4,7},{5,4},{6,5},{7,6},{8,11},{9,8},{10,9... | collective-permute-start | bytes 4718600 | tf_op jit(solution)/shard_map/ppermute | solution.py:290
  34.9 44.8 %collective-permute-start.1 = (bf16[192,4096]{1,0:T(8,128)(2,1)}, bf16[192,4096]{1,0:T(8,128)(2,1)S(1)}, u32[]{:S(2)}, u32[]{:S(2)}) collective-permute-start(bf16[192,4096]{1,0:T(8,128)(2,1)} %bitcast.5.own_ref), channel_id=1, source_target_pairs={{0,1},{1,2},{2,3},{3,0},{4,5},{5,6},{6,7},{7,4},{8,9},{9,10},{10,1... | collective-permute-start | bytes 4718600 | tf_op jit(solution)/shard_map/ppermute | solution.py:290
  36.8 4.0 %collective-permute-start.3 = (bf16[1024,192]{1,0:T(8,128)(2,1)}, bf16[1024,192]{1,0:T(8,128)(2,1)S(1)}, u32[]{:S(2)}, u32[]{:S(2)}) collective-permute-start(bf16[1024,192]{1,0:T(8,128)(2,1)} %bitcast.13), channel_id=1, source_target_pairs={{0,4},{4,0},{8,12},{12,8},{16,20},{20,16},{24,28},{28,24},{32,36},... | collective-permute-start | bytes 1179656 | tf_op jit(solution)/shard_map/ppermute | solution.py:298
  40.8 1.1 copy-start.5
  41.9 1.0 copy-start.6
  45.8 42.9 %collective-permute-start.7 = (bf16[384,256]{1,0:T(8,128)(2,1)S(1)}, bf16[384,256]{1,0:T(8,128)(2,1)S(1)}, u32[]{:S(2)}, u32[]{:S(2)}) collective-permute-start(bf16[384,256]{1,0:T(8,128)(2,1)S(1)} %get-tuple-element.26), channel_id=1, source_target_pairs={{0,2},{1,3},{2,0},{3,1},{4,6},{5,7},{6,4},{7,5},{8,10},{9,11},{10,... | collective-permute-start | bytes 589832 | tf_op jit(solution)/shard_map/ppermute | solution.py:290
  50.0 38.7 %collective-permute-start.8 = (bf16[384,256]{1,0:T(8,128)(2,1)S(1)}, bf16[384,256]{1,0:T(8,128)(2,1)S(1)}, u32[]{:S(2)}, u32[]{:S(2)}) collective-permute-start(bf16[384,256]{1,0:T(8,128)(2,1)S(1)} %get-tuple-element.27), channel_id=1, source_target_pairs={{0,3},{1,0},{2,1},{3,2},{4,7},{5,4},{6,5},{7,6},{8,11},{9,8},{10,9... | collective-permute-start | bytes 589832 | tf_op jit(solution)/shard_map/ppermute | solution.py:290
  53.0 35.7 %collective-permute-start.6 = (bf16[384,256]{1,0:T(8,128)(2,1)S(1)}, bf16[384,256]{1,0:T(8,128)(2,1)S(1)}, u32[]{:S(2)}, u32[]{:S(2)}) collective-permute-start(bf16[384,256]{1,0:T(8,128)(2,1)S(1)} %get-tuple-element.21), channel_id=1, source_target_pairs={{0,1},{1,2},{2,3},{3,0},{4,5},{5,6},{6,7},{7,4},{8,9},{9,10},{10,1... | collective-permute-start | bytes 589832 | tf_op jit(solution)/shard_map/ppermute | solution.py:290
  81.6 23.3 %collective-permute-start.4 = (bf16[96,4096]{1,0:T(8,128)(2,1)}, bf16[96,4096]{1,0:T(8,128)(2,1)}, u32[]{:S(2)}, u32[]{:S(2)}) collective-permute-start(bf16[96,4096]{1,0:T(8,128)(2,1)} %slice.6), channel_id=1, source_target_pairs={{0,1},{1,2},{2,3},{3,0},{4,5},{5,6},{6,7},{7,4},{8,9},{9,10},{10,1... | collective-permute-start | bytes 2359304 | tf_op jit(solution)/shard_map/ppermute | solution.py:290
  83.6 21.4 %collective-permute-start.5 = (bf16[96,4096]{1,0:T(8,128)(2,1)}, bf16[96,4096]{1,0:T(8,128)(2,1)}, u32[]{:S(2)}, u32[]{:S(2)}) collective-permute-start(bf16[96,4096]{1,0:T(8,128)(2,1)} %slice.7), channel_id=1, source_target_pairs={{0,3},{1,0},{2,1},{3,2},{4,7},{5,4},{6,5},{7,6},{8,11},{9,8},{10,9... | collective-permute-start | bytes 2359304 | tf_op jit(solution)/shard_map/ppermute | solution.py:290
  89.9 0.8 copy-start.2
  94.0 31.9 %all-to-all-start.1 = ((bf16[128,8,256]{2,1,0:T(8,128)(2,1)}), bf16[128,8,256]{2,1,0:T(8,128)(2,1)}, u32[]{:S(2)}, u32[]{:S(2)}) async-start(bf16[128,8,256]{2,1,0:T(8,128)(2,1)} %bitcast.12), calls=%async_computation.1 | async-start | bytes 1048576 | tf_op jit(solution)/shard_map/all_to_all | solution.py:304
  104.9 1.2 copy-start.3
  108.5 17.4 %copy-start.9 = (bf16[128,768]{1,0:T(8,128)(2,1)S(1)}, bf16[128,768]{1,0:T(8,128)(2,1)}, u32[]{:S(2)}) copy-start(bf16[128,768]{1,0:T(8,128)(2,1)} %grad_probes_ref.1) | copy-start | bytes 589828
  115.8 1.0 copy-start.10
  116.9 18.9 %collective-permute-start.9 = (bf16[128,1024]{1,0:T(8,128)(2,1)S(1)}, bf16[128,1024]{1,0:T(8,128)(2,1)S(1)}, u32[]{:S(2)}, u32[]{:S(2)}) collective-permute-start(bf16[128,1024]{1,0:T(8,128)(2,1)S(1)} %get-tuple-element.30), channel_id=1, source_target_pairs={{0,1},{1,2},{2,3},{3,0},{4,5},{5,6},{6,7},{7,4},{8,9},{9,10},{10,1... | collective-permute-start | bytes 786440 | tf_op jit(solution)/shard_map/ppermute | solution.py:290
  118.8 17.0 %collective-permute-start.10 = (bf16[128,1024]{1,0:T(8,128)(2,1)S(1)}, bf16[128,1024]{1,0:T(8,128)(2,1)S(1)}, u32[]{:S(2)}, u32[]{:S(2)}) collective-permute-start(bf16[128,1024]{1,0:T(8,128)(2,1)S(1)} %get-tuple-element.31), channel_id=1, source_target_pairs={{0,2},{1,3},{2,0},{3,1},{4,6},{5,7},{6,4},{7,5},{8,10},{9,11},{10,... | collective-permute-start | bytes 786440 | tf_op jit(solution)/shard_map/ppermute | solution.py:290
  122.2 14.3 %collective-permute-start.11 = (bf16[128,1024]{1,0:T(8,128)(2,1)S(1)}, bf16[128,1024]{1,0:T(8,128)(2,1)S(1)}, u32[]{:S(2)}, u32[]{:S(2)}) collective-permute-start(bf16[128,1024]{1,0:T(8,128)(2,1)S(1)} %get-tuple-element.32), channel_id=1, source_target_pairs={{0,3},{1,0},{2,1},{3,2},{4,7},{5,4},{6,5},{7,6},{8,11},{9,8},{10,9... | collective-permute-start | bytes 786440 | tf_op jit(solution)/shard_map/ppermute | solution.py:290
  125.9 1.3 copy-start.11
  130.9 10.5 %all-to-all-start.2 = ((bf16[4,192,128]{2,1,0:T(8,128)(2,1)}), bf16[4,192,128]{2,1,0:T(8,128)(2,1)S(1)}, u32[]{:S(2)}, u32[]{:S(2)}) async-start(bf16[4,192,128]{2,1,0:T(8,128)(2,1)} %bitcast.10), calls=%async_computation.2 | async-start | bytes 393216 | tf_op jit(solution)/shard_map/all_to_all | solution.py:395

commit v14 on v9

--- a/solution.py
+++ b/solution.py
@@ -369,6 +369,7 @@
     input_sketch = kernel_call(
         finish_input, sds((SHARE, R), F32), [SM] + [VM] * 4, 1 << 20, 2 * MIB, 6
     )(inverse, *inputs)
+    own_sketch, input_sketch = lax.optimization_barrier((own_sketch, input_sketch))
     grad_sketch = kernel_call(
         finish_grad, sds((UNITS, R), F32), [SM] * 2 + [VM] * 2, 1 << 18, MIB // 4, 4
     )(pos, inverse, own_sketch, sketches)

time: 141 us -> 143 us (1.014)
  starting transfers between devices: 67.5 us -> 69.5 us
    ppermute x10, waiting for transfers between devices: 20.5 us -> 25.6 us  [shift(): lax.ppermute(block, 'rep', [(i, (i + k) % REPS) for i in range(REPS)])]
    all_to_all x2, starting transfers between devices: 26.1 us -> 28.9 us  [to_owners(): lax.all_to_all(rows, 'ep', split_axis=0, concat_axis=0, tiled=True)]
    all_to_all x2, waiting for transfers between devices: 6 us -> 3.23 us  [to_owners(): lax.all_to_all(rows, 'ep', split_axis=0, concat_axis=0, tiled=True)]
    all_to_all x1, waiting for transfers between devices: 5.6 us -> 2.89 us  [local(): lax.all_to_all(sketch.reshape(REPS, UNITS, R), 'rep', split_axis=0, conca...]
    ppermute x10, starting transfers between devices: 34.2 us -> 32.6 us  [shift(): lax.ppermute(block, 'rep', [(i, (i + k) % REPS) for i in range(REPS)])]
  transfers between devices with their start and end apart: 15 -> 15, of which waited for: 6 -> 7; matrix products, arithmetic and copies ran while one was open for 2% -> 2% of each run, Pallas kernels for 13% -> 12%
where the time goes in v14:
time: 143 us; the launch traced here: 142 us
  starting transfers between devices  69.5 us (49%)
  waiting for transfers between devices  35.8 us (25%)
  Pallas kernels  23.6 us (17%)
  local copies, waits for them, and re-layouts  11.5 us (8%)
  between operations  1.62 us (1%)
    ppermute x10, starting transfers between devices, shift(): lax.ppermute(block, 'rep', [(i, (i + k) % REPS) for i in range(REPS)])  32.6 us
    all_to_all x2, starting transfers between devices, to_owners(): lax.all_to_all(rows, 'ep', split_axis=0, concat_axis=0, tiled=True)  28.9 us
    ppermute x10, waiting for transfers between devices, shift(): lax.ppermute(block, 'rep', [(i, (i + k) % REPS) for i in range(REPS)])  25.6 us
    unnamed x27, local copies, waits for them, and re-layouts  9.53 us
    pallas_call x1, Pallas kernels, local(): kernel_call(products, [sds((FFW, ALL), F32)] + [sds((R, SHARE), kind) for...  7.23 us
    pallas_call x1, Pallas kernels, local(): kernel_call(send_rows, sds((ROWS, SHARE + STRIP), BF), [SM] + [VM] * 3, 1...  4.26 us
    all_to_all x1, starting transfers between devices, local(): lax.all_to_all(sketch.reshape(REPS, UNITS, R), 'rep', split_axis=0, conca...  4.18 us
    ppermute x2, waiting for transfers between devices, swap(): return lax.ppermute(block, 'ep', [(i, i ^ 1) for i in range(OWNERS)])  4.06 us
  transfers between devices with their start and end apart: 15, of which 7 were waited for; matrix products, arithmetic and copies ran while one was open for 2% of the time, Pallas kernels for 12%

profile of v14, /device:TPU:8, one launch (start us, length us, event | category | flops | bytes accessed | tf_op | source)
XLA Modules:
  0.0 142.1 jit_solution(3926289169525766196)
XLA Ops:
  0.6 0.0 copy-start.6
  0.7 0.1 pad_add_fusion.pos_ref
  0.7 1.2 copy-done.2
  2.0 0.7 copy-done.5
  2.6 0.6 shard_map.86
  3.2 1.9 %collective-permute-start = (bf16[144,2048]{1,0:T(8,128)(2,1)S(1)}, bf16[144,2048]{1,0:T(8,128)(2,1)S(1)}, u32[]{:S(2)}, u32[]{:S(2)}) collective-permute-start(bf16[144,2048]{1,0:T(8,128)(2,1)S(1)} %shard_map.86), channel_id=1, source_target_pairs={{0,4},{4,0},{8,12},{12,8},{16,20},{20,16},{24,28},{28,24},{32,36},... | collective-permute-start | bytes 1769480 | tf_op jit(solution)/shard_map/ppermute | solution.py:277
  5.2 2.0 %collective-permute-done.other_ref = bf16[144,2048]{1,0:T(8,128)(2,1)S(1)} collective-permute-done((bf16[144,2048]{1,0:T(8,128)(2,1)S(1)}, bf16[144,2048]{1,0:T(8,128)(2,1)S(1)}, u32[]{:S(2)}, u32[]{:S(2)}) %collective-permute-start) | collective-permute-done | bytes 589856 | tf_op jit(solution)/shard_map/ppermute | solution.py:277
  7.1 4.3 %shard_map.87 = bf16[1024,1280]{1,0:T(8,128)(2,1)} custom-call(s32[2]{0:T(128)S(1)} %pad_add_fusion.pos_ref, s32[8,128]{1,0:T(8,128)S(1)} %bitcast.16, bf16[128,4096]{1,0:T(8,128)(2,1)S(1)} %copy-done.3, bf16[144,2048]{1,0:T(8,128)(2,1)S(1)} %collective-permute-done.other_ref), custom_call_target="tpu_custom_call" | custom-call | flops 2147483648 | bytes 5242880 | tf_op jit(solution)/shard_map/pallas_call | solution.py:305
  11.4 17.9 %all-to-all-start = ((bf16[128,8,1280]{2,1,0:T(8,128)(2,1)}), bf16[128,8,1280]{2,1,0:T(8,128)(2,1)}, u32[]{:S(2)}, u32[]{:S(2)}) async-start(bf16[128,8,1280]{2,1,0:T(8,128)(2,1)} %bitcast.3), calls=%async_computation | async-start | bytes 5242880 | tf_op jit(solution)/shard_map/all_to_all | solution.py:283
  29.3 1.2 copy.9
  30.5 4.7 %collective-permute-start.2 = (bf16[192,4096]{1,0:T(8,128)(2,1)}, bf16[192,4096]{1,0:T(8,128)(2,1)S(1)}, u32[]{:S(2)}, u32[]{:S(2)}) collective-permute-start(bf16[192,4096]{1,0:T(8,128)(2,1)} %bitcast.5.own_ref), channel_id=1, source_target_pairs={{0,3},{1,0},{2,1},{3,2},{4,7},{5,4},{6,5},{7,6},{8,11},{9,8},{10,9... | collective-permute-start | bytes 4718600 | tf_op jit(solution)/shard_map/ppermute | solution.py:269
  35.2 1.9 %collective-permute-start.1 = (bf16[192,4096]{1,0:T(8,128)(2,1)}, bf16[192,4096]{1,0:T(8,128)(2,1)S(1)}, u32[]{:S(2)}, u32[]{:S(2)}) collective-permute-start(bf16[192,4096]{1,0:T(8,128)(2,1)} %bitcast.5.own_ref), channel_id=1, source_target_pairs={{0,1},{1,2},{2,3},{3,0},{4,5},{5,6},{6,7},{7,4},{8,9},{9,10},{10,1... | collective-permute-start | bytes 4718600 | tf_op jit(solution)/shard_map/ppermute | solution.py:269
  37.1 1.9 %collective-permute-start.3 = (bf16[1024,192]{1,0:T(8,128)(2,1)}, bf16[1024,192]{1,0:T(8,128)(2,1)S(1)}, u32[]{:S(2)}, u32[]{:S(2)}) collective-permute-start(bf16[1024,192]{1,0:T(8,128)(2,1)} %bitcast.13), channel_id=1, source_target_pairs={{0,4},{4,0},{8,12},{12,8},{16,20},{20,16},{24,28},{28,24},{32,36},... | collective-permute-start | bytes 1179656 | tf_op jit(solution)/shard_map/ppermute | solution.py:277
  39.1 2.1 %collective-permute-done.3.other_grads_ref = bf16[1024,192]{1,0:T(8,128)(2,1)S(1)} collective-permute-done((bf16[1024,192]{1,0:T(8,128)(2,1)}, bf16[1024,192]{1,0:T(8,128)(2,1)S(1)}, u32[]{:S(2)}, u32[]{:S(2)}) %collective-permute-start.3) | collective-permute-done | bytes 393248 | tf_op jit(solution)/shard_map/ppermute | solution.py:277
  41.1 1.0 copy-done.4
  42.2 1.1 copy-done.8
  43.2 2.8 %shard_map.88 = (bf16[384,256]{1,0:T(8,128)(2,1)S(1)}, bf16[384,256]{1,0:T(8,128)(2,1)S(1)}, bf16[384,256]{1,0:T(8,128)(2,1)S(1)}, bf16[384,256]{1,0:T(8,128)(2,1)S(1)}) custom-call(s32[2]{0:T(128)S(1)} %pad_add_fusion.pos_ref, s32[8,128]{1,0:T(8,128)S(1)} %bitcast.17, bf16[144,2048]{1,0:T(8,128)(2,1)S(1)} %copy-done.8, bf16[1024,192]{1,0:T(8,128)(2,1)S(1)} %bitcast.14, ...), custom_call_target="tpu_custom_call" | custom-call | flops 5368709120 | bytes 3145728 | tf_op jit(solution)/shard_map/pallas_call | solution.py:324
  46.1 4.2 %collective-permute-start.7 = (bf16[384,256]{1,0:T(8,128)(2,1)S(1)}, bf16[384,256]{1,0:T(8,128)(2,1)S(1)}, u32[]{:S(2)}, u32[]{:S(2)}) collective-permute-start(bf16[384,256]{1,0:T(8,128)(2,1)S(1)} %get-tuple-element.26), channel_id=1, source_target_pairs={{0,2},{1,3},{2,0},{3,1},{4,6},{5,7},{6,4},{7,5},{8,10},{9,11},{10,... | collective-permute-start | bytes 589832 | tf_op jit(solution)/shard_map/ppermute | solution.py:269
  50.3 3.0 %collective-permute-start.8 = (bf16[384,256]{1,0:T(8,128)(2,1)S(1)}, bf16[384,256]{1,0:T(8,128)(2,1)S(1)}, u32[]{:S(2)}, u32[]{:S(2)}) collective-permute-start(bf16[384,256]{1,0:T(8,128)(2,1)S(1)} %get-tuple-element.27), channel_id=1, source_target_pairs={{0,3},{1,0},{2,1},{3,2},{4,7},{5,4},{6,5},{7,6},{8,11},{9,8},{10,9... | collective-permute-start | bytes 589832 | tf_op jit(solution)/shard_map/ppermute | solution.py:269
  53.3 2.8 %collective-permute-start.6 = (bf16[384,256]{1,0:T(8,128)(2,1)S(1)}, bf16[384,256]{1,0:T(8,128)(2,1)S(1)}, u32[]{:S(2)}, u32[]{:S(2)}) collective-permute-start(bf16[384,256]{1,0:T(8,128)(2,1)S(1)} %get-tuple-element.21), channel_id=1, source_target_pairs={{0,1},{1,2},{2,3},{3,0},{4,5},{5,6},{6,7},{7,4},{8,9},{9,10},{10,1... | collective-permute-start | bytes 589832 | tf_op jit(solution)/shard_map/ppermute | solution.py:269
  56.1 18.2 %collective-permute-done.2.right_ref = bf16[192,4096]{1,0:T(8,128)(2,1)S(1)} collective-permute-done((bf16[192,4096]{1,0:T(8,128)(2,1)}, bf16[192,4096]{1,0:T(8,128)(2,1)S(1)}, u32[]{:S(2)}, u32[]{:S(2)}) %collective-permute-start.2) | collective-permute-done | bytes 1572896 | tf_op jit(solution)/shard_map/ppermute | solution.py:269
  74.3 5.7 %collective-permute-done.1.left_ref = bf16[192,4096]{1,0:T(8,128)(2,1)S(1)} collective-permute-done((bf16[192,4096]{1,0:T(8,128)(2,1)}, bf16[192,4096]{1,0:T(8,128)(2,1)S(1)}, u32[]{:S(2)}, u32[]{:S(2)}) %collective-permute-start.1) | collective-permute-done | bytes 1572896 | tf_op jit(solution)/shard_map/ppermute | solution.py:269
  80.0 0.9 slice.7
  80.9 1.0 slice.6
  82.0 1.9 %collective-permute-start.4 = (bf16[96,4096]{1,0:T(8,128)(2,1)}, bf16[96,4096]{1,0:T(8,128)(2,1)}, u32[]{:S(2)}, u32[]{:S(2)}) collective-permute-start(bf16[96,4096]{1,0:T(8,128)(2,1)} %slice.6), channel_id=1, source_target_pairs={{0,1},{1,2},{2,3},{3,0},{4,5},{5,6},{6,7},{7,4},{8,9},{9,10},{10,1... | collective-permute-start | bytes 2359304 | tf_op jit(solution)/shard_map/ppermute | solution.py:269
  83.9 5.1 %collective-permute-start.5 = (bf16[96,4096]{1,0:T(8,128)(2,1)}, bf16[96,4096]{1,0:T(8,128)(2,1)}, u32[]{:S(2)}, u32[]{:S(2)}) collective-permute-start(bf16[96,4096]{1,0:T(8,128)(2,1)} %slice.7), channel_id=1, source_target_pairs={{0,3},{1,0},{2,1},{3,2},{4,7},{5,4},{6,5},{7,6},{8,11},{9,8},{10,9... | collective-permute-start | bytes 2359304 | tf_op jit(solution)/shard_map/ppermute | solution.py:269
  89.0 0.0 collective-permute-done.7.g2
  89.1 1.2 shard_map.91
  90.2 0.0 copy-start
  90.2 0.8 copy-done
  91.0 3.2 %all-to-all-done = bf16[128,8,1280]{2,1,0:T(8,128)(2,1)} async-done(((bf16[128,8,1280]{2,1,0:T(8,128)(2,1)}), bf16[128,8,1280]{2,1,0:T(8,128)(2,1)}, u32[]{:S(2)}, u32[]{:S(2)}) %all-to-all-start) | async-done | bytes 2621472 | tf_op jit(solution)/shard_map/all_to_all | solution.py:283
  94.2 11.0 %all-to-all-start.1 = ((bf16[128,8,256]{2,1,0:T(8,128)(2,1)}), bf16[128,8,256]{2,1,0:T(8,128)(2,1)}, u32[]{:S(2)}, u32[]{:S(2)}) async-start(bf16[128,8,256]{2,1,0:T(8,128)(2,1)} %bitcast.12), calls=%async_computation.1 | async-start | bytes 1048576 | tf_op jit(solution)/shard_map/all_to_all | solution.py:283
  105.3 0.0 copy-start.1
  105.3 1.2 copy-done.1
  106.5 2.3 %shard_map.89.weights_ref = bf16[896,4096]{1,0:T(8,128)(2,1)S(1)} custom-call(s32[2]{0:T(128)S(1)} %pad_add_fusion.pos_ref, bf16[128,4096]{1,0:T(8,128)(2,1)S(1)} %copy-done.1, bf16[192,4096]{1,0:T(8,128)(2,1)} %bitcast.5.own_ref, bf16[192,4096]{1,0:T(8,128)(2,1)S(1)} %collective-permute-done.2.right_ref, bf16[96,4096]{1,0:T(8,128)(2,1)} %collective-permute-done.4.top_ref, ...), custom_call_target="tpu_custom_call" | custom-call | flops 1000 | bytes 14680064 | tf_op jit(solution)/shard_map/pallas_call | solution.py:339
  108.8 0.0 copy-start.9
  108.8 7.2 %shard_map.90 = (f32[768,384]{1,0:T(8,128)S(1)}, f32[128,1024]{1,0:T(8,128)S(1)}, bf16[128,1024]{1,0:T(8,128)(2,1)S(1)}, bf16[128,1024]{1,0:T(8,128)(2,1)S(1)}, bf16[128,1024]{1,0:T(8,128)(2,1)S(1)}) custom-call(s32[2]{0:T(128)S(1)} %pad_add_fusion.pos_ref, bf16[1024,1280]{1,0:T(8,128)(2,1)} %bitcast.4.rows_ref, bf16[896,4096]{1,0:T(8,128)(2,1)S(1)} %shard_map.89.weights_ref), custom_call_target="tpu_custom_call" | custom-call | flops 4294967296 | bytes 12582912 | tf_op jit(solution)/shard_map/pallas_call | solution.py:345
  116.1 1.0 copy-done.10
  117.1 1.9 %collective-permute-start.9 = (bf16[128,1024]{1,0:T(8,128)(2,1)S(1)}, bf16[128,1024]{1,0:T(8,128)(2,1)S(1)}, u32[]{:S(2)}, u32[]{:S(2)}) collective-permute-start(bf16[128,1024]{1,0:T(8,128)(2,1)S(1)} %get-tuple-element.30), channel_id=1, source_target_pairs={{0,1},{1,2},{2,3},{3,0},{4,5},{5,6},{6,7},{7,4},{8,9},{9,10},{10,1... | collective-permute-start | bytes 786440 | tf_op jit(solution)/shard_map/ppermute | solution.py:269
  119.0 3.4 %collective-permute-start.10 = (bf16[128,1024]{1,0:T(8,128)(2,1)S(1)}, bf16[128,1024]{1,0:T(8,128)(2,1)S(1)}, u32[]{:S(2)}, u32[]{:S(2)}) collective-permute-start(bf16[128,1024]{1,0:T(8,128)(2,1)S(1)} %get-tuple-element.31), channel_id=1, source_target_pairs={{0,2},{1,3},{2,0},{3,1},{4,6},{5,7},{6,4},{7,5},{8,10},{9,11},{10,... | collective-permute-start | bytes 786440 | tf_op jit(solution)/shard_map/ppermute | solution.py:269
  122.4 3.7 %collective-permute-start.11 = (bf16[128,1024]{1,0:T(8,128)(2,1)S(1)}, bf16[128,1024]{1,0:T(8,128)(2,1)S(1)}, u32[]{:S(2)}, u32[]{:S(2)}) collective-permute-start(bf16[128,1024]{1,0:T(8,128)(2,1)S(1)} %get-tuple-element.32), channel_id=1, source_target_pairs={{0,3},{1,0},{2,1},{3,2},{4,7},{5,4},{6,5},{7,6},{8,11},{9,8},{10,9... | collective-permute-start | bytes 786440 | tf_op jit(solution)/shard_map/ppermute | solution.py:269
  126.1 1.3 copy-done.11
  127.4 3.0 %shard_map.92 = (f32[192,128]{1,0:T(8,128)S(1)}, bf16[768,128]{1,0:T(8,128)(2,1)}) custom-call(s32[2]{0:T(128)S(1)} %pad_add_fusion.pos_ref, bf16[128,768]{1,0:T(8,128)(2,1)S(1)} %copy-done.9, f32[768,384]{1,0:T(8,128)S(1)} %copy-done.11, bf16[1024,256]{1,0:T(8,128)(2,1)} %bitcast.8.got_ref), custom_call_target="tpu_custom_call" | custom-call | flops 1073741824 | bytes 3145728 | tf_op jit(solution)/shard_map/pallas_call | solution.py:356
  130.4 4.2 %all-to-all-start.2 = ((bf16[4,192,128]{2,1,0:T(8,128)(2,1)}), bf16[4,192,128]{2,1,0:T(8,128)(2,1)S(1)}, u32[]{:S(2)}, u32[]{:S(2)}) async-start(bf16[4,192,128]{2,1,0:T(8,128)(2,1)} %bitcast.10), calls=%async_computation.2 | async-start | bytes 393216 | tf_op jit(solution)/shard_map/all_to_all | solution.py:365
  135.3 1.7 %collective-permute-done.11.i3 = bf16[128,1024]{1,0:T(8,128)(2,1)S(1)} collective-permute-done((bf16[128,1024]{1,0:T(8,128)(2,1)S(1)}, bf16[128,1024]{1,0:T(8,128)(2,1)S(1)}, u32[]{:S(2)}, u32[]{:S(2)}) %collective-permute-start.11) | collective-permute-done | bytes 262176 | tf_op jit(solution)/shard_map/ppermute | solution.py:269
  137.0 1.0 shard_map.93
  138.0 2.9 %all-to-all-done.2.parts_ref = bf16[4,192,128]{2,1,0:T(8,128)(2,1)S(1)} async-done(((bf16[4,192,128]{2,1,0:T(8,128)(2,1)}), bf16[4,192,128]{2,1,0:T(8,128)(2,1)S(1)}, u32[]{:S(2)}, u32[]{:S(2)}) %all-to-all-start.2) | async-done | bytes 196640 | tf_op jit(solution)/shard_map/all_to_all | solution.py:365
  140.9 1.2 shard_map.94
  (21 shorter events, 0.0 us)
Async XLA Ops:
  0.6 6.5 %copy-start.6 = (s32[128,8]{0,1:T(8,128)S(1)}, s32[128,8]{0,1:T(8,128)}, u32[]{:S(2)}) copy-start(s32[128,8]{0,1:T(8,128)} %param.8) | copy-start | bytes 12292
  0.7 1.2 copy-start.2
  2.0 0.7 copy-start.5
  2.6 4.5 %copy-start.3 = (bf16[128,4096]{1,0:T(8,128)(2,1)S(1)}, bf16[128,4096]{1,0:T(8,128)(2,1)}, u32[]{:S(2)}) copy-start(bf16[128,4096]{1,0:T(8,128)(2,1)} %tokens_ref.3) | copy-start | bytes 3145732
  3.2 3.9 %collective-permute-start = (bf16[144,2048]{1,0:T(8,128)(2,1)S(1)}, bf16[144,2048]{1,0:T(8,128)(2,1)S(1)}, u32[]{:S(2)}, u32[]{:S(2)}) collective-permute-start(bf16[144,2048]{1,0:T(8,128)(2,1)S(1)} %shard_map.86), channel_id=1, source_target_pairs={{0,4},{4,0},{8,12},{12,8},{16,20},{20,16},{24,28},{28,24},{32,36},... | collective-permute-start | bytes 1769480 | tf_op jit(solution)/shard_map/ppermute | solution.py:277
  7.1 4.3 %copy-start.7 = (bf16[144,2048]{1,0:T(8,128)(2,1)}, bf16[144,2048]{1,0:T(8,128)(2,1)S(1)}, u32[]{:S(2)}) copy-start(bf16[144,2048]{1,0:T(8,128)(2,1)S(1)} %collective-permute-done.other_ref) | copy-start | bytes 1769476
  11.4 17.9 %copy-start.12 = (bf16[128,8,192]{0,2,1:T(8,128)(2,1)S(1)}, bf16[128,8,192]{0,2,1:T(8,128)(2,1)}, u32[]{:S(2)}) copy-start(bf16[128,8,192]{0,2,1:T(8,128)(2,1)} %param.9) | copy-start | bytes 1179652
  11.4 82.9 %all-to-all-start = ((bf16[128,8,1280]{2,1,0:T(8,128)(2,1)}), bf16[128,8,1280]{2,1,0:T(8,128)(2,1)}, u32[]{:S(2)}, u32[]{:S(2)}) async-start(bf16[128,8,1280]{2,1,0:T(8,128)(2,1)} %bitcast.3), calls=%async_computation | async-start | bytes 5242880 | tf_op jit(solution)/shard_map/all_to_all | solution.py:283
  30.5 43.8 %collective-permute-start.2 = (bf16[192,4096]{1,0:T(8,128)(2,1)}, bf16[192,4096]{1,0:T(8,128)(2,1)S(1)}, u32[]{:S(2)}, u32[]{:S(2)}) collective-permute-start(bf16[192,4096]{1,0:T(8,128)(2,1)} %bitcast.5.own_ref), channel_id=1, source_target_pairs={{0,3},{1,0},{2,1},{3,2},{4,7},{5,4},{6,5},{7,6},{8,11},{9,8},{10,9... | collective-permute-start | bytes 4718600 | tf_op jit(solution)/shard_map/ppermute | solution.py:269
  35.2 44.8 %collective-permute-start.1 = (bf16[192,4096]{1,0:T(8,128)(2,1)}, bf16[192,4096]{1,0:T(8,128)(2,1)S(1)}, u32[]{:S(2)}, u32[]{:S(2)}) collective-permute-start(bf16[192,4096]{1,0:T(8,128)(2,1)} %bitcast.5.own_ref), channel_id=1, source_target_pairs={{0,1},{1,2},{2,3},{3,0},{4,5},{5,6},{6,7},{7,4},{8,9},{9,10},{10,1... | collective-permute-start | bytes 4718600 | tf_op jit(solution)/shard_map/ppermute | solution.py:269
  37.1 4.0 %collective-permute-start.3 = (bf16[1024,192]{1,0:T(8,128)(2,1)}, bf16[1024,192]{1,0:T(8,128)(2,1)S(1)}, u32[]{:S(2)}, u32[]{:S(2)}) collective-permute-start(bf16[1024,192]{1,0:T(8,128)(2,1)} %bitcast.13), channel_id=1, source_target_pairs={{0,4},{4,0},{8,12},{12,8},{16,20},{20,16},{24,28},{28,24},{32,36},... | collective-permute-start | bytes 1179656 | tf_op jit(solution)/shard_map/ppermute | solution.py:277
  41.1 1.0 copy-start.4
  42.2 1.1 copy-start.8
  46.1 42.9 %collective-permute-start.7 = (bf16[384,256]{1,0:T(8,128)(2,1)S(1)}, bf16[384,256]{1,0:T(8,128)(2,1)S(1)}, u32[]{:S(2)}, u32[]{:S(2)}) collective-permute-start(bf16[384,256]{1,0:T(8,128)(2,1)S(1)} %get-tuple-element.26), channel_id=1, source_target_pairs={{0,2},{1,3},{2,0},{3,1},{4,6},{5,7},{6,4},{7,5},{8,10},{9,11},{10,... | collective-permute-start | bytes 589832 | tf_op jit(solution)/shard_map/ppermute | solution.py:269
  50.3 38.8 %collective-permute-start.8 = (bf16[384,256]{1,0:T(8,128)(2,1)S(1)}, bf16[384,256]{1,0:T(8,128)(2,1)S(1)}, u32[]{:S(2)}, u32[]{:S(2)}) collective-permute-start(bf16[384,256]{1,0:T(8,128)(2,1)S(1)} %get-tuple-element.27), channel_id=1, source_target_pairs={{0,3},{1,0},{2,1},{3,2},{4,7},{5,4},{6,5},{7,6},{8,11},{9,8},{10,9... | collective-permute-start | bytes 589832 | tf_op jit(solution)/shard_map/ppermute | solution.py:269
  53.3 35.7 %collective-permute-start.6 = (bf16[384,256]{1,0:T(8,128)(2,1)S(1)}, bf16[384,256]{1,0:T(8,128)(2,1)S(1)}, u32[]{:S(2)}, u32[]{:S(2)}) collective-permute-start(bf16[384,256]{1,0:T(8,128)(2,1)S(1)} %get-tuple-element.21), channel_id=1, source_target_pairs={{0,1},{1,2},{2,3},{3,0},{4,5},{5,6},{6,7},{7,4},{8,9},{9,10},{10,1... | collective-permute-start | bytes 589832 | tf_op jit(solution)/shard_map/ppermute | solution.py:269
  82.0 23.3 %collective-permute-start.4 = (bf16[96,4096]{1,0:T(8,128)(2,1)}, bf16[96,4096]{1,0:T(8,128)(2,1)}, u32[]{:S(2)}, u32[]{:S(2)}) collective-permute-start(bf16[96,4096]{1,0:T(8,128)(2,1)} %slice.6), channel_id=1, source_target_pairs={{0,1},{1,2},{2,3},{3,0},{4,5},{5,6},{6,7},{7,4},{8,9},{9,10},{10,1... | collective-permute-start | bytes 2359304 | tf_op jit(solution)/shard_map/ppermute | solution.py:269
  83.9 21.4 %collective-permute-start.5 = (bf16[96,4096]{1,0:T(8,128)(2,1)}, bf16[96,4096]{1,0:T(8,128)(2,1)}, u32[]{:S(2)}, u32[]{:S(2)}) collective-permute-start(bf16[96,4096]{1,0:T(8,128)(2,1)} %slice.7), channel_id=1, source_target_pairs={{0,3},{1,0},{2,1},{3,2},{4,7},{5,4},{6,5},{7,6},{8,11},{9,8},{10,9... | collective-permute-start | bytes 2359304 | tf_op jit(solution)/shard_map/ppermute | solution.py:269
  90.2 0.8 copy-start
  94.2 31.8 %all-to-all-start.1 = ((bf16[128,8,256]{2,1,0:T(8,128)(2,1)}), bf16[128,8,256]{2,1,0:T(8,128)(2,1)}, u32[]{:S(2)}, u32[]{:S(2)}) async-start(bf16[128,8,256]{2,1,0:T(8,128)(2,1)} %bitcast.12), calls=%async_computation.1 | async-start | bytes 1048576 | tf_op jit(solution)/shard_map/all_to_all | solution.py:283
  105.3 1.2 copy-start.1
  108.8 17.3 %copy-start.9 = (bf16[128,768]{1,0:T(8,128)(2,1)S(1)}, bf16[128,768]{1,0:T(8,128)(2,1)}, u32[]{:S(2)}) copy-start(bf16[128,768]{1,0:T(8,128)(2,1)} %grad_probes_ref.1) | copy-start | bytes 589828
  116.1 1.0 copy-start.10
  117.1 18.1 %collective-permute-start.9 = (bf16[128,1024]{1,0:T(8,128)(2,1)S(1)}, bf16[128,1024]{1,0:T(8,128)(2,1)S(1)}, u32[]{:S(2)}, u32[]{:S(2)}) collective-permute-start(bf16[128,1024]{1,0:T(8,128)(2,1)S(1)} %get-tuple-element.30), channel_id=1, source_target_pairs={{0,1},{1,2},{2,3},{3,0},{4,5},{5,6},{6,7},{7,4},{8,9},{9,10},{10,1... | collective-permute-start | bytes 786440 | tf_op jit(solution)/shard_map/ppermute | solution.py:269
  119.0 16.2 %collective-permute-start.10 = (bf16[128,1024]{1,0:T(8,128)(2,1)S(1)}, bf16[128,1024]{1,0:T(8,128)(2,1)S(1)}, u32[]{:S(2)}, u32[]{:S(2)}) collective-permute-start(bf16[128,1024]{1,0:T(8,128)(2,1)S(1)} %get-tuple-element.31), channel_id=1, source_target_pairs={{0,2},{1,3},{2,0},{3,1},{4,6},{5,7},{6,4},{7,5},{8,10},{9,11},{10,... | collective-permute-start | bytes 786440 | tf_op jit(solution)/shard_map/ppermute | solution.py:269
  122.4 14.6 %collective-permute-start.11 = (bf16[128,1024]{1,0:T(8,128)(2,1)S(1)}, bf16[128,1024]{1,0:T(8,128)(2,1)S(1)}, u32[]{:S(2)}, u32[]{:S(2)}) collective-permute-start(bf16[128,1024]{1,0:T(8,128)(2,1)S(1)} %get-tuple-element.32), channel_id=1, source_target_pairs={{0,3},{1,0},{2,1},{3,2},{4,7},{5,4},{6,5},{7,6},{8,11},{9,8},{10,9... | collective-permute-start | bytes 786440 | tf_op jit(solution)/shard_map/ppermute | solution.py:269
  126.1 1.3 copy-start.11
  130.4 10.5 %all-to-all-start.2 = ((bf16[4,192,128]{2,1,0:T(8,128)(2,1)}), bf16[4,192,128]{2,1,0:T(8,128)(2,1)S(1)}, u32[]{:S(2)}, u32[]{:S(2)}) async-start(bf16[4,192,128]{2,1,0:T(8,128)(2,1)} %bitcast.10), calls=%async_computation.2 | async-start | bytes 393216 | tf_op jit(solution)/shard_map/all_to_all | solution.py:365
